TPU v7x, 32 devices: a whole 2x2x4 slice. The times are simulated.
32 devices in a mesh: row: 8 (over y, x, core), col: 4 (over z).
Axes of the slice: x: 2, y: 2, z: 4, core: 2. Of those that a mesh axis runs over, the one named last changes fastest.
Arguments:
- features: bfloat16 [16384, 256], P('row', 'col'), may hold values from -12 to 12
- tile_vals: bfloat16 [1024, 512, 128], P('row', 'col'), may hold values from 0 to 4, as said below
- tile_src: int32 [8, 512], P('row', 'col'), may hold values from 0 to 15
- row_counts: int32 [8, 128], P('row', 'col'), may hold values from 1 to 6, as said below
Outputs:
- propagated: bfloat16 [16384, 256], P(('row', 'col'))
Inputs may be any that keep to these rules, and one draw needn't show every extreme that they name: `tile_vals`: each entry is zero or a weight between 0.25 and 4. `row_counts`: on every group the 32 counts sum to at most 128; some groups reach 128 exactly.
All inputs are finite; a program needn't handle non-finite values.
Results may differ from a plain program's by a relative error of at most 0.009.
Values may be sent and summed in bfloat16 or wider, within the bound.
No kernel may reach another device: no remote copies, remote signals or barrier semaphores. Data moves between devices by JAX's collectives and lax.ppermute only.
A program may use at most 128 MiB of HBM per device.

v0:
```python
import jax
import jax.numpy as jnp
from jax import lax
from jax.sharding import PartitionSpec as P

ITERS = 3


TELEPORT = 0.1


def slot_block():
    return 64


def slot_layout(counts, tile_max):
    row_ends = jnp.cumsum(counts, dtype=jnp.int32)
    slot_ids = jnp.arange(tile_max, dtype=jnp.int32)
    dest_tiles = jnp.sum(
        (row_ends[None, :] <= slot_ids[:, None]).astype(jnp.int32), axis=1, dtype=jnp.int32
    )
    live_slots = slot_ids < row_ends[-1]
    return (dest_tiles, live_slots, row_ends)


def tile_products(
    tile_vals, sources, dest_tiles, live_slots, source_rows, turn_count, dest_count, block_slots
):
    tile_size = tile_vals.shape[1]
    feat_width = source_rows.shape[1]
    grouped = source_rows.reshape(-1, tile_size, feat_width)

    def one_turn(turn_index, running):
        first_slot = (turn_index * block_slots).astype(jnp.int32)
        tile_block = lax.dynamic_slice_in_dim(tile_vals, first_slot, block_slots, 0)
        picked = jnp.take(
            grouped, lax.dynamic_slice_in_dim(sources, first_slot, block_slots, 0), axis=0
        )
        products = jnp.einsum(
            "tsd,tsf->tdf", tile_block, picked, preferred_element_type=jnp.float32
        )
        keep_mask = lax.dynamic_slice_in_dim(live_slots, first_slot, block_slots, 0)
        products = jnp.where(keep_mask[:, None, None], products, 0.0)
        targets = lax.dynamic_slice_in_dim(dest_tiles, first_slot, block_slots, 0)
        return running.at[targets].add(products, mode="drop")

    running = jnp.zeros((dest_count, tile_size, feat_width), jnp.float32)
    running = lax.fori_loop(0, turn_count, one_turn, running)
    return running.reshape(dest_count * tile_size, feat_width)


def on_device(features, tile_vals, tile_src, row_counts):
    col_index = lax.axis_index("col")
    col_count = lax.axis_size("col")
    tile_max = tile_vals.shape[0]
    tile_size = tile_vals.shape[1]
    dest_count = row_counts.shape[1]
    own_count = features.shape[0] // col_count
    block_slots = slot_block()
    dest_tiles, live_slots, row_ends = slot_layout(row_counts[0], tile_max)
    sources = tile_src[0]
    source_rows = lax.all_gather(features, "col", axis=1, tiled=True)
    own_rows = lax.dynamic_slice_in_dim(source_rows, col_index * own_count, own_count, 0)
    unit_vector = jnp.ones((tile_size,), jnp.bfloat16)
    column_sums = jnp.einsum(
        "tsd,s->td", tile_vals, unit_vector, preferred_element_type=jnp.float32
    )
    column_sums = jnp.where(live_slots[:, None], column_sums, 0.0)
    weight_sums = (
        jnp.zeros((dest_count, tile_size), jnp.float32).at[dest_tiles].add(column_sums, mode="drop")
    )
    degree = 1.0 + lax.psum_scatter(
        weight_sums.reshape(-1).astype(jnp.bfloat16), "row", scatter_dimension=0, tiled=True
    ).astype(jnp.float32)
    turn_count = tile_max // block_slots
    restart = TELEPORT * own_rows.astype(jnp.float32)
    iterate = own_rows
    for iteration in range(ITERS):
        if iteration > 0:
            source_rows = lax.all_gather(iterate, "col", axis=0, tiled=True)
        term_rows = tile_products(
            tile_vals,
            sources,
            dest_tiles,
            live_slots,
            source_rows,
            turn_count,
            dest_count,
            block_slots,
        )
        summed = lax.psum_scatter(
            term_rows.astype(jnp.bfloat16), "row", scatter_dimension=0, tiled=True
        ).astype(jnp.float32)
        iterate = (
            (1.0 - TELEPORT) * (summed + iterate.astype(jnp.float32)) / degree[:, None] + restart
        ).astype(jnp.bfloat16)
    return iterate


def solution(mesh):
    placed = (P("row", "col"), P("row", "col", None), P("row", "col"), P("row", "col"))
    return jax.shard_map(
        on_device, mesh=mesh, in_specs=placed, out_specs=P(("row", "col"), None), check_vma=False
    )
```

profile of v0, /device:TPU:0, one launch (start us, length us, event | category | flops | bytes accessed | tf_op | source)
XLA Modules:
  0.0 429.4 jit_solution(4328440572961907524)
XLA Ops:
  8.8 6.3 %copy.33 = bf16[128,128,128]{1,2,0:T(8,128)(2,1)} copy(bf16[128,128,128]{2,1,0:T(8,128)(2,1)} %param.13) | data formatting | bytes 8388608 | tf_op jit(solution)/shard_map/while | solution.py:48
  16.0 23.6 %all-gather.4.cloned.1.call-done = bf16[2048,256]{0,1:T(8,128)(2,1)} async-done(((bf16[2048,64]{0,1:T(8,128)(2,1)}), bf16[2048,256]{0,1:T(8,128)(2,1)}) %all-gather.4.cloned.1.call-update) | async-done | bytes 1048592 | tf_op jit(solution)/shard_map/all_gather | solution.py:62
  43.5 57.0 %while.39 = (s32[]{:T(128)}, f32[32,128,256]{2,1,0:T(8,128)}, s32[128]{0:T(128)S(1)}, pred[128]{0:T(512)(128)(4,1)S(1)}, bf16[128,128,128]{1,2,0:T(8,128)(2,1)},...) while((s32[]{:T(128)}, f32[32,128,256]{2,1,0:T(8,128)}, ...), condition=%wide.region_4.6_spmd, body=%wide.region_2.5_spmd.sunk | while | flops 543163968 | bytes 48240872 | solution.py:48
  46.4 7.4 %broadcast_select_fusion.6 = f32[64,128,256]{2,1,0:T(8,128)} fusion(pred[64]{0:T(512)(128)(4,1)S(1)} %dynamic_slice.117, bf16[64,128,256]{2,1,0:T(8,128)(2,1)} %gather_fusion, pred[64]{0:T(512)(128)(4,1)S(1)} %get-tuple-element.635, bf16[128,128,128]{1,2,0:T(8,128)(2,1)} %get-tuple-element.680, s32[]{:T(128)S(6)} %select_n.154), kind=kOutput, calls=%fused_computation.9.clone.1 | convolution fusion | flops 541065216 | bytes 14680196 | tf_op jit(solution)/shard_map/while/body/eval_jaxpr/tsd,tsf->tdf/dot_general | solution.py:39
  53.9 18.4 %scatter_fusion = f32[32,128,256]{2,1,0:T(8,128)} fusion(f32[32,128,256]{2,1,0:T(8,128)} %get-tuple-element.666, s32[64]{0:T(128)S(1)} %compare_select_fusion.13, f32[64,128,256]{2,1,0:T(8,128)} %broadcast_select_fusion.6), kind=kCustom, calls=%fused_computation.3.clone.1 | custom fusion | flops 2097152 | bytes 25166080 | tf_op jit(solution)/shard_map/while/body/eval_jaxpr/scatter-add | solution.py:45
  75.3 7.4 %broadcast_select_fusion.6 = f32[64,128,256]{2,1,0:T(8,128)} fusion(pred[64]{0:T(512)(128)(4,1)S(1)} %dynamic_slice.117, bf16[64,128,256]{2,1,0:T(8,128)(2,1)} %gather_fusion, pred[64]{0:T(512)(128)(4,1)S(1)} %get-tuple-element.635, bf16[128,128,128]{1,2,0:T(8,128)(2,1)} %get-tuple-element.680, s32[]{:T(128)S(6)} %select_n.154), kind=kOutput, calls=%fused_computation.9.clone.1 | convolution fusion | flops 541065216 | bytes 14680196 | tf_op jit(solution)/shard_map/while/body/eval_jaxpr/tsd,tsf->tdf/dot_general | solution.py:39
  82.7 17.8 %scatter_fusion = f32[32,128,256]{2,1,0:T(8,128)} fusion(f32[32,128,256]{2,1,0:T(8,128)} %get-tuple-element.666, s32[64]{0:T(128)S(1)} %compare_select_fusion.13, f32[64,128,256]{2,1,0:T(8,128)} %broadcast_select_fusion.6), kind=kCustom, calls=%fused_computation.3.clone.1 | custom fusion | flops 2097152 | bytes 25166080 | tf_op jit(solution)/shard_map/while/body/eval_jaxpr/scatter-add | solution.py:45
  111.3 13.7 %all-reduce = bf16[4096]{0:T(1024)(128)(2,1)S(1)} all-reduce(bf16[4096]{0:T(1024)(128)(2,1)S(1)} %convert_bitcast_fusion), channel_id=3, replica_groups=mesh['row'=8,'col'=4] {'row'}, use_global_device_ids=true, to_apply=%region_7.9.clone | all-reduce | flops 4096 | bytes 16384
  125.1 21.8 %reduce-scatter.4.cloned.1.call-done = bf16[512,256]{0,1:T(8,128)(2,1)} async-done(((bf16[4096,256]{0,1:T(8,128)(2,1)}), bf16[512,256]{0,1:T(8,128)(2,1)}) %reduce-scatter.4.cloned.1.call-update) | async-done | bytes 262160 | tf_op jit(solution)/shard_map/reduce_scatter | solution.py:91
  148.7 28.0 %all-gather.6.cloned.1.call-done = bf16[2048,256]{0,1:T(8,128)(2,1)} async-done(((bf16[512,256]{0,1:T(8,128)(2,1)}), bf16[2048,256]{0,1:T(8,128)(2,1)}) %all-gather.6.cloned.1.call-update) | async-done | bytes 1048592 | tf_op jit(solution)/shard_map/all_gather | solution.py:80
  180.7 56.7 %while.40 = (s32[]{:T(128)}, f32[32,128,256]{2,1,0:T(8,128)}, s32[128]{0:T(128)S(1)}, pred[128]{0:T(512)(128)(4,1)S(1)}, bf16[128,128,128]{1,2,0:T(8,128)(2,1)},...) while((s32[]{:T(128)}, f32[32,128,256]{2,1,0:T(8,128)}, ...), condition=%wide.region_10.12_spmd, body=%wide.region_8.11_spmd.sunk | while | flops 543163968 | bytes 48240872 | solution.py:48
  183.6 7.4 %broadcast_select_fusion.7 = f32[64,128,256]{2,1,0:T(8,128)} fusion(pred[64]{0:T(512)(128)(4,1)S(1)} %dynamic_slice.120, bf16[64,128,256]{2,1,0:T(8,128)(2,1)} %gather_fusion.1, pred[64]{0:T(512)(128)(4,1)S(1)} %get-tuple-element.644, bf16[128,128,128]{1,2,0:T(8,128)(2,1)} %get-tuple-element.713, s32[]{:T(128)S(6)} %select_n.158), kind=kOutput, calls=%fused_computation.21.clone.1 | convolution fusion | flops 541065216 | bytes 14680196 | tf_op jit(solution)/shard_map/while/body/eval_jaxpr/tsd,tsf->tdf/dot_general | solution.py:39
  191.1 18.5 %scatter_fusion.1 = f32[32,128,256]{2,1,0:T(8,128)} fusion(f32[32,128,256]{2,1,0:T(8,128)} %get-tuple-element.699, s32[64]{0:T(128)S(1)} %compare_select_fusion.14, f32[64,128,256]{2,1,0:T(8,128)} %broadcast_select_fusion.7), kind=kCustom, calls=%fused_computation.4.clone.1 | custom fusion | flops 2097152 | bytes 25166080 | tf_op jit(solution)/shard_map/while/body/eval_jaxpr/scatter-add | solution.py:45
  212.5 7.4 %broadcast_select_fusion.7 = f32[64,128,256]{2,1,0:T(8,128)} fusion(pred[64]{0:T(512)(128)(4,1)S(1)} %dynamic_slice.120, bf16[64,128,256]{2,1,0:T(8,128)(2,1)} %gather_fusion.1, pred[64]{0:T(512)(128)(4,1)S(1)} %get-tuple-element.644, bf16[128,128,128]{1,2,0:T(8,128)(2,1)} %get-tuple-element.713, s32[]{:T(128)S(6)} %select_n.158), kind=kOutput, calls=%fused_computation.21.clone.1 | convolution fusion | flops 541065216 | bytes 14680196 | tf_op jit(solution)/shard_map/while/body/eval_jaxpr/tsd,tsf->tdf/dot_general | solution.py:39
  219.9 17.5 %scatter_fusion.1 = f32[32,128,256]{2,1,0:T(8,128)} fusion(f32[32,128,256]{2,1,0:T(8,128)} %get-tuple-element.699, s32[64]{0:T(128)S(1)} %compare_select_fusion.14, f32[64,128,256]{2,1,0:T(8,128)} %broadcast_select_fusion.7), kind=kCustom, calls=%fused_computation.4.clone.1 | custom fusion | flops 2097152 | bytes 25166080 | tf_op jit(solution)/shard_map/while/body/eval_jaxpr/scatter-add | solution.py:45
  239.9 2.9 copy.41
  242.9 40.9 %reduce-scatter.6.cloned.1.call-done = bf16[512,256]{0,1:T(8,128)(2,1)} async-done(((bf16[4096,256]{0,1:T(8,128)(2,1)}), bf16[512,256]{0,1:T(8,128)(2,1)}) %reduce-scatter.6.cloned.1.call-update) | async-done | bytes 262160 | tf_op jit(solution)/shard_map/reduce_scatter | solution.py:91
  285.8 27.8 %all-gather.8.cloned.1.call-done = bf16[2048,256]{0,1:T(8,128)(2,1)} async-done(((bf16[512,256]{0,1:T(8,128)(2,1)}), bf16[2048,256]{0,1:T(8,128)(2,1)}) %all-gather.8.cloned.1.call-update) | async-done | bytes 1048592 | tf_op jit(solution)/shard_map/all_gather | solution.py:80
  317.6 56.7 %while.41 = (s32[]{:T(128)}, f32[32,128,256]{2,1,0:T(8,128)}, s32[128]{0:T(128)S(1)}, pred[128]{0:T(512)(128)(4,1)S(1)}, bf16[128,128,128]{1,2,0:T(8,128)(2,1)},...) while((s32[]{:T(128)}, f32[32,128,256]{2,1,0:T(8,128)}, ...), condition=%wide.region_14.16_spmd, body=%wide.region_12.15_spmd.sunk | while | flops 543163968 | bytes 48240872 | solution.py:48
  320.5 7.4 %broadcast_select_fusion.8 = f32[64,128,256]{2,1,0:T(8,128)} fusion(pred[64]{0:T(512)(128)(4,1)S(1)} %dynamic_slice.123, bf16[64,128,256]{2,1,0:T(8,128)(2,1)} %gather_fusion.2, pred[64]{0:T(512)(128)(4,1)S(1)} %get-tuple-element.653, bf16[128,128,128]{1,2,0:T(8,128)(2,1)} %get-tuple-element.746, s32[]{:T(128)S(6)} %select_n.162), kind=kOutput, calls=%fused_computation.33.clone.1 | convolution fusion | flops 541065216 | bytes 14680196 | tf_op jit(solution)/shard_map/while/body/eval_jaxpr/tsd,tsf->tdf/dot_general | solution.py:39
  327.9 18.5 %scatter_fusion.2 = f32[32,128,256]{2,1,0:T(8,128)} fusion(f32[32,128,256]{2,1,0:T(8,128)} %get-tuple-element.732, s32[64]{0:T(128)S(1)} %compare_select_fusion.15, f32[64,128,256]{2,1,0:T(8,128)} %broadcast_select_fusion.8), kind=kCustom, calls=%fused_computation.5.clone.1 | custom fusion | flops 2097152 | bytes 25166080 | tf_op jit(solution)/shard_map/while/body/eval_jaxpr/scatter-add | solution.py:45
  349.3 7.4 %broadcast_select_fusion.8 = f32[64,128,256]{2,1,0:T(8,128)} fusion(pred[64]{0:T(512)(128)(4,1)S(1)} %dynamic_slice.123, bf16[64,128,256]{2,1,0:T(8,128)(2,1)} %gather_fusion.2, pred[64]{0:T(512)(128)(4,1)S(1)} %get-tuple-element.653, bf16[128,128,128]{1,2,0:T(8,128)(2,1)} %get-tuple-element.746, s32[]{:T(128)S(6)} %select_n.162), kind=kOutput, calls=%fused_computation.33.clone.1 | convolution fusion | flops 541065216 | bytes 14680196 | tf_op jit(solution)/shard_map/while/body/eval_jaxpr/tsd,tsf->tdf/dot_general | solution.py:39
  356.8 17.5 %scatter_fusion.2 = f32[32,128,256]{2,1,0:T(8,128)} fusion(f32[32,128,256]{2,1,0:T(8,128)} %get-tuple-element.732, s32[64]{0:T(128)S(1)} %compare_select_fusion.15, f32[64,128,256]{2,1,0:T(8,128)} %broadcast_select_fusion.8), kind=kCustom, calls=%fused_computation.5.clone.1 | custom fusion | flops 2097152 | bytes 25166080 | tf_op jit(solution)/shard_map/while/body/eval_jaxpr/scatter-add | solution.py:45
  379.7 40.9 %reduce-scatter.8.cloned.1.call-done = bf16[512,256]{0,1:T(8,128)(2,1)} async-done(((bf16[4096,256]{0,1:T(8,128)(2,1)}), bf16[512,256]{0,1:T(8,128)(2,1)}) %reduce-scatter.8.cloned.1.call-update) | async-done | bytes 262160 | tf_op jit(solution)/shard_map/reduce_scatter | solution.py:91
  (79 shorter events, 56.6 us)
Async XLA Ops:
  6.5 33.1 %all-gather.4.cloned.1.call-start = ((), (), s32[]{:S(2)}) async-start(), calls=%async_computation.3 | async-start | bytes 1310720 | tf_op jit(solution)/shard_map/all_gather | solution.py:62
  7.3 139.6 %reduce-scatter.4.cloned.1.call-start = ((), (), s32[]{:S(2)}) async-start(), calls=%async_computation.4 | async-start | bytes 2359296 | tf_op jit(solution)/shard_map/reduce_scatter | solution.py:91
  15.2 28.3 %copy-start.3 = (s32[1,128]{1,0:T(1,128)S(1)}, s32[1,128]{1,0:T(1,128)}, u32[]{:S(2)}) copy-start(s32[1,128]{1,0:T(1,128)} %param.14) | copy-start | bytes 1540
  103.0 3.0 copy-start.4
  105.9 40.9 %copy-start = (bf16[2048,256]{0,1:T(8,128)(2,1)S(1)}, bf16[2048,256]{0,1:T(8,128)(2,1)}, u32[]{:S(2)}) copy-start(bf16[2048,256]{0,1:T(8,128)(2,1)} %all-gather.4.cloned.1.call-done) | copy-start | bytes 3145732
  105.9 70.8 %all-gather.6.cloned.1.call-start = ((), (), s32[]{:S(2)}) async-start(), calls=%async_computation.5 | async-start | bytes 1310720 | tf_op jit(solution)/shard_map/all_gather | solution.py:80
  148.7 135.1 %reduce-scatter.6.cloned.1.call-start = ((), (), s32[]{:S(2)}) async-start(), calls=%async_computation.6 | async-start | bytes 2359296 | tf_op jit(solution)/shard_map/reduce_scatter | solution.py:91
  239.9 43.9 %copy-start.2 = (bf16[512,256]{0,1:T(8,128)(2,1)S(1)}, bf16[512,256]{0,1:T(8,128)(2,1)}, u32[]{:S(2)}) copy-start(bf16[512,256]{0,1:T(8,128)(2,1)} %fusion.30) | copy-start | bytes 786436
  242.9 70.8 %all-gather.8.cloned.1.call-start = ((), (), s32[]{:S(2)}) async-start(), calls=%async_computation.7 | async-start | bytes 1310720 | tf_op jit(solution)/shard_map/all_gather | solution.py:80
  285.6 135.0 %reduce-scatter.8.cloned.1.call-start = ((), (), s32[]{:S(2)}) async-start(), calls=%async_computation.8 | async-start | bytes 2359296 | tf_op jit(solution)/shard_map/reduce_scatter | solution.py:91
  376.8 43.8 %copy-start.1 = (bf16[512,256]{0,1:T(8,128)(2,1)S(1)}, bf16[512,256]{0,1:T(8,128)(2,1)}, u32[]{:S(2)}) copy-start(bf16[512,256]{0,1:T(8,128)(2,1)} %fusion.31) | copy-start | bytes 786436
Sparse Core Ops, SparseCore 0:
  8.9 30.6 all-gather.3
  106.1 40.7 reduce-scatter.3
  148.8 27.9 all-gather.5
  243.0 40.7 reduce-scatter.5
  285.7 27.9 all-gather.7
  379.9 40.6 reduce-scatter.7
where the time goes:
time: 430 us; the launch traced here: 429 us
  waiting for transfers between devices  184 us (43%)
  other arithmetic  123 us (29%)
  matrix products  47.1 us (11%)
  local copies, waits for them, and re-layouts  46.6 us (11%)
  between operations  14.3 us (3%)
  blocking collectives  13.7 us (3%)
    scatter-add x6, other arithmetic, one_turn(): return running.at[targets].add(products, mode='drop')  108 us
    reduce_scatter x3, waiting for transfers between devices, on_device(): lax.psum_scatter(term_rows.astype(jnp.bfloat16), 'row', scatter_dimension...  104 us
    all_gather x2, waiting for transfers between devices, on_device(): source_rows = lax.all_gather(iterate, 'col', axis=0, tiled=True)  55.9 us
    dot_general x6, matrix products, one_turn(): jnp.einsum('tsd,tsf->tdf', tile_block, picked, preferred_element_type=jnp...  44.2 us
    all_gather x1, waiting for transfers between devices, on_device(): source_rows = lax.all_gather(features, 'col', axis=1, tiled=True)  23.6 us
    gather x6, local copies, waits for them, and re-layouts, one_turn(): jnp.take(grouped, lax.dynamic_slice_in_dim(sources, first_slot, block_slo...  16.5 us
    unnamed x1, blocking collectives  13.7 us
    while x4, local copies, waits for them, and re-layouts, tile_products(): running = lax.fori_loop(0, turn_count, one_turn, running)  10.8 us
  transfers between devices with their start and end apart: 6, of which 6 were waited for; matrix products, arithmetic and copies ran while one was open for 3% of the time, Pallas kernels for 0%

commit v1 on v0

v1 whole, which is shorter than its diff:
```python
import functools

import jax
import jax.numpy as jnp
from jax import lax
from jax.experimental import pallas as pl
from jax.experimental.pallas import tpu as pltpu
from jax.sharding import PartitionSpec as P

ITERS = 3


TELEPORT = 0.1


CHUNKS = 2


UNROLL = 8


def vmem(count):
    return [pl.BlockSpec(memory_space=pltpu.VMEM)] * count


def smem(count):
    return [pl.BlockSpec(memory_space=pltpu.SMEM)] * count


def pair_capacity(tile_max, dest_count):
    most = (tile_max + dest_count // 2) // 2
    return -(-most // UNROLL) * UNROLL


def prepare_kernel(
    tiles_per_owner,
    place_ref,
    src_ref,
    count_ref,
    tile_ref,
    turned_ref,
    weight_ref,
    slot_ref,
    first_ref,
    second_ref,
    row_ref,
    go_on_ref,
    turns_ref,
):
    tile_max, tile_size, _ = tile_ref.shape
    dest_count = count_ref.shape[1]
    capacity = slot_ref.shape[1]
    zero_tile = place_ref[2]
    my_row = place_ref[0]

    for half in range(2):

        def one_dest(dest, carry, half=half):
            start, used = carry
            owner = dest // tiles_per_owner
            relative = lax.bitwise_xor(owner, my_row)
            count = count_ref[0, dest]
            mine = lax.bitwise_and(relative, 1) == half
            pairs = jnp.where(mine, (count + 1) // 2, 0)
            out_row = (
                (relative // 2) * tiles_per_owner + dest - owner * tiles_per_owner
            ) * tile_size

            def one_pair(pair, carry):
                at = used + pair
                slot = start + 2 * pair
                next_slot = jnp.minimum(slot + 1, tile_max - 1)
                slot_ref[half, at] = slot
                first_ref[half, at] = src_ref[0, slot] * tile_size
                second_ref[half, at] = (
                    jnp.where(2 * pair + 1 < count, src_ref[0, next_slot], zero_tile) * tile_size
                )
                row_ref[half, at] = out_row
                go_on_ref[half, at] = jnp.where(pair > 0, 1, 0)
                return carry

            lax.fori_loop(0, pairs, one_pair, 0)
            return start + count, used + pairs

        _, used = lax.fori_loop(0, dest_count, one_dest, (jnp.int32(0), jnp.int32(0)))
        turns = (used + UNROLL - 1) // UNROLL
        last_row = row_ref[half, used - 1]

        def one_pad(at, carry, half=half, last_row=last_row):
            slot_ref[half, at] = 0
            first_ref[half, at] = zero_tile * tile_size
            second_ref[half, at] = zero_tile * tile_size
            row_ref[half, at] = last_row
            go_on_ref[half, at] = 1
            return carry

        lax.fori_loop(used, turns * UNROLL, one_pad, 0)
        turns_ref[half] = turns

    def one_turn(dest, start):
        count = count_ref[0, dest]
        owner = dest // tiles_per_owner
        relative = lax.bitwise_xor(owner, my_row)

        def one_slot(slot, running):
            tile = tile_ref[slot]
            turned_ref[slot] = tile.T
            return running + jnp.sum(tile.astype(jnp.float32), axis=0, keepdims=True)

        total = lax.fori_loop(
            start, start + count, one_slot, jnp.zeros((1, tile_size), jnp.float32)
        )
        weight_ref[relative, pl.ds(dest - owner * tiles_per_owner, 1), :] = total
        return start + count

    live = lax.fori_loop(0, dest_count, one_turn, jnp.int32(0))

    def one_dead(slot, carry):
        turned_ref[slot] = jnp.zeros((tile_size, tile_size), turned_ref.dtype)
        return carry

    lax.fori_loop(live, tile_max, one_dead, 0)


def prepare(place, tile_src, row_counts, tile_vals, row_size, tiles_per_owner):
    tile_max, tile_size, _ = tile_vals.shape
    capacity = pair_capacity(tile_max, row_counts.shape[1])
    listing = jax.ShapeDtypeStruct((2, capacity), jnp.int32)
    return pl.pallas_call(
        functools.partial(prepare_kernel, tiles_per_owner),
        out_shape=[
            jax.ShapeDtypeStruct(tile_vals.shape, tile_vals.dtype),
            jax.ShapeDtypeStruct((row_size, tiles_per_owner, tile_size), jnp.float32),
            listing,
            listing,
            listing,
            listing,
            listing,
            jax.ShapeDtypeStruct((2,), jnp.int32),
        ],
        in_specs=smem(3) + vmem(1),
        out_specs=vmem(2) + smem(6),
        compiler_params=pltpu.CompilerParams(vmem_limit_bytes=24 * 2**20),
        name="prepare",
    )(place, tile_src, row_counts, tile_vals)


def product_kernel(
    half,
    packed,
    blocks,
    place_ref,
    slot_ref,
    first_ref,
    second_ref,
    row_ref,
    go_on_ref,
    turns_ref,
    turned_ref,
    *refs,
):
    block_refs = refs[: 2 * blocks - 1]
    out_ref = refs[2 * blocks - 1]
    own_ref = refs[2 * blocks] if packed else None
    held_ref = refs[-2 if packed else -1]
    staged_ref = refs[-1] if packed else held_ref
    col = place_ref[1]
    rows, width = block_refs[0].shape
    tile_size = turned_ref.shape[1]

    def put(block, ref):
        staged_ref[pl.ds(pl.multiple_of(block * rows, rows), rows), :] = ref[...]

    put(col, block_refs[0])
    for step in range(1, blocks):
        pl.when(col >= step)(functools.partial(put, col - step, block_refs[2 * step - 1]))
        pl.when(col + step < blocks)(functools.partial(put, col + step, block_refs[2 * step]))
    if packed:
        piece = width // blocks
        for group in range(blocks):
            lanes = slice(group * piece, (group + 1) * piece)
            held_ref[group * rows : (group + 1) * rows, :] = jnp.concatenate(
                [staged_ref[b * rows : (b + 1) * rows, lanes] for b in range(blocks)], axis=1
            )
        own_ref[...] = held_ref[pl.ds(pl.multiple_of(col * rows, rows), rows), :]
    held_ref[blocks * rows :, :] = jnp.zeros((tile_size, width), held_ref.dtype)

    tile_max = turned_ref.shape[0]

    def one_turn(turn, running):
        for step in range(UNROLL):
            at = turn * UNROLL + step
            slot = slot_ref[half, at]
            left = jnp.concatenate(
                [turned_ref[slot], turned_ref[jnp.minimum(slot + 1, tile_max - 1)]], axis=1
            )
            first = pl.multiple_of(first_ref[half, at], tile_size)
            second = pl.multiple_of(second_ref[half, at], tile_size)
            right = jnp.concatenate(
                [held_ref[pl.ds(first, tile_size), :], held_ref[pl.ds(second, tile_size), :]],
                axis=0,
            )
            term = jnp.dot(left, right, preferred_element_type=jnp.float32)
            running = running * go_on_ref[half, at].astype(jnp.float32) + term
            out_row = pl.multiple_of(row_ref[half, at], tile_size)
            out_ref[pl.ds(out_row, tile_size), :] = running.astype(out_ref.dtype)
        return running

    lax.fori_loop(0, turns_ref[half], one_turn, jnp.zeros((tile_size, width), jnp.float32))


def product(half, place, lists, turned, gathered, blocks, row_size, packed):
    rows, width = gathered[0].shape
    tile_size = turned.shape[1]
    out_shape = [jax.ShapeDtypeStruct((row_size // 2 * rows, width), jnp.bfloat16)]
    scratch = [pltpu.VMEM((blocks * rows + tile_size, width), jnp.bfloat16)]
    if packed:
        out_shape.append(jax.ShapeDtypeStruct((rows, width), jnp.bfloat16))
        scratch.append(pltpu.VMEM((blocks * rows, width), jnp.bfloat16))
    return pl.pallas_call(
        functools.partial(product_kernel, half, packed, blocks),
        out_shape=out_shape,
        in_specs=smem(1 + len(lists)) + vmem(1 + len(gathered)),
        out_specs=vmem(len(out_shape)),
        scratch_shapes=scratch,
        compiler_params=pltpu.CompilerParams(vmem_limit_bytes=24 * 2**20),
        name="product",
    )(place, *lists, turned, *gathered)


def gather_line(block, size):
    found = [block]
    from_left = from_right = block
    for step in range(1, size):
        from_left = lax.ppermute(from_left, "col", [(i, i + 1) for i in range(step - 1, size - 1)])
        from_right = lax.ppermute(from_right, "col", [(i, i - 1) for i in range(1, size - step + 1)])
        found += [from_left, from_right]
    return found


def swap(block, bit, row_size):
    return lax.ppermute(block, "row", [(i, i ^ (1 << bit)) for i in range(row_size)])


def halve(state, bits, order, row_size):
    bits = list(bits)
    for bit in order:
        axis = bits.index(bit)
        send = lax.index_in_dim(state, 1, axis, keepdims=False).astype(jnp.bfloat16)
        keep = lax.index_in_dim(state, 0, axis, keepdims=False)
        state = keep + swap(send, bit, row_size).astype(jnp.float32)
        bits.remove(bit)
    return state


def on_device(features, tile_vals, tile_src, row_counts):
    row_size = lax.axis_size("row")
    blocks = lax.axis_size("col")
    my_row = lax.axis_index("row").astype(jnp.int32)
    my_col = lax.axis_index("col").astype(jnp.int32)
    tile_size = tile_vals.shape[1]
    dest_count = row_counts.shape[1]
    rows = features.shape[0] // blocks
    source_tiles = features.shape[0] // tile_size
    width = features.shape[1] * blocks // CHUNKS
    piece = features.shape[1] // CHUNKS
    tiles_per_owner = dest_count // row_size
    row_bits = row_size.bit_length() - 1
    chip_bits = list(range(row_bits - 1, 0, -1))
    place = jnp.stack([my_row, my_col, jnp.int32(source_tiles)])

    parts = features.reshape(blocks, rows, CHUNKS, piece).transpose(2, 1, 0, 3)
    parts = parts.reshape(CHUNKS, rows, blocks * piece)
    gathered = [gather_line(parts[chunk], blocks) for chunk in range(CHUNKS)]

    turned, weight_sums, *lists = prepare(
        place, tile_src, row_counts, tile_vals, row_size, tiles_per_owner
    )
    all_bits = [0] + chip_bits
    weights = weight_sums
    state = weights.reshape((2,) * row_bits + (tiles_per_owner, tile_size))
    bits = list(range(row_bits - 1, -1, -1))
    for bit in [0] + chip_bits:
        axis = bits.index(bit)
        send = lax.index_in_dim(state, 1, axis, keepdims=False)
        state = lax.index_in_dim(state, 0, axis, keepdims=False) + swap(send, bit, row_size)
        bits.remove(bit)
    scale = ((1.0 - TELEPORT) / (1.0 + state)).reshape(rows, 1)
    scale = jnp.broadcast_to(scale, (rows, width))

    iterates = [None] * CHUNKS
    restarts = [None] * CHUNKS
    for iteration in range(ITERS):
        for chunk in range(CHUNKS):
            packed = iteration == 0
            sent, *rest = product(
                1, place, lists, turned, gathered[chunk], blocks, row_size, packed
            )
            if packed:
                iterates[chunk] = rest[0]
                restarts[chunk] = TELEPORT * rest[0].astype(jnp.float32)
            other = swap(sent, 0, row_size)
            kept = product(0, place, lists, turned, gathered[chunk], blocks, row_size, packed)[0]
            shape = (2,) * len(chip_bits) + (2, rows // 2, width)
            state = kept.astype(jnp.float32) + other.astype(jnp.float32)
            state = state.reshape(shape)
            summed = []
            for half in range(2):
                turn = half % max(len(chip_bits), 1)
                order = chip_bits[turn:] + chip_bits[:turn]
                summed.append(
                    halve(state[..., half, :, :], chip_bits, order, row_size)
                )
            summed = jnp.concatenate(summed, axis=0)
            iterates[chunk] = (
                scale * (summed + iterates[chunk].astype(jnp.float32)) + restarts[chunk]
            ).astype(jnp.bfloat16)
            if iteration + 1 < ITERS:
                gathered[chunk] = gather_line(iterates[chunk], blocks)
    out = jnp.stack(iterates).reshape(CHUNKS, rows, blocks, piece).transpose(1, 2, 0, 3)
    return out.reshape(rows, CHUNKS * width)


def solution(mesh):
    placed = (P("row", "col"), P("row", "col", None), P("row", "col"), P("row", "col"))
    return jax.shard_map(
        on_device, mesh=mesh, in_specs=placed, out_specs=P(("row", "col"), None), check_vma=False
    )
```

time: 430 us -> 246 us (0.57)
  other arithmetic: 123 us -> 1.99 us
  starting transfers between devices: 0.39 us -> 93 us
  waiting for transfers between devices: 184 us -> 108 us
  matrix products: 47.1 us -> 0 us
  local copies, waits for them, and re-layouts: 46.6 us -> 13 us
  Pallas kernels: 0 us -> 30.7 us
  blocking collectives: 13.7 us -> 0 us
  between operations: 14.3 us -> 1.1 us
    scatter-add x7 -> x0, other arithmetic: 109 us -> none  [the longest x6 108 us: one_turn(): return running.at[targets].add(products, mode='drop')]
    ppermute x0 -> x69, waiting for transfers between devices: none -> 108 us  [the longest x18 73.9 us: gather_line(): lax.ppermute(from_right, 'col', [(i, i - 1) for i in range(1, size - step...]
    reduce_scatter x3 -> x0, waiting for transfers between devices: 104 us -> none  [on_device(): lax.psum_scatter(term_rows.astype(jnp.bfloat16), 'row', scatter_dimension...]
    ppermute x0 -> x69, starting transfers between devices: none -> 93 us  [the longest x33 45.6 us: swap(): lax.ppermute(block, 'row', [(i, i ^ 1 << bit) for i in range(row_size)])]
    all_gather x3 -> x0, waiting for transfers between devices: 79.5 us -> none  [the longest x2 55.9 us: on_device(): source_rows = lax.all_gather(iterate, 'col', axis=0, tiled=True)]
    dot_general x7 -> x0, matrix products: 47.1 us -> none  [the longest x6 44.2 us: one_turn(): jnp.einsum('tsd,tsf->tdf', tile_block, picked, preferred_element_type=jnp...]
    pallas_call x0 -> x13, Pallas kernels: none -> 30.7 us  [the longest x12 22.5 us: product(): pl.pallas_call(functools.partial(product_kernel, half, packed, blocks), o...]
    gather x6 -> x0, local copies, waits for them, and re-layouts: 16.5 us -> none  [one_turn(): jnp.take(grouped, lax.dynamic_slice_in_dim(sources, first_slot, block_slo...]
  transfers between devices with their start and end apart: 6 -> 69, of which waited for: 6 -> 38; matrix products, arithmetic and copies ran while one was open for 3% -> 1% of each run, Pallas kernels for 0% -> 10%
where the time goes in v1:
time: 246 us; the launch traced here: 248 us
  waiting for transfers between devices  108 us (44%)
  starting transfers between devices  93 us (38%)
  Pallas kernels  30.7 us (12%)
  local copies, waits for them, and re-layouts  13 us (5%)
    ppermute x18, waiting for transfers between devices, gather_line(): lax.ppermute(from_right, 'col', [(i, i - 1) for i in range(1, size - step...  73.9 us
    ppermute x33, starting transfers between devices, swap(): lax.ppermute(block, 'row', [(i, i ^ 1 << bit) for i in range(row_size)])  45.6 us
    ppermute x33, waiting for transfers between devices, swap(): lax.ppermute(block, 'row', [(i, i ^ 1 << bit) for i in range(row_size)])  29.4 us
    ppermute x18, starting transfers between devices, gather_line(): lax.ppermute(from_left, 'col', [(i, i + 1) for i in range(step - 1, size...  24.2 us
    ppermute x18, starting transfers between devices, gather_line(): lax.ppermute(from_right, 'col', [(i, i - 1) for i in range(1, size - step...  23.1 us
    pallas_call x12, Pallas kernels, product(): pl.pallas_call(functools.partial(product_kernel, half, packed, blocks), o...  22.5 us
    unnamed x12, local copies, waits for them, and re-layouts  9.84 us
    pallas_call x1, Pallas kernels, prepare(): pl.pallas_call(functools.partial(prepare_kernel, tiles_per_owner), out_sh...  8.17 us
  transfers between devices with their start and end apart: 69, of which 38 were waited for; matrix products, arithmetic and copies ran while one was open for 1% of the time, Pallas kernels for 10%

profile of v1, /device:TPU:0, one launch (start us, length us, event | category | flops | bytes accessed | tf_op | source)
XLA Modules:
  0.0 247.8 jit_solution(15179319637214636924)
XLA Ops:
  1.4 4.9 %collective-permute-start.3 = (bf16[512,128]{1,0:T(8,128)(2,1)S(1)}, bf16[512,128]{1,0:T(8,128)(2,1)S(1)}, u32[]{:S(2)}, u32[]{:S(2)}) collective-permute-start(bf16[512,128]{1,0:T(8,128)(2,1)S(1)} %copy.49.refs_0_), channel_id=1, source_target_pairs={{0,1},{1,2},{2,3},{4,5},{5,6},{6,7},{8,9},{9,10},{10,11},{12,13},{... | collective-permute-start | bytes 393224 | tf_op jit(solution)/shard_map/ppermute | solution.py:235
  11.2 8.2 %prepare.1 = (bf16[128,128,128]{2,1,0:T(8,128)(2,1)S(1)}, f32[8,4,128]{2,1,0:T(4,128)S(1)}, s32[2,72]{1,0:T(2,128)S(1)}, s32[2,72]{1,0:T(2,128)S(1)}, s32[2,72]{...) custom-call(s32[3]{0:T(128)S(1)} %pad_add_fusion.place_ref, s32[1,128]{1,0:T(1,128)S(1)} %copy-done.4, ...), custom_call_target="tpu_custom_call" | custom-call | tf_op jit(solution)/shard_map/prepare/pallas_call | solution.py:129
  24.2 9.4 %collective-permute-done.6.refs_4_ = bf16[512,128]{1,0:T(8,128)(2,1)S(1)} collective-permute-done((bf16[512,128]{1,0:T(8,128)(2,1)S(1)}, bf16[512,128]{1,0:T(8,128)(2,1)S(1)}, u32[]{:S(2)}, u32[]{:S(2)}) %collective-permute-start.6) | collective-permute-done | bytes 131104 | tf_op jit(solution)/shard_map/ppermute | solution.py:236
  34.9 4.4 %collective-permute-start.1 = (f32[2,4,128]{2,1,0:T(4,128)S(1)}, f32[2,4,128]{2,1,0:T(4,128)S(1)}, u32[]{:S(2)}, u32[]{:S(2)}) collective-permute-start(f32[2,4,128]{2,1,0:T(4,128)S(1)} %slice_bitcast_fusion.20), channel_id=1, source_target_pairs={{0,16},{4,20},{8,24},{12,28},{16,0},{20,4},{24,8},{28,12},{1,17},{... | collective-permute-start | bytes 12296 | tf_op jit(solution)/shard_map/ppermute | solution.py:242
  39.4 4.6 %collective-permute-start.36 = (bf16[512,128]{1,0:T(8,128)(2,1)S(1)}, bf16[512,128]{1,0:T(8,128)(2,1)S(1)}, u32[]{:S(2)}, u32[]{:S(2)}) collective-permute-start(bf16[512,128]{1,0:T(8,128)(2,1)S(1)} %copy.64.refs_0_), channel_id=1, source_target_pairs={{0,1},{1,2},{2,3},{4,5},{5,6},{6,7},{8,9},{9,10},{10,11},{12,13},{... | collective-permute-start | bytes 393224 | tf_op jit(solution)/shard_map/ppermute | solution.py:235
  52.1 3.5 %collective-permute-start.2 = (f32[4,128]{1,0:T(4,128)S(1)}, f32[4,128]{1,0:T(4,128)S(1)}, u32[]{:S(2)}, u32[]{:S(2)}) collective-permute-start(f32[4,128]{1,0:T(4,128)S(1)} %slice_bitcast_fusion.22), channel_id=1, source_target_pairs={{0,8},{4,12},{8,0},{12,4},{16,24},{20,28},{24,16},{28,20},{1,9},{5... | collective-permute-start | bytes 6152 | tf_op jit(solution)/shard_map/ppermute | solution.py:242
  56.3 3.8 %collective-permute-done.39.refs_4_ = bf16[512,128]{1,0:T(8,128)(2,1)S(1)} collective-permute-done((bf16[512,128]{1,0:T(8,128)(2,1)S(1)}, bf16[512,128]{1,0:T(8,128)(2,1)S(1)}, u32[]{:S(2)}, u32[]{:S(2)}) %collective-permute-start.39) | collective-permute-done | bytes 131104 | tf_op jit(solution)/shard_map/ppermute | solution.py:236
  61.3 5.6 %collective-permute-done.41.refs_6_ = bf16[512,128]{1,0:T(8,128)(2,1)S(1)} collective-permute-done((bf16[512,128]{1,0:T(8,128)(2,1)S(1)}, bf16[512,128]{1,0:T(8,128)(2,1)S(1)}, u32[]{:S(2)}, u32[]{:S(2)}) %collective-permute-start.41) | collective-permute-done | bytes 131104 | tf_op jit(solution)/shard_map/ppermute | solution.py:236
  72.2 5.6 %collective-permute-start.12 = (bf16[2,256,128]{2,1,0:T(8,128)(2,1)S(1)}, bf16[2,256,128]{2,1,0:T(8,128)(2,1)S(1)}, u32[]{:S(2)}, u32[]{:S(2)}) collective-permute-start(bf16[2,256,128]{2,1,0:T(8,128)(2,1)S(1)} %fusion.30), channel_id=1, source_target_pairs={{0,8},{4,12},{8,0},{12,4},{16,24},{20,28},{24,16},{28,20},{1,9},{5... | collective-permute-start | bytes 393224 | tf_op jit(solution)/shard_map/ppermute | solution.py:242
  78.1 3.8 %collective-permute-start.11 = (bf16[256,128]{1,0:T(8,128)(2,1)S(1)}, bf16[256,128]{1,0:T(8,128)(2,1)S(1)}, u32[]{:S(2)}, u32[]{:S(2)}) collective-permute-start(bf16[256,128]{1,0:T(8,128)(2,1)S(1)} %fusion.54), channel_id=1, source_target_pairs={{0,8},{4,12},{8,0},{12,4},{16,24},{20,28},{24,16},{28,20},{1,9},{5... | collective-permute-start | bytes 196616 | tf_op jit(solution)/shard_map/ppermute | solution.py:242
  91.1 3.7 %collective-permute-done.15.refs_2_ = bf16[512,128]{1,0:T(8,128)(2,1)S(1)} collective-permute-done((bf16[512,128]{1,0:T(8,128)(2,1)S(1)}, bf16[512,128]{1,0:T(8,128)(2,1)S(1)}, u32[]{:S(2)}, u32[]{:S(2)}) %collective-permute-start.15) | collective-permute-done | bytes 131104 | tf_op jit(solution)/shard_map/ppermute | solution.py:236
  103.0 5.4 %collective-permute-done.19.refs_6_ = bf16[512,128]{1,0:T(8,128)(2,1)S(1)} collective-permute-done((bf16[512,128]{1,0:T(8,128)(2,1)S(1)}, bf16[512,128]{1,0:T(8,128)(2,1)S(1)}, u32[]{:S(2)}, u32[]{:S(2)}) %collective-permute-start.19) | collective-permute-done | bytes 131104 | tf_op jit(solution)/shard_map/ppermute | solution.py:236
  130.2 3.7 %collective-permute-done.26.refs_2_ = bf16[512,128]{1,0:T(8,128)(2,1)S(1)} collective-permute-done((bf16[512,128]{1,0:T(8,128)(2,1)S(1)}, bf16[512,128]{1,0:T(8,128)(2,1)S(1)}, u32[]{:S(2)}, u32[]{:S(2)}) %collective-permute-start.26) | collective-permute-done | bytes 131104 | tf_op jit(solution)/shard_map/ppermute | solution.py:236
  136.7 4.2 %collective-permute-done.28.refs_4_ = bf16[512,128]{1,0:T(8,128)(2,1)S(1)} collective-permute-done((bf16[512,128]{1,0:T(8,128)(2,1)S(1)}, bf16[512,128]{1,0:T(8,128)(2,1)S(1)}, u32[]{:S(2)}, u32[]{:S(2)}) %collective-permute-start.28) | collective-permute-done | bytes 131104 | tf_op jit(solution)/shard_map/ppermute | solution.py:236
  142.2 5.5 %collective-permute-done.30.refs_6_ = bf16[512,128]{1,0:T(8,128)(2,1)S(1)} collective-permute-done((bf16[512,128]{1,0:T(8,128)(2,1)S(1)}, bf16[512,128]{1,0:T(8,128)(2,1)S(1)}, u32[]{:S(2)}, u32[]{:S(2)}) %collective-permute-start.30) | collective-permute-done | bytes 131104 | tf_op jit(solution)/shard_map/ppermute | solution.py:236
  150.4 3.6 %collective-permute-done.46 = bf16[256,128]{1,0:T(8,128)(2,1)S(1)} collective-permute-done((bf16[256,128]{1,0:T(8,128)(2,1)S(1)}, bf16[256,128]{1,0:T(8,128)(2,1)S(1)}, u32[]{:S(2)}, u32[]{:S(2)}) %collective-permute-start.46) | collective-permute-done | bytes 65568 | tf_op jit(solution)/shard_map/ppermute | solution.py:242
  156.8 3.0 %collective-permute-start.34 = (bf16[2,256,128]{2,1,0:T(8,128)(2,1)S(1)}, bf16[2,256,128]{2,1,0:T(8,128)(2,1)S(1)}, u32[]{:S(2)}, u32[]{:S(2)}) collective-permute-start(bf16[2,256,128]{2,1,0:T(8,128)(2,1)S(1)} %fusion.32), channel_id=1, source_target_pairs={{0,8},{4,12},{8,0},{12,4},{16,24},{20,28},{24,16},{28,20},{1,9},{5... | collective-permute-start | bytes 393224 | tf_op jit(solution)/shard_map/ppermute | solution.py:242
  172.7 4.1 %collective-permute-done.48.refs_2_ = bf16[512,128]{1,0:T(8,128)(2,1)S(1)} collective-permute-done((bf16[512,128]{1,0:T(8,128)(2,1)S(1)}, bf16[512,128]{1,0:T(8,128)(2,1)S(1)}, u32[]{:S(2)}, u32[]{:S(2)}) %collective-permute-start.48) | collective-permute-done | bytes 131104 | tf_op jit(solution)/shard_map/ppermute | solution.py:236
  178.8 6.1 %collective-permute-done.50.refs_4_ = bf16[512,128]{1,0:T(8,128)(2,1)S(1)} collective-permute-done((bf16[512,128]{1,0:T(8,128)(2,1)S(1)}, bf16[512,128]{1,0:T(8,128)(2,1)S(1)}, u32[]{:S(2)}, u32[]{:S(2)}) %collective-permute-start.50) | collective-permute-done | bytes 131104 | tf_op jit(solution)/shard_map/ppermute | solution.py:236
  186.2 5.6 %collective-permute-done.52.refs_6_ = bf16[512,128]{1,0:T(8,128)(2,1)S(1)} collective-permute-done((bf16[512,128]{1,0:T(8,128)(2,1)S(1)}, bf16[512,128]{1,0:T(8,128)(2,1)S(1)}, u32[]{:S(2)}, u32[]{:S(2)}) %collective-permute-start.52) | collective-permute-done | bytes 131104 | tf_op jit(solution)/shard_map/ppermute | solution.py:236
  198.2 3.2 %collective-permute-done.54 = bf16[2,256,128]{2,1,0:T(8,128)(2,1)S(1)} collective-permute-done((bf16[2,256,128]{2,1,0:T(8,128)(2,1)S(1)}, bf16[2,256,128]{2,1,0:T(8,128)(2,1)S(1)}, u32[]{:S(2)}, u32[]{:S(2)}) %collective-permute-start.54) | collective-permute-done | bytes 131104 | tf_op jit(solution)/shard_map/ppermute | solution.py:242
  212.4 3.7 %collective-permute-done.59.refs_2_ = bf16[512,128]{1,0:T(8,128)(2,1)S(1)} collective-permute-done((bf16[512,128]{1,0:T(8,128)(2,1)S(1)}, bf16[512,128]{1,0:T(8,128)(2,1)S(1)}, u32[]{:S(2)}, u32[]{:S(2)}) %collective-permute-start.59) | collective-permute-done | bytes 131104 | tf_op jit(solution)/shard_map/ppermute | solution.py:236
  218.1 4.9 %collective-permute-done.61.refs_4_ = bf16[512,128]{1,0:T(8,128)(2,1)S(1)} collective-permute-done((bf16[512,128]{1,0:T(8,128)(2,1)S(1)}, bf16[512,128]{1,0:T(8,128)(2,1)S(1)}, u32[]{:S(2)}, u32[]{:S(2)}) %collective-permute-start.61) | collective-permute-done | bytes 131104 | tf_op jit(solution)/shard_map/ppermute | solution.py:236
  224.3 5.6 %collective-permute-done.63.refs_6_ = bf16[512,128]{1,0:T(8,128)(2,1)S(1)} collective-permute-done((bf16[512,128]{1,0:T(8,128)(2,1)S(1)}, bf16[512,128]{1,0:T(8,128)(2,1)S(1)}, u32[]{:S(2)}, u32[]{:S(2)}) %collective-permute-start.63) | collective-permute-done | bytes 131104 | tf_op jit(solution)/shard_map/ppermute | solution.py:236
  (222 shorter events, 130.9 us)
Async XLA Ops:
  1.4 20.1 %collective-permute-start.3 = (bf16[512,128]{1,0:T(8,128)(2,1)S(1)}, bf16[512,128]{1,0:T(8,128)(2,1)S(1)}, u32[]{:S(2)}, u32[]{:S(2)}) collective-permute-start(bf16[512,128]{1,0:T(8,128)(2,1)S(1)} %copy.49.refs_0_), channel_id=1, source_target_pairs={{0,1},{1,2},{2,3},{4,5},{5,6},{6,7},{8,9},{9,10},{10,11},{12,13},{... | collective-permute-start | bytes 393224 | tf_op jit(solution)/shard_map/ppermute | solution.py:235
  6.3 15.8 %collective-permute-start.4 = (bf16[512,128]{1,0:T(8,128)(2,1)S(1)}, bf16[512,128]{1,0:T(8,128)(2,1)S(1)}, u32[]{:S(2)}, u32[]{:S(2)}) collective-permute-start(bf16[512,128]{1,0:T(8,128)(2,1)S(1)} %copy.49.refs_0_), channel_id=1, source_target_pairs={{1,0},{2,1},{3,2},{5,4},{6,5},{7,6},{9,8},{10,9},{11,10},{13,12},{... | collective-permute-start | bytes 393224 | tf_op jit(solution)/shard_map/ppermute | solution.py:236
  22.2 11.4 %collective-permute-start.6 = (bf16[512,128]{1,0:T(8,128)(2,1)S(1)}, bf16[512,128]{1,0:T(8,128)(2,1)S(1)}, u32[]{:S(2)}, u32[]{:S(2)}) collective-permute-start(bf16[512,128]{1,0:T(8,128)(2,1)S(1)} %collective-permute-done.4.refs_2_), channel_id=1, source_target_pairs={{1,0},{2,1},{5,4},{6,5},{9,8},{10,9},{13,12},{14,13},{17,16},{18,1... | collective-permute-start | bytes 393224 | tf_op jit(solution)/shard_map/ppermute | solution.py:236
  23.5 21.8 %collective-permute-start.7 = (bf16[512,128]{1,0:T(8,128)(2,1)S(1)}, bf16[512,128]{1,0:T(8,128)(2,1)S(1)}, u32[]{:S(2)}, u32[]{:S(2)}) collective-permute-start(bf16[512,128]{1,0:T(8,128)(2,1)S(1)} %collective-permute-done.5.refs_3_), channel_id=1, source_target_pairs={{2,3},{6,7},{10,11},{14,15},{18,19},{22,23},{26,27},{30,31}} | collective-permute-start | bytes 393224 | tf_op jit(solution)/shard_map/ppermute | solution.py:235
  33.6 11.7 %collective-permute-start.8 = (bf16[512,128]{1,0:T(8,128)(2,1)S(1)}, bf16[512,128]{1,0:T(8,128)(2,1)S(1)}, u32[]{:S(2)}, u32[]{:S(2)}) collective-permute-start(bf16[512,128]{1,0:T(8,128)(2,1)S(1)} %collective-permute-done.6.refs_4_), channel_id=1, source_target_pairs={{1,0},{5,4},{9,8},{13,12},{17,16},{21,20},{25,24},{29,28}} | collective-permute-start | bytes 393224 | tf_op jit(solution)/shard_map/ppermute | solution.py:236
  34.9 14.8 %collective-permute-start.1 = (f32[2,4,128]{2,1,0:T(4,128)S(1)}, f32[2,4,128]{2,1,0:T(4,128)S(1)}, u32[]{:S(2)}, u32[]{:S(2)}) collective-permute-start(f32[2,4,128]{2,1,0:T(4,128)S(1)} %slice_bitcast_fusion.20), channel_id=1, source_target_pairs={{0,16},{4,20},{8,24},{12,28},{16,0},{20,4},{24,8},{28,12},{1,17},{... | collective-permute-start | bytes 12296 | tf_op jit(solution)/shard_map/ppermute | solution.py:242
  39.4 10.3 %collective-permute-start.36 = (bf16[512,128]{1,0:T(8,128)(2,1)S(1)}, bf16[512,128]{1,0:T(8,128)(2,1)S(1)}, u32[]{:S(2)}, u32[]{:S(2)}) collective-permute-start(bf16[512,128]{1,0:T(8,128)(2,1)S(1)} %copy.64.refs_0_), channel_id=1, source_target_pairs={{0,1},{1,2},{2,3},{4,5},{5,6},{6,7},{8,9},{9,10},{10,11},{12,13},{... | collective-permute-start | bytes 393224 | tf_op jit(solution)/shard_map/ppermute | solution.py:235
  49.6 22.3 %collective-permute-start.9 = (bf16[2048,128]{1,0:T(8,128)(2,1)S(1)}, bf16[2048,128]{1,0:T(8,128)(2,1)S(1)}, u32[]{:S(2)}, u32[]{:S(2)}) collective-permute-start(bf16[2048,128]{1,0:T(8,128)(2,1)S(1)} %get-tuple-element.28), channel_id=1, source_target_pairs={{0,4},{4,0},{8,12},{12,8},{16,20},{20,16},{24,28},{28,24},{1,5},{5... | collective-permute-start | bytes 1572872 | tf_op jit(solution)/shard_map/ppermute | solution.py:242
  50.8 9.2 %collective-permute-start.39 = (bf16[512,128]{1,0:T(8,128)(2,1)S(1)}, bf16[512,128]{1,0:T(8,128)(2,1)S(1)}, u32[]{:S(2)}, u32[]{:S(2)}) collective-permute-start(bf16[512,128]{1,0:T(8,128)(2,1)S(1)} %collective-permute-done.37.refs_2_), channel_id=1, source_target_pairs={{1,0},{2,1},{5,4},{6,5},{9,8},{10,9},{13,12},{14,13},{17,16},{18,1... | collective-permute-start | bytes 393224 | tf_op jit(solution)/shard_map/ppermute | solution.py:236
  52.1 9.2 %collective-permute-start.2 = (f32[4,128]{1,0:T(4,128)S(1)}, f32[4,128]{1,0:T(4,128)S(1)}, u32[]{:S(2)}, u32[]{:S(2)}) collective-permute-start(f32[4,128]{1,0:T(4,128)S(1)} %slice_bitcast_fusion.22), channel_id=1, source_target_pairs={{0,8},{4,12},{8,0},{12,4},{16,24},{20,28},{24,16},{28,20},{1,9},{5... | collective-permute-start | bytes 6152 | tf_op jit(solution)/shard_map/ppermute | solution.py:242
  60.0 7.0 %collective-permute-start.41 = (bf16[512,128]{1,0:T(8,128)(2,1)S(1)}, bf16[512,128]{1,0:T(8,128)(2,1)S(1)}, u32[]{:S(2)}, u32[]{:S(2)}) collective-permute-start(bf16[512,128]{1,0:T(8,128)(2,1)S(1)} %collective-permute-done.39.refs_4_), channel_id=1, source_target_pairs={{1,0},{5,4},{9,8},{13,12},{17,16},{21,20},{25,24},{29,28}} | collective-permute-start | bytes 393224 | tf_op jit(solution)/shard_map/ppermute | solution.py:236
  69.1 33.8 %collective-permute-start.42 = (bf16[2048,128]{1,0:T(8,128)(2,1)S(1)}, bf16[2048,128]{1,0:T(8,128)(2,1)S(1)}, u32[]{:S(2)}, u32[]{:S(2)}) collective-permute-start(bf16[2048,128]{1,0:T(8,128)(2,1)S(1)} %get-tuple-element.31), channel_id=1, source_target_pairs={{0,4},{4,0},{8,12},{12,8},{16,20},{20,16},{24,28},{28,24},{1,5},{5... | collective-permute-start | bytes 1572872 | tf_op jit(solution)/shard_map/ppermute | solution.py:242
  72.2 9.7 %collective-permute-start.12 = (bf16[2,256,128]{2,1,0:T(8,128)(2,1)S(1)}, bf16[2,256,128]{2,1,0:T(8,128)(2,1)S(1)}, u32[]{:S(2)}, u32[]{:S(2)}) collective-permute-start(bf16[2,256,128]{2,1,0:T(8,128)(2,1)S(1)} %fusion.30), channel_id=1, source_target_pairs={{0,8},{4,12},{8,0},{12,4},{16,24},{20,28},{24,16},{28,20},{1,9},{5... | collective-permute-start | bytes 393224 | tf_op jit(solution)/shard_map/ppermute | solution.py:242
  87.9 6.9 %collective-permute-start.15 = (bf16[512,128]{1,0:T(8,128)(2,1)S(1)}, bf16[512,128]{1,0:T(8,128)(2,1)S(1)}, u32[]{:S(2)}, u32[]{:S(2)}) collective-permute-start(bf16[512,128]{1,0:T(8,128)(2,1)S(1)} %fusion.6.refs_0_), channel_id=1, source_target_pairs={{1,0},{2,1},{3,2},{5,4},{6,5},{7,6},{9,8},{10,9},{11,10},{13,12},{... | collective-permute-start | bytes 393224 | tf_op jit(solution)/shard_map/ppermute | solution.py:236
  90.4 8.4 %collective-permute-start.16 = (bf16[512,128]{1,0:T(8,128)(2,1)S(1)}, bf16[512,128]{1,0:T(8,128)(2,1)S(1)}, u32[]{:S(2)}, u32[]{:S(2)}) collective-permute-start(bf16[512,128]{1,0:T(8,128)(2,1)S(1)} %collective-permute-done.14.refs_1_), channel_id=1, source_target_pairs={{1,2},{2,3},{5,6},{6,7},{9,10},{10,11},{13,14},{14,15},{17,18},{18... | collective-permute-start | bytes 393224 | tf_op jit(solution)/shard_map/ppermute | solution.py:235
  110.2 18.2 %collective-permute-start.43 = (bf16[2,256,128]{2,1,0:T(8,128)(2,1)S(1)}, bf16[2,256,128]{2,1,0:T(8,128)(2,1)S(1)}, u32[]{:S(2)}, u32[]{:S(2)}) collective-permute-start(bf16[2,256,128]{2,1,0:T(8,128)(2,1)S(1)} %fusion.39), channel_id=1, source_target_pairs={{0,16},{4,20},{8,24},{12,28},{16,0},{20,4},{24,8},{28,12},{1,17},{... | collective-permute-start | bytes 393224 | tf_op jit(solution)/shard_map/ppermute | solution.py:242
  111.3 30.9 %collective-permute-start.45 = (bf16[2,256,128]{2,1,0:T(8,128)(2,1)S(1)}, bf16[2,256,128]{2,1,0:T(8,128)(2,1)S(1)}, u32[]{:S(2)}, u32[]{:S(2)}) collective-permute-start(bf16[2,256,128]{2,1,0:T(8,128)(2,1)S(1)} %fusion.33), channel_id=1, source_target_pairs={{0,8},{4,12},{8,0},{12,4},{16,24},{20,28},{24,16},{28,20},{1,9},{5... | collective-permute-start | bytes 393224 | tf_op jit(solution)/shard_map/ppermute | solution.py:242
  133.9 7.0 %collective-permute-start.28 = (bf16[512,128]{1,0:T(8,128)(2,1)S(1)}, bf16[512,128]{1,0:T(8,128)(2,1)S(1)}, u32[]{:S(2)}, u32[]{:S(2)}) collective-permute-start(bf16[512,128]{1,0:T(8,128)(2,1)S(1)} %collective-permute-done.26.refs_2_), channel_id=1, source_target_pairs={{1,0},{2,1},{5,4},{6,5},{9,8},{10,9},{13,12},{14,13},{17,16},{18,1... | collective-permute-start | bytes 393224 | tf_op jit(solution)/shard_map/ppermute | solution.py:236
  135.2 15.1 %collective-permute-start.44 = (bf16[256,128]{1,0:T(8,128)(2,1)S(1)}, bf16[256,128]{1,0:T(8,128)(2,1)S(1)}, u32[]{:S(2)}, u32[]{:S(2)}) collective-permute-start(bf16[256,128]{1,0:T(8,128)(2,1)S(1)} %fusion.60), channel_id=1, source_target_pairs={{0,8},{4,12},{8,0},{12,4},{16,24},{20,28},{24,16},{28,20},{1,9},{5... | collective-permute-start | bytes 196616 | tf_op jit(solution)/shard_map/ppermute | solution.py:242
  169.5 7.3 %collective-permute-start.48 = (bf16[512,128]{1,0:T(8,128)(2,1)S(1)}, bf16[512,128]{1,0:T(8,128)(2,1)S(1)}, u32[]{:S(2)}, u32[]{:S(2)}) collective-permute-start(bf16[512,128]{1,0:T(8,128)(2,1)S(1)} %get-tuple-element.36.refs_0_), channel_id=1, source_target_pairs={{1,0},{2,1},{3,2},{5,4},{6,5},{7,6},{9,8},{10,9},{11,10},{13,12},{... | collective-permute-start | bytes 393224 | tf_op jit(solution)/shard_map/ppermute | solution.py:236
  176.8 8.1 %collective-permute-start.50 = (bf16[512,128]{1,0:T(8,128)(2,1)S(1)}, bf16[512,128]{1,0:T(8,128)(2,1)S(1)}, u32[]{:S(2)}, u32[]{:S(2)}) collective-permute-start(bf16[512,128]{1,0:T(8,128)(2,1)S(1)} %collective-permute-done.48.refs_2_), channel_id=1, source_target_pairs={{1,0},{2,1},{5,4},{6,5},{9,8},{10,9},{13,12},{14,13},{17,16},{18,1... | collective-permute-start | bytes 393224 | tf_op jit(solution)/shard_map/ppermute | solution.py:236
  178.1 8.1 %collective-permute-start.51 = (bf16[512,128]{1,0:T(8,128)(2,1)S(1)}, bf16[512,128]{1,0:T(8,128)(2,1)S(1)}, u32[]{:S(2)}, u32[]{:S(2)}) collective-permute-start(bf16[512,128]{1,0:T(8,128)(2,1)S(1)} %collective-permute-done.49.refs_3_), channel_id=1, source_target_pairs={{2,3},{6,7},{10,11},{14,15},{18,19},{22,23},{26,27},{30,31}} | collective-permute-start | bytes 393224 | tf_op jit(solution)/shard_map/ppermute | solution.py:235
  196.0 7.2 %collective-permute-start.56 = (bf16[2,256,128]{2,1,0:T(8,128)(2,1)S(1)}, bf16[2,256,128]{2,1,0:T(8,128)(2,1)S(1)}, u32[]{:S(2)}, u32[]{:S(2)}) collective-permute-start(bf16[2,256,128]{2,1,0:T(8,128)(2,1)S(1)} %fusion.34), channel_id=1, source_target_pairs={{0,8},{4,12},{8,0},{12,4},{16,24},{20,28},{24,16},{28,20},{1,9},{5... | collective-permute-start | bytes 393224 | tf_op jit(solution)/shard_map/ppermute | solution.py:242
  209.3 6.9 %collective-permute-start.59 = (bf16[512,128]{1,0:T(8,128)(2,1)S(1)}, bf16[512,128]{1,0:T(8,128)(2,1)S(1)}, u32[]{:S(2)}, u32[]{:S(2)}) collective-permute-start(bf16[512,128]{1,0:T(8,128)(2,1)S(1)} %fusion.11.refs_0_), channel_id=1, source_target_pairs={{1,0},{2,1},{3,2},{5,4},{6,5},{7,6},{9,8},{10,9},{11,10},{13,12},{... | collective-permute-start | bytes 393224 | tf_op jit(solution)/shard_map/ppermute | solution.py:236
  (51 other events, 245.2 us)

commit v2 on v1

--- a/solution.py
+++ b/solution.py
@@ -159,9 +159,9 @@
     turned_ref,
     *refs,
 ):
-    block_refs = refs[: 2 * blocks - 1]
-    out_ref = refs[2 * blocks - 1]
-    own_ref = refs[2 * blocks] if packed else None
+    block_refs = refs[:blocks]
+    out_ref = refs[blocks]
+    own_ref = refs[blocks + 1] if packed else None
     held_ref = refs[-2 if packed else -1]
     staged_ref = refs[-1] if packed else held_ref
     col = place_ref[1]
@@ -171,10 +171,8 @@
     def put(block, ref):
         staged_ref[pl.ds(pl.multiple_of(block * rows, rows), rows), :] = ref[...]
 
-    put(col, block_refs[0])
-    for step in range(1, blocks):
-        pl.when(col >= step)(functools.partial(put, col - step, block_refs[2 * step - 1]))
-        pl.when(col + step < blocks)(functools.partial(put, col + step, block_refs[2 * step]))
+    for mask in range(blocks):
+        put(lax.bitwise_xor(col, mask), block_refs[mask])
     if packed:
         piece = width // blocks
         for group in range(blocks):
@@ -223,34 +221,17 @@
         in_specs=smem(1 + len(lists)) + vmem(1 + len(gathered)),
         out_specs=vmem(len(out_shape)),
         scratch_shapes=scratch,
-        compiler_params=pltpu.CompilerParams(vmem_limit_bytes=24 * 2**20),
+        compiler_params=pltpu.CompilerParams(vmem_limit_bytes=4 * 2**20),
         name="product",
     )(place, *lists, turned, *gathered)
 
 
+def exchange(block, axis, mask, size):
+    return lax.ppermute(block, axis, [(i, i ^ mask) for i in range(size)])
+
+
 def gather_line(block, size):
-    found = [block]
-    from_left = from_right = block
-    for step in range(1, size):
-        from_left = lax.ppermute(from_left, "col", [(i, i + 1) for i in range(step - 1, size - 1)])
-        from_right = lax.ppermute(from_right, "col", [(i, i - 1) for i in range(1, size - step + 1)])
-        found += [from_left, from_right]
-    return found
-
-
-def swap(block, bit, row_size):
-    return lax.ppermute(block, "row", [(i, i ^ (1 << bit)) for i in range(row_size)])
-
-
-def halve(state, bits, order, row_size):
-    bits = list(bits)
-    for bit in order:
-        axis = bits.index(bit)
-        send = lax.index_in_dim(state, 1, axis, keepdims=False).astype(jnp.bfloat16)
-        keep = lax.index_in_dim(state, 0, axis, keepdims=False)
-        state = keep + swap(send, bit, row_size).astype(jnp.float32)
-        bits.remove(bit)
-    return state
+    return [block] + [exchange(block, "col", mask, size) for mask in range(size - 1, 0, -1)][::-1]
 
 
 def on_device(features, tile_vals, tile_src, row_counts):
@@ -265,58 +246,55 @@
     width = features.shape[1] * blocks // CHUNKS
     piece = features.shape[1] // CHUNKS
     tiles_per_owner = dest_count // row_size
-    row_bits = row_size.bit_length() - 1
-    chip_bits = list(range(row_bits - 1, 0, -1))
+    chips = row_size // 2
     place = jnp.stack([my_row, my_col, jnp.int32(source_tiles)])
 
     parts = features.reshape(blocks, rows, CHUNKS, piece).transpose(2, 1, 0, 3)
     parts = parts.reshape(CHUNKS, rows, blocks * piece)
-    gathered = [gather_line(parts[chunk], blocks) for chunk in range(CHUNKS)]
 
     turned, weight_sums, *lists = prepare(
         place, tile_src, row_counts, tile_vals, row_size, tiles_per_owner
     )
-    all_bits = [0] + chip_bits
-    weights = weight_sums
-    state = weights.reshape((2,) * row_bits + (tiles_per_owner, tile_size))
-    bits = list(range(row_bits - 1, -1, -1))
-    for bit in [0] + chip_bits:
-        axis = bits.index(bit)
-        send = lax.index_in_dim(state, 1, axis, keepdims=False)
-        state = lax.index_in_dim(state, 0, axis, keepdims=False) + swap(send, bit, row_size)
-        bits.remove(bit)
-    scale = ((1.0 - TELEPORT) / (1.0 + state)).reshape(rows, 1)
+    other = exchange(weight_sums.reshape(row_size // 2, 2, tiles_per_owner, tile_size)[:, 1], "row", 1, row_size)
+    weights = weight_sums.reshape(row_size // 2, 2, tiles_per_owner, tile_size)[:, 0] + other
+    weight_total = 1.0 + weights[0]
+    for mask in range(1, chips):
+        weight_total = weight_total + exchange(weights[mask], "row", 2 * mask, row_size)
+    scale = ((1.0 - TELEPORT) / weight_total).reshape(rows, 1)
     scale = jnp.broadcast_to(scale, (rows, width))
 
+    gathered = [None] * CHUNKS
     iterates = [None] * CHUNKS
     restarts = [None] * CHUNKS
+    gathered[0] = gather_line(parts[0], blocks)
     for iteration in range(ITERS):
         for chunk in range(CHUNKS):
             packed = iteration == 0
+            after = (chunk + 1) % CHUNKS
+            source = parts[1] if packed and chunk == 0 else iterates[after]
+            if iteration + 1 < ITERS or chunk == 0:
+                held, source = lax.optimization_barrier((gathered[chunk], source))
+                gathered[chunk] = held
+                gathered[after] = gather_line(source, blocks)
             sent, *rest = product(
                 1, place, lists, turned, gathered[chunk], blocks, row_size, packed
             )
             if packed:
                 iterates[chunk] = rest[0]
                 restarts[chunk] = TELEPORT * rest[0].astype(jnp.float32)
-            other = swap(sent, 0, row_size)
+            other = exchange(sent, "row", 1, row_size)
             kept = product(0, place, lists, turned, gathered[chunk], blocks, row_size, packed)[0]
-            shape = (2,) * len(chip_bits) + (2, rows // 2, width)
-            state = kept.astype(jnp.float32) + other.astype(jnp.float32)
-            state = state.reshape(shape)
-            summed = []
-            for half in range(2):
-                turn = half % max(len(chip_bits), 1)
-                order = chip_bits[turn:] + chip_bits[:turn]
-                summed.append(
-                    halve(state[..., half, :, :], chip_bits, order, row_size)
-                )
-            summed = jnp.concatenate(summed, axis=0)
+            both = (kept.astype(jnp.float32) + other.astype(jnp.float32)).reshape(
+                chips, rows, width
+            )
+            summed = both[0]
+            for mask in range(1, chips):
+                summed = summed + exchange(
+                    both[mask].astype(jnp.bfloat16), "row", 2 * mask, row_size
+                ).astype(jnp.float32)
             iterates[chunk] = (
                 scale * (summed + iterates[chunk].astype(jnp.float32)) + restarts[chunk]
             ).astype(jnp.bfloat16)
-            if iteration + 1 < ITERS:
-                gathered[chunk] = gather_line(iterates[chunk], blocks)
     out = jnp.stack(iterates).reshape(CHUNKS, rows, blocks, piece).transpose(1, 2, 0, 3)
     return out.reshape(rows, CHUNKS * width)
 

time: 246 us -> 165 us (0.67)
  waiting for transfers between devices: 108 us -> 52.3 us
  starting transfers between devices: 93 us -> 66.6 us
    ppermute x69 -> x46, waiting for transfers between devices: 108 us -> 52.3 us  [exchange(): return lax.ppermute(block, axis, [(i, i ^ mask) for i in range(size)])]
    ppermute x69 -> x46, starting transfers between devices: 93 us -> 66.6 us  [exchange(): return lax.ppermute(block, axis, [(i, i ^ mask) for i in range(size)])]
    unnamed x12 -> x16, local copies, waits for them, and re-layouts: 9.84 us -> 9.85 us
  transfers between devices with their start and end apart: 69 -> 46, of which waited for: 38 -> 18; matrix products, arithmetic and copies ran while one was open for 1% -> 1% of each run, Pallas kernels for 10% -> 13%
where the time goes in v2:
time: 165 us
  starting transfers between devices  66.6 us (40%)
  waiting for transfers between devices  52.3 us (32%)
  Pallas kernels  30.8 us (19%)
  local copies, waits for them, and re-layouts  12.9 us (8%)
  other arithmetic  1.74 us (1%)
    ppermute x46, starting transfers between devices, exchange(): return lax.ppermute(block, axis, [(i, i ^ mask) for i in range(size)])  66.6 us
    ppermute x46, waiting for transfers between devices, exchange(): return lax.ppermute(block, axis, [(i, i ^ mask) for i in range(size)])  52.3 us
    pallas_call x12, Pallas kernels, product(): pl.pallas_call(functools.partial(product_kernel, half, packed, blocks), o...  22 us
    unnamed x16, local copies, waits for them, and re-layouts  9.85 us
    pallas_call x1, Pallas kernels, prepare(): pl.pallas_call(functools.partial(prepare_kernel, tiles_per_owner), out_sh...  8.85 us
  transfers between devices with their start and end apart: 46, of which 18 were waited for; matrix products, arithmetic and copies ran while one was open for 1% of the time, Pallas kernels for 13%

profile of v2, /device:TPU:0, one launch (start us, length us, event | category | flops | bytes accessed | tf_op | source)
XLA Modules:
  0.0 164.8 jit_solution(11905797853131405136)
XLA Ops:
  1.4 3.1 %collective-permute-start.4 = (bf16[512,128]{1,0:T(8,128)(2,1)S(1)}, bf16[512,128]{1,0:T(8,128)(2,1)S(1)}, u32[]{:S(2)}, u32[]{:S(2)}) collective-permute-start(bf16[512,128]{1,0:T(8,128)(2,1)S(1)} %copy.25), channel_id=1, source_target_pairs={{0,1},{1,0},{2,3},{3,2},{4,5},{5,4},{6,7},{7,6},{8,9},{9,8},{10,11... | collective-permute-start | bytes 393224 | tf_op jit(solution)/shard_map/ppermute | solution.py:230
  4.5 2.6 %collective-permute-start.5 = (bf16[512,128]{1,0:T(8,128)(2,1)S(1)}, bf16[512,128]{1,0:T(8,128)(2,1)S(1)}, u32[]{:S(2)}, u32[]{:S(2)}) collective-permute-start(bf16[512,128]{1,0:T(8,128)(2,1)S(1)} %copy.25), channel_id=1, source_target_pairs={{0,2},{1,3},{2,0},{3,1},{4,6},{5,7},{6,4},{7,5},{8,10},{9,11},{10,... | collective-permute-start | bytes 393224 | tf_op jit(solution)/shard_map/ppermute | solution.py:230
  7.2 2.2 %copy-done.5 = bf16[128,128,128]{2,1,0:T(8,128)(2,1)S(1)} copy-done((bf16[128,128,128]{2,1,0:T(8,128)(2,1)S(1)}, bf16[128,128,128]{2,1,0:T(8,128)(2,1)}, u32[]{:S(2)}) %copy-start.5) | copy-done | bytes 4194328
  10.7 8.8 %prepare.1 = (bf16[128,128,128]{2,1,0:T(8,128)(2,1)S(1)}, f32[8,4,128]{2,1,0:T(4,128)S(1)}, s32[2,72]{1,0:T(2,128)S(1)}, s32[2,72]{1,0:T(2,128)S(1)}, s32[2,72]{...) custom-call(s32[3]{0:T(128)S(1)} %pad_add_fusion.place_ref, s32[1,128]{1,0:T(1,128)S(1)} %copy-done.6, ...), custom_call_target="tpu_custom_call" | custom-call | tf_op jit(solution)/shard_map/prepare/pallas_call | solution.py:129
  21.7 2.2 %copy-done.1 = bf16[128,128,128]{2,1,0:T(8,128)(2,1)S(1)} copy-done((bf16[128,128,128]{2,1,0:T(8,128)(2,1)S(1)}, bf16[128,128,128]{2,1,0:T(8,128)(2,1)}, u32[]{:S(2)}) %copy-start.1) | copy-done | bytes 4194328
  23.9 2.1 %product.13 = (bf16[2048,128]{1,0:T(8,128)(2,1)S(1)}, bf16[512,128]{1,0:T(8,128)(2,1)S(1)}) custom-call(s32[3]{0:T(128)S(1)} %pad_add_fusion.place_ref, s32[2,72]{1,0:T(2,128)S(1)} %get-tuple-element.45.slot_ref, s32[2,72]{1,0:T(2,128)S(1)} %get-tuple-element.46.first_ref, s32[2,72]{1,0:T(2,128)S(1)} %get-tuple-element.47.second_ref, ...), custom_call_target="tpu_custom_call" | custom-call | tf_op jit(solution)/shard_map/product/pallas_call | solution.py:218
  31.4 2.7 %product.12 = (bf16[2048,128]{1,0:T(8,128)(2,1)S(1)}, bf16[512,128]{1,0:T(8,128)(2,1)}) custom-call(s32[3]{0:T(128)S(1)} %pad_add_fusion.place_ref, s32[2,72]{1,0:T(2,128)S(1)} %get-tuple-element.45.slot_ref, s32[2,72]{1,0:T(2,128)S(1)} %get-tuple-element.46.first_ref, s32[2,72]{1,0:T(2,128)S(1)} %get-tuple-element.47.second_ref, ...), custom_call_target="tpu_custom_call" | custom-call | tf_op jit(solution)/shard_map/product/pallas_call | solution.py:218
  38.0 6.0 %collective-permute-start.7 = (bf16[512,128]{1,0:T(8,128)(2,1)S(1)}, bf16[512,128]{1,0:T(8,128)(2,1)S(1)}, u32[]{:S(2)}, u32[]{:S(2)}) collective-permute-start(bf16[512,128]{1,0:T(8,128)(2,1)S(1)} %copy.29), channel_id=1, source_target_pairs={{0,1},{1,0},{2,3},{3,2},{4,5},{5,4},{6,7},{7,6},{8,9},{9,8},{10,11... | collective-permute-start | bytes 393224 | tf_op jit(solution)/shard_map/ppermute | solution.py:230
  44.0 4.0 %collective-permute-start.8 = (bf16[512,128]{1,0:T(8,128)(2,1)S(1)}, bf16[512,128]{1,0:T(8,128)(2,1)S(1)}, u32[]{:S(2)}, u32[]{:S(2)}) collective-permute-start(bf16[512,128]{1,0:T(8,128)(2,1)S(1)} %copy.29), channel_id=1, source_target_pairs={{0,2},{1,3},{2,0},{3,1},{4,6},{5,7},{6,4},{7,5},{8,10},{9,11},{10,... | collective-permute-start | bytes 393224 | tf_op jit(solution)/shard_map/ppermute | solution.py:230
  49.3 6.9 %collective-permute-done.8.refs_2_ = bf16[512,128]{1,0:T(8,128)(2,1)S(1)} collective-permute-done((bf16[512,128]{1,0:T(8,128)(2,1)S(1)}, bf16[512,128]{1,0:T(8,128)(2,1)S(1)}, u32[]{:S(2)}, u32[]{:S(2)}) %collective-permute-start.8) | collective-permute-done | bytes 131104 | tf_op jit(solution)/shard_map/ppermute | solution.py:230
  56.4 2.2 %copy-done.3 = bf16[128,128,128]{2,1,0:T(8,128)(2,1)S(1)} copy-done((bf16[128,128,128]{2,1,0:T(8,128)(2,1)S(1)}, bf16[128,128,128]{2,1,0:T(8,128)(2,1)}, u32[]{:S(2)}) %copy-start.3) | copy-done | bytes 4194328
  60.7 2.7 %product.14 = (bf16[2048,128]{1,0:T(8,128)(2,1)S(1)}, bf16[512,128]{1,0:T(8,128)(2,1)}) custom-call(s32[3]{0:T(128)S(1)} %pad_add_fusion.place_ref, s32[2,72]{1,0:T(2,128)S(1)} %get-tuple-element.45.slot_ref, s32[2,72]{1,0:T(2,128)S(1)} %get-tuple-element.46.first_ref, s32[2,72]{1,0:T(2,128)S(1)} %get-tuple-element.47.second_ref, ...), custom_call_target="tpu_custom_call" | custom-call | tf_op jit(solution)/shard_map/product/pallas_call | solution.py:218
  67.2 2.2 %collective-permute-start.14 = (bf16[512,128]{1,0:T(8,128)(2,1)S(1)}, bf16[512,128]{1,0:T(8,128)(2,1)S(1)}, u32[]{:S(2)}, u32[]{:S(2)}) collective-permute-start(bf16[512,128]{1,0:T(8,128)(2,1)S(1)} %fusion.6.refs_0_), channel_id=1, source_target_pairs={{0,1},{1,0},{2,3},{3,2},{4,5},{5,4},{6,7},{7,6},{8,9},{9,8},{10,11... | collective-permute-start | bytes 393224 | tf_op jit(solution)/shard_map/ppermute | solution.py:230
  71.4 2.3 %collective-permute-start.16 = (bf16[512,128]{1,0:T(8,128)(2,1)S(1)}, bf16[512,128]{1,0:T(8,128)(2,1)S(1)}, u32[]{:S(2)}, u32[]{:S(2)}) collective-permute-start(bf16[512,128]{1,0:T(8,128)(2,1)S(1)} %fusion.6.refs_0_), channel_id=1, source_target_pairs={{0,3},{1,2},{2,1},{3,0},{4,7},{5,6},{6,5},{7,4},{8,11},{9,10},{10,... | collective-permute-start | bytes 393224 | tf_op jit(solution)/shard_map/ppermute | solution.py:230
  74.0 8.2 %collective-permute-done.15.refs_2_ = bf16[512,128]{1,0:T(8,128)(2,1)S(1)} collective-permute-done((bf16[512,128]{1,0:T(8,128)(2,1)S(1)}, bf16[512,128]{1,0:T(8,128)(2,1)S(1)}, u32[]{:S(2)}, u32[]{:S(2)}) %collective-permute-start.15) | collective-permute-done | bytes 131104 | tf_op jit(solution)/shard_map/ppermute | solution.py:230
  89.5 2.5 %collective-permute-start.21 = (bf16[512,128]{1,0:T(8,128)(2,1)S(1)}, bf16[512,128]{1,0:T(8,128)(2,1)S(1)}, u32[]{:S(2)}, u32[]{:S(2)}) collective-permute-start(bf16[512,128]{1,0:T(8,128)(2,1)S(1)} %fusion.10.refs_0_), channel_id=1, source_target_pairs={{0,1},{1,0},{2,3},{3,2},{4,5},{5,4},{6,7},{7,6},{8,9},{9,8},{10,11... | collective-permute-start | bytes 393224 | tf_op jit(solution)/shard_map/ppermute | solution.py:230
  92.9 2.1 %collective-permute-start.23 = (bf16[512,128]{1,0:T(8,128)(2,1)S(1)}, bf16[512,128]{1,0:T(8,128)(2,1)S(1)}, u32[]{:S(2)}, u32[]{:S(2)}) collective-permute-start(bf16[512,128]{1,0:T(8,128)(2,1)S(1)} %fusion.10.refs_0_), channel_id=1, source_target_pairs={{0,3},{1,2},{2,1},{3,0},{4,7},{5,6},{6,5},{7,4},{8,11},{9,10},{10,... | collective-permute-start | bytes 393224 | tf_op jit(solution)/shard_map/ppermute | solution.py:230
  96.5 8.3 %collective-permute-done.22.refs_2_ = bf16[512,128]{1,0:T(8,128)(2,1)S(1)} collective-permute-done((bf16[512,128]{1,0:T(8,128)(2,1)S(1)}, bf16[512,128]{1,0:T(8,128)(2,1)S(1)}, u32[]{:S(2)}, u32[]{:S(2)}) %collective-permute-start.22) | collective-permute-done | bytes 131104 | tf_op jit(solution)/shard_map/ppermute | solution.py:230
  112.0 2.5 %collective-permute-start.28 = (bf16[512,128]{1,0:T(8,128)(2,1)S(1)}, bf16[512,128]{1,0:T(8,128)(2,1)S(1)}, u32[]{:S(2)}, u32[]{:S(2)}) collective-permute-start(bf16[512,128]{1,0:T(8,128)(2,1)S(1)} %fusion.7.refs_0_), channel_id=1, source_target_pairs={{0,1},{1,0},{2,3},{3,2},{4,5},{5,4},{6,7},{7,6},{8,9},{9,8},{10,11... | collective-permute-start | bytes 393224 | tf_op jit(solution)/shard_map/ppermute | solution.py:230
  119.0 8.3 %collective-permute-done.29.refs_2_ = bf16[512,128]{1,0:T(8,128)(2,1)S(1)} collective-permute-done((bf16[512,128]{1,0:T(8,128)(2,1)S(1)}, bf16[512,128]{1,0:T(8,128)(2,1)S(1)}, u32[]{:S(2)}, u32[]{:S(2)}) %collective-permute-start.29) | collective-permute-done | bytes 131104 | tf_op jit(solution)/shard_map/ppermute | solution.py:230
  135.0 2.2 %collective-permute-done.39.refs_1_ = bf16[512,128]{1,0:T(8,128)(2,1)S(1)} collective-permute-done((bf16[512,128]{1,0:T(8,128)(2,1)S(1)}, bf16[512,128]{1,0:T(8,128)(2,1)S(1)}, u32[]{:S(2)}, u32[]{:S(2)}) %collective-permute-start.39) | collective-permute-done | bytes 131104 | tf_op jit(solution)/shard_map/ppermute | solution.py:230
  137.2 6.7 %collective-permute-done.40.refs_2_ = bf16[512,128]{1,0:T(8,128)(2,1)S(1)} collective-permute-done((bf16[512,128]{1,0:T(8,128)(2,1)S(1)}, bf16[512,128]{1,0:T(8,128)(2,1)S(1)}, u32[]{:S(2)}, u32[]{:S(2)}) %collective-permute-start.40) | collective-permute-done | bytes 131104 | tf_op jit(solution)/shard_map/ppermute | solution.py:230
  148.8 2.3 %collective-permute-start.37 = (bf16[512,128]{1,0:T(8,128)(2,1)S(1)}, bf16[512,128]{1,0:T(8,128)(2,1)S(1)}, u32[]{:S(2)}, u32[]{:S(2)}) collective-permute-start(bf16[512,128]{1,0:T(8,128)(2,1)S(1)} %get-tuple-element.97), channel_id=1, source_target_pairs={{0,16},{4,20},{8,24},{12,28},{16,0},{20,4},{24,8},{28,12},{1,17},{... | collective-permute-start | bytes 393224 | tf_op jit(solution)/shard_map/ppermute | solution.py:230
  159.8 3.7 %collective-permute-done.44 = bf16[512,128]{1,0:T(8,128)(2,1)S(1)} collective-permute-done((bf16[512,128]{1,0:T(8,128)(2,1)S(1)}, bf16[512,128]{1,0:T(8,128)(2,1)S(1)}, u32[]{:S(2)}, u32[]{:S(2)}) %collective-permute-start.44) | collective-permute-done | bytes 131104 | tf_op jit(solution)/shard_map/ppermute | solution.py:230
  (132 shorter events, 67.6 us)
Async XLA Ops:
  1.4 20.1 %collective-permute-start.4 = (bf16[512,128]{1,0:T(8,128)(2,1)S(1)}, bf16[512,128]{1,0:T(8,128)(2,1)S(1)}, u32[]{:S(2)}, u32[]{:S(2)}) collective-permute-start(bf16[512,128]{1,0:T(8,128)(2,1)S(1)} %copy.25), channel_id=1, source_target_pairs={{0,1},{1,0},{2,3},{3,2},{4,5},{5,4},{6,7},{7,6},{8,9},{9,8},{10,11... | collective-permute-start | bytes 393224 | tf_op jit(solution)/shard_map/ppermute | solution.py:230
  4.5 17.0 %collective-permute-start.5 = (bf16[512,128]{1,0:T(8,128)(2,1)S(1)}, bf16[512,128]{1,0:T(8,128)(2,1)S(1)}, u32[]{:S(2)}, u32[]{:S(2)}) collective-permute-start(bf16[512,128]{1,0:T(8,128)(2,1)S(1)} %copy.25), channel_id=1, source_target_pairs={{0,2},{1,3},{2,0},{3,1},{4,6},{5,7},{6,4},{7,5},{8,10},{9,11},{10,... | collective-permute-start | bytes 393224 | tf_op jit(solution)/shard_map/ppermute | solution.py:230
  7.1 14.5 %collective-permute-start.6 = (bf16[512,128]{1,0:T(8,128)(2,1)S(1)}, bf16[512,128]{1,0:T(8,128)(2,1)S(1)}, u32[]{:S(2)}, u32[]{:S(2)}) collective-permute-start(bf16[512,128]{1,0:T(8,128)(2,1)S(1)} %copy.25), channel_id=1, source_target_pairs={{0,3},{1,2},{2,1},{3,0},{4,7},{5,6},{6,5},{7,4},{8,11},{9,10},{10,... | collective-permute-start | bytes 393224 | tf_op jit(solution)/shard_map/ppermute | solution.py:230
  27.9 9.8 %collective-permute-start.1 = (f32[4,128]{1,0:T(4,128)S(1)}, f32[4,128]{1,0:T(4,128)S(1)}, u32[]{:S(2)}, u32[]{:S(2)}) collective-permute-start(f32[4,128]{1,0:T(4,128)S(1)} %get-tuple-element.115), channel_id=1, source_target_pairs={{0,8},{4,12},{8,0},{12,4},{16,24},{20,28},{24,16},{28,20},{1,9},{5... | collective-permute-start | bytes 6152 | tf_op jit(solution)/shard_map/ppermute | solution.py:230
  29.3 8.6 %collective-permute-start.2 = (f32[4,128]{1,0:T(4,128)S(1)}, f32[4,128]{1,0:T(4,128)S(1)}, u32[]{:S(2)}, u32[]{:S(2)}) collective-permute-start(f32[4,128]{1,0:T(4,128)S(1)} %get-tuple-element.117), channel_id=1, source_target_pairs={{0,16},{4,20},{8,24},{12,28},{16,0},{20,4},{24,8},{28,12},{1,17},{... | collective-permute-start | bytes 6152 | tf_op jit(solution)/shard_map/ppermute | solution.py:230
  34.3 13.6 %collective-permute-start.11 = (bf16[512,128]{1,0:T(8,128)(2,1)S(1)}, bf16[512,128]{1,0:T(8,128)(2,1)S(1)}, u32[]{:S(2)}, u32[]{:S(2)}) collective-permute-start(bf16[512,128]{1,0:T(8,128)(2,1)S(1)} %get-tuple-element.110), channel_id=1, source_target_pairs={{0,8},{4,12},{8,0},{12,4},{16,24},{20,28},{24,16},{28,20},{1,9},{5... | collective-permute-start | bytes 393224 | tf_op jit(solution)/shard_map/ppermute | solution.py:230
  35.7 13.5 %collective-permute-start.12 = (bf16[512,128]{1,0:T(8,128)(2,1)S(1)}, bf16[512,128]{1,0:T(8,128)(2,1)S(1)}, u32[]{:S(2)}, u32[]{:S(2)}) collective-permute-start(bf16[512,128]{1,0:T(8,128)(2,1)S(1)} %get-tuple-element.112), channel_id=1, source_target_pairs={{0,16},{4,20},{8,24},{12,28},{16,0},{20,4},{24,8},{28,12},{1,17},{... | collective-permute-start | bytes 393224 | tf_op jit(solution)/shard_map/ppermute | solution.py:230
  37.7 11.5 %collective-permute-start.13 = (bf16[512,128]{1,0:T(8,128)(2,1)S(1)}, bf16[512,128]{1,0:T(8,128)(2,1)S(1)}, u32[]{:S(2)}, u32[]{:S(2)}) collective-permute-start(bf16[512,128]{1,0:T(8,128)(2,1)S(1)} %get-tuple-element.111), channel_id=1, source_target_pairs={{0,24},{4,28},{8,16},{12,20},{16,8},{20,12},{24,0},{28,4},{1,25},{... | collective-permute-start | bytes 393224 | tf_op jit(solution)/shard_map/ppermute | solution.py:230
  38.0 11.3 %collective-permute-start.7 = (bf16[512,128]{1,0:T(8,128)(2,1)S(1)}, bf16[512,128]{1,0:T(8,128)(2,1)S(1)}, u32[]{:S(2)}, u32[]{:S(2)}) collective-permute-start(bf16[512,128]{1,0:T(8,128)(2,1)S(1)} %copy.29), channel_id=1, source_target_pairs={{0,1},{1,0},{2,3},{3,2},{4,5},{5,4},{6,7},{7,6},{8,9},{9,8},{10,11... | collective-permute-start | bytes 393224 | tf_op jit(solution)/shard_map/ppermute | solution.py:230
  44.0 12.3 %collective-permute-start.8 = (bf16[512,128]{1,0:T(8,128)(2,1)S(1)}, bf16[512,128]{1,0:T(8,128)(2,1)S(1)}, u32[]{:S(2)}, u32[]{:S(2)}) collective-permute-start(bf16[512,128]{1,0:T(8,128)(2,1)S(1)} %copy.29), channel_id=1, source_target_pairs={{0,2},{1,3},{2,0},{3,1},{4,6},{5,7},{6,4},{7,5},{8,10},{9,11},{10,... | collective-permute-start | bytes 393224 | tf_op jit(solution)/shard_map/ppermute | solution.py:230
  64.5 9.2 %collective-permute-start.19 = (bf16[512,128]{1,0:T(8,128)(2,1)S(1)}, bf16[512,128]{1,0:T(8,128)(2,1)S(1)}, u32[]{:S(2)}, u32[]{:S(2)}) collective-permute-start(bf16[512,128]{1,0:T(8,128)(2,1)S(1)} %get-tuple-element.109), channel_id=1, source_target_pairs={{0,16},{4,20},{8,24},{12,28},{16,0},{20,4},{24,8},{28,12},{1,17},{... | collective-permute-start | bytes 393224 | tf_op jit(solution)/shard_map/ppermute | solution.py:230
  69.4 12.9 %collective-permute-start.15 = (bf16[512,128]{1,0:T(8,128)(2,1)S(1)}, bf16[512,128]{1,0:T(8,128)(2,1)S(1)}, u32[]{:S(2)}, u32[]{:S(2)}) collective-permute-start(bf16[512,128]{1,0:T(8,128)(2,1)S(1)} %fusion.6.refs_0_), channel_id=1, source_target_pairs={{0,2},{1,3},{2,0},{3,1},{4,6},{5,7},{6,4},{7,5},{8,10},{9,11},{10,... | collective-permute-start | bytes 393224 | tf_op jit(solution)/shard_map/ppermute | solution.py:230
  71.4 10.9 %collective-permute-start.16 = (bf16[512,128]{1,0:T(8,128)(2,1)S(1)}, bf16[512,128]{1,0:T(8,128)(2,1)S(1)}, u32[]{:S(2)}, u32[]{:S(2)}) collective-permute-start(bf16[512,128]{1,0:T(8,128)(2,1)S(1)} %fusion.6.refs_0_), channel_id=1, source_target_pairs={{0,3},{1,2},{2,1},{3,0},{4,7},{5,6},{6,5},{7,4},{8,11},{9,10},{10,... | collective-permute-start | bytes 393224 | tf_op jit(solution)/shard_map/ppermute | solution.py:230
  92.1 12.7 %collective-permute-start.22 = (bf16[512,128]{1,0:T(8,128)(2,1)S(1)}, bf16[512,128]{1,0:T(8,128)(2,1)S(1)}, u32[]{:S(2)}, u32[]{:S(2)}) collective-permute-start(bf16[512,128]{1,0:T(8,128)(2,1)S(1)} %fusion.10.refs_0_), channel_id=1, source_target_pairs={{0,2},{1,3},{2,0},{3,1},{4,6},{5,7},{6,4},{7,5},{8,10},{9,11},{10,... | collective-permute-start | bytes 393224 | tf_op jit(solution)/shard_map/ppermute | solution.py:230
  92.9 11.9 %collective-permute-start.23 = (bf16[512,128]{1,0:T(8,128)(2,1)S(1)}, bf16[512,128]{1,0:T(8,128)(2,1)S(1)}, u32[]{:S(2)}, u32[]{:S(2)}) collective-permute-start(bf16[512,128]{1,0:T(8,128)(2,1)S(1)} %fusion.10.refs_0_), channel_id=1, source_target_pairs={{0,3},{1,2},{2,1},{3,0},{4,7},{5,6},{6,5},{7,4},{8,11},{9,10},{10,... | collective-permute-start | bytes 393224 | tf_op jit(solution)/shard_map/ppermute | solution.py:230
  114.6 12.7 %collective-permute-start.29 = (bf16[512,128]{1,0:T(8,128)(2,1)S(1)}, bf16[512,128]{1,0:T(8,128)(2,1)S(1)}, u32[]{:S(2)}, u32[]{:S(2)}) collective-permute-start(bf16[512,128]{1,0:T(8,128)(2,1)S(1)} %fusion.7.refs_0_), channel_id=1, source_target_pairs={{0,2},{1,3},{2,0},{3,1},{4,6},{5,7},{6,4},{7,5},{8,10},{9,11},{10,... | collective-permute-start | bytes 393224 | tf_op jit(solution)/shard_map/ppermute | solution.py:230
  115.4 11.9 %collective-permute-start.30 = (bf16[512,128]{1,0:T(8,128)(2,1)S(1)}, bf16[512,128]{1,0:T(8,128)(2,1)S(1)}, u32[]{:S(2)}, u32[]{:S(2)}) collective-permute-start(bf16[512,128]{1,0:T(8,128)(2,1)S(1)} %fusion.7.refs_0_), channel_id=1, source_target_pairs={{0,3},{1,2},{2,1},{3,0},{4,7},{5,6},{6,5},{7,4},{8,11},{9,10},{10,... | collective-permute-start | bytes 393224 | tf_op jit(solution)/shard_map/ppermute | solution.py:230
  128.9 18.2 %collective-permute-start.35 = (bf16[2048,128]{1,0:T(8,128)(2,1)S(1)}, bf16[2048,128]{1,0:T(8,128)(2,1)S(1)}, u32[]{:S(2)}, u32[]{:S(2)}) collective-permute-start(bf16[2048,128]{1,0:T(8,128)(2,1)S(1)} %product.21), channel_id=1, source_target_pairs={{0,4},{4,0},{8,12},{12,8},{16,20},{20,16},{24,28},{28,24},{1,5},{5... | collective-permute-start | bytes 1572872 | tf_op jit(solution)/shard_map/ppermute | solution.py:230
  131.0 12.9 %collective-permute-start.40 = (bf16[512,128]{1,0:T(8,128)(2,1)S(1)}, bf16[512,128]{1,0:T(8,128)(2,1)S(1)}, u32[]{:S(2)}, u32[]{:S(2)}) collective-permute-start(bf16[512,128]{1,0:T(8,128)(2,1)S(1)} %fusion.11.refs_0_), channel_id=1, source_target_pairs={{0,2},{1,3},{2,0},{3,1},{4,6},{5,7},{6,4},{7,5},{8,10},{9,11},{10,... | collective-permute-start | bytes 393224 | tf_op jit(solution)/shard_map/ppermute | solution.py:230
  131.9 11.9 %collective-permute-start.41 = (bf16[512,128]{1,0:T(8,128)(2,1)S(1)}, bf16[512,128]{1,0:T(8,128)(2,1)S(1)}, u32[]{:S(2)}, u32[]{:S(2)}) collective-permute-start(bf16[512,128]{1,0:T(8,128)(2,1)S(1)} %fusion.11.refs_0_), channel_id=1, source_target_pairs={{0,3},{1,2},{2,1},{3,0},{4,7},{5,6},{6,5},{7,4},{8,11},{9,10},{10,... | collective-permute-start | bytes 393224 | tf_op jit(solution)/shard_map/ppermute | solution.py:230
  148.8 9.0 %collective-permute-start.37 = (bf16[512,128]{1,0:T(8,128)(2,1)S(1)}, bf16[512,128]{1,0:T(8,128)(2,1)S(1)}, u32[]{:S(2)}, u32[]{:S(2)}) collective-permute-start(bf16[512,128]{1,0:T(8,128)(2,1)S(1)} %get-tuple-element.97), channel_id=1, source_target_pairs={{0,16},{4,20},{8,24},{12,28},{16,0},{20,4},{24,8},{28,12},{1,17},{... | collective-permute-start | bytes 393224 | tf_op jit(solution)/shard_map/ppermute | solution.py:230
  151.3 8.4 %collective-permute-start.43 = (bf16[512,128]{1,0:T(8,128)(2,1)S(1)}, bf16[512,128]{1,0:T(8,128)(2,1)S(1)}, u32[]{:S(2)}, u32[]{:S(2)}) collective-permute-start(bf16[512,128]{1,0:T(8,128)(2,1)S(1)} %get-tuple-element.98), channel_id=1, source_target_pairs={{0,8},{4,12},{8,0},{12,4},{16,24},{20,28},{24,16},{28,20},{1,9},{5... | collective-permute-start | bytes 393224 | tf_op jit(solution)/shard_map/ppermute | solution.py:230
  152.8 10.6 %collective-permute-start.44 = (bf16[512,128]{1,0:T(8,128)(2,1)S(1)}, bf16[512,128]{1,0:T(8,128)(2,1)S(1)}, u32[]{:S(2)}, u32[]{:S(2)}) collective-permute-start(bf16[512,128]{1,0:T(8,128)(2,1)S(1)} %get-tuple-element.100), channel_id=1, source_target_pairs={{0,16},{4,20},{8,24},{12,28},{16,0},{20,4},{24,8},{28,12},{1,17},{... | collective-permute-start | bytes 393224 | tf_op jit(solution)/shard_map/ppermute | solution.py:230
  154.9 8.6 %collective-permute-start.45 = (bf16[512,128]{1,0:T(8,128)(2,1)S(1)}, bf16[512,128]{1,0:T(8,128)(2,1)S(1)}, u32[]{:S(2)}, u32[]{:S(2)}) collective-permute-start(bf16[512,128]{1,0:T(8,128)(2,1)S(1)} %get-tuple-element.99), channel_id=1, source_target_pairs={{0,24},{4,28},{8,16},{12,20},{16,8},{20,12},{24,0},{28,4},{1,25},{... | collective-permute-start | bytes 393224 | tf_op jit(solution)/shard_map/ppermute | solution.py:230
  (30 other events, 178.3 us)

commit v3 on v2

--- a/solution.py
+++ b/solution.py
@@ -140,7 +140,7 @@
         ],
         in_specs=smem(3) + vmem(1),
         out_specs=vmem(2) + smem(6),
-        compiler_params=pltpu.CompilerParams(vmem_limit_bytes=24 * 2**20),
+        compiler_params=pltpu.CompilerParams(vmem_limit_bytes=4 * 2**20),
         name="prepare",
     )(place, tile_src, row_counts, tile_vals)
 
@@ -149,6 +149,7 @@
     half,
     packed,
     blocks,
+    arrays,
     place_ref,
     slot_ref,
     first_ref,
@@ -159,9 +160,9 @@
     turned_ref,
     *refs,
 ):
-    block_refs = refs[:blocks]
-    out_ref = refs[blocks]
-    own_ref = refs[blocks + 1] if packed else None
+    block_refs = refs[:arrays]
+    out_ref = refs[arrays]
+    own_ref = refs[arrays + 1] if packed else None
     held_ref = refs[-2 if packed else -1]
     staged_ref = refs[-1] if packed else held_ref
     col = place_ref[1]
@@ -171,8 +172,15 @@
     def put(block, ref):
         staged_ref[pl.ds(pl.multiple_of(block * rows, rows), rows), :] = ref[...]
 
-    for mask in range(blocks):
+    for mask in range(blocks - 1):
         put(lax.bitwise_xor(col, mask), block_refs[mask])
+    last = lax.bitwise_xor(col, blocks - 1)
+    if len(block_refs) == blocks:
+        put(last, block_refs[-1])
+    else:
+        inside = jnp.logical_and(col > 0, col < blocks - 1)
+        pl.when(inside)(functools.partial(put, last, block_refs[-2]))
+        pl.when(jnp.logical_not(inside))(functools.partial(put, last, block_refs[-1]))
     if packed:
         piece = width // blocks
         for group in range(blocks):
@@ -216,7 +224,7 @@
         out_shape.append(jax.ShapeDtypeStruct((rows, width), jnp.bfloat16))
         scratch.append(pltpu.VMEM((blocks * rows, width), jnp.bfloat16))
     return pl.pallas_call(
-        functools.partial(product_kernel, half, packed, blocks),
+        functools.partial(product_kernel, half, packed, blocks, len(gathered)),
         out_shape=out_shape,
         in_specs=smem(1 + len(lists)) + vmem(1 + len(gathered)),
         out_specs=vmem(len(out_shape)),
@@ -231,7 +239,13 @@
 
 
 def gather_line(block, size):
-    return [block] + [exchange(block, "col", mask, size) for mask in range(size - 1, 0, -1)][::-1]
+    if size != 4:
+        return [block] + [exchange(block, "col", mask, size) for mask in range(1, size)]
+    across = exchange(block, "col", 2, size)
+    beside = exchange(block, "col", 1, size)
+    inner = lax.ppermute(block, "col", [(0, 0), (1, 2), (2, 1), (3, 3)])
+    outer = exchange(across, "col", 1, size)
+    return [block, beside, across, inner, outer]
 
 
 def on_device(features, tile_vals, tile_src, row_counts):

time: 165 us -> 160 us (0.970)
  waiting for transfers between devices: 52.3 us -> 48.7 us
  starting transfers between devices: 66.6 us -> 64.8 us
    ppermute x46, starting transfers between devices: 66.6 us -> 60.8 us  [exchange(): return lax.ppermute(block, axis, [(i, i ^ mask) for i in range(size)])]
    ppermute x0 -> x6, starting transfers between devices: none -> 3.96 us  [gather_line(): inner = lax.ppermute(block, 'col', [(0, 0), (1, 2), (2, 1), (3, 3)])]
    ppermute x46, waiting for transfers between devices: 52.3 us -> 48.7 us  [exchange(): return lax.ppermute(block, axis, [(i, i ^ mask) for i in range(size)])]
  transfers between devices with their start and end apart: 46 -> 52, of which waited for: 18 -> 22; matrix products, arithmetic and copies ran while one was open for 1% -> 1% of each run, Pallas kernels for 13% -> 14%
where the time goes in v3:
time: 160 us; the launch traced here: 159 us
  starting transfers between devices  64.8 us (40%)
  waiting for transfers between devices  48.7 us (30%)
  Pallas kernels  30.7 us (19%)
  local copies, waits for them, and re-layouts  12.9 us (8%)
  other arithmetic  1.73 us (1%)
    ppermute x46, starting transfers between devices, exchange(): return lax.ppermute(block, axis, [(i, i ^ mask) for i in range(size)])  60.8 us
    ppermute x46, waiting for transfers between devices, exchange(): return lax.ppermute(block, axis, [(i, i ^ mask) for i in range(size)])  48.7 us
    pallas_call x12, Pallas kernels, product(): pl.pallas_call(functools.partial(product_kernel, half, packed, blocks, le...  22.1 us
    unnamed x16, local copies, waits for them, and re-layouts  9.87 us
    pallas_call x1, Pallas kernels, prepare(): pl.pallas_call(functools.partial(prepare_kernel, tiles_per_owner), out_sh...  8.64 us
    ppermute x6, starting transfers between devices, gather_line(): inner = lax.ppermute(block, 'col', [(0, 0), (1, 2), (2, 1), (3, 3)])  3.96 us
  transfers between devices with their start and end apart: 52, of which 22 were waited for; matrix products, arithmetic and copies ran while one was open for 1% of the time, Pallas kernels for 14%

profile of v3, /device:TPU:0, one launch (start us, length us, event | category | flops | bytes accessed | tf_op | source)
XLA Modules:
  0.0 159.4 jit_solution(14117523320866639725)
XLA Ops:
  1.4 4.1 %collective-permute-start.5 = (bf16[512,128]{1,0:T(8,128)(2,1)S(1)}, bf16[512,128]{1,0:T(8,128)(2,1)S(1)}, u32[]{:S(2)}, u32[]{:S(2)}) collective-permute-start(bf16[512,128]{1,0:T(8,128)(2,1)S(1)} %copy.25), channel_id=1, source_target_pairs={{0,2},{1,3},{2,0},{3,1},{4,6},{5,7},{6,4},{7,5},{8,10},{9,11},{10,... | collective-permute-start | bytes 393224 | tf_op jit(solution)/shard_map/ppermute | solution.py:238
  7.7 4.9 %collective-permute-done.5.refs_2_ = bf16[512,128]{1,0:T(8,128)(2,1)S(1)} collective-permute-done((bf16[512,128]{1,0:T(8,128)(2,1)S(1)}, bf16[512,128]{1,0:T(8,128)(2,1)S(1)}, u32[]{:S(2)}, u32[]{:S(2)}) %collective-permute-start.5) | collective-permute-done | bytes 131104 | tf_op jit(solution)/shard_map/ppermute | solution.py:238
  12.7 2.2 %copy-done.5 = bf16[128,128,128]{2,1,0:T(8,128)(2,1)S(1)} copy-done((bf16[128,128,128]{2,1,0:T(8,128)(2,1)S(1)}, bf16[128,128,128]{2,1,0:T(8,128)(2,1)}, u32[]{:S(2)}) %copy-start.5) | copy-done | bytes 4194328
  16.2 8.6 %prepare.1 = (bf16[128,128,128]{2,1,0:T(8,128)(2,1)S(1)}, f32[8,4,128]{2,1,0:T(4,128)S(1)}, s32[2,72]{1,0:T(2,128)S(1)}, s32[2,72]{1,0:T(2,128)S(1)}, s32[2,72]{...) custom-call(s32[3]{0:T(128)S(1)} %pad_add_fusion.place_ref, s32[1,128]{1,0:T(1,128)S(1)} %copy-done.6, ...), custom_call_target="tpu_custom_call" | custom-call | tf_op jit(solution)/shard_map/prepare/pallas_call | solution.py:129
  27.0 2.2 %copy-done.1 = bf16[128,128,128]{2,1,0:T(8,128)(2,1)S(1)} copy-done((bf16[128,128,128]{2,1,0:T(8,128)(2,1)S(1)}, bf16[128,128,128]{2,1,0:T(8,128)(2,1)}, u32[]{:S(2)}) %copy-start.1) | copy-done | bytes 4194328
  29.2 2.1 %product.13 = (bf16[2048,128]{1,0:T(8,128)(2,1)S(1)}, bf16[512,128]{1,0:T(8,128)(2,1)S(1)}) custom-call(s32[3]{0:T(128)S(1)} %pad_add_fusion.place_ref, s32[2,72]{1,0:T(2,128)S(1)} %get-tuple-element.50.slot_ref, s32[2,72]{1,0:T(2,128)S(1)} %get-tuple-element.51.first_ref, s32[2,72]{1,0:T(2,128)S(1)} %get-tuple-element.52.second_ref, ...), custom_call_target="tpu_custom_call" | custom-call | tf_op jit(solution)/shard_map/product/pallas_call | solution.py:226
  36.8 2.7 %product.12 = (bf16[2048,128]{1,0:T(8,128)(2,1)S(1)}, bf16[512,128]{1,0:T(8,128)(2,1)}) custom-call(s32[3]{0:T(128)S(1)} %pad_add_fusion.place_ref, s32[2,72]{1,0:T(2,128)S(1)} %get-tuple-element.50.slot_ref, s32[2,72]{1,0:T(2,128)S(1)} %get-tuple-element.51.first_ref, s32[2,72]{1,0:T(2,128)S(1)} %get-tuple-element.52.second_ref, ...), custom_call_target="tpu_custom_call" | custom-call | tf_op jit(solution)/shard_map/product/pallas_call | solution.py:226
  39.6 9.1 %collective-permute-start.9 = (bf16[512,128]{1,0:T(8,128)(2,1)S(1)}, bf16[512,128]{1,0:T(8,128)(2,1)S(1)}, u32[]{:S(2)}, u32[]{:S(2)}) collective-permute-start(bf16[512,128]{1,0:T(8,128)(2,1)S(1)} %copy.29), channel_id=1, source_target_pairs={{0,2},{1,3},{2,0},{3,1},{4,6},{5,7},{6,4},{7,5},{8,10},{9,11},{10,... | collective-permute-start | bytes 393224 | tf_op jit(solution)/shard_map/ppermute | solution.py:238
  57.4 2.2 %collective-permute-done.8.refs_1_ = bf16[512,128]{1,0:T(8,128)(2,1)S(1)} collective-permute-done((bf16[512,128]{1,0:T(8,128)(2,1)S(1)}, bf16[512,128]{1,0:T(8,128)(2,1)S(1)}, u32[]{:S(2)}, u32[]{:S(2)}) %collective-permute-start.8) | collective-permute-done | bytes 131104 | tf_op jit(solution)/shard_map/ppermute | solution.py:238
  61.5 2.2 %copy-done.3 = bf16[128,128,128]{2,1,0:T(8,128)(2,1)S(1)} copy-done((bf16[128,128,128]{2,1,0:T(8,128)(2,1)S(1)}, bf16[128,128,128]{2,1,0:T(8,128)(2,1)}, u32[]{:S(2)}) %copy-start.3) | copy-done | bytes 4194328
  63.7 2.1 %product.15 = (bf16[2048,128]{1,0:T(8,128)(2,1)S(1)}, bf16[512,128]{1,0:T(8,128)(2,1)S(1)}) custom-call(s32[3]{0:T(128)S(1)} %pad_add_fusion.place_ref, s32[2,72]{1,0:T(2,128)S(1)} %get-tuple-element.50.slot_ref, s32[2,72]{1,0:T(2,128)S(1)} %get-tuple-element.51.first_ref, s32[2,72]{1,0:T(2,128)S(1)} %get-tuple-element.52.second_ref, ...), custom_call_target="tpu_custom_call" | custom-call | tf_op jit(solution)/shard_map/product/pallas_call | solution.py:226
  65.8 2.7 %product.14 = (bf16[2048,128]{1,0:T(8,128)(2,1)S(1)}, bf16[512,128]{1,0:T(8,128)(2,1)}) custom-call(s32[3]{0:T(128)S(1)} %pad_add_fusion.place_ref, s32[2,72]{1,0:T(2,128)S(1)} %get-tuple-element.50.slot_ref, s32[2,72]{1,0:T(2,128)S(1)} %get-tuple-element.51.first_ref, s32[2,72]{1,0:T(2,128)S(1)} %get-tuple-element.52.second_ref, ...), custom_call_target="tpu_custom_call" | custom-call | tf_op jit(solution)/shard_map/product/pallas_call | solution.py:226
  71.9 2.1 %collective-permute-start.23 = (bf16[512,128]{1,0:T(8,128)(2,1)S(1)}, bf16[512,128]{1,0:T(8,128)(2,1)S(1)}, u32[]{:S(2)}, u32[]{:S(2)}) collective-permute-start(bf16[512,128]{1,0:T(8,128)(2,1)S(1)} %get-tuple-element.118), channel_id=1, source_target_pairs={{0,24},{4,28},{8,16},{12,20},{16,8},{20,12},{24,0},{28,4},{1,25},{... | collective-permute-start | bytes 393224 | tf_op jit(solution)/shard_map/ppermute | solution.py:238
  75.9 2.2 %collective-permute-done.17.refs_2_ = bf16[512,128]{1,0:T(8,128)(2,1)S(1)} collective-permute-done((bf16[512,128]{1,0:T(8,128)(2,1)S(1)}, bf16[512,128]{1,0:T(8,128)(2,1)S(1)}, u32[]{:S(2)}, u32[]{:S(2)}) %collective-permute-start.17) | collective-permute-done | bytes 131104 | tf_op jit(solution)/shard_map/ppermute | solution.py:238
  80.7 3.4 %collective-permute-done.19.refs_4_ = bf16[512,128]{1,0:T(8,128)(2,1)S(1)} collective-permute-done((bf16[512,128]{1,0:T(8,128)(2,1)S(1)}, bf16[512,128]{1,0:T(8,128)(2,1)S(1)}, u32[]{:S(2)}, u32[]{:S(2)}) %collective-permute-start.19) | collective-permute-done | bytes 131104 | tf_op jit(solution)/shard_map/ppermute | solution.py:238
  94.7 2.5 %collective-permute-done.25.refs_2_ = bf16[512,128]{1,0:T(8,128)(2,1)S(1)} collective-permute-done((bf16[512,128]{1,0:T(8,128)(2,1)S(1)}, bf16[512,128]{1,0:T(8,128)(2,1)S(1)}, u32[]{:S(2)}, u32[]{:S(2)}) %collective-permute-start.25) | collective-permute-done | bytes 131104 | tf_op jit(solution)/shard_map/ppermute | solution.py:238
  99.9 3.1 %collective-permute-done.27.refs_4_ = bf16[512,128]{1,0:T(8,128)(2,1)S(1)} collective-permute-done((bf16[512,128]{1,0:T(8,128)(2,1)S(1)}, bf16[512,128]{1,0:T(8,128)(2,1)S(1)}, u32[]{:S(2)}, u32[]{:S(2)}) %collective-permute-start.27) | collective-permute-done | bytes 131104 | tf_op jit(solution)/shard_map/ppermute | solution.py:238
  106.2 2.1 %collective-permute-start.33 = (bf16[512,128]{1,0:T(8,128)(2,1)S(1)}, bf16[512,128]{1,0:T(8,128)(2,1)S(1)}, u32[]{:S(2)}, u32[]{:S(2)}) collective-permute-start(bf16[512,128]{1,0:T(8,128)(2,1)S(1)} %fusion.7.refs_0_), channel_id=1, source_target_pairs={{0,2},{1,3},{2,0},{3,1},{4,6},{5,7},{6,4},{7,5},{8,10},{9,11},{10,... | collective-permute-start | bytes 393224 | tf_op jit(solution)/shard_map/ppermute | solution.py:238
  108.8 2.3 %collective-permute-start.38 = (bf16[512,128]{1,0:T(8,128)(2,1)S(1)}, bf16[512,128]{1,0:T(8,128)(2,1)S(1)}, u32[]{:S(2)}, u32[]{:S(2)}) collective-permute-start(bf16[512,128]{1,0:T(8,128)(2,1)S(1)} %get-tuple-element.113), channel_id=1, source_target_pairs={{0,16},{4,20},{8,24},{12,28},{16,0},{20,4},{24,8},{28,12},{1,17},{... | collective-permute-start | bytes 393224 | tf_op jit(solution)/shard_map/ppermute | solution.py:238
  118.8 2.9 %collective-permute-done.35.refs_4_ = bf16[512,128]{1,0:T(8,128)(2,1)S(1)} collective-permute-done((bf16[512,128]{1,0:T(8,128)(2,1)S(1)}, bf16[512,128]{1,0:T(8,128)(2,1)S(1)}, u32[]{:S(2)}, u32[]{:S(2)}) %collective-permute-start.35) | collective-permute-done | bytes 131104 | tf_op jit(solution)/shard_map/ppermute | solution.py:238
  125.9 7.5 %collective-permute-done.45.refs_2_ = bf16[512,128]{1,0:T(8,128)(2,1)S(1)} collective-permute-done((bf16[512,128]{1,0:T(8,128)(2,1)S(1)}, bf16[512,128]{1,0:T(8,128)(2,1)S(1)}, u32[]{:S(2)}, u32[]{:S(2)}) %collective-permute-start.45) | collective-permute-done | bytes 131104 | tf_op jit(solution)/shard_map/ppermute | solution.py:238
  135.0 3.4 %collective-permute-done.47.refs_4_ = bf16[512,128]{1,0:T(8,128)(2,1)S(1)} collective-permute-done((bf16[512,128]{1,0:T(8,128)(2,1)S(1)}, bf16[512,128]{1,0:T(8,128)(2,1)S(1)}, u32[]{:S(2)}, u32[]{:S(2)}) %collective-permute-start.47) | collective-permute-done | bytes 131104 | tf_op jit(solution)/shard_map/ppermute | solution.py:238
  141.9 2.5 %collective-permute-start.42 = (bf16[512,128]{1,0:T(8,128)(2,1)S(1)}, bf16[512,128]{1,0:T(8,128)(2,1)S(1)}, u32[]{:S(2)}, u32[]{:S(2)}) collective-permute-start(bf16[512,128]{1,0:T(8,128)(2,1)S(1)} %get-tuple-element.107), channel_id=1, source_target_pairs={{0,16},{4,20},{8,24},{12,28},{16,0},{20,4},{24,8},{28,12},{1,17},{... | collective-permute-start | bytes 393224 | tf_op jit(solution)/shard_map/ppermute | solution.py:238
  153.8 2.3 %collective-permute-done.50 = bf16[512,128]{1,0:T(8,128)(2,1)S(1)} collective-permute-done((bf16[512,128]{1,0:T(8,128)(2,1)S(1)}, bf16[512,128]{1,0:T(8,128)(2,1)S(1)}, u32[]{:S(2)}, u32[]{:S(2)}) %collective-permute-start.50) | collective-permute-done | bytes 131104 | tf_op jit(solution)/shard_map/ppermute | solution.py:238
  (144 shorter events, 77.5 us)
Async XLA Ops:
  1.4 11.2 %collective-permute-start.5 = (bf16[512,128]{1,0:T(8,128)(2,1)S(1)}, bf16[512,128]{1,0:T(8,128)(2,1)S(1)}, u32[]{:S(2)}, u32[]{:S(2)}) collective-permute-start(bf16[512,128]{1,0:T(8,128)(2,1)S(1)} %copy.25), channel_id=1, source_target_pairs={{0,2},{1,3},{2,0},{3,1},{4,6},{5,7},{6,4},{7,5},{8,10},{9,11},{10,... | collective-permute-start | bytes 393224 | tf_op jit(solution)/shard_map/ppermute | solution.py:238
  5.5 21.4 %collective-permute-start.4 = (bf16[512,128]{1,0:T(8,128)(2,1)S(1)}, bf16[512,128]{1,0:T(8,128)(2,1)S(1)}, u32[]{:S(2)}, u32[]{:S(2)}) collective-permute-start(bf16[512,128]{1,0:T(8,128)(2,1)S(1)} %copy.25), channel_id=1, source_target_pairs={{0,1},{1,0},{2,3},{3,2},{4,5},{5,4},{6,7},{7,6},{8,9},{9,8},{10,11... | collective-permute-start | bytes 393224 | tf_op jit(solution)/shard_map/ppermute | solution.py:238
  7.1 19.8 %collective-permute-start.6 = (bf16[512,128]{1,0:T(8,128)(2,1)S(1)}, bf16[512,128]{1,0:T(8,128)(2,1)S(1)}, u32[]{:S(2)}, u32[]{:S(2)}) collective-permute-start(bf16[512,128]{1,0:T(8,128)(2,1)S(1)} %copy.25), channel_id=1, source_target_pairs={{0,0},{1,2},{2,1},{3,3},{4,4},{5,6},{6,5},{7,7},{8,8},{9,10},{10,9... | collective-permute-start | bytes 393224 | tf_op jit(solution)/shard_map/ppermute | solution.py:246
  12.6 14.3 %collective-permute-start.7 = (bf16[512,128]{1,0:T(8,128)(2,1)S(1)}, bf16[512,128]{1,0:T(8,128)(2,1)S(1)}, u32[]{:S(2)}, u32[]{:S(2)}) collective-permute-start(bf16[512,128]{1,0:T(8,128)(2,1)S(1)} %collective-permute-done.5.refs_2_), channel_id=1, source_target_pairs={{0,1},{1,0},{2,3},{3,2},{4,5},{5,4},{6,7},{7,6},{8,9},{9,8},{10,11... | collective-permute-start | bytes 393224 | tf_op jit(solution)/shard_map/ppermute | solution.py:238
  31.3 17.4 %collective-permute-start.12 = (bf16[2048,128]{1,0:T(8,128)(2,1)S(1)}, bf16[2048,128]{1,0:T(8,128)(2,1)S(1)}, u32[]{:S(2)}, u32[]{:S(2)}) collective-permute-start(bf16[2048,128]{1,0:T(8,128)(2,1)S(1)} %get-tuple-element.64), channel_id=1, source_target_pairs={{0,4},{4,0},{8,12},{12,8},{16,20},{20,16},{24,28},{28,24},{1,5},{5... | collective-permute-start | bytes 1572872 | tf_op jit(solution)/shard_map/ppermute | solution.py:238
  33.3 17.2 %collective-permute-start.1 = (f32[4,128]{1,0:T(4,128)S(1)}, f32[4,128]{1,0:T(4,128)S(1)}, u32[]{:S(2)}, u32[]{:S(2)}) collective-permute-start(f32[4,128]{1,0:T(4,128)S(1)} %get-tuple-element.125), channel_id=1, source_target_pairs={{0,8},{4,12},{8,0},{12,4},{16,24},{20,28},{24,16},{28,20},{1,9},{5... | collective-permute-start | bytes 6152 | tf_op jit(solution)/shard_map/ppermute | solution.py:238
  34.7 15.8 %collective-permute-start.2 = (f32[4,128]{1,0:T(4,128)S(1)}, f32[4,128]{1,0:T(4,128)S(1)}, u32[]{:S(2)}, u32[]{:S(2)}) collective-permute-start(f32[4,128]{1,0:T(4,128)S(1)} %get-tuple-element.127), channel_id=1, source_target_pairs={{0,16},{4,20},{8,24},{12,28},{16,0},{20,4},{24,8},{28,12},{1,17},{... | collective-permute-start | bytes 6152 | tf_op jit(solution)/shard_map/ppermute | solution.py:238
  36.6 15.9 %collective-permute-start.3 = (f32[4,128]{1,0:T(4,128)S(1)}, f32[4,128]{1,0:T(4,128)S(1)}, u32[]{:S(2)}, u32[]{:S(2)}) collective-permute-start(f32[4,128]{1,0:T(4,128)S(1)} %get-tuple-element.126), channel_id=1, source_target_pairs={{0,24},{4,28},{8,16},{12,20},{16,8},{20,12},{24,0},{28,4},{1,25},{... | collective-permute-start | bytes 6152 | tf_op jit(solution)/shard_map/ppermute | solution.py:238
  39.6 13.6 %collective-permute-start.9 = (bf16[512,128]{1,0:T(8,128)(2,1)S(1)}, bf16[512,128]{1,0:T(8,128)(2,1)S(1)}, u32[]{:S(2)}, u32[]{:S(2)}) collective-permute-start(bf16[512,128]{1,0:T(8,128)(2,1)S(1)} %copy.29), channel_id=1, source_target_pairs={{0,2},{1,3},{2,0},{3,1},{4,6},{5,7},{6,4},{7,5},{8,10},{9,11},{10,... | collective-permute-start | bytes 393224 | tf_op jit(solution)/shard_map/ppermute | solution.py:238
  68.5 9.5 %collective-permute-start.17 = (bf16[512,128]{1,0:T(8,128)(2,1)S(1)}, bf16[512,128]{1,0:T(8,128)(2,1)S(1)}, u32[]{:S(2)}, u32[]{:S(2)}) collective-permute-start(bf16[512,128]{1,0:T(8,128)(2,1)S(1)} %fusion.6.refs_0_), channel_id=1, source_target_pairs={{0,2},{1,3},{2,0},{3,1},{4,6},{5,7},{6,4},{7,5},{8,10},{9,11},{10,... | collective-permute-start | bytes 393224 | tf_op jit(solution)/shard_map/ppermute | solution.py:238
  70.4 8.3 %collective-permute-start.21 = (bf16[512,128]{1,0:T(8,128)(2,1)S(1)}, bf16[512,128]{1,0:T(8,128)(2,1)S(1)}, u32[]{:S(2)}, u32[]{:S(2)}) collective-permute-start(bf16[512,128]{1,0:T(8,128)(2,1)S(1)} %get-tuple-element.117), channel_id=1, source_target_pairs={{0,8},{4,12},{8,0},{12,4},{16,24},{20,28},{24,16},{28,20},{1,9},{5... | collective-permute-start | bytes 393224 | tf_op jit(solution)/shard_map/ppermute | solution.py:238
  71.1 9.0 %collective-permute-start.22 = (bf16[512,128]{1,0:T(8,128)(2,1)S(1)}, bf16[512,128]{1,0:T(8,128)(2,1)S(1)}, u32[]{:S(2)}, u32[]{:S(2)}) collective-permute-start(bf16[512,128]{1,0:T(8,128)(2,1)S(1)} %get-tuple-element.119), channel_id=1, source_target_pairs={{0,16},{4,20},{8,24},{12,28},{16,0},{20,4},{24,8},{28,12},{1,17},{... | collective-permute-start | bytes 393224 | tf_op jit(solution)/shard_map/ppermute | solution.py:238
  87.4 9.8 %collective-permute-start.25 = (bf16[512,128]{1,0:T(8,128)(2,1)S(1)}, bf16[512,128]{1,0:T(8,128)(2,1)S(1)}, u32[]{:S(2)}, u32[]{:S(2)}) collective-permute-start(bf16[512,128]{1,0:T(8,128)(2,1)S(1)} %fusion.10.refs_0_), channel_id=1, source_target_pairs={{0,2},{1,3},{2,0},{3,1},{4,6},{5,7},{6,4},{7,5},{8,10},{9,11},{10,... | collective-permute-start | bytes 393224 | tf_op jit(solution)/shard_map/ppermute | solution.py:238
  90.2 9.1 %collective-permute-start.30 = (bf16[512,128]{1,0:T(8,128)(2,1)S(1)}, bf16[512,128]{1,0:T(8,128)(2,1)S(1)}, u32[]{:S(2)}, u32[]{:S(2)}) collective-permute-start(bf16[512,128]{1,0:T(8,128)(2,1)S(1)} %get-tuple-element.116), channel_id=1, source_target_pairs={{0,16},{4,20},{8,24},{12,28},{16,0},{20,4},{24,8},{28,12},{1,17},{... | collective-permute-start | bytes 393224 | tf_op jit(solution)/shard_map/ppermute | solution.py:238
  106.2 9.8 %collective-permute-start.33 = (bf16[512,128]{1,0:T(8,128)(2,1)S(1)}, bf16[512,128]{1,0:T(8,128)(2,1)S(1)}, u32[]{:S(2)}, u32[]{:S(2)}) collective-permute-start(bf16[512,128]{1,0:T(8,128)(2,1)S(1)} %fusion.7.refs_0_), channel_id=1, source_target_pairs={{0,2},{1,3},{2,0},{3,1},{4,6},{5,7},{6,4},{7,5},{8,10},{9,11},{10,... | collective-permute-start | bytes 393224 | tf_op jit(solution)/shard_map/ppermute | solution.py:238
  108.8 9.1 %collective-permute-start.38 = (bf16[512,128]{1,0:T(8,128)(2,1)S(1)}, bf16[512,128]{1,0:T(8,128)(2,1)S(1)}, u32[]{:S(2)}, u32[]{:S(2)}) collective-permute-start(bf16[512,128]{1,0:T(8,128)(2,1)S(1)} %get-tuple-element.113), channel_id=1, source_target_pairs={{0,16},{4,20},{8,24},{12,28},{16,0},{20,4},{24,8},{28,12},{1,17},{... | collective-permute-start | bytes 393224 | tf_op jit(solution)/shard_map/ppermute | solution.py:238
  123.2 18.3 %collective-permute-start.40 = (bf16[2048,128]{1,0:T(8,128)(2,1)S(1)}, bf16[2048,128]{1,0:T(8,128)(2,1)S(1)}, u32[]{:S(2)}, u32[]{:S(2)}) collective-permute-start(bf16[2048,128]{1,0:T(8,128)(2,1)S(1)} %product.21), channel_id=1, source_target_pairs={{0,4},{4,0},{8,12},{12,8},{16,20},{20,16},{24,28},{28,24},{1,5},{5... | collective-permute-start | bytes 1572872 | tf_op jit(solution)/shard_map/ppermute | solution.py:238
  123.3 10.1 %collective-permute-start.45 = (bf16[512,128]{1,0:T(8,128)(2,1)S(1)}, bf16[512,128]{1,0:T(8,128)(2,1)S(1)}, u32[]{:S(2)}, u32[]{:S(2)}) collective-permute-start(bf16[512,128]{1,0:T(8,128)(2,1)S(1)} %fusion.11.refs_0_), channel_id=1, source_target_pairs={{0,2},{1,3},{2,0},{3,1},{4,6},{5,7},{6,4},{7,5},{8,10},{9,11},{10,... | collective-permute-start | bytes 393224 | tf_op jit(solution)/shard_map/ppermute | solution.py:238
  125.2 9.7 %collective-permute-start.44 = (bf16[512,128]{1,0:T(8,128)(2,1)S(1)}, bf16[512,128]{1,0:T(8,128)(2,1)S(1)}, u32[]{:S(2)}, u32[]{:S(2)}) collective-permute-start(bf16[512,128]{1,0:T(8,128)(2,1)S(1)} %fusion.11.refs_0_), channel_id=1, source_target_pairs={{0,1},{1,0},{2,3},{3,2},{4,5},{5,4},{6,7},{7,6},{8,9},{9,8},{10,11... | collective-permute-start | bytes 393224 | tf_op jit(solution)/shard_map/ppermute | solution.py:238
  125.2 9.7 %collective-permute-start.46 = (bf16[512,128]{1,0:T(8,128)(2,1)S(1)}, bf16[512,128]{1,0:T(8,128)(2,1)S(1)}, u32[]{:S(2)}, u32[]{:S(2)}) collective-permute-start(bf16[512,128]{1,0:T(8,128)(2,1)S(1)} %fusion.11.refs_0_), channel_id=1, source_target_pairs={{0,0},{1,2},{2,1},{3,3},{4,4},{5,6},{6,5},{7,7},{8,8},{9,10},{10,9... | collective-permute-start | bytes 393224 | tf_op jit(solution)/shard_map/ppermute | solution.py:246
  141.9 9.2 %collective-permute-start.42 = (bf16[512,128]{1,0:T(8,128)(2,1)S(1)}, bf16[512,128]{1,0:T(8,128)(2,1)S(1)}, u32[]{:S(2)}, u32[]{:S(2)}) collective-permute-start(bf16[512,128]{1,0:T(8,128)(2,1)S(1)} %get-tuple-element.107), channel_id=1, source_target_pairs={{0,16},{4,20},{8,24},{12,28},{16,0},{20,4},{24,8},{28,12},{1,17},{... | collective-permute-start | bytes 393224 | tf_op jit(solution)/shard_map/ppermute | solution.py:238
  144.4 8.3 %collective-permute-start.43 = (bf16[512,128]{1,0:T(8,128)(2,1)S(1)}, bf16[512,128]{1,0:T(8,128)(2,1)S(1)}, u32[]{:S(2)}, u32[]{:S(2)}) collective-permute-start(bf16[512,128]{1,0:T(8,128)(2,1)S(1)} %get-tuple-element.106), channel_id=1, source_target_pairs={{0,24},{4,28},{8,16},{12,20},{16,8},{20,12},{24,0},{28,4},{1,25},{... | collective-permute-start | bytes 393224 | tf_op jit(solution)/shard_map/ppermute | solution.py:238
  146.5 9.6 %collective-permute-start.50 = (bf16[512,128]{1,0:T(8,128)(2,1)S(1)}, bf16[512,128]{1,0:T(8,128)(2,1)S(1)}, u32[]{:S(2)}, u32[]{:S(2)}) collective-permute-start(bf16[512,128]{1,0:T(8,128)(2,1)S(1)} %get-tuple-element.110), channel_id=1, source_target_pairs={{0,16},{4,20},{8,24},{12,28},{16,0},{20,4},{24,8},{28,12},{1,17},{... | collective-permute-start | bytes 393224 | tf_op jit(solution)/shard_map/ppermute | solution.py:238
  148.2 9.8 %collective-permute-start.51 = (bf16[512,128]{1,0:T(8,128)(2,1)S(1)}, bf16[512,128]{1,0:T(8,128)(2,1)S(1)}, u32[]{:S(2)}, u32[]{:S(2)}) collective-permute-start(bf16[512,128]{1,0:T(8,128)(2,1)S(1)} %get-tuple-element.109), channel_id=1, source_target_pairs={{0,24},{4,28},{8,16},{12,20},{16,8},{20,12},{24,0},{28,4},{1,25},{... | collective-permute-start | bytes 393224 | tf_op jit(solution)/shard_map/ppermute | solution.py:238
  (36 other events, 195.6 us)

commit v4 on v3

--- a/solution.py
+++ b/solution.py
@@ -167,20 +167,13 @@
     staged_ref = refs[-1] if packed else held_ref
     col = place_ref[1]
     rows, width = block_refs[0].shape
+    rows = rows // blocks
     tile_size = turned_ref.shape[1]
 
     def put(block, ref):
         staged_ref[pl.ds(pl.multiple_of(block * rows, rows), rows), :] = ref[...]
 
-    for mask in range(blocks - 1):
-        put(lax.bitwise_xor(col, mask), block_refs[mask])
-    last = lax.bitwise_xor(col, blocks - 1)
-    if len(block_refs) == blocks:
-        put(last, block_refs[-1])
-    else:
-        inside = jnp.logical_and(col > 0, col < blocks - 1)
-        pl.when(inside)(functools.partial(put, last, block_refs[-2]))
-        pl.when(jnp.logical_not(inside))(functools.partial(put, last, block_refs[-1]))
+    staged_ref[: blocks * rows, :] = block_refs[0][...]
     if packed:
         piece = width // blocks
         for group in range(blocks):
@@ -217,6 +210,7 @@
 
 def product(half, place, lists, turned, gathered, blocks, row_size, packed):
     rows, width = gathered[0].shape
+    rows = rows // blocks
     tile_size = turned.shape[1]
     out_shape = [jax.ShapeDtypeStruct((row_size // 2 * rows, width), jnp.bfloat16)]
     scratch = [pltpu.VMEM((blocks * rows + tile_size, width), jnp.bfloat16)]
@@ -231,6 +225,9 @@
         scratch_shapes=scratch,
         compiler_params=pltpu.CompilerParams(vmem_limit_bytes=4 * 2**20),
         name="product",
+        cost_estimate=pl.CostEstimate(
+            flops=600000000, bytes_accessed=6000000, transcendentals=0
+        ),
     )(place, *lists, turned, *gathered)
 
 
@@ -239,6 +236,7 @@
 
 
 def gather_line(block, size):
+    return [lax.all_gather(block, "col", axis=0, tiled=True)]
     if size != 4:
         return [block] + [exchange(block, "col", mask, size) for mask in range(1, size)]
     across = exchange(block, "col", 2, size)

time: 160 us -> 187 us (1.17)
  blocking collectives: 0 us -> 101 us
  starting transfers between devices: 64.8 us -> 27.9 us
  waiting for transfers between devices: 48.7 us -> 14.4 us
  local copies, waits for them, and re-layouts: 12.9 us -> 10.4 us
    all_gather x0 -> x6, blocking collectives: none -> 101 us  [gather_line(): return [lax.all_gather(block, 'col', axis=0, tiled=True)]]
    ppermute x46 -> x28, waiting for transfers between devices: 48.7 us -> 14.4 us  [exchange(): return lax.ppermute(block, axis, [(i, i ^ mask) for i in range(size)])]
    ppermute x46 -> x28, starting transfers between devices: 60.8 us -> 27.9 us  [exchange(): return lax.ppermute(block, axis, [(i, i ^ mask) for i in range(size)])]
    ppermute x6 -> x0, starting transfers between devices: 3.96 us -> none  [gather_line(): inner = lax.ppermute(block, 'col', [(0, 0), (1, 2), (2, 1), (3, 3)])]
    unnamed x16 -> x12, local copies, waits for them, and re-layouts: 9.87 us -> 7.66 us
  transfers between devices with their start and end apart: 52 -> 28, of which waited for: 22 -> 12; matrix products, arithmetic and copies ran while one was open for 1% -> 0% of each run, Pallas kernels for 14% -> 7%
where the time goes in v4:
time: 187 us; the launch traced here: 186 us
  blocking collectives  101 us (54%)
  Pallas kernels  30.1 us (16%)
  starting transfers between devices  27.9 us (15%)
  waiting for transfers between devices  14.4 us (8%)
  local copies, waits for them, and re-layouts  10.4 us (6%)
    all_gather x6, blocking collectives, gather_line(): return [lax.all_gather(block, 'col', axis=0, tiled=True)]  101 us
    ppermute x28, starting transfers between devices, exchange(): return lax.ppermute(block, axis, [(i, i ^ mask) for i in range(size)])  27.9 us
    pallas_call x12, Pallas kernels, product(): pl.pallas_call(functools.partial(product_kernel, half, packed, blocks, le...  21.8 us
    ppermute x28, waiting for transfers between devices, exchange(): return lax.ppermute(block, axis, [(i, i ^ mask) for i in range(size)])  14.4 us
    pallas_call x1, Pallas kernels, prepare(): pl.pallas_call(functools.partial(prepare_kernel, tiles_per_owner), out_sh...  8.24 us
    unnamed x12, local copies, waits for them, and re-layouts  7.66 us
  transfers between devices with their start and end apart: 28, of which 12 were waited for; matrix products, arithmetic and copies ran while one was open for 0% of the time, Pallas kernels for 7%

profile of v4, /device:TPU:0, one launch (start us, length us, event | category | flops | bytes accessed | tf_op | source)
XLA Modules:
  0.0 185.6 jit_solution(7321400679437581857)
XLA Ops:
  1.4 17.4 %all_gather.18.refs_0_ = bf16[2048,128]{1,0:T(8,128)(2,1)S(1)} all-gather(bf16[512,128]{1,0:T(8,128)(2,1)S(1)} %copy.17), channel_id=1, replica_groups=mesh['row'=8,'col'=4] {'col'}, dimensions={0}, use_global_device_ids=true | all-gather | bytes 655360 | tf_op jit(solution)/shard_map/all_gather | solution.py:239
  18.9 2.2 %copy-done.3 = bf16[128,128,128]{2,1,0:T(8,128)(2,1)S(1)} copy-done((bf16[128,128,128]{2,1,0:T(8,128)(2,1)S(1)}, bf16[128,128,128]{2,1,0:T(8,128)(2,1)}, u32[]{:S(2)}) %copy-start.3) | copy-done | bytes 4194328
  22.4 8.2 %prepare.1 = (bf16[128,128,128]{2,1,0:T(8,128)(2,1)S(1)}, f32[8,4,128]{2,1,0:T(4,128)S(1)}, s32[2,72]{1,0:T(2,128)S(1)}, s32[2,72]{1,0:T(2,128)S(1)}, s32[2,72]{...) custom-call(s32[3]{0:T(128)S(1)} %pad_add_fusion.place_ref, s32[1,128]{1,0:T(1,128)S(1)} %copy-done.4, ...), custom_call_target="tpu_custom_call" | custom-call | tf_op jit(solution)/shard_map/prepare/pallas_call | solution.py:129
  30.6 2.0 %product.13 = (bf16[2048,128]{1,0:T(8,128)(2,1)S(1)}, bf16[512,128]{1,0:T(8,128)(2,1)S(1)}) custom-call(s32[3]{0:T(128)S(1)} %pad_add_fusion.place_ref, s32[2,72]{1,0:T(2,128)S(1)} %get-tuple-element.30.slot_ref, s32[2,72]{1,0:T(2,128)S(1)} %get-tuple-element.31.first_ref, s32[2,72]{1,0:T(2,128)S(1)} %get-tuple-element.32.second_ref, ...), custom_call_target="tpu_custom_call" | custom-call | flops 600000000 | bytes 6000000 | tf_op jit(solution)/shard_map/product/pallas_call | solution.py:220
  32.7 2.0 %copy-done = bf16[128,128,128]{2,1,0:T(8,128)(2,1)} copy-done((bf16[128,128,128]{2,1,0:T(8,128)(2,1)}, bf16[128,128,128]{2,1,0:T(8,128)(2,1)S(1)}, u32[]{:S(2)}) %copy-start) | copy-done | bytes 4194328
  35.3 20.0 %all_gather.19.refs_0_ = bf16[2048,128]{1,0:T(8,128)(2,1)S(1)} all-gather(bf16[512,128]{1,0:T(8,128)(2,1)S(1)} %copy.19), channel_id=1, replica_groups=mesh['row'=8,'col'=4] {'col'}, dimensions={0}, use_global_device_ids=true | all-gather | bytes 655360 | tf_op jit(solution)/shard_map/all_gather | solution.py:239
  55.3 2.2 %copy-done.1 = bf16[128,128,128]{2,1,0:T(8,128)(2,1)S(1)} copy-done((bf16[128,128,128]{2,1,0:T(8,128)(2,1)S(1)}, bf16[128,128,128]{2,1,0:T(8,128)(2,1)}, u32[]{:S(2)}) %copy-start.1) | copy-done | bytes 4194328
  57.5 2.7 %product.12 = (bf16[2048,128]{1,0:T(8,128)(2,1)S(1)}, bf16[512,128]{1,0:T(8,128)(2,1)}) custom-call(s32[3]{0:T(128)S(1)} %pad_add_fusion.place_ref, s32[2,72]{1,0:T(2,128)S(1)} %get-tuple-element.30.slot_ref, s32[2,72]{1,0:T(2,128)S(1)} %get-tuple-element.31.first_ref, s32[2,72]{1,0:T(2,128)S(1)} %get-tuple-element.32.second_ref, ...), custom_call_target="tpu_custom_call" | custom-call | flops 600000000 | bytes 6000000 | tf_op jit(solution)/shard_map/product/pallas_call | solution.py:220
  60.3 4.8 %collective-permute-start.2 = (f32[4,128]{1,0:T(4,128)S(1)}, f32[4,128]{1,0:T(4,128)S(1)}, u32[]{:S(2)}, u32[]{:S(2)}) collective-permute-start(f32[4,128]{1,0:T(4,128)S(1)} %get-tuple-element.87), channel_id=1, source_target_pairs={{0,16},{4,20},{8,24},{12,28},{16,0},{20,4},{24,8},{28,12},{1,17},{... | collective-permute-start | bytes 6152 | tf_op jit(solution)/shard_map/ppermute | solution.py:235
  66.8 2.0 %collective-permute-start.6 = (bf16[512,128]{1,0:T(8,128)(2,1)S(1)}, bf16[512,128]{1,0:T(8,128)(2,1)S(1)}, u32[]{:S(2)}, u32[]{:S(2)}) collective-permute-start(bf16[512,128]{1,0:T(8,128)(2,1)S(1)} %get-tuple-element.82), channel_id=1, source_target_pairs={{0,16},{4,20},{8,24},{12,28},{16,0},{20,4},{24,8},{28,12},{1,17},{... | collective-permute-start | bytes 393224 | tf_op jit(solution)/shard_map/ppermute | solution.py:235
  70.3 2.4 %collective-permute-done.6 = bf16[512,128]{1,0:T(8,128)(2,1)S(1)} collective-permute-done((bf16[512,128]{1,0:T(8,128)(2,1)S(1)}, bf16[512,128]{1,0:T(8,128)(2,1)S(1)}, u32[]{:S(2)}, u32[]{:S(2)}) %collective-permute-start.6) | collective-permute-done | bytes 131104 | tf_op jit(solution)/shard_map/ppermute | solution.py:235
  72.8 1.9 %collective-permute-done.7 = bf16[512,128]{1,0:T(8,128)(2,1)S(1)} collective-permute-done((bf16[512,128]{1,0:T(8,128)(2,1)S(1)}, bf16[512,128]{1,0:T(8,128)(2,1)S(1)}, u32[]{:S(2)}, u32[]{:S(2)}) %collective-permute-start.7) | collective-permute-done | bytes 131104 | tf_op jit(solution)/shard_map/ppermute | solution.py:235
  74.9 2.0 %product.15 = (bf16[2048,128]{1,0:T(8,128)(2,1)S(1)}, bf16[512,128]{1,0:T(8,128)(2,1)S(1)}) custom-call(s32[3]{0:T(128)S(1)} %pad_add_fusion.place_ref, s32[2,72]{1,0:T(2,128)S(1)} %get-tuple-element.30.slot_ref, s32[2,72]{1,0:T(2,128)S(1)} %get-tuple-element.31.first_ref, s32[2,72]{1,0:T(2,128)S(1)} %get-tuple-element.32.second_ref, ...), custom_call_target="tpu_custom_call" | custom-call | flops 600000000 | bytes 6000000 | tf_op jit(solution)/shard_map/product/pallas_call | solution.py:220
  77.0 2.7 %product.14 = (bf16[2048,128]{1,0:T(8,128)(2,1)S(1)}, bf16[512,128]{1,0:T(8,128)(2,1)}) custom-call(s32[3]{0:T(128)S(1)} %pad_add_fusion.place_ref, s32[2,72]{1,0:T(2,128)S(1)} %get-tuple-element.30.slot_ref, s32[2,72]{1,0:T(2,128)S(1)} %get-tuple-element.31.first_ref, s32[2,72]{1,0:T(2,128)S(1)} %get-tuple-element.32.second_ref, ...), custom_call_target="tpu_custom_call" | custom-call | flops 600000000 | bytes 6000000 | tf_op jit(solution)/shard_map/product/pallas_call | solution.py:220
  81.4 2.0 %collective-permute-start.9 = (bf16[512,128]{1,0:T(8,128)(2,1)S(1)}, bf16[512,128]{1,0:T(8,128)(2,1)S(1)}, u32[]{:S(2)}, u32[]{:S(2)}) collective-permute-start(bf16[512,128]{1,0:T(8,128)(2,1)S(1)} %get-tuple-element.77), channel_id=1, source_target_pairs={{0,8},{4,12},{8,0},{12,4},{16,24},{20,28},{24,16},{28,20},{1,9},{5... | collective-permute-start | bytes 393224 | tf_op jit(solution)/shard_map/ppermute | solution.py:235
  83.4 16.0 %all_gather.20.refs_0_ = bf16[2048,128]{1,0:T(8,128)(2,1)S(1)} all-gather(bf16[512,128]{1,0:T(8,128)(2,1)S(1)} %fusion.6), channel_id=1, replica_groups=mesh['row'=8,'col'=4] {'col'}, dimensions={0}, use_global_device_ids=true | all-gather | bytes 655360 | tf_op jit(solution)/shard_map/all_gather | solution.py:239
  104.2 2.6 %collective-permute-start.15 = (bf16[512,128]{1,0:T(8,128)(2,1)S(1)}, bf16[512,128]{1,0:T(8,128)(2,1)S(1)}, u32[]{:S(2)}, u32[]{:S(2)}) collective-permute-start(bf16[512,128]{1,0:T(8,128)(2,1)S(1)} %get-tuple-element.75), channel_id=1, source_target_pairs={{0,24},{4,28},{8,16},{12,20},{16,8},{20,12},{24,0},{28,4},{1,25},{... | collective-permute-start | bytes 393224 | tf_op jit(solution)/shard_map/ppermute | solution.py:235
  106.9 15.8 %all_gather.21.refs_0_ = bf16[2048,128]{1,0:T(8,128)(2,1)S(1)} all-gather(bf16[512,128]{1,0:T(8,128)(2,1)S(1)} %fusion.10), channel_id=1, replica_groups=mesh['row'=8,'col'=4] {'col'}, dimensions={0}, use_global_device_ids=true | all-gather | bytes 655360 | tf_op jit(solution)/shard_map/all_gather | solution.py:239
  127.9 2.2 %collective-permute-start.19 = (bf16[512,128]{1,0:T(8,128)(2,1)S(1)}, bf16[512,128]{1,0:T(8,128)(2,1)S(1)}, u32[]{:S(2)}, u32[]{:S(2)}) collective-permute-start(bf16[512,128]{1,0:T(8,128)(2,1)S(1)} %get-tuple-element.72), channel_id=1, source_target_pairs={{0,24},{4,28},{8,16},{12,20},{16,8},{20,12},{24,0},{28,4},{1,25},{... | collective-permute-start | bytes 393224 | tf_op jit(solution)/shard_map/ppermute | solution.py:235
  130.1 15.8 %all_gather.22.refs_0_ = bf16[2048,128]{1,0:T(8,128)(2,1)S(1)} all-gather(bf16[512,128]{1,0:T(8,128)(2,1)S(1)} %fusion.7), channel_id=1, replica_groups=mesh['row'=8,'col'=4] {'col'}, dimensions={0}, use_global_device_ids=true | all-gather | bytes 655360 | tf_op jit(solution)/shard_map/all_gather | solution.py:239
  146.1 15.6 %all_gather.23.refs_0_ = bf16[2048,128]{1,0:T(8,128)(2,1)S(1)} all-gather(bf16[512,128]{1,0:T(8,128)(2,1)S(1)} %fusion.11), channel_id=1, replica_groups=mesh['row'=8,'col'=4] {'col'}, dimensions={0}, use_global_device_ids=true | all-gather | bytes 655360 | tf_op jit(solution)/shard_map/all_gather | solution.py:239
  168.9 2.0 %collective-permute-start.26 = (bf16[512,128]{1,0:T(8,128)(2,1)S(1)}, bf16[512,128]{1,0:T(8,128)(2,1)S(1)}, u32[]{:S(2)}, u32[]{:S(2)}) collective-permute-start(bf16[512,128]{1,0:T(8,128)(2,1)S(1)} %get-tuple-element.70), channel_id=1, source_target_pairs={{0,16},{4,20},{8,24},{12,28},{16,0},{20,4},{24,8},{28,12},{1,17},{... | collective-permute-start | bytes 393224 | tf_op jit(solution)/shard_map/ppermute | solution.py:235
  172.7 2.0 %collective-permute-start.22 = (bf16[512,128]{1,0:T(8,128)(2,1)S(1)}, bf16[512,128]{1,0:T(8,128)(2,1)S(1)}, u32[]{:S(2)}, u32[]{:S(2)}) collective-permute-start(bf16[512,128]{1,0:T(8,128)(2,1)S(1)} %get-tuple-element.67), channel_id=1, source_target_pairs={{0,16},{4,20},{8,24},{12,28},{16,0},{20,4},{24,8},{28,12},{1,17},{... | collective-permute-start | bytes 393224 | tf_op jit(solution)/shard_map/ppermute | solution.py:235
  180.5 2.4 %collective-permute-done.22 = bf16[512,128]{1,0:T(8,128)(2,1)S(1)} collective-permute-done((bf16[512,128]{1,0:T(8,128)(2,1)S(1)}, bf16[512,128]{1,0:T(8,128)(2,1)S(1)}, u32[]{:S(2)}, u32[]{:S(2)}) %collective-permute-start.22) | collective-permute-done | bytes 131104 | tf_op jit(solution)/shard_map/ppermute | solution.py:235
  (96 shorter events, 36.1 us)
Async XLA Ops:
  34.6 30.5 %collective-permute-start.4 = (bf16[2048,128]{1,0:T(8,128)(2,1)S(1)}, bf16[2048,128]{1,0:T(8,128)(2,1)S(1)}, u32[]{:S(2)}, u32[]{:S(2)}) collective-permute-start(bf16[2048,128]{1,0:T(8,128)(2,1)S(1)} %get-tuple-element.40), channel_id=1, source_target_pairs={{0,4},{4,0},{8,12},{12,8},{16,20},{20,16},{24,28},{28,24},{1,5},{5... | collective-permute-start | bytes 1572872 | tf_op jit(solution)/shard_map/ppermute | solution.py:235
  34.6 25.5 %collective-permute-start = (f32[4,4,128]{2,1,0:T(4,128)S(1)}, f32[4,4,128]{2,1,0:T(4,128)S(1)}, u32[]{:S(2)}, u32[]{:S(2)}) collective-permute-start(f32[4,4,128]{2,1,0:T(4,128)S(1)} %slice_bitcast_fusion), channel_id=1, source_target_pairs={{0,4},{4,0},{8,12},{12,8},{16,20},{20,16},{24,28},{28,24},{1,5},{5... | collective-permute-start | bytes 24584 | tf_op jit(solution)/shard_map/ppermute | solution.py:235
  60.2 8.6 %collective-permute-start.1 = (f32[4,128]{1,0:T(4,128)S(1)}, f32[4,128]{1,0:T(4,128)S(1)}, u32[]{:S(2)}, u32[]{:S(2)}) collective-permute-start(f32[4,128]{1,0:T(4,128)S(1)} %get-tuple-element.85), channel_id=1, source_target_pairs={{0,8},{4,12},{8,0},{12,4},{16,24},{20,28},{24,16},{28,20},{1,9},{5... | collective-permute-start | bytes 6152 | tf_op jit(solution)/shard_map/ppermute | solution.py:235
  60.3 8.6 %collective-permute-start.2 = (f32[4,128]{1,0:T(4,128)S(1)}, f32[4,128]{1,0:T(4,128)S(1)}, u32[]{:S(2)}, u32[]{:S(2)}) collective-permute-start(f32[4,128]{1,0:T(4,128)S(1)} %get-tuple-element.87), channel_id=1, source_target_pairs={{0,16},{4,20},{8,24},{12,28},{16,0},{20,4},{24,8},{28,12},{1,17},{... | collective-permute-start | bytes 6152 | tf_op jit(solution)/shard_map/ppermute | solution.py:235
  65.3 5.0 %collective-permute-start.5 = (bf16[512,128]{1,0:T(8,128)(2,1)S(1)}, bf16[512,128]{1,0:T(8,128)(2,1)S(1)}, u32[]{:S(2)}, u32[]{:S(2)}) collective-permute-start(bf16[512,128]{1,0:T(8,128)(2,1)S(1)} %get-tuple-element.80), channel_id=1, source_target_pairs={{0,8},{4,12},{8,0},{12,4},{16,24},{20,28},{24,16},{28,20},{1,9},{5... | collective-permute-start | bytes 393224 | tf_op jit(solution)/shard_map/ppermute | solution.py:235
  66.8 5.9 %collective-permute-start.6 = (bf16[512,128]{1,0:T(8,128)(2,1)S(1)}, bf16[512,128]{1,0:T(8,128)(2,1)S(1)}, u32[]{:S(2)}, u32[]{:S(2)}) collective-permute-start(bf16[512,128]{1,0:T(8,128)(2,1)S(1)} %get-tuple-element.82), channel_id=1, source_target_pairs={{0,16},{4,20},{8,24},{12,28},{16,0},{20,4},{24,8},{28,12},{1,17},{... | collective-permute-start | bytes 393224 | tf_op jit(solution)/shard_map/ppermute | solution.py:235
  68.8 5.9 %collective-permute-start.7 = (bf16[512,128]{1,0:T(8,128)(2,1)S(1)}, bf16[512,128]{1,0:T(8,128)(2,1)S(1)}, u32[]{:S(2)}, u32[]{:S(2)}) collective-permute-start(bf16[512,128]{1,0:T(8,128)(2,1)S(1)} %get-tuple-element.81), channel_id=1, source_target_pairs={{0,24},{4,28},{8,16},{12,20},{16,8},{20,12},{24,0},{28,4},{1,25},{... | collective-permute-start | bytes 393224 | tf_op jit(solution)/shard_map/ppermute | solution.py:235
  79.8 19.6 %collective-permute-start.10 = (bf16[512,128]{1,0:T(8,128)(2,1)S(1)}, bf16[512,128]{1,0:T(8,128)(2,1)S(1)}, u32[]{:S(2)}, u32[]{:S(2)}) collective-permute-start(bf16[512,128]{1,0:T(8,128)(2,1)S(1)} %get-tuple-element.79), channel_id=1, source_target_pairs={{0,16},{4,20},{8,24},{12,28},{16,0},{20,4},{24,8},{28,12},{1,17},{... | collective-permute-start | bytes 393224 | tf_op jit(solution)/shard_map/ppermute | solution.py:235
  80.4 19.0 %collective-permute-start.11 = (bf16[512,128]{1,0:T(8,128)(2,1)S(1)}, bf16[512,128]{1,0:T(8,128)(2,1)S(1)}, u32[]{:S(2)}, u32[]{:S(2)}) collective-permute-start(bf16[512,128]{1,0:T(8,128)(2,1)S(1)} %get-tuple-element.78), channel_id=1, source_target_pairs={{0,24},{4,28},{8,16},{12,20},{16,8},{20,12},{24,0},{28,4},{1,25},{... | collective-permute-start | bytes 393224 | tf_op jit(solution)/shard_map/ppermute | solution.py:235
  81.4 18.0 %collective-permute-start.9 = (bf16[512,128]{1,0:T(8,128)(2,1)S(1)}, bf16[512,128]{1,0:T(8,128)(2,1)S(1)}, u32[]{:S(2)}, u32[]{:S(2)}) collective-permute-start(bf16[512,128]{1,0:T(8,128)(2,1)S(1)} %get-tuple-element.77), channel_id=1, source_target_pairs={{0,8},{4,12},{8,0},{12,4},{16,24},{20,28},{24,16},{28,20},{1,9},{5... | collective-permute-start | bytes 393224 | tf_op jit(solution)/shard_map/ppermute | solution.py:235
  103.3 19.4 %collective-permute-start.13 = (bf16[512,128]{1,0:T(8,128)(2,1)S(1)}, bf16[512,128]{1,0:T(8,128)(2,1)S(1)}, u32[]{:S(2)}, u32[]{:S(2)}) collective-permute-start(bf16[512,128]{1,0:T(8,128)(2,1)S(1)} %get-tuple-element.74), channel_id=1, source_target_pairs={{0,8},{4,12},{8,0},{12,4},{16,24},{20,28},{24,16},{28,20},{1,9},{5... | collective-permute-start | bytes 393224 | tf_op jit(solution)/shard_map/ppermute | solution.py:235
  103.4 19.3 %collective-permute-start.14 = (bf16[512,128]{1,0:T(8,128)(2,1)S(1)}, bf16[512,128]{1,0:T(8,128)(2,1)S(1)}, u32[]{:S(2)}, u32[]{:S(2)}) collective-permute-start(bf16[512,128]{1,0:T(8,128)(2,1)S(1)} %get-tuple-element.76), channel_id=1, source_target_pairs={{0,16},{4,20},{8,24},{12,28},{16,0},{20,4},{24,8},{28,12},{1,17},{... | collective-permute-start | bytes 393224 | tf_op jit(solution)/shard_map/ppermute | solution.py:235
  104.2 18.5 %collective-permute-start.15 = (bf16[512,128]{1,0:T(8,128)(2,1)S(1)}, bf16[512,128]{1,0:T(8,128)(2,1)S(1)}, u32[]{:S(2)}, u32[]{:S(2)}) collective-permute-start(bf16[512,128]{1,0:T(8,128)(2,1)S(1)} %get-tuple-element.75), channel_id=1, source_target_pairs={{0,24},{4,28},{8,16},{12,20},{16,8},{20,12},{24,0},{28,4},{1,25},{... | collective-permute-start | bytes 393224 | tf_op jit(solution)/shard_map/ppermute | solution.py:235
  126.6 19.4 %collective-permute-start.17 = (bf16[512,128]{1,0:T(8,128)(2,1)S(1)}, bf16[512,128]{1,0:T(8,128)(2,1)S(1)}, u32[]{:S(2)}, u32[]{:S(2)}) collective-permute-start(bf16[512,128]{1,0:T(8,128)(2,1)S(1)} %get-tuple-element.71), channel_id=1, source_target_pairs={{0,8},{4,12},{8,0},{12,4},{16,24},{20,28},{24,16},{28,20},{1,9},{5... | collective-permute-start | bytes 393224 | tf_op jit(solution)/shard_map/ppermute | solution.py:235
  126.6 19.3 %collective-permute-start.18 = (bf16[512,128]{1,0:T(8,128)(2,1)S(1)}, bf16[512,128]{1,0:T(8,128)(2,1)S(1)}, u32[]{:S(2)}, u32[]{:S(2)}) collective-permute-start(bf16[512,128]{1,0:T(8,128)(2,1)S(1)} %get-tuple-element.73), channel_id=1, source_target_pairs={{0,16},{4,20},{8,24},{12,28},{16,0},{20,4},{24,8},{28,12},{1,17},{... | collective-permute-start | bytes 393224 | tf_op jit(solution)/shard_map/ppermute | solution.py:235
  127.9 18.1 %collective-permute-start.19 = (bf16[512,128]{1,0:T(8,128)(2,1)S(1)}, bf16[512,128]{1,0:T(8,128)(2,1)S(1)}, u32[]{:S(2)}, u32[]{:S(2)}) collective-permute-start(bf16[512,128]{1,0:T(8,128)(2,1)S(1)} %get-tuple-element.72), channel_id=1, source_target_pairs={{0,24},{4,28},{8,16},{12,20},{16,8},{20,12},{24,0},{28,4},{1,25},{... | collective-permute-start | bytes 393224 | tf_op jit(solution)/shard_map/ppermute | solution.py:235
  163.3 5.3 %collective-permute-start.24 = (bf16[2048,128]{1,0:T(8,128)(2,1)S(1)}, bf16[2048,128]{1,0:T(8,128)(2,1)S(1)}, u32[]{:S(2)}, u32[]{:S(2)}) collective-permute-start(bf16[2048,128]{1,0:T(8,128)(2,1)S(1)} %product.23), channel_id=1, source_target_pairs={{0,4},{4,0},{8,12},{12,8},{16,20},{20,16},{24,28},{28,24},{1,5},{5... | collective-permute-start | bytes 1572872 | tf_op jit(solution)/shard_map/ppermute | solution.py:235
  164.9 7.4 %collective-permute-start.20 = (bf16[2048,128]{1,0:T(8,128)(2,1)S(1)}, bf16[2048,128]{1,0:T(8,128)(2,1)S(1)}, u32[]{:S(2)}, u32[]{:S(2)}) collective-permute-start(bf16[2048,128]{1,0:T(8,128)(2,1)S(1)} %product.21), channel_id=1, source_target_pairs={{0,4},{4,0},{8,12},{12,8},{16,20},{20,16},{24,28},{28,24},{1,5},{5... | collective-permute-start | bytes 1572872 | tf_op jit(solution)/shard_map/ppermute | solution.py:235
  168.8 6.0 %collective-permute-start.25 = (bf16[512,128]{1,0:T(8,128)(2,1)S(1)}, bf16[512,128]{1,0:T(8,128)(2,1)S(1)}, u32[]{:S(2)}, u32[]{:S(2)}) collective-permute-start(bf16[512,128]{1,0:T(8,128)(2,1)S(1)} %get-tuple-element.68), channel_id=1, source_target_pairs={{0,8},{4,12},{8,0},{12,4},{16,24},{20,28},{24,16},{28,20},{1,9},{5... | collective-permute-start | bytes 393224 | tf_op jit(solution)/shard_map/ppermute | solution.py:235
  168.9 8.6 %collective-permute-start.26 = (bf16[512,128]{1,0:T(8,128)(2,1)S(1)}, bf16[512,128]{1,0:T(8,128)(2,1)S(1)}, u32[]{:S(2)}, u32[]{:S(2)}) collective-permute-start(bf16[512,128]{1,0:T(8,128)(2,1)S(1)} %get-tuple-element.70), channel_id=1, source_target_pairs={{0,16},{4,20},{8,24},{12,28},{16,0},{20,4},{24,8},{28,12},{1,17},{... | collective-permute-start | bytes 393224 | tf_op jit(solution)/shard_map/ppermute | solution.py:235
  170.9 7.8 %collective-permute-start.27 = (bf16[512,128]{1,0:T(8,128)(2,1)S(1)}, bf16[512,128]{1,0:T(8,128)(2,1)S(1)}, u32[]{:S(2)}, u32[]{:S(2)}) collective-permute-start(bf16[512,128]{1,0:T(8,128)(2,1)S(1)} %get-tuple-element.69), channel_id=1, source_target_pairs={{0,24},{4,28},{8,16},{12,20},{16,8},{20,12},{24,0},{28,4},{1,25},{... | collective-permute-start | bytes 393224 | tf_op jit(solution)/shard_map/ppermute | solution.py:235
  172.5 7.9 %collective-permute-start.21 = (bf16[512,128]{1,0:T(8,128)(2,1)S(1)}, bf16[512,128]{1,0:T(8,128)(2,1)S(1)}, u32[]{:S(2)}, u32[]{:S(2)}) collective-permute-start(bf16[512,128]{1,0:T(8,128)(2,1)S(1)} %get-tuple-element.65), channel_id=1, source_target_pairs={{0,8},{4,12},{8,0},{12,4},{16,24},{20,28},{24,16},{28,20},{1,9},{5... | collective-permute-start | bytes 393224 | tf_op jit(solution)/shard_map/ppermute | solution.py:235
  172.7 10.2 %collective-permute-start.22 = (bf16[512,128]{1,0:T(8,128)(2,1)S(1)}, bf16[512,128]{1,0:T(8,128)(2,1)S(1)}, u32[]{:S(2)}, u32[]{:S(2)}) collective-permute-start(bf16[512,128]{1,0:T(8,128)(2,1)S(1)} %get-tuple-element.67), channel_id=1, source_target_pairs={{0,16},{4,20},{8,24},{12,28},{16,0},{20,4},{24,8},{28,12},{1,17},{... | collective-permute-start | bytes 393224 | tf_op jit(solution)/shard_map/ppermute | solution.py:235
  174.8 9.4 %collective-permute-start.23 = (bf16[512,128]{1,0:T(8,128)(2,1)S(1)}, bf16[512,128]{1,0:T(8,128)(2,1)S(1)}, u32[]{:S(2)}, u32[]{:S(2)}) collective-permute-start(bf16[512,128]{1,0:T(8,128)(2,1)S(1)} %get-tuple-element.66), channel_id=1, source_target_pairs={{0,24},{4,28},{8,16},{12,20},{16,8},{20,12},{24,0},{28,4},{1,25},{... | collective-permute-start | bytes 393224 | tf_op jit(solution)/shard_map/ppermute | solution.py:235
  (10 other events, 36.2 us)

commit v5 on v2

v5 whole, which is shorter than its diff:
```python
import functools

import jax
import jax.numpy as jnp
from jax import lax
from jax.experimental import pallas as pl
from jax.experimental.pallas import tpu as pltpu
from jax.sharding import PartitionSpec as P

ITERS = 3


TELEPORT = 0.1


CHUNKS = 2


UNROLL = 8


EXTRA = 16


MOST = 8


def vmem(count):
    return [pl.BlockSpec(memory_space=pltpu.VMEM)] * count


def smem(count):
    return [pl.BlockSpec(memory_space=pltpu.SMEM)] * count


def anywhere(count):
    return [pl.BlockSpec(memory_space=pl.ANY)] * count


def pair_capacity(tile_max, dest_count):
    most = (tile_max + dest_count // 2) // 2
    return -(-most // UNROLL) * UNROLL


def prepare_kernel(
    tiles_per_owner,
    place_ref,
    src_ref,
    count_ref,
    tile_ref,
    turned_ref,
    weight_ref,
    slot_ref,
    first_ref,
    second_ref,
    row_ref,
    go_on_ref,
    turns_ref,
    held_ref,
    sum_ref,
    sems,
):
    tile_max, tile_size, _ = tile_ref.shape
    dest_count = count_ref.shape[1]
    zero_tile = place_ref[2]
    my_row = place_ref[0]
    pieces = sems.shape[0]
    piece = tile_max // pieces
    copies = []
    for index in range(pieces):
        span = pl.ds(index * piece, piece)
        copies.append(
            pltpu.make_async_copy(tile_ref.at[span], held_ref.at[span], sems.at[index])
        )
        copies[-1].start()

    for half in range(2):

        def one_dest(dest, carry, half=half):
            start, used = carry
            owner = lax.div(dest, tiles_per_owner)
            relative = lax.bitwise_xor(owner, my_row)
            count = count_ref[0, dest]
            mine = lax.bitwise_and(relative, 1) == half
            pairs = jnp.where(mine, lax.div(count + 1, 2), 0)
            out_row = (
                lax.div(relative, 2) * tiles_per_owner + dest - owner * tiles_per_owner
            ) * tile_size

            def one_pair(pair, carry):
                at = used + pair
                slot = start + 2 * pair
                next_slot = jnp.minimum(slot + 1, tile_max - 1)
                slot_ref[half, at] = slot
                first_ref[half, at] = src_ref[0, slot] * tile_size
                second_ref[half, at] = (
                    jnp.where(2 * pair + 1 < count, src_ref[0, next_slot], zero_tile) * tile_size
                )
                row_ref[half, at] = out_row
                go_on_ref[half, at] = jnp.where(pair > 0, 1, 0)
                return carry

            lax.fori_loop(0, pairs, one_pair, 0)
            return start + count, used + pairs

        _, used = lax.fori_loop(0, dest_count, one_dest, (jnp.int32(0), jnp.int32(0)))
        turns = lax.div(used + UNROLL - 1, UNROLL)
        last_row = row_ref[half, used - 1]

        def one_pad(at, carry, half=half, last_row=last_row):
            slot_ref[half, at] = 0
            first_ref[half, at] = zero_tile * tile_size
            second_ref[half, at] = zero_tile * tile_size
            row_ref[half, at] = last_row
            go_on_ref[half, at] = 1
            return carry

        lax.fori_loop(used, turns * UNROLL, one_pad, 0)
        turns_ref[half] = turns

    group = min(8, piece)
    for index in range(pieces):
        copies[index].wait()

        def one_group(at, carry, index=index):
            for step in range(group):
                slot = index * piece + at * group + step
                tile = held_ref[slot]
                turned_ref[slot] = tile.T
                sum_ref[pl.ds(slot, 1), :] = jnp.sum(
                    tile.astype(jnp.float32), axis=0, keepdims=True
                )
            return carry

        lax.fori_loop(0, piece // group, one_group, 0)

    sum_ref[tile_max:, :] = jnp.zeros((MOST, tile_size), jnp.float32)
    weight_ref[...] = jnp.zeros(weight_ref.shape, weight_ref.dtype)
    places = lax.broadcasted_iota(jnp.int32, (MOST, tile_size), 0)

    def weigh(at, start):
        for step in range(tiles_per_owner):
            count = count_ref[0, at * tiles_per_owner + step]
            sums = jnp.where(places < count, sum_ref[pl.ds(start, MOST), :], 0.0)
            weight_ref[lax.bitwise_xor(at, my_row), step : step + 1, :] = jnp.sum(
                sums, axis=0, keepdims=True
            )
            start = start + count
        return start

    lax.fori_loop(0, dest_count // tiles_per_owner, weigh, jnp.int32(0))


def prepare(place, tile_src, row_counts, tile_vals, row_size, tiles_per_owner):
    tile_max, tile_size, _ = tile_vals.shape
    capacity = pair_capacity(tile_max, row_counts.shape[1])
    listing = jax.ShapeDtypeStruct((2, capacity), jnp.int32)
    return pl.pallas_call(
        functools.partial(prepare_kernel, tiles_per_owner),
        out_shape=[
            jax.ShapeDtypeStruct(tile_vals.shape, tile_vals.dtype),
            jax.ShapeDtypeStruct((row_size, EXTRA, tile_size), jnp.float32),
            listing,
            listing,
            listing,
            listing,
            listing,
            jax.ShapeDtypeStruct((2,), jnp.int32),
        ],
        in_specs=smem(3) + anywhere(1),
        out_specs=vmem(2) + smem(6),
        scratch_shapes=[
            pltpu.VMEM(tile_vals.shape, tile_vals.dtype),
            pltpu.VMEM((tile_max + MOST, tile_size), jnp.float32),
            pltpu.SemaphoreType.DMA((8,)),
        ],
        compiler_params=pltpu.CompilerParams(vmem_limit_bytes=24 * 2**20),
        name="prepare",
    )(place, tile_src, row_counts, tile_vals)


def assemble_kernel(packed, blocks, arrays, place_ref, *refs):
    block_refs = refs[:arrays]
    held_ref = refs[arrays + 1]
    staged_ref = refs[-1] if packed else held_ref
    col = place_ref[1]
    rows, width = block_refs[0].shape

    def put(mask, ref):
        first = pl.multiple_of(lax.bitwise_xor(col, mask) * rows, rows)
        staged_ref[pl.ds(first, rows), :] = ref[...]

    for mask in range(blocks - 1):
        put(mask, block_refs[mask])
    if arrays == blocks:
        put(blocks - 1, block_refs[-1])
    else:
        inside = jnp.logical_and(col > 0, col < blocks - 1)
        pl.when(inside)(functools.partial(put, blocks - 1, block_refs[-2]))
        pl.when(jnp.logical_not(inside))(functools.partial(put, blocks - 1, block_refs[-1]))
    if packed:
        piece = width // blocks
        for group in range(blocks):
            lanes = slice(group * piece, (group + 1) * piece)
            held_ref[group * rows : (group + 1) * rows, :] = jnp.concatenate(
                [staged_ref[b * rows : (b + 1) * rows, lanes] for b in range(blocks)], axis=1
            )
        own_ref = refs[arrays + 2]
        own_ref[...] = held_ref[pl.ds(pl.multiple_of(col * rows, rows), rows), :]
    zeros = held_ref.shape[0] - blocks * rows
    held_ref[blocks * rows :, :] = jnp.zeros((zeros, width), held_ref.dtype)


def assemble(place, gathered, after, blocks, tile_size, packed):
    arrays = len(gathered)
    rows, width = gathered[0].shape
    out_shape = [jax.ShapeDtypeStruct((blocks * rows + tile_size, width), jnp.bfloat16)]
    scratch = []
    if packed:
        out_shape.append(jax.ShapeDtypeStruct((rows, width), jnp.bfloat16))
        scratch.append(pltpu.VMEM((blocks * rows, width), jnp.bfloat16))
    return pl.pallas_call(
        functools.partial(assemble_kernel, packed, blocks, arrays),
        out_shape=out_shape,
        in_specs=smem(1) + vmem(arrays) + anywhere(1),
        out_specs=vmem(len(out_shape)),
        scratch_shapes=scratch,
        compiler_params=pltpu.CompilerParams(vmem_limit_bytes=4 * 2**20),
        cost_estimate=pl.CostEstimate(flops=0, bytes_accessed=4 * 2**20, transcendentals=0),
        name="assemble",
    )(place, *gathered, after)


def product_kernel(
    half,
    rows,
    slot_ref,
    first_ref,
    second_ref,
    row_ref,
    go_on_ref,
    turns_ref,
    turned_ref,
    held_ref,
    weight_ref,
    out_ref,
):
    tile_max, tile_size, _ = turned_ref.shape
    chips, out_rows, width = out_ref.shape
    if out_rows > rows:
        for chip in range(chips):
            out_ref[chip, rows:, :] = weight_ref[2 * chip + half].astype(out_ref.dtype)

    def one_turn(turn, running):
        for step in range(UNROLL):
            at = turn * UNROLL + step
            slot = slot_ref[half, at]
            left = jnp.concatenate(
                [turned_ref[slot], turned_ref[jnp.minimum(slot + 1, tile_max - 1)]], axis=1
            )
            first = pl.multiple_of(first_ref[half, at], tile_size)
            second = pl.multiple_of(second_ref[half, at], tile_size)
            right = jnp.concatenate(
                [held_ref[pl.ds(first, tile_size), :], held_ref[pl.ds(second, tile_size), :]],
                axis=0,
            )
            term = jnp.dot(left, right, preferred_element_type=jnp.float32)
            running = running * go_on_ref[half, at].astype(jnp.float32) + term
            out_row = row_ref[half, at]
            chip = lax.div(out_row, rows)
            out_row = pl.multiple_of(out_row - chip * rows, tile_size)
            out_ref[chip, pl.ds(out_row, tile_size), :] = running.astype(out_ref.dtype)
        return running

    lax.fori_loop(0, turns_ref[half], one_turn, jnp.zeros((tile_size, width), jnp.float32))


def product(half, lists, turned, held, weights, rows, chips, extra):
    return pl.pallas_call(
        functools.partial(product_kernel, half, rows),
        out_shape=jax.ShapeDtypeStruct((chips, rows + extra, held.shape[1]), jnp.bfloat16),
        in_specs=smem(len(lists)) + vmem(3),
        out_specs=vmem(1)[0],
        compiler_params=pltpu.CompilerParams(vmem_limit_bytes=4 * 2**20),
        cost_estimate=pl.CostEstimate(
            flops=600000000, bytes_accessed=6000000, transcendentals=0
        ),
        name="product",
    )(*lists, turned, held, weights)


def update_kernel(parts, *refs):
    kept_refs = refs[:parts]
    arrived_refs = refs[parts : 2 * parts]
    iterate_ref, restart_ref, scale_ref, out_ref = refs[2 * parts :]
    rows = out_ref.shape[0] // parts
    for part in range(parts):
        span = slice(part * rows, (part + 1) * rows)
        summed = kept_refs[part][:rows, :] + arrived_refs[part][:rows, :].astype(jnp.float32)
        out_ref[span, :] = (
            scale_ref[span, :] * (summed + iterate_ref[span, :].astype(jnp.float32))
            + TELEPORT * restart_ref[span, :].astype(jnp.float32)
        ).astype(out_ref.dtype)


def update(kept, arrived, iterate, restart, scale):
    return pl.pallas_call(
        functools.partial(update_kernel, len(kept)),
        out_shape=jax.ShapeDtypeStruct(iterate.shape, iterate.dtype),
        in_specs=vmem(2 * len(kept) + 3),
        out_specs=vmem(1)[0],
        compiler_params=pltpu.CompilerParams(vmem_limit_bytes=4 * 2**20),
        cost_estimate=pl.CostEstimate(flops=0, bytes_accessed=1, transcendentals=0),
        name="update",
    )(*kept, *arrived, iterate, restart, scale)


def exchange(block, axis, mask, size):
    return lax.ppermute(block, axis, [(i, i ^ mask) for i in range(size)])


def gather_first(block, size):
    masks = (1, 2) if size == 4 else range(1, size)
    return [block] + [exchange(block, "col", mask, size) for mask in masks]


def gather_second(found, size):
    if size != 4:
        return found
    inner = lax.ppermute(found[0], "col", [(0, 0), (1, 2), (2, 1), (3, 3)])
    return found + [inner, exchange(found[2], "col", 1, size)]


def halve(state, bits, bit, row_size):
    axis = bits.index(bit)
    send = lax.index_in_dim(state, 1, axis, keepdims=False).astype(jnp.bfloat16)
    keep = lax.index_in_dim(state, 0, axis, keepdims=False)
    return keep, exchange(send, "row", 1 << bit, row_size)


def on_device(features, tile_vals, tile_src, row_counts):
    row_size = lax.axis_size("row")
    blocks = lax.axis_size("col")
    my_row = lax.axis_index("row").astype(jnp.int32)
    my_col = lax.axis_index("col").astype(jnp.int32)
    tile_size = tile_vals.shape[1]
    dest_count = row_counts.shape[1]
    rows = features.shape[0] // blocks
    source_tiles = features.shape[0] // tile_size
    width = features.shape[1] * blocks // CHUNKS
    piece = features.shape[1] // CHUNKS
    tiles_per_owner = dest_count // row_size
    chips = row_size // 2
    chip_bits = list(range(row_size.bit_length() - 2, 0, -1))
    place = jnp.stack([my_row, my_col, jnp.int32(source_tiles)])

    parts = features.reshape(blocks, rows, CHUNKS, piece).transpose(2, 1, 0, 3)
    parts = parts.reshape(CHUNKS, rows, blocks * piece)

    turned, weights, *lists = prepare(
        place, tile_src, row_counts, tile_vals, row_size, tiles_per_owner
    )

    gathered = [gather_second(gather_first(parts[0], blocks), blocks), None]
    iterates = [None] * CHUNKS
    restarts = [None] * CHUNKS
    scale = None
    last = place
    for phase in range(ITERS * CHUNKS):
        chunk = phase % CHUNKS
        after = 1 - chunk
        first = phase < CHUNKS
        extra = EXTRA if phase == 0 else 0
        if phase > 0:
            iterates[after] = last = update(*pending)
        held, *own = assemble(place, gathered[chunk], last, blocks, tile_size, first)
        if first:
            iterates[chunk] = restarts[chunk] = own[0]
        if phase == 0:
            held, parts = lax.optimization_barrier((held, parts))
            found = gather_first(parts[1], blocks)
        elif phase + 1 < ITERS * CHUNKS:
            found = gather_first(iterates[after], blocks)
        else:
            found = []
        sent = product(1, lists, turned, held, weights, rows, chips, extra)
        other = exchange(sent, "row", 1, row_size)
        kept = product(0, lists, turned, held, weights, rows, chips, extra)
        both = kept.astype(jnp.float32) + other.astype(jnp.float32)
        states, arrivals, orders = [], [], []
        for half in range(2):
            state = both[:, : rows // 2] if half == 0 else both[:, rows // 2 :]
            states.append(state.reshape((2,) * len(chip_bits) + state.shape[1:]))
            arrivals.append(None)
            turn = half % len(chip_bits)
            orders.append(chip_bits[turn:] + chip_bits[:turn])
        left = [list(chip_bits), list(chip_bits)]
        for step in range(len(chip_bits)):
            for half in range(2):
                if step > 0:
                    states[half] = states[half] + arrivals[half].astype(jnp.float32)
                bit = orders[half][step]
                states[half], arrivals[half] = halve(states[half], left[half], bit, row_size)
                left[half].remove(bit)
            if step == 0:
                found, arrivals = lax.optimization_barrier((found, arrivals))
                if found:
                    gathered[after] = gather_second(found, blocks)
        sums = states
        if phase == 0:
            weight_rows = slice(rows // 2, rows // 2 + tiles_per_owner)
            total = 1.0 + sums[1][weight_rows] + arrivals[1][weight_rows].astype(jnp.float32)
            scale = jnp.broadcast_to(
                ((1.0 - TELEPORT) / total).reshape(rows, 1), (rows, width)
            )
        pending = (sums, arrivals, iterates[chunk], restarts[chunk], scale)
    iterates[chunk] = update(*pending)
    out = jnp.stack(iterates).reshape(CHUNKS, rows, blocks, piece).transpose(1, 2, 0, 3)
    return out.reshape(rows, CHUNKS * width)


def solution(mesh):
    placed = (P("row", "col"), P("row", "col", None), P("row", "col"), P("row", "col"))
    return jax.shard_map(
        on_device, mesh=mesh, in_specs=placed, out_specs=P(("row", "col"), None), check_vma=False
    )
```

time: 165 us -> 160 us (0.970)
  starting transfers between devices: 66.6 us -> 73.1 us
  local copies, waits for them, and re-layouts: 12.9 us -> 7.86 us
  waiting for transfers between devices: 52.3 us -> 47.9 us
  Pallas kernels: 30.8 us -> 28.6 us
    unnamed x16 -> x12, local copies, waits for them, and re-layouts: 9.85 us -> 4.39 us
    ppermute x46 -> x48, waiting for transfers between devices: 52.3 us -> 47.9 us  [exchange(): return lax.ppermute(block, axis, [(i, i ^ mask) for i in range(size)])]
    ppermute x0 -> x6, starting transfers between devices: none -> 3.94 us  [gather_second(): inner = lax.ppermute(found[0], 'col', [(0, 0), (1, 2), (2, 1), (3, 3)])]
    pallas_call x1, Pallas kernels: 8.85 us -> 5.3 us  [prepare(): pl.pallas_call(functools.partial(prepare_kernel, tiles_per_owner), out_sh...]
    ppermute x46 -> x48, starting transfers between devices: 66.6 us -> 69.1 us  [exchange(): return lax.ppermute(block, axis, [(i, i ^ mask) for i in range(size)])]
    pallas_call x12 -> x24, Pallas kernels: 22 us -> 23.3 us  [the longest x12 18.3 us: product(): pl.pallas_call(functools.partial(product_kernel, half, rows), out_shape=j...]
  transfers between devices with their start and end apart: 46 -> 54, of which waited for: 18 -> 27; matrix products, arithmetic and copies ran while one was open for 1% -> 1% of each run, Pallas kernels for 13% -> 9%
where the time goes in v5:
time: 160 us; the launch traced here: 159 us
  starting transfers between devices  73.1 us (46%)
  waiting for transfers between devices  47.9 us (30%)
  Pallas kernels  28.6 us (18%)
  local copies, waits for them, and re-layouts  7.86 us (5%)
    ppermute x48, starting transfers between devices, exchange(): return lax.ppermute(block, axis, [(i, i ^ mask) for i in range(size)])  69.1 us
    ppermute x48, waiting for transfers between devices, exchange(): return lax.ppermute(block, axis, [(i, i ^ mask) for i in range(size)])  47.9 us
    pallas_call x12, Pallas kernels, product(): pl.pallas_call(functools.partial(product_kernel, half, rows), out_shape=j...  18.3 us
    pallas_call x1, Pallas kernels, prepare(): pl.pallas_call(functools.partial(prepare_kernel, tiles_per_owner), out_sh...  5.3 us
    pallas_call x6, Pallas kernels, assemble(): pl.pallas_call(functools.partial(assemble_kernel, packed, blocks, arrays)...  4.51 us
    unnamed x12, local copies, waits for them, and re-layouts  4.39 us
    ppermute x6, starting transfers between devices, gather_second(): inner = lax.ppermute(found[0], 'col', [(0, 0), (1, 2), (2, 1), (3, 3)])  3.94 us
  transfers between devices with their start and end apart: 54, of which 27 were waited for; matrix products, arithmetic and copies ran while one was open for 1% of the time, Pallas kernels for 9%

profile of v5, /device:TPU:0, one launch (start us, length us, event | category | flops | bytes accessed | tf_op | source)
XLA Modules:
  0.0 159.5 jit_solution(13223693549937732574)
XLA Ops:
  1.4 4.1 %collective-permute-start.1 = (bf16[512,128]{1,0:T(8,128)(2,1)S(1)}, bf16[512,128]{1,0:T(8,128)(2,1)S(1)}, u32[]{:S(2)}, u32[]{:S(2)}) collective-permute-start(bf16[512,128]{1,0:T(8,128)(2,1)S(1)} %copy.32.refs_0_), channel_id=1, source_target_pairs={{0,2},{1,3},{2,0},{3,1},{4,6},{5,7},{6,4},{7,5},{8,10},{9,11},{10,... | collective-permute-start | bytes 393224 | tf_op jit(solution)/shard_map/ppermute | solution.py:319
  6.1 2.9 %collective-permute-start = (bf16[512,128]{1,0:T(8,128)(2,1)S(1)}, bf16[512,128]{1,0:T(8,128)(2,1)S(1)}, u32[]{:S(2)}, u32[]{:S(2)}) collective-permute-start(bf16[512,128]{1,0:T(8,128)(2,1)S(1)} %copy.32.refs_0_), channel_id=1, source_target_pairs={{0,1},{1,0},{2,3},{3,2},{4,5},{5,4},{6,7},{7,6},{8,9},{9,8},{10,11... | collective-permute-start | bytes 393224 | tf_op jit(solution)/shard_map/ppermute | solution.py:319
  9.0 3.6 %collective-permute-done.1.refs_2_ = bf16[512,128]{1,0:T(8,128)(2,1)S(1)} collective-permute-done((bf16[512,128]{1,0:T(8,128)(2,1)S(1)}, bf16[512,128]{1,0:T(8,128)(2,1)S(1)}, u32[]{:S(2)}, u32[]{:S(2)}) %collective-permute-start.1) | collective-permute-done | bytes 131104 | tf_op jit(solution)/shard_map/ppermute | solution.py:319
  15.0 5.3 %prepare.1 = (bf16[128,128,128]{2,1,0:T(8,128)(2,1)S(1)}, f32[8,16,128]{2,1,0:T(8,128)S(1)}, s32[2,72]{1,0:T(2,128)S(1)}, s32[2,72]{1,0:T(2,128)S(1)}, s32[2,72]...) custom-call(s32[3]{0:T(128)S(1)} %pad_add_fusion.place_ref.refs_5_, ...), custom_call_target="tpu_custom_call" | custom-call | tf_op jit(solution)/shard_map/prepare/pallas_call | solution.py:158
  29.0 3.1 %collective-permute-start.6 = (bf16[512,128]{1,0:T(8,128)(2,1)S(1)}, bf16[512,128]{1,0:T(8,128)(2,1)S(1)}, u32[]{:S(2)}, u32[]{:S(2)}) collective-permute-start(bf16[512,128]{1,0:T(8,128)(2,1)S(1)} %slice_bitcast_fusion.12.refs_0_), channel_id=1, source_target_pairs={{0,2},{1,3},{2,0},{3,1},{4,6},{5,7},{6,4},{7,5},{8,10},{9,11},{10,... | collective-permute-start | bytes 393224 | tf_op jit(solution)/shard_map/ppermute | solution.py:319
  34.1 4.5 %collective-permute-done.6.refs_2_ = bf16[512,128]{1,0:T(8,128)(2,1)S(1)} collective-permute-done((bf16[512,128]{1,0:T(8,128)(2,1)S(1)}, bf16[512,128]{1,0:T(8,128)(2,1)S(1)}, u32[]{:S(2)}, u32[]{:S(2)}) %collective-permute-start.6) | collective-permute-done | bytes 131104 | tf_op jit(solution)/shard_map/ppermute | solution.py:319
  42.4 2.9 %collective-permute-start.14 = (bf16[512,128]{1,0:T(8,128)(2,1)S(1)}, bf16[512,128]{1,0:T(8,128)(2,1)S(1)}, u32[]{:S(2)}, u32[]{:S(2)}) collective-permute-start(bf16[512,128]{1,0:T(8,128)(2,1)S(1)} %collective-permute-done.6.refs_2_), channel_id=1, source_target_pairs={{0,1},{1,0},{2,3},{3,2},{4,5},{5,4},{6,7},{7,6},{8,9},{9,8},{10,11... | collective-permute-start | bytes 393224 | tf_op jit(solution)/shard_map/ppermute | solution.py:319
  51.0 3.1 %collective-permute-start.12 = (bf16[512,128]{1,0:T(8,128)(2,1)S(1)}, bf16[512,128]{1,0:T(8,128)(2,1)S(1)}, u32[]{:S(2)}, u32[]{:S(2)}) collective-permute-start(bf16[512,128]{1,0:T(8,128)(2,1)S(1)} %update.6.refs_5_.refs_0_.refs_4_), channel_id=1, source_target_pairs={{0,2},{1,3},{2,0},{3,1},{4,6},{5,7},{6,4},{7,5},{8,10},{9,11},{10,... | collective-permute-start | bytes 393224 | tf_op jit(solution)/shard_map/ppermute | solution.py:319
  58.3 2.8 %collective-permute-done.12.refs_2_ = bf16[512,128]{1,0:T(8,128)(2,1)S(1)} collective-permute-done((bf16[512,128]{1,0:T(8,128)(2,1)S(1)}, bf16[512,128]{1,0:T(8,128)(2,1)S(1)}, u32[]{:S(2)}, u32[]{:S(2)}) %collective-permute-start.12) | collective-permute-done | bytes 131104 | tf_op jit(solution)/shard_map/ppermute | solution.py:319
  65.7 4.0 %collective-permute-start.19 = (bf16[512,128]{1,0:T(8,128)(2,1)S(1)}, bf16[512,128]{1,0:T(8,128)(2,1)S(1)}, u32[]{:S(2)}, u32[]{:S(2)}) collective-permute-start(bf16[512,128]{1,0:T(8,128)(2,1)S(1)} %collective-permute-done.12.refs_2_), channel_id=1, source_target_pairs={{0,1},{1,0},{2,3},{3,2},{4,5},{5,4},{6,7},{7,6},{8,9},{9,8},{10,11... | collective-permute-start | bytes 393224 | tf_op jit(solution)/shard_map/ppermute | solution.py:319
  69.9 2.8 %collective-permute-done.19.refs_4_ = bf16[512,128]{1,0:T(8,128)(2,1)S(1)} collective-permute-done((bf16[512,128]{1,0:T(8,128)(2,1)S(1)}, bf16[512,128]{1,0:T(8,128)(2,1)S(1)}, u32[]{:S(2)}, u32[]{:S(2)}) %collective-permute-start.19) | collective-permute-done | bytes 131104 | tf_op jit(solution)/shard_map/ppermute | solution.py:319
  74.9 2.8 %collective-permute-start.24 = (bf16[512,128]{1,0:T(8,128)(2,1)S(1)}, bf16[512,128]{1,0:T(8,128)(2,1)S(1)}, u32[]{:S(2)}, u32[]{:S(2)}) collective-permute-start(bf16[512,128]{1,0:T(8,128)(2,1)S(1)} %update.7.refs_5_.refs_0_.refs_4_), channel_id=1, source_target_pairs={{0,2},{1,3},{2,0},{3,1},{4,6},{5,7},{6,4},{7,5},{8,10},{9,11},{10,... | collective-permute-start | bytes 393224 | tf_op jit(solution)/shard_map/ppermute | solution.py:319
  80.8 3.9 %collective-permute-done.24.refs_2_ = bf16[512,128]{1,0:T(8,128)(2,1)S(1)} collective-permute-done((bf16[512,128]{1,0:T(8,128)(2,1)S(1)}, bf16[512,128]{1,0:T(8,128)(2,1)S(1)}, u32[]{:S(2)}, u32[]{:S(2)}) %collective-permute-start.24) | collective-permute-done | bytes 131104 | tf_op jit(solution)/shard_map/ppermute | solution.py:319
  88.7 3.8 %collective-permute-start.32 = (bf16[512,128]{1,0:T(8,128)(2,1)S(1)}, bf16[512,128]{1,0:T(8,128)(2,1)S(1)}, u32[]{:S(2)}, u32[]{:S(2)}) collective-permute-start(bf16[512,128]{1,0:T(8,128)(2,1)S(1)} %collective-permute-done.24.refs_2_), channel_id=1, source_target_pairs={{0,1},{1,0},{2,3},{3,2},{4,5},{5,4},{6,7},{7,6},{8,9},{9,8},{10,11... | collective-permute-start | bytes 393224 | tf_op jit(solution)/shard_map/ppermute | solution.py:319
  92.6 2.8 %collective-permute-done.32.refs_4_ = bf16[512,128]{1,0:T(8,128)(2,1)S(1)} collective-permute-done((bf16[512,128]{1,0:T(8,128)(2,1)S(1)}, bf16[512,128]{1,0:T(8,128)(2,1)S(1)}, u32[]{:S(2)}, u32[]{:S(2)}) %collective-permute-start.32) | collective-permute-done | bytes 131104 | tf_op jit(solution)/shard_map/ppermute | solution.py:319
  97.6 2.7 %collective-permute-start.30 = (bf16[512,128]{1,0:T(8,128)(2,1)S(1)}, bf16[512,128]{1,0:T(8,128)(2,1)S(1)}, u32[]{:S(2)}, u32[]{:S(2)}) collective-permute-start(bf16[512,128]{1,0:T(8,128)(2,1)S(1)} %update.8.refs_5_.refs_0_.refs_4_), channel_id=1, source_target_pairs={{0,2},{1,3},{2,0},{3,1},{4,6},{5,7},{6,4},{7,5},{8,10},{9,11},{10,... | collective-permute-start | bytes 393224 | tf_op jit(solution)/shard_map/ppermute | solution.py:319
  104.3 2.9 %collective-permute-done.30.refs_2_ = bf16[512,128]{1,0:T(8,128)(2,1)S(1)} collective-permute-done((bf16[512,128]{1,0:T(8,128)(2,1)S(1)}, bf16[512,128]{1,0:T(8,128)(2,1)S(1)}, u32[]{:S(2)}, u32[]{:S(2)}) %collective-permute-start.30) | collective-permute-done | bytes 131104 | tf_op jit(solution)/shard_map/ppermute | solution.py:319
  111.9 4.1 %collective-permute-start.37 = (bf16[512,128]{1,0:T(8,128)(2,1)S(1)}, bf16[512,128]{1,0:T(8,128)(2,1)S(1)}, u32[]{:S(2)}, u32[]{:S(2)}) collective-permute-start(bf16[512,128]{1,0:T(8,128)(2,1)S(1)} %collective-permute-done.30.refs_2_), channel_id=1, source_target_pairs={{0,1},{1,0},{2,3},{3,2},{4,5},{5,4},{6,7},{7,6},{8,9},{9,8},{10,11... | collective-permute-start | bytes 393224 | tf_op jit(solution)/shard_map/ppermute | solution.py:319
  116.1 2.8 %collective-permute-done.37.refs_4_ = bf16[512,128]{1,0:T(8,128)(2,1)S(1)} collective-permute-done((bf16[512,128]{1,0:T(8,128)(2,1)S(1)}, bf16[512,128]{1,0:T(8,128)(2,1)S(1)}, u32[]{:S(2)}, u32[]{:S(2)}) %collective-permute-start.37) | collective-permute-done | bytes 131104 | tf_op jit(solution)/shard_map/ppermute | solution.py:319
  121.1 2.8 %collective-permute-start.42 = (bf16[512,128]{1,0:T(8,128)(2,1)S(1)}, bf16[512,128]{1,0:T(8,128)(2,1)S(1)}, u32[]{:S(2)}, u32[]{:S(2)}) collective-permute-start(bf16[512,128]{1,0:T(8,128)(2,1)S(1)} %update.9.refs_5_.refs_0_.refs_4_), channel_id=1, source_target_pairs={{0,2},{1,3},{2,0},{3,1},{4,6},{5,7},{6,4},{7,5},{8,10},{9,11},{10,... | collective-permute-start | bytes 393224 | tf_op jit(solution)/shard_map/ppermute | solution.py:319
  126.9 3.9 %collective-permute-done.42.refs_2_ = bf16[512,128]{1,0:T(8,128)(2,1)S(1)} collective-permute-done((bf16[512,128]{1,0:T(8,128)(2,1)S(1)}, bf16[512,128]{1,0:T(8,128)(2,1)S(1)}, u32[]{:S(2)}, u32[]{:S(2)}) %collective-permute-start.42) | collective-permute-done | bytes 131104 | tf_op jit(solution)/shard_map/ppermute | solution.py:319
  134.8 3.8 %collective-permute-start.48 = (bf16[512,128]{1,0:T(8,128)(2,1)S(1)}, bf16[512,128]{1,0:T(8,128)(2,1)S(1)}, u32[]{:S(2)}, u32[]{:S(2)}) collective-permute-start(bf16[512,128]{1,0:T(8,128)(2,1)S(1)} %collective-permute-done.42.refs_2_), channel_id=1, source_target_pairs={{0,1},{1,0},{2,3},{3,2},{4,5},{5,4},{6,7},{7,6},{8,9},{9,8},{10,11... | collective-permute-start | bytes 393224 | tf_op jit(solution)/shard_map/ppermute | solution.py:319
  138.8 2.8 %collective-permute-done.48.refs_4_ = bf16[512,128]{1,0:T(8,128)(2,1)S(1)} collective-permute-done((bf16[512,128]{1,0:T(8,128)(2,1)S(1)}, bf16[512,128]{1,0:T(8,128)(2,1)S(1)}, u32[]{:S(2)}, u32[]{:S(2)}) %collective-permute-start.48) | collective-permute-done | bytes 131104 | tf_op jit(solution)/shard_map/ppermute | solution.py:319
  148.6 3.4 %collective-permute-done.50 = bf16[2,256,128]{2,1,0:T(8,128)(2,1)S(1)} collective-permute-done((bf16[2,256,128]{2,1,0:T(8,128)(2,1)S(1)}, bf16[2,256,128]{2,1,0:T(8,128)(2,1)S(1)}, u32[]{:S(2)}, u32[]{:S(2)}) %collective-permute-start.50) | collective-permute-done | bytes 131104 | tf_op jit(solution)/shard_map/ppermute | solution.py:319
  (195 shorter events, 76.7 us)
Async XLA Ops:
  1.4 11.2 %collective-permute-start.1 = (bf16[512,128]{1,0:T(8,128)(2,1)S(1)}, bf16[512,128]{1,0:T(8,128)(2,1)S(1)}, u32[]{:S(2)}, u32[]{:S(2)}) collective-permute-start(bf16[512,128]{1,0:T(8,128)(2,1)S(1)} %copy.32.refs_0_), channel_id=1, source_target_pairs={{0,2},{1,3},{2,0},{3,1},{4,6},{5,7},{6,4},{7,5},{8,10},{9,11},{10,... | collective-permute-start | bytes 393224 | tf_op jit(solution)/shard_map/ppermute | solution.py:319
  5.5 14.8 %collective-permute-start.2 = (bf16[512,128]{1,0:T(8,128)(2,1)S(1)}, bf16[512,128]{1,0:T(8,128)(2,1)S(1)}, u32[]{:S(2)}, u32[]{:S(2)}) collective-permute-start(bf16[512,128]{1,0:T(8,128)(2,1)S(1)} %copy.32.refs_0_), channel_id=1, source_target_pairs={{0,0},{1,2},{2,1},{3,3},{4,4},{5,6},{6,5},{7,7},{8,8},{9,10},{10,9... | collective-permute-start | bytes 393224 | tf_op jit(solution)/shard_map/ppermute | solution.py:330
  6.1 14.2 %collective-permute-start = (bf16[512,128]{1,0:T(8,128)(2,1)S(1)}, bf16[512,128]{1,0:T(8,128)(2,1)S(1)}, u32[]{:S(2)}, u32[]{:S(2)}) collective-permute-start(bf16[512,128]{1,0:T(8,128)(2,1)S(1)} %copy.32.refs_0_), channel_id=1, source_target_pairs={{0,1},{1,0},{2,3},{3,2},{4,5},{5,4},{6,7},{7,6},{8,9},{9,8},{10,11... | collective-permute-start | bytes 393224 | tf_op jit(solution)/shard_map/ppermute | solution.py:319
  12.6 7.7 %collective-permute-start.3 = (bf16[512,128]{1,0:T(8,128)(2,1)S(1)}, bf16[512,128]{1,0:T(8,128)(2,1)S(1)}, u32[]{:S(2)}, u32[]{:S(2)}) collective-permute-start(bf16[512,128]{1,0:T(8,128)(2,1)S(1)} %collective-permute-done.1.refs_2_), channel_id=1, source_target_pairs={{0,1},{1,0},{2,3},{3,2},{4,5},{5,4},{6,7},{7,6},{8,9},{9,8},{10,11... | collective-permute-start | bytes 393224 | tf_op jit(solution)/shard_map/ppermute | solution.py:319
  27.4 11.5 %collective-permute-start.8 = (bf16[2,272,128]{2,1,0:T(8,128)(2,1)S(1)}, bf16[2,272,128]{2,1,0:T(8,128)(2,1)S(1)}, u32[]{:S(2)}, u32[]{:S(2)}) collective-permute-start(bf16[2,272,128]{2,1,0:T(8,128)(2,1)S(1)} %fusion.6), channel_id=1, source_target_pairs={{0,8},{4,12},{8,0},{12,4},{16,24},{20,28},{24,16},{28,20},{1,9},{5... | collective-permute-start | bytes 417800 | tf_op jit(solution)/shard_map/ppermute | solution.py:319
  29.0 9.6 %collective-permute-start.6 = (bf16[512,128]{1,0:T(8,128)(2,1)S(1)}, bf16[512,128]{1,0:T(8,128)(2,1)S(1)}, u32[]{:S(2)}, u32[]{:S(2)}) collective-permute-start(bf16[512,128]{1,0:T(8,128)(2,1)S(1)} %slice_bitcast_fusion.12.refs_0_), channel_id=1, source_target_pairs={{0,2},{1,3},{2,0},{3,1},{4,6},{5,7},{6,4},{7,5},{8,10},{9,11},{10,... | collective-permute-start | bytes 393224 | tf_op jit(solution)/shard_map/ppermute | solution.py:319
  32.1 6.7 %collective-permute-start.5 = (bf16[512,128]{1,0:T(8,128)(2,1)S(1)}, bf16[512,128]{1,0:T(8,128)(2,1)S(1)}, u32[]{:S(2)}, u32[]{:S(2)}) collective-permute-start(bf16[512,128]{1,0:T(8,128)(2,1)S(1)} %slice_bitcast_fusion.12.refs_0_), channel_id=1, source_target_pairs={{0,1},{1,0},{2,3},{3,2},{4,5},{5,4},{6,7},{7,6},{8,9},{9,8},{10,11... | collective-permute-start | bytes 393224 | tf_op jit(solution)/shard_map/ppermute | solution.py:319
  32.4 6.4 %collective-permute-start.7 = (bf16[2,256,128]{2,1,0:T(8,128)(2,1)S(1)}, bf16[2,256,128]{2,1,0:T(8,128)(2,1)S(1)}, u32[]{:S(2)}, u32[]{:S(2)}) collective-permute-start(bf16[2,256,128]{2,1,0:T(8,128)(2,1)S(1)} %slice.423), channel_id=1, source_target_pairs={{0,16},{4,20},{8,24},{12,28},{16,0},{20,4},{24,8},{28,12},{1,17},{... | collective-permute-start | bytes 393224 | tf_op jit(solution)/shard_map/ppermute | solution.py:319
  51.0 10.1 %collective-permute-start.12 = (bf16[512,128]{1,0:T(8,128)(2,1)S(1)}, bf16[512,128]{1,0:T(8,128)(2,1)S(1)}, u32[]{:S(2)}, u32[]{:S(2)}) collective-permute-start(bf16[512,128]{1,0:T(8,128)(2,1)S(1)} %update.6.refs_5_.refs_0_.refs_4_), channel_id=1, source_target_pairs={{0,2},{1,3},{2,0},{3,1},{4,6},{5,7},{6,4},{7,5},{8,10},{9,11},{10,... | collective-permute-start | bytes 393224 | tf_op jit(solution)/shard_map/ppermute | solution.py:319
  54.2 7.2 %collective-permute-start.11 = (bf16[512,128]{1,0:T(8,128)(2,1)S(1)}, bf16[512,128]{1,0:T(8,128)(2,1)S(1)}, u32[]{:S(2)}, u32[]{:S(2)}) collective-permute-start(bf16[512,128]{1,0:T(8,128)(2,1)S(1)} %update.6.refs_5_.refs_0_.refs_4_), channel_id=1, source_target_pairs={{0,1},{1,0},{2,3},{3,2},{4,5},{5,4},{6,7},{7,6},{8,9},{9,8},{10,11... | collective-permute-start | bytes 393224 | tf_op jit(solution)/shard_map/ppermute | solution.py:319
  62.3 7.5 %collective-permute-start.21 = (bf16[256,128]{1,0:T(8,128)(2,1)S(1)}, bf16[256,128]{1,0:T(8,128)(2,1)S(1)}, u32[]{:S(2)}, u32[]{:S(2)}) collective-permute-start(bf16[256,128]{1,0:T(8,128)(2,1)S(1)} %fusion.15), channel_id=1, source_target_pairs={{0,16},{4,20},{8,24},{12,28},{16,0},{20,4},{24,8},{28,12},{1,17},{... | collective-permute-start | bytes 196616 | tf_op jit(solution)/shard_map/ppermute | solution.py:319
  65.7 6.9 %collective-permute-start.19 = (bf16[512,128]{1,0:T(8,128)(2,1)S(1)}, bf16[512,128]{1,0:T(8,128)(2,1)S(1)}, u32[]{:S(2)}, u32[]{:S(2)}) collective-permute-start(bf16[512,128]{1,0:T(8,128)(2,1)S(1)} %collective-permute-done.12.refs_2_), channel_id=1, source_target_pairs={{0,1},{1,0},{2,3},{3,2},{4,5},{5,4},{6,7},{7,6},{8,9},{9,8},{10,11... | collective-permute-start | bytes 393224 | tf_op jit(solution)/shard_map/ppermute | solution.py:319
  74.9 9.8 %collective-permute-start.24 = (bf16[512,128]{1,0:T(8,128)(2,1)S(1)}, bf16[512,128]{1,0:T(8,128)(2,1)S(1)}, u32[]{:S(2)}, u32[]{:S(2)}) collective-permute-start(bf16[512,128]{1,0:T(8,128)(2,1)S(1)} %update.7.refs_5_.refs_0_.refs_4_), channel_id=1, source_target_pairs={{0,2},{1,3},{2,0},{3,1},{4,6},{5,7},{6,4},{7,5},{8,10},{9,11},{10,... | collective-permute-start | bytes 393224 | tf_op jit(solution)/shard_map/ppermute | solution.py:319
  77.7 6.9 %collective-permute-start.23 = (bf16[512,128]{1,0:T(8,128)(2,1)S(1)}, bf16[512,128]{1,0:T(8,128)(2,1)S(1)}, u32[]{:S(2)}, u32[]{:S(2)}) collective-permute-start(bf16[512,128]{1,0:T(8,128)(2,1)S(1)} %update.7.refs_5_.refs_0_.refs_4_), channel_id=1, source_target_pairs={{0,1},{1,0},{2,3},{3,2},{4,5},{5,4},{6,7},{7,6},{8,9},{9,8},{10,11... | collective-permute-start | bytes 393224 | tf_op jit(solution)/shard_map/ppermute | solution.py:319
  85.9 6.5 %collective-permute-start.28 = (bf16[256,128]{1,0:T(8,128)(2,1)S(1)}, bf16[256,128]{1,0:T(8,128)(2,1)S(1)}, u32[]{:S(2)}, u32[]{:S(2)}) collective-permute-start(bf16[256,128]{1,0:T(8,128)(2,1)S(1)} %fusion.17), channel_id=1, source_target_pairs={{0,16},{4,20},{8,24},{12,28},{16,0},{20,4},{24,8},{28,12},{1,17},{... | collective-permute-start | bytes 196616 | tf_op jit(solution)/shard_map/ppermute | solution.py:319
  88.7 6.7 %collective-permute-start.32 = (bf16[512,128]{1,0:T(8,128)(2,1)S(1)}, bf16[512,128]{1,0:T(8,128)(2,1)S(1)}, u32[]{:S(2)}, u32[]{:S(2)}) collective-permute-start(bf16[512,128]{1,0:T(8,128)(2,1)S(1)} %collective-permute-done.24.refs_2_), channel_id=1, source_target_pairs={{0,1},{1,0},{2,3},{3,2},{4,5},{5,4},{6,7},{7,6},{8,9},{9,8},{10,11... | collective-permute-start | bytes 393224 | tf_op jit(solution)/shard_map/ppermute | solution.py:319
  97.6 9.6 %collective-permute-start.30 = (bf16[512,128]{1,0:T(8,128)(2,1)S(1)}, bf16[512,128]{1,0:T(8,128)(2,1)S(1)}, u32[]{:S(2)}, u32[]{:S(2)}) collective-permute-start(bf16[512,128]{1,0:T(8,128)(2,1)S(1)} %update.8.refs_5_.refs_0_.refs_4_), channel_id=1, source_target_pairs={{0,2},{1,3},{2,0},{3,1},{4,6},{5,7},{6,4},{7,5},{8,10},{9,11},{10,... | collective-permute-start | bytes 393224 | tf_op jit(solution)/shard_map/ppermute | solution.py:319
  100.3 6.9 %collective-permute-start.29 = (bf16[512,128]{1,0:T(8,128)(2,1)S(1)}, bf16[512,128]{1,0:T(8,128)(2,1)S(1)}, u32[]{:S(2)}, u32[]{:S(2)}) collective-permute-start(bf16[512,128]{1,0:T(8,128)(2,1)S(1)} %update.8.refs_5_.refs_0_.refs_4_), channel_id=1, source_target_pairs={{0,1},{1,0},{2,3},{3,2},{4,5},{5,4},{6,7},{7,6},{8,9},{9,8},{10,11... | collective-permute-start | bytes 393224 | tf_op jit(solution)/shard_map/ppermute | solution.py:319
  108.5 7.5 %collective-permute-start.39 = (bf16[256,128]{1,0:T(8,128)(2,1)S(1)}, bf16[256,128]{1,0:T(8,128)(2,1)S(1)}, u32[]{:S(2)}, u32[]{:S(2)}) collective-permute-start(bf16[256,128]{1,0:T(8,128)(2,1)S(1)} %fusion.19), channel_id=1, source_target_pairs={{0,16},{4,20},{8,24},{12,28},{16,0},{20,4},{24,8},{28,12},{1,17},{... | collective-permute-start | bytes 196616 | tf_op jit(solution)/shard_map/ppermute | solution.py:319
  111.9 7.0 %collective-permute-start.37 = (bf16[512,128]{1,0:T(8,128)(2,1)S(1)}, bf16[512,128]{1,0:T(8,128)(2,1)S(1)}, u32[]{:S(2)}, u32[]{:S(2)}) collective-permute-start(bf16[512,128]{1,0:T(8,128)(2,1)S(1)} %collective-permute-done.30.refs_2_), channel_id=1, source_target_pairs={{0,1},{1,0},{2,3},{3,2},{4,5},{5,4},{6,7},{7,6},{8,9},{9,8},{10,11... | collective-permute-start | bytes 393224 | tf_op jit(solution)/shard_map/ppermute | solution.py:319
  121.1 9.7 %collective-permute-start.42 = (bf16[512,128]{1,0:T(8,128)(2,1)S(1)}, bf16[512,128]{1,0:T(8,128)(2,1)S(1)}, u32[]{:S(2)}, u32[]{:S(2)}) collective-permute-start(bf16[512,128]{1,0:T(8,128)(2,1)S(1)} %update.9.refs_5_.refs_0_.refs_4_), channel_id=1, source_target_pairs={{0,2},{1,3},{2,0},{3,1},{4,6},{5,7},{6,4},{7,5},{8,10},{9,11},{10,... | collective-permute-start | bytes 393224 | tf_op jit(solution)/shard_map/ppermute | solution.py:319
  123.9 6.9 %collective-permute-start.41 = (bf16[512,128]{1,0:T(8,128)(2,1)S(1)}, bf16[512,128]{1,0:T(8,128)(2,1)S(1)}, u32[]{:S(2)}, u32[]{:S(2)}) collective-permute-start(bf16[512,128]{1,0:T(8,128)(2,1)S(1)} %update.9.refs_5_.refs_0_.refs_4_), channel_id=1, source_target_pairs={{0,1},{1,0},{2,3},{3,2},{4,5},{5,4},{6,7},{7,6},{8,9},{9,8},{10,11... | collective-permute-start | bytes 393224 | tf_op jit(solution)/shard_map/ppermute | solution.py:319
  132.1 6.6 %collective-permute-start.46 = (bf16[256,128]{1,0:T(8,128)(2,1)S(1)}, bf16[256,128]{1,0:T(8,128)(2,1)S(1)}, u32[]{:S(2)}, u32[]{:S(2)}) collective-permute-start(bf16[256,128]{1,0:T(8,128)(2,1)S(1)} %fusion.21), channel_id=1, source_target_pairs={{0,16},{4,20},{8,24},{12,28},{16,0},{20,4},{24,8},{28,12},{1,17},{... | collective-permute-start | bytes 196616 | tf_op jit(solution)/shard_map/ppermute | solution.py:319
  134.8 6.8 %collective-permute-start.48 = (bf16[512,128]{1,0:T(8,128)(2,1)S(1)}, bf16[512,128]{1,0:T(8,128)(2,1)S(1)}, u32[]{:S(2)}, u32[]{:S(2)}) collective-permute-start(bf16[512,128]{1,0:T(8,128)(2,1)S(1)} %collective-permute-done.42.refs_2_), channel_id=1, source_target_pairs={{0,1},{1,0},{2,3},{3,2},{4,5},{5,4},{6,7},{7,6},{8,9},{9,8},{10,11... | collective-permute-start | bytes 393224 | tf_op jit(solution)/shard_map/ppermute | solution.py:319
  (36 other events, 197.1 us)

commit v6 on v5

--- a/solution.py
+++ b/solution.py
@@ -179,9 +179,9 @@
     )(place, tile_src, row_counts, tile_vals)
 
 
-def assemble_kernel(packed, blocks, arrays, place_ref, *refs):
-    block_refs = refs[:arrays]
-    held_ref = refs[arrays + 1]
+def assemble_kernel(packed, blocks, place_ref, *refs):
+    block_refs = refs[:blocks]
+    held_ref = refs[blocks + 1]
     staged_ref = refs[-1] if packed else held_ref
     col = place_ref[1]
     rows, width = block_refs[0].shape
@@ -190,14 +190,8 @@
         first = pl.multiple_of(lax.bitwise_xor(col, mask) * rows, rows)
         staged_ref[pl.ds(first, rows), :] = ref[...]
 
-    for mask in range(blocks - 1):
+    for mask in range(blocks):
         put(mask, block_refs[mask])
-    if arrays == blocks:
-        put(blocks - 1, block_refs[-1])
-    else:
-        inside = jnp.logical_and(col > 0, col < blocks - 1)
-        pl.when(inside)(functools.partial(put, blocks - 1, block_refs[-2]))
-        pl.when(jnp.logical_not(inside))(functools.partial(put, blocks - 1, block_refs[-1]))
     if packed:
         piece = width // blocks
         for group in range(blocks):
@@ -205,14 +199,14 @@
             held_ref[group * rows : (group + 1) * rows, :] = jnp.concatenate(
                 [staged_ref[b * rows : (b + 1) * rows, lanes] for b in range(blocks)], axis=1
             )
-        own_ref = refs[arrays + 2]
+        own_ref = refs[blocks + 2]
         own_ref[...] = held_ref[pl.ds(pl.multiple_of(col * rows, rows), rows), :]
     zeros = held_ref.shape[0] - blocks * rows
     held_ref[blocks * rows :, :] = jnp.zeros((zeros, width), held_ref.dtype)
 
 
-def assemble(place, gathered, after, blocks, tile_size, packed):
-    arrays = len(gathered)
+def assemble(place, gathered, after, tile_size, packed):
+    blocks = len(gathered)
     rows, width = gathered[0].shape
     out_shape = [jax.ShapeDtypeStruct((blocks * rows + tile_size, width), jnp.bfloat16)]
     scratch = []
@@ -220,9 +214,9 @@
         out_shape.append(jax.ShapeDtypeStruct((rows, width), jnp.bfloat16))
         scratch.append(pltpu.VMEM((blocks * rows, width), jnp.bfloat16))
     return pl.pallas_call(
-        functools.partial(assemble_kernel, packed, blocks, arrays),
+        functools.partial(assemble_kernel, packed, blocks),
         out_shape=out_shape,
-        in_specs=smem(1) + vmem(arrays) + anywhere(1),
+        in_specs=smem(1) + vmem(blocks) + anywhere(1),
         out_specs=vmem(len(out_shape)),
         scratch_shapes=scratch,
         compiler_params=pltpu.CompilerParams(vmem_limit_bytes=4 * 2**20),
@@ -289,53 +283,57 @@
     )(*lists, turned, held, weights)
 
 
-def update_kernel(parts, *refs):
-    kept_refs = refs[:parts]
-    arrived_refs = refs[parts : 2 * parts]
-    iterate_ref, restart_ref, scale_ref, out_ref = refs[2 * parts :]
-    rows = out_ref.shape[0] // parts
-    for part in range(parts):
-        span = slice(part * rows, (part + 1) * rows)
-        summed = kept_refs[part][:rows, :] + arrived_refs[part][:rows, :].astype(jnp.float32)
-        out_ref[span, :] = (
-            scale_ref[span, :] * (summed + iterate_ref[span, :].astype(jnp.float32))
-            + TELEPORT * restart_ref[span, :].astype(jnp.float32)
-        ).astype(out_ref.dtype)
+def update_kernel(kept_ref, *refs):
+    *arrived_refs, iterate_ref, restart_ref, scale_ref, out_ref = refs
+    rows = out_ref.shape[0]
+    summed = kept_ref[:rows, :]
+    for ref in arrived_refs:
+        summed = summed + ref[:rows, :].astype(jnp.float32)
+    out_ref[...] = (
+        scale_ref[...] * (summed + iterate_ref[...].astype(jnp.float32))
+        + TELEPORT * restart_ref[...].astype(jnp.float32)
+    ).astype(out_ref.dtype)
 
 
 def update(kept, arrived, iterate, restart, scale):
     return pl.pallas_call(
-        functools.partial(update_kernel, len(kept)),
+        update_kernel,
         out_shape=jax.ShapeDtypeStruct(iterate.shape, iterate.dtype),
-        in_specs=vmem(2 * len(kept) + 3),
+        in_specs=vmem(len(arrived) + 4),
         out_specs=vmem(1)[0],
         compiler_params=pltpu.CompilerParams(vmem_limit_bytes=4 * 2**20),
         cost_estimate=pl.CostEstimate(flops=0, bytes_accessed=1, transcendentals=0),
         name="update",
-    )(*kept, *arrived, iterate, restart, scale)
+    )(kept, *arrived, iterate, restart, scale)
 
 
 def exchange(block, axis, mask, size):
     return lax.ppermute(block, axis, [(i, i ^ mask) for i in range(size)])
 
 
-def gather_first(block, size):
-    masks = (1, 2) if size == 4 else range(1, size)
-    return [block] + [exchange(block, "col", mask, size) for mask in masks]
-
-
-def gather_second(found, size):
-    if size != 4:
-        return found
-    inner = lax.ppermute(found[0], "col", [(0, 0), (1, 2), (2, 1), (3, 3)])
-    return found + [inner, exchange(found[2], "col", 1, size)]
-
-
-def halve(state, bits, bit, row_size):
-    axis = bits.index(bit)
-    send = lax.index_in_dim(state, 1, axis, keepdims=False).astype(jnp.bfloat16)
-    keep = lax.index_in_dim(state, 0, axis, keepdims=False)
-    return keep, exchange(send, "row", 1 << bit, row_size)
+def gather_line(block, size):
+    return [block] + [exchange(block, "col", mask, size) for mask in range(1, size)]
+
+
+def reduce_chips(both, cut, chip_bits, row_size):
+    kept, arrived = [], []
+    for half in range(2):
+        state = both[:, :cut] if half == 0 else both[:, cut:]
+        state = state.reshape((2,) * len(chip_bits) + state.shape[1:])
+        left = list(chip_bits)
+        turn = half % len(chip_bits)
+        got = None
+        for bit in chip_bits[turn:] + chip_bits[:turn]:
+            if got is not None:
+                state = state + got.astype(jnp.float32)
+            axis = left.index(bit)
+            send = lax.index_in_dim(state, 1, axis, keepdims=False).astype(jnp.bfloat16)
+            state = lax.index_in_dim(state, 0, axis, keepdims=False)
+            got = exchange(send, "row", 1 << bit, row_size)
+            left.remove(bit)
+        kept.append(state)
+        arrived.append(got)
+    return jnp.concatenate(kept), jnp.concatenate(arrived)
 
 
 def on_device(features, tile_vals, tile_src, row_counts):
@@ -361,7 +359,7 @@
         place, tile_src, row_counts, tile_vals, row_size, tiles_per_owner
     )
 
-    gathered = [gather_second(gather_first(parts[0], blocks), blocks), None]
+    gathered = [gather_line(parts[0], blocks), None]
     iterates = [None] * CHUNKS
     restarts = [None] * CHUNKS
     scale = None
@@ -373,47 +371,26 @@
         extra = EXTRA if phase == 0 else 0
         if phase > 0:
             iterates[after] = last = update(*pending)
-        held, *own = assemble(place, gathered[chunk], last, blocks, tile_size, first)
+        held, *own = assemble(place, gathered[chunk], last, tile_size, first)
         if first:
             iterates[chunk] = restarts[chunk] = own[0]
         if phase == 0:
             held, parts = lax.optimization_barrier((held, parts))
-            found = gather_first(parts[1], blocks)
+            gathered[after] = gather_line(parts[1], blocks)
         elif phase + 1 < ITERS * CHUNKS:
-            found = gather_first(iterates[after], blocks)
-        else:
-            found = []
+            gathered[after] = gather_line(iterates[after], blocks)
         sent = product(1, lists, turned, held, weights, rows, chips, extra)
         other = exchange(sent, "row", 1, row_size)
         kept = product(0, lists, turned, held, weights, rows, chips, extra)
         both = kept.astype(jnp.float32) + other.astype(jnp.float32)
-        states, arrivals, orders = [], [], []
-        for half in range(2):
-            state = both[:, : rows // 2] if half == 0 else both[:, rows // 2 :]
-            states.append(state.reshape((2,) * len(chip_bits) + state.shape[1:]))
-            arrivals.append(None)
-            turn = half % len(chip_bits)
-            orders.append(chip_bits[turn:] + chip_bits[:turn])
-        left = [list(chip_bits), list(chip_bits)]
-        for step in range(len(chip_bits)):
-            for half in range(2):
-                if step > 0:
-                    states[half] = states[half] + arrivals[half].astype(jnp.float32)
-                bit = orders[half][step]
-                states[half], arrivals[half] = halve(states[half], left[half], bit, row_size)
-                left[half].remove(bit)
-            if step == 0:
-                found, arrivals = lax.optimization_barrier((found, arrivals))
-                if found:
-                    gathered[after] = gather_second(found, blocks)
-        sums = states
+        kept, arrived = reduce_chips(both, rows // 2, chip_bits, row_size)
         if phase == 0:
-            weight_rows = slice(rows // 2, rows // 2 + tiles_per_owner)
-            total = 1.0 + sums[1][weight_rows] + arrivals[1][weight_rows].astype(jnp.float32)
+            weight_rows = slice(rows, rows + tiles_per_owner)
+            total = 1.0 + kept[weight_rows] + arrived[weight_rows].astype(jnp.float32)
             scale = jnp.broadcast_to(
                 ((1.0 - TELEPORT) / total).reshape(rows, 1), (rows, width)
             )
-        pending = (sums, arrivals, iterates[chunk], restarts[chunk], scale)
+        pending = (kept, [arrived], iterates[chunk], restarts[chunk], scale)
     iterates[chunk] = update(*pending)
     out = jnp.stack(iterates).reshape(CHUNKS, rows, blocks, piece).transpose(1, 2, 0, 3)
     return out.reshape(rows, CHUNKS * width)

time: 160 us -> 142 us (0.89)
  starting transfers between devices: 73.1 us -> 55.2 us
  local copies, waits for them, and re-layouts: 7.86 us -> 10.1 us
  waiting for transfers between devices: 47.9 us -> 46 us
    ppermute x48, starting transfers between devices: 69.1 us -> 55.2 us  [exchange(): return lax.ppermute(block, axis, [(i, i ^ mask) for i in range(size)])]
    ppermute x6 -> x0, starting transfers between devices: 3.94 us -> none  [gather_second(): inner = lax.ppermute(found[0], 'col', [(0, 0), (1, 2), (2, 1), (3, 3)])]
    unnamed x12 -> x14, local copies, waits for them, and re-layouts: 4.39 us -> 6.57 us
    ppermute x48, waiting for transfers between devices: 47.9 us -> 46 us  [exchange(): return lax.ppermute(block, axis, [(i, i ^ mask) for i in range(size)])]
  transfers between devices with their start and end apart: 54 -> 48, of which waited for: 27 -> 23; matrix products, arithmetic and copies ran while one was open for 1% -> 2% of each run, Pallas kernels for 9% -> 10%
where the time goes in v6:
time: 142 us
  starting transfers between devices  55.2 us (39%)
  waiting for transfers between devices  46 us (32%)
  Pallas kernels  28.5 us (20%)
  local copies, waits for them, and re-layouts  10.1 us (7%)
    ppermute x48, starting transfers between devices, exchange(): return lax.ppermute(block, axis, [(i, i ^ mask) for i in range(size)])  55.2 us
    ppermute x48, waiting for transfers between devices, exchange(): return lax.ppermute(block, axis, [(i, i ^ mask) for i in range(size)])  46 us
    pallas_call x12, Pallas kernels, product(): pl.pallas_call(functools.partial(product_kernel, half, rows), out_shape=j...  18.3 us
    unnamed x14, local copies, waits for them, and re-layouts  6.57 us
    pallas_call x1, Pallas kernels, prepare(): pl.pallas_call(functools.partial(prepare_kernel, tiles_per_owner), out_sh...  5.29 us
    pallas_call x6, Pallas kernels, assemble(): pl.pallas_call(functools.partial(assemble_kernel, packed, blocks), out_sh...  4.5 us
  transfers between devices with their start and end apart: 48, of which 23 were waited for; matrix products, arithmetic and copies ran while one was open for 2% of the time, Pallas kernels for 10%

profile of v6, /device:TPU:0, one launch (start us, length us, event | category | flops | bytes accessed | tf_op | source)
XLA Modules:
  0.0 142.1 jit_solution(8853220497013483467)
XLA Ops:
  1.4 3.1 %collective-permute-start = (bf16[512,128]{1,0:T(8,128)(2,1)S(1)}, bf16[512,128]{1,0:T(8,128)(2,1)S(1)}, u32[]{:S(2)}, u32[]{:S(2)}) collective-permute-start(bf16[512,128]{1,0:T(8,128)(2,1)S(1)} %copy.44.refs_0_), channel_id=1, source_target_pairs={{0,1},{1,0},{2,3},{3,2},{4,5},{5,4},{6,7},{7,6},{8,9},{9,8},{10,11... | collective-permute-start | bytes 393224 | tf_op jit(solution)/shard_map/ppermute | solution.py:311
  4.5 2.6 %collective-permute-start.1 = (bf16[512,128]{1,0:T(8,128)(2,1)S(1)}, bf16[512,128]{1,0:T(8,128)(2,1)S(1)}, u32[]{:S(2)}, u32[]{:S(2)}) collective-permute-start(bf16[512,128]{1,0:T(8,128)(2,1)S(1)} %copy.44.refs_0_), channel_id=1, source_target_pairs={{0,2},{1,3},{2,0},{3,1},{4,6},{5,7},{6,4},{7,5},{8,10},{9,11},{10,... | collective-permute-start | bytes 393224 | tf_op jit(solution)/shard_map/ppermute | solution.py:311
  7.2 2.2 %copy-done.4 = bf16[128,128,128]{2,1,0:T(8,128)(2,1)S(1)} copy-done((bf16[128,128,128]{2,1,0:T(8,128)(2,1)S(1)}, bf16[128,128,128]{2,1,0:T(8,128)(2,1)}, u32[]{:S(2)}) %copy-start.4) | copy-done | bytes 4194328
  9.4 5.3 %prepare.1 = (bf16[128,128,128]{2,1,0:T(8,128)(2,1)S(1)}, f32[8,16,128]{2,1,0:T(8,128)S(1)}, s32[2,72]{1,0:T(2,128)S(1)}, s32[2,72]{1,0:T(2,128)S(1)}, s32[2,72]...) custom-call(s32[3]{0:T(128)S(1)} %pad_add_fusion.place_ref.refs_4_, ...), custom_call_target="tpu_custom_call" | custom-call | tf_op jit(solution)/shard_map/prepare/pallas_call | solution.py:158
  14.7 2.7 %collective-permute-done.1.refs_2_ = bf16[512,128]{1,0:T(8,128)(2,1)S(1)} collective-permute-done((bf16[512,128]{1,0:T(8,128)(2,1)S(1)}, bf16[512,128]{1,0:T(8,128)(2,1)S(1)}, u32[]{:S(2)}, u32[]{:S(2)}) %collective-permute-start.1) | collective-permute-done | bytes 131104 | tf_op jit(solution)/shard_map/ppermute | solution.py:311
  24.8 2.2 %copy-done.1 = bf16[128,128,128]{2,1,0:T(8,128)(2,1)S(1)} copy-done((bf16[128,128,128]{2,1,0:T(8,128)(2,1)S(1)}, bf16[128,128,128]{2,1,0:T(8,128)(2,1)}, u32[]{:S(2)}) %copy-start.1) | copy-done | bytes 4194328
  28.7 2.2 %collective-permute-start.4 = (bf16[2,256,128]{2,1,0:T(8,128)(2,1)S(1)}, bf16[2,256,128]{2,1,0:T(8,128)(2,1)S(1)}, u32[]{:S(2)}, u32[]{:S(2)}) collective-permute-start(bf16[2,256,128]{2,1,0:T(8,128)(2,1)S(1)} %slice.423), channel_id=1, source_target_pairs={{0,16},{4,20},{8,24},{12,28},{16,0},{20,4},{24,8},{28,12},{1,17},{... | collective-permute-start | bytes 393224 | tf_op jit(solution)/shard_map/ppermute | solution.py:311
  31.9 2.8 %collective-permute-done.4 = bf16[2,256,128]{2,1,0:T(8,128)(2,1)S(1)} collective-permute-done((bf16[2,256,128]{2,1,0:T(8,128)(2,1)S(1)}, bf16[2,256,128]{2,1,0:T(8,128)(2,1)S(1)}, u32[]{:S(2)}, u32[]{:S(2)}) %collective-permute-start.4) | collective-permute-done | bytes 131104 | tf_op jit(solution)/shard_map/ppermute | solution.py:311
  37.4 3.4 %collective-permute-done.7 = bf16[272,128]{1,0:T(8,128)(2,1)S(1)} collective-permute-done((bf16[272,128]{1,0:T(8,128)(2,1)S(1)}, bf16[272,128]{1,0:T(8,128)(2,1)S(1)}, u32[]{:S(2)}, u32[]{:S(2)}) %collective-permute-start.7) | collective-permute-done | bytes 69664 | tf_op jit(solution)/shard_map/ppermute | solution.py:311
  43.8 2.5 %collective-permute-start.10 = (bf16[512,128]{1,0:T(8,128)(2,1)S(1)}, bf16[512,128]{1,0:T(8,128)(2,1)S(1)}, u32[]{:S(2)}, u32[]{:S(2)}) collective-permute-start(bf16[512,128]{1,0:T(8,128)(2,1)S(1)} %update.6.refs_4_.refs_0_.refs_1_), channel_id=1, source_target_pairs={{0,3},{1,2},{2,1},{3,0},{4,7},{5,6},{6,5},{7,4},{8,11},{9,10},{10,... | collective-permute-start | bytes 393224 | tf_op jit(solution)/shard_map/ppermute | solution.py:311
  52.2 3.5 %collective-permute-done.15 = bf16[2,256,128]{2,1,0:T(8,128)(2,1)S(1)} collective-permute-done((bf16[2,256,128]{2,1,0:T(8,128)(2,1)S(1)}, bf16[2,256,128]{2,1,0:T(8,128)(2,1)S(1)}, u32[]{:S(2)}, u32[]{:S(2)}) %collective-permute-start.15) | collective-permute-done | bytes 131104 | tf_op jit(solution)/shard_map/ppermute | solution.py:311
  58.0 2.7 %collective-permute-done.17 = bf16[256,128]{1,0:T(8,128)(2,1)S(1)} collective-permute-done((bf16[256,128]{1,0:T(8,128)(2,1)S(1)}, bf16[256,128]{1,0:T(8,128)(2,1)S(1)}, u32[]{:S(2)}, u32[]{:S(2)}) %collective-permute-start.17) | collective-permute-done | bytes 65568 | tf_op jit(solution)/shard_map/ppermute | solution.py:311
  64.6 2.3 %collective-permute-start.28 = (bf16[512,128]{1,0:T(8,128)(2,1)S(1)}, bf16[512,128]{1,0:T(8,128)(2,1)S(1)}, u32[]{:S(2)}, u32[]{:S(2)}) collective-permute-start(bf16[512,128]{1,0:T(8,128)(2,1)S(1)} %update.7.refs_4_.refs_0_.refs_1_), channel_id=1, source_target_pairs={{0,2},{1,3},{2,0},{3,1},{4,6},{5,7},{6,4},{7,5},{8,10},{9,11},{10,... | collective-permute-start | bytes 393224 | tf_op jit(solution)/shard_map/ppermute | solution.py:311
  72.6 3.2 %collective-permute-done.20 = bf16[2,256,128]{2,1,0:T(8,128)(2,1)S(1)} collective-permute-done((bf16[2,256,128]{2,1,0:T(8,128)(2,1)S(1)}, bf16[2,256,128]{2,1,0:T(8,128)(2,1)S(1)}, u32[]{:S(2)}, u32[]{:S(2)}) %collective-permute-start.20) | collective-permute-done | bytes 131104 | tf_op jit(solution)/shard_map/ppermute | solution.py:311
  78.6 2.1 %collective-permute-done.22 = bf16[256,128]{1,0:T(8,128)(2,1)S(1)} collective-permute-done((bf16[256,128]{1,0:T(8,128)(2,1)S(1)}, bf16[256,128]{1,0:T(8,128)(2,1)S(1)}, u32[]{:S(2)}, u32[]{:S(2)}) %collective-permute-start.22) | collective-permute-done | bytes 65568 | tf_op jit(solution)/shard_map/ppermute | solution.py:311
  84.4 2.6 %collective-permute-start.25 = (bf16[512,128]{1,0:T(8,128)(2,1)S(1)}, bf16[512,128]{1,0:T(8,128)(2,1)S(1)}, u32[]{:S(2)}, u32[]{:S(2)}) collective-permute-start(bf16[512,128]{1,0:T(8,128)(2,1)S(1)} %update.8.refs_4_.refs_0_.refs_1_), channel_id=1, source_target_pairs={{0,2},{1,3},{2,0},{3,1},{4,6},{5,7},{6,4},{7,5},{8,10},{9,11},{10,... | collective-permute-start | bytes 393224 | tf_op jit(solution)/shard_map/ppermute | solution.py:311
  92.7 3.5 %collective-permute-done.31 = bf16[2,256,128]{2,1,0:T(8,128)(2,1)S(1)} collective-permute-done((bf16[2,256,128]{2,1,0:T(8,128)(2,1)S(1)}, bf16[2,256,128]{2,1,0:T(8,128)(2,1)S(1)}, u32[]{:S(2)}, u32[]{:S(2)}) %collective-permute-start.31) | collective-permute-done | bytes 131104 | tf_op jit(solution)/shard_map/ppermute | solution.py:311
  98.7 2.5 %collective-permute-done.33 = bf16[256,128]{1,0:T(8,128)(2,1)S(1)} collective-permute-done((bf16[256,128]{1,0:T(8,128)(2,1)S(1)}, bf16[256,128]{1,0:T(8,128)(2,1)S(1)}, u32[]{:S(2)}, u32[]{:S(2)}) %collective-permute-start.33) | collective-permute-done | bytes 65568 | tf_op jit(solution)/shard_map/ppermute | solution.py:311
  104.4 2.6 %collective-permute-start.41 = (bf16[512,128]{1,0:T(8,128)(2,1)S(1)}, bf16[512,128]{1,0:T(8,128)(2,1)S(1)}, u32[]{:S(2)}, u32[]{:S(2)}) collective-permute-start(bf16[512,128]{1,0:T(8,128)(2,1)S(1)} %update.9.refs_4_.refs_0_.refs_1_), channel_id=1, source_target_pairs={{0,2},{1,3},{2,0},{3,1},{4,6},{5,7},{6,4},{7,5},{8,10},{9,11},{10,... | collective-permute-start | bytes 393224 | tf_op jit(solution)/shard_map/ppermute | solution.py:311
  113.0 3.2 %collective-permute-done.36 = bf16[2,256,128]{2,1,0:T(8,128)(2,1)S(1)} collective-permute-done((bf16[2,256,128]{2,1,0:T(8,128)(2,1)S(1)}, bf16[2,256,128]{2,1,0:T(8,128)(2,1)S(1)}, u32[]{:S(2)}, u32[]{:S(2)}) %collective-permute-start.36) | collective-permute-done | bytes 131104 | tf_op jit(solution)/shard_map/ppermute | solution.py:311
  119.0 2.3 %collective-permute-done.38 = bf16[256,128]{1,0:T(8,128)(2,1)S(1)} collective-permute-done((bf16[256,128]{1,0:T(8,128)(2,1)S(1)}, bf16[256,128]{1,0:T(8,128)(2,1)S(1)}, u32[]{:S(2)}, u32[]{:S(2)}) %collective-permute-start.38) | collective-permute-done | bytes 65568 | tf_op jit(solution)/shard_map/ppermute | solution.py:311
  124.9 2.2 %copy-done.3 = bf16[128,128,128]{2,1,0:T(8,128)(2,1)S(1)} copy-done((bf16[128,128,128]{2,1,0:T(8,128)(2,1)S(1)}, bf16[128,128,128]{2,1,0:T(8,128)(2,1)}, u32[]{:S(2)}) %copy-start.3) | copy-done | bytes 4194328
  131.0 4.1 %collective-permute-done.44 = bf16[2,256,128]{2,1,0:T(8,128)(2,1)S(1)} collective-permute-done((bf16[2,256,128]{2,1,0:T(8,128)(2,1)S(1)}, bf16[2,256,128]{2,1,0:T(8,128)(2,1)S(1)}, u32[]{:S(2)}, u32[]{:S(2)}) %collective-permute-start.44) | collective-permute-done | bytes 131104 | tf_op jit(solution)/shard_map/ppermute | solution.py:311
  137.6 2.5 %collective-permute-done.46 = bf16[256,128]{1,0:T(8,128)(2,1)S(1)} collective-permute-done((bf16[256,128]{1,0:T(8,128)(2,1)S(1)}, bf16[256,128]{1,0:T(8,128)(2,1)S(1)}, u32[]{:S(2)}, u32[]{:S(2)}) %collective-permute-start.46) | collective-permute-done | bytes 65568 | tf_op jit(solution)/shard_map/ppermute | solution.py:311
  (198 shorter events, 73.1 us)
Async XLA Ops:
  1.4 13.3 %collective-permute-start = (bf16[512,128]{1,0:T(8,128)(2,1)S(1)}, bf16[512,128]{1,0:T(8,128)(2,1)S(1)}, u32[]{:S(2)}, u32[]{:S(2)}) collective-permute-start(bf16[512,128]{1,0:T(8,128)(2,1)S(1)} %copy.44.refs_0_), channel_id=1, source_target_pairs={{0,1},{1,0},{2,3},{3,2},{4,5},{5,4},{6,7},{7,6},{8,9},{9,8},{10,11... | collective-permute-start | bytes 393224 | tf_op jit(solution)/shard_map/ppermute | solution.py:311
  4.5 12.9 %collective-permute-start.1 = (bf16[512,128]{1,0:T(8,128)(2,1)S(1)}, bf16[512,128]{1,0:T(8,128)(2,1)S(1)}, u32[]{:S(2)}, u32[]{:S(2)}) collective-permute-start(bf16[512,128]{1,0:T(8,128)(2,1)S(1)} %copy.44.refs_0_), channel_id=1, source_target_pairs={{0,2},{1,3},{2,0},{3,1},{4,6},{5,7},{6,4},{7,5},{8,10},{9,11},{10,... | collective-permute-start | bytes 393224 | tf_op jit(solution)/shard_map/ppermute | solution.py:311
  7.1 10.3 %collective-permute-start.2 = (bf16[512,128]{1,0:T(8,128)(2,1)S(1)}, bf16[512,128]{1,0:T(8,128)(2,1)S(1)}, u32[]{:S(2)}, u32[]{:S(2)}) collective-permute-start(bf16[512,128]{1,0:T(8,128)(2,1)S(1)} %copy.44.refs_0_), channel_id=1, source_target_pairs={{0,3},{1,2},{2,1},{3,0},{4,7},{5,6},{6,5},{7,4},{8,11},{9,10},{10,... | collective-permute-start | bytes 393224 | tf_op jit(solution)/shard_map/ppermute | solution.py:311
  20.0 8.5 %collective-permute-start.3 = (bf16[4,528,128]{2,1,0:T(8,128)(2,1)S(1)}, bf16[4,528,128]{2,1,0:T(8,128)(2,1)S(1)}, u32[]{:S(2)}, u32[]{:S(2)}) collective-permute-start(bf16[4,528,128]{2,1,0:T(8,128)(2,1)S(1)} %product.13), channel_id=1, source_target_pairs={{0,4},{4,0},{8,12},{12,8},{16,20},{20,16},{24,28},{28,24},{1,5},{5... | collective-permute-start | bytes 1622024 | tf_op jit(solution)/shard_map/ppermute | solution.py:311
  20.3 20.7 %collective-permute-start.11 = (bf16[512,128]{1,0:T(8,128)(2,1)S(1)}, bf16[512,128]{1,0:T(8,128)(2,1)S(1)}, u32[]{:S(2)}, u32[]{:S(2)}) collective-permute-start(bf16[512,128]{1,0:T(8,128)(2,1)S(1)} %slice_bitcast_fusion.11.refs_0_), channel_id=1, source_target_pairs={{0,1},{1,0},{2,3},{3,2},{4,5},{5,4},{6,7},{7,6},{8,9},{9,8},{10,11... | collective-permute-start | bytes 393224 | tf_op jit(solution)/shard_map/ppermute | solution.py:311
  22.3 18.7 %collective-permute-start.12 = (bf16[512,128]{1,0:T(8,128)(2,1)S(1)}, bf16[512,128]{1,0:T(8,128)(2,1)S(1)}, u32[]{:S(2)}, u32[]{:S(2)}) collective-permute-start(bf16[512,128]{1,0:T(8,128)(2,1)S(1)} %slice_bitcast_fusion.11.refs_0_), channel_id=1, source_target_pairs={{0,2},{1,3},{2,0},{3,1},{4,6},{5,7},{6,4},{7,5},{8,10},{9,11},{10,... | collective-permute-start | bytes 393224 | tf_op jit(solution)/shard_map/ppermute | solution.py:311
  23.4 17.7 %collective-permute-start.13 = (bf16[512,128]{1,0:T(8,128)(2,1)S(1)}, bf16[512,128]{1,0:T(8,128)(2,1)S(1)}, u32[]{:S(2)}, u32[]{:S(2)}) collective-permute-start(bf16[512,128]{1,0:T(8,128)(2,1)S(1)} %slice_bitcast_fusion.11.refs_0_), channel_id=1, source_target_pairs={{0,3},{1,2},{2,1},{3,0},{4,7},{5,6},{6,5},{7,4},{8,11},{9,10},{10,... | collective-permute-start | bytes 393224 | tf_op jit(solution)/shard_map/ppermute | solution.py:311
  43.7 6.1 %collective-permute-start.14 = (bf16[4,512,128]{2,1,0:T(8,128)(2,1)S(1)}, bf16[4,512,128]{2,1,0:T(8,128)(2,1)S(1)}, u32[]{:S(2)}, u32[]{:S(2)}) collective-permute-start(bf16[4,512,128]{2,1,0:T(8,128)(2,1)S(1)} %product.15), channel_id=1, source_target_pairs={{0,4},{4,0},{8,12},{12,8},{16,20},{20,16},{24,28},{28,24},{1,5},{5... | collective-permute-start | bytes 1572872 | tf_op jit(solution)/shard_map/ppermute | solution.py:311
  43.8 17.8 %collective-permute-start.10 = (bf16[512,128]{1,0:T(8,128)(2,1)S(1)}, bf16[512,128]{1,0:T(8,128)(2,1)S(1)}, u32[]{:S(2)}, u32[]{:S(2)}) collective-permute-start(bf16[512,128]{1,0:T(8,128)(2,1)S(1)} %update.6.refs_4_.refs_0_.refs_1_), channel_id=1, source_target_pairs={{0,3},{1,2},{2,1},{3,0},{4,7},{5,6},{6,5},{7,4},{8,11},{9,10},{10,... | collective-permute-start | bytes 393224 | tf_op jit(solution)/shard_map/ppermute | solution.py:311
  46.3 15.3 %collective-permute-start.8 = (bf16[512,128]{1,0:T(8,128)(2,1)S(1)}, bf16[512,128]{1,0:T(8,128)(2,1)S(1)}, u32[]{:S(2)}, u32[]{:S(2)}) collective-permute-start(bf16[512,128]{1,0:T(8,128)(2,1)S(1)} %update.6.refs_4_.refs_0_.refs_1_), channel_id=1, source_target_pairs={{0,1},{1,0},{2,3},{3,2},{4,5},{5,4},{6,7},{7,6},{8,9},{9,8},{10,11... | collective-permute-start | bytes 393224 | tf_op jit(solution)/shard_map/ppermute | solution.py:311
  47.1 14.6 %collective-permute-start.9 = (bf16[512,128]{1,0:T(8,128)(2,1)S(1)}, bf16[512,128]{1,0:T(8,128)(2,1)S(1)}, u32[]{:S(2)}, u32[]{:S(2)}) collective-permute-start(bf16[512,128]{1,0:T(8,128)(2,1)S(1)} %update.6.refs_4_.refs_0_.refs_1_), channel_id=1, source_target_pairs={{0,2},{1,3},{2,0},{3,1},{4,6},{5,7},{6,4},{7,5},{8,10},{9,11},{10,... | collective-permute-start | bytes 393224 | tf_op jit(solution)/shard_map/ppermute | solution.py:311
  63.8 6.1 %collective-permute-start.19 = (bf16[4,512,128]{2,1,0:T(8,128)(2,1)S(1)}, bf16[4,512,128]{2,1,0:T(8,128)(2,1)S(1)}, u32[]{:S(2)}, u32[]{:S(2)}) collective-permute-start(bf16[4,512,128]{2,1,0:T(8,128)(2,1)S(1)} %product.17), channel_id=1, source_target_pairs={{0,4},{4,0},{8,12},{12,8},{16,20},{20,16},{24,28},{28,24},{1,5},{5... | collective-permute-start | bytes 1572872 | tf_op jit(solution)/shard_map/ppermute | solution.py:311
  63.9 18.1 %collective-permute-start.27 = (bf16[512,128]{1,0:T(8,128)(2,1)S(1)}, bf16[512,128]{1,0:T(8,128)(2,1)S(1)}, u32[]{:S(2)}, u32[]{:S(2)}) collective-permute-start(bf16[512,128]{1,0:T(8,128)(2,1)S(1)} %update.7.refs_4_.refs_0_.refs_1_), channel_id=1, source_target_pairs={{0,1},{1,0},{2,3},{3,2},{4,5},{5,4},{6,7},{7,6},{8,9},{9,8},{10,11... | collective-permute-start | bytes 393224 | tf_op jit(solution)/shard_map/ppermute | solution.py:311
  64.6 17.4 %collective-permute-start.28 = (bf16[512,128]{1,0:T(8,128)(2,1)S(1)}, bf16[512,128]{1,0:T(8,128)(2,1)S(1)}, u32[]{:S(2)}, u32[]{:S(2)}) collective-permute-start(bf16[512,128]{1,0:T(8,128)(2,1)S(1)} %update.7.refs_4_.refs_0_.refs_1_), channel_id=1, source_target_pairs={{0,2},{1,3},{2,0},{3,1},{4,6},{5,7},{6,4},{7,5},{8,10},{9,11},{10,... | collective-permute-start | bytes 393224 | tf_op jit(solution)/shard_map/ppermute | solution.py:311
  67.0 15.1 %collective-permute-start.29 = (bf16[512,128]{1,0:T(8,128)(2,1)S(1)}, bf16[512,128]{1,0:T(8,128)(2,1)S(1)}, u32[]{:S(2)}, u32[]{:S(2)}) collective-permute-start(bf16[512,128]{1,0:T(8,128)(2,1)S(1)} %update.7.refs_4_.refs_0_.refs_1_), channel_id=1, source_target_pairs={{0,3},{1,2},{2,1},{3,0},{4,7},{5,6},{6,5},{7,4},{8,11},{9,10},{10,... | collective-permute-start | bytes 393224 | tf_op jit(solution)/shard_map/ppermute | solution.py:311
  84.2 6.1 %collective-permute-start.30 = (bf16[4,512,128]{2,1,0:T(8,128)(2,1)S(1)}, bf16[4,512,128]{2,1,0:T(8,128)(2,1)S(1)}, u32[]{:S(2)}, u32[]{:S(2)}) collective-permute-start(bf16[4,512,128]{2,1,0:T(8,128)(2,1)S(1)} %product.19), channel_id=1, source_target_pairs={{0,4},{4,0},{8,12},{12,8},{16,20},{20,16},{24,28},{28,24},{1,5},{5... | collective-permute-start | bytes 1572872 | tf_op jit(solution)/shard_map/ppermute | solution.py:311
  84.3 17.8 %collective-permute-start.24 = (bf16[512,128]{1,0:T(8,128)(2,1)S(1)}, bf16[512,128]{1,0:T(8,128)(2,1)S(1)}, u32[]{:S(2)}, u32[]{:S(2)}) collective-permute-start(bf16[512,128]{1,0:T(8,128)(2,1)S(1)} %update.8.refs_4_.refs_0_.refs_1_), channel_id=1, source_target_pairs={{0,1},{1,0},{2,3},{3,2},{4,5},{5,4},{6,7},{7,6},{8,9},{9,8},{10,11... | collective-permute-start | bytes 393224 | tf_op jit(solution)/shard_map/ppermute | solution.py:311
  84.4 17.8 %collective-permute-start.25 = (bf16[512,128]{1,0:T(8,128)(2,1)S(1)}, bf16[512,128]{1,0:T(8,128)(2,1)S(1)}, u32[]{:S(2)}, u32[]{:S(2)}) collective-permute-start(bf16[512,128]{1,0:T(8,128)(2,1)S(1)} %update.8.refs_4_.refs_0_.refs_1_), channel_id=1, source_target_pairs={{0,2},{1,3},{2,0},{3,1},{4,6},{5,7},{6,4},{7,5},{8,10},{9,11},{10,... | collective-permute-start | bytes 393224 | tf_op jit(solution)/shard_map/ppermute | solution.py:311
  87.0 15.1 %collective-permute-start.26 = (bf16[512,128]{1,0:T(8,128)(2,1)S(1)}, bf16[512,128]{1,0:T(8,128)(2,1)S(1)}, u32[]{:S(2)}, u32[]{:S(2)}) collective-permute-start(bf16[512,128]{1,0:T(8,128)(2,1)S(1)} %update.8.refs_4_.refs_0_.refs_1_), channel_id=1, source_target_pairs={{0,3},{1,2},{2,1},{3,0},{4,7},{5,6},{6,5},{7,4},{8,11},{9,10},{10,... | collective-permute-start | bytes 393224 | tf_op jit(solution)/shard_map/ppermute | solution.py:311
  104.3 6.1 %collective-permute-start.35 = (bf16[4,512,128]{2,1,0:T(8,128)(2,1)S(1)}, bf16[4,512,128]{2,1,0:T(8,128)(2,1)S(1)}, u32[]{:S(2)}, u32[]{:S(2)}) collective-permute-start(bf16[4,512,128]{2,1,0:T(8,128)(2,1)S(1)} %product.21), channel_id=1, source_target_pairs={{0,4},{4,0},{8,12},{12,8},{16,20},{20,16},{24,28},{28,24},{1,5},{5... | collective-permute-start | bytes 1572872 | tf_op jit(solution)/shard_map/ppermute | solution.py:311
  104.4 18.1 %collective-permute-start.40 = (bf16[512,128]{1,0:T(8,128)(2,1)S(1)}, bf16[512,128]{1,0:T(8,128)(2,1)S(1)}, u32[]{:S(2)}, u32[]{:S(2)}) collective-permute-start(bf16[512,128]{1,0:T(8,128)(2,1)S(1)} %update.9.refs_4_.refs_0_.refs_1_), channel_id=1, source_target_pairs={{0,1},{1,0},{2,3},{3,2},{4,5},{5,4},{6,7},{7,6},{8,9},{9,8},{10,11... | collective-permute-start | bytes 393224 | tf_op jit(solution)/shard_map/ppermute | solution.py:311
  104.4 18.1 %collective-permute-start.41 = (bf16[512,128]{1,0:T(8,128)(2,1)S(1)}, bf16[512,128]{1,0:T(8,128)(2,1)S(1)}, u32[]{:S(2)}, u32[]{:S(2)}) collective-permute-start(bf16[512,128]{1,0:T(8,128)(2,1)S(1)} %update.9.refs_4_.refs_0_.refs_1_), channel_id=1, source_target_pairs={{0,2},{1,3},{2,0},{3,1},{4,6},{5,7},{6,4},{7,5},{8,10},{9,11},{10,... | collective-permute-start | bytes 393224 | tf_op jit(solution)/shard_map/ppermute | solution.py:311
  107.1 15.4 %collective-permute-start.42 = (bf16[512,128]{1,0:T(8,128)(2,1)S(1)}, bf16[512,128]{1,0:T(8,128)(2,1)S(1)}, u32[]{:S(2)}, u32[]{:S(2)}) collective-permute-start(bf16[512,128]{1,0:T(8,128)(2,1)S(1)} %update.9.refs_4_.refs_0_.refs_1_), channel_id=1, source_target_pairs={{0,3},{1,2},{2,1},{3,0},{4,7},{5,6},{6,5},{7,4},{8,11},{9,10},{10,... | collective-permute-start | bytes 393224 | tf_op jit(solution)/shard_map/ppermute | solution.py:311
  128.8 6.3 %collective-permute-start.44 = (bf16[2,256,128]{2,1,0:T(8,128)(2,1)S(1)}, bf16[2,256,128]{2,1,0:T(8,128)(2,1)S(1)}, u32[]{:S(2)}, u32[]{:S(2)}) collective-permute-start(bf16[2,256,128]{2,1,0:T(8,128)(2,1)S(1)} %slice.418), channel_id=1, source_target_pairs={{0,16},{4,20},{8,24},{12,28},{16,0},{20,4},{24,8},{28,12},{1,17},{... | collective-permute-start | bytes 393224 | tf_op jit(solution)/shard_map/ppermute | solution.py:311
  (31 other events, 151.0 us)

commit v7 on v6

v7 whole, which is shorter than its diff:
```python
import functools

import jax
import jax.numpy as jnp
from jax import lax
from jax.experimental import pallas as pl
from jax.experimental.pallas import tpu as pltpu
from jax.sharding import PartitionSpec as P

ITERS = 3


TELEPORT = 0.1


CHUNKS = 2


UNROLL = 8


EXTRA = 16


MOST = 8


def vmem(count):
    return [pl.BlockSpec(memory_space=pltpu.VMEM)] * count


def smem(count):
    return [pl.BlockSpec(memory_space=pltpu.SMEM)] * count


def anywhere(count):
    return [pl.BlockSpec(memory_space=pl.ANY)] * count


def hbm(count):
    return [pl.BlockSpec(memory_space=pltpu.HBM)] * count


def pair_capacity(tile_max, dest_count):
    most = (tile_max + dest_count // 2) // 2
    return -(-most // UNROLL) * UNROLL


SLOT, FIRST, SECOND, CHIP, ROW, GO_ON, TURNS, FIELDS = range(8)


def chip_place(relative, owner, chip_bits):
    place = jnp.int32(0)
    turned = jnp.int32(0)
    for bit in range(chip_bits):
        value = lax.bitwise_and(lax.shift_right_logical(relative, bit + 1), 1)
        place = place + value * (1 << bit)
        turned = turned + value * (1 << (chip_bits - 1 - bit))
    return jnp.where(lax.bitwise_and(owner, 1) == 0, place, turned)


def prepare_kernel(
    tiles_per_owner,
    chip_bits,
    place_ref,
    src_ref,
    count_ref,
    tile_ref,
    turned_ref,
    weight_ref,
    list_ref,
    held_ref,
    staged_ref,
    sum_ref,
    in_sems,
    out_sems,
):
    tile_max, tile_size, _ = tile_ref.shape
    dest_count = count_ref.shape[1]
    zero_tile = place_ref[2]
    my_row = place_ref[0]
    pieces = in_sems.shape[0]
    piece = tile_max // pieces
    spans = [pl.ds(index * piece, piece) for index in range(pieces)]
    copies_in = [
        pltpu.make_async_copy(tile_ref.at[span], held_ref.at[span], in_sems.at[index])
        for index, span in enumerate(spans)
    ]
    copies_out = [
        pltpu.make_async_copy(staged_ref.at[span], turned_ref.at[span], out_sems.at[index])
        for index, span in enumerate(spans)
    ]
    for copy in copies_in:
        copy.start()

    for half in range(2):
        base = half * FIELDS

        def one_dest(dest, carry, half=half, base=base):
            start, used = carry
            owner = lax.div(dest, tiles_per_owner)
            relative = lax.bitwise_xor(owner, my_row)
            count = count_ref[0, dest]
            mine = lax.bitwise_and(relative, 1) == half
            pairs = jnp.where(mine, lax.div(count + 1, 2), 0)
            chip = chip_place(relative, owner, chip_bits)
            out_row = (dest - owner * tiles_per_owner) * tile_size

            def one_pair(pair, carry):
                at = used + pair
                slot = start + 2 * pair
                next_slot = jnp.minimum(slot + 1, tile_max - 1)
                list_ref[base + SLOT, at] = slot
                list_ref[base + FIRST, at] = src_ref[0, slot] * tile_size
                list_ref[base + SECOND, at] = (
                    jnp.where(2 * pair + 1 < count, src_ref[0, next_slot], zero_tile) * tile_size
                )
                list_ref[base + CHIP, at] = chip
                list_ref[base + ROW, at] = out_row
                list_ref[base + GO_ON, at] = jnp.where(pair > 0, 1, 0)
                return carry

            lax.fori_loop(0, pairs, one_pair, 0)
            return start + count, used + pairs

        _, used = lax.fori_loop(0, dest_count, one_dest, (jnp.int32(0), jnp.int32(0)))
        turns = lax.div(used + UNROLL - 1, UNROLL)
        last_chip = list_ref[base + CHIP, used - 1]
        last_row = list_ref[base + ROW, used - 1]

        def one_pad(at, carry, base=base, last_chip=last_chip, last_row=last_row):
            list_ref[base + SLOT, at] = 0
            list_ref[base + FIRST, at] = zero_tile * tile_size
            list_ref[base + SECOND, at] = zero_tile * tile_size
            list_ref[base + CHIP, at] = last_chip
            list_ref[base + ROW, at] = last_row
            list_ref[base + GO_ON, at] = 1
            return carry

        lax.fori_loop(used, turns * UNROLL, one_pad, 0)
        list_ref[base + TURNS, 0] = turns

    group = min(8, piece)
    for index in range(pieces):
        copies_in[index].wait()

        def one_group(at, carry, index=index):
            for step in range(group):
                slot = index * piece + at * group + step
                tile = held_ref[slot]
                staged_ref[slot] = tile.T
                sum_ref[pl.ds(slot, 1), :] = jnp.sum(
                    tile.astype(jnp.float32), axis=0, keepdims=True
                )
            return carry

        lax.fori_loop(0, piece // group, one_group, 0)
        copies_out[index].start()

    sum_ref[tile_max:, :] = jnp.zeros((MOST, tile_size), jnp.float32)
    weight_ref[...] = jnp.zeros(weight_ref.shape, weight_ref.dtype)
    places = lax.broadcasted_iota(jnp.int32, (MOST, tile_size), 0)

    def weigh(owner, start):
        relative = lax.bitwise_xor(owner, my_row)
        chip = chip_place(relative, owner, chip_bits)
        for step in range(tiles_per_owner):
            count = count_ref[0, owner * tiles_per_owner + step]
            sums = jnp.where(places < count, sum_ref[pl.ds(start, MOST), :], 0.0)
            weight_ref[lax.bitwise_and(relative, 1), chip, step : step + 1, :] = jnp.sum(
                sums, axis=0, keepdims=True
            )
            start = start + count
        return start

    lax.fori_loop(0, dest_count // tiles_per_owner, weigh, jnp.int32(0))
    for copy in copies_out:
        copy.wait()


def prepare(place, tile_src, row_counts, tile_vals, row_size, tiles_per_owner):
    tile_max, tile_size, _ = tile_vals.shape
    capacity = pair_capacity(tile_max, row_counts.shape[1])
    chips = row_size // 2
    return pl.pallas_call(
        functools.partial(prepare_kernel, tiles_per_owner, chips.bit_length() - 1),
        out_shape=[
            jax.ShapeDtypeStruct(tile_vals.shape, tile_vals.dtype),
            jax.ShapeDtypeStruct((2, chips, EXTRA, tile_size), jnp.float32),
            jax.ShapeDtypeStruct((2 * FIELDS, capacity), jnp.int32),
        ],
        in_specs=smem(3) + hbm(1),
        out_specs=hbm(1) + vmem(1) + smem(1),
        scratch_shapes=[
            pltpu.VMEM(tile_vals.shape, tile_vals.dtype),
            pltpu.VMEM(tile_vals.shape, tile_vals.dtype),
            pltpu.VMEM((tile_max + MOST, tile_size), jnp.float32),
            pltpu.SemaphoreType.DMA((8,)),
            pltpu.SemaphoreType.DMA((8,)),
        ],
        compiler_params=pltpu.CompilerParams(vmem_limit_bytes=24 * 2**20),
        name="prepare",
    )(place, tile_src, row_counts, tile_vals)


def assemble_kernel(packed, blocks, *refs):
    block_refs = refs[:blocks]
    held_ref = refs[blocks + 1]
    staged_ref = refs[-1] if packed else held_ref
    col = lax.axis_index("col")
    rows, width = block_refs[0].shape

    def put(mask, ref):
        first = pl.multiple_of(lax.bitwise_xor(col, mask) * rows, rows)
        staged_ref[pl.ds(first, rows), :] = ref[...]

    for mask in range(blocks):
        put(mask, block_refs[mask])
    if packed:
        piece = width // blocks
        for group in range(blocks):
            lanes = slice(group * piece, (group + 1) * piece)
            held_ref[group * rows : (group + 1) * rows, :] = jnp.concatenate(
                [staged_ref[b * rows : (b + 1) * rows, lanes] for b in range(blocks)], axis=1
            )
        own_ref = refs[blocks + 2]
        own_ref[...] = held_ref[pl.ds(pl.multiple_of(col * rows, rows), rows), :]
    zeros = held_ref.shape[0] - blocks * rows
    held_ref[blocks * rows :, :] = jnp.zeros((zeros, width), held_ref.dtype)


def assemble(gathered, after, tile_size, packed):
    blocks = len(gathered)
    rows, width = gathered[0].shape
    out_shape = [jax.ShapeDtypeStruct((blocks * rows + tile_size, width), jnp.bfloat16)]
    scratch = []
    if packed:
        out_shape.append(jax.ShapeDtypeStruct((rows, width), jnp.bfloat16))
        scratch.append(pltpu.VMEM((blocks * rows, width), jnp.bfloat16))
    return pl.pallas_call(
        functools.partial(assemble_kernel, packed, blocks),
        out_shape=out_shape,
        in_specs=vmem(blocks) + anywhere(1),
        out_specs=vmem(len(out_shape)),
        scratch_shapes=scratch,
        compiler_params=pltpu.CompilerParams(vmem_limit_bytes=4 * 2**20),
        cost_estimate=pl.CostEstimate(flops=0, bytes_accessed=4 * 2**20, transcendentals=0),
        name="assemble",
    )(*gathered, after)


def product_kernel(half, rows, list_ref, turned_ref, held_ref, weight_ref, out_ref):
    tile_max, tile_size, _ = turned_ref.shape
    chips, out_rows, width = out_ref.shape
    base = half * FIELDS
    if out_rows > rows:
        out_ref[:, rows:, :] = weight_ref[half].astype(out_ref.dtype)

    def one_turn(turn, running):
        for step in range(UNROLL):
            at = turn * UNROLL + step
            slot = list_ref[base + SLOT, at]
            left = jnp.concatenate(
                [turned_ref[slot], turned_ref[jnp.minimum(slot + 1, tile_max - 1)]], axis=1
            )
            first = pl.multiple_of(list_ref[base + FIRST, at], tile_size)
            second = pl.multiple_of(list_ref[base + SECOND, at], tile_size)
            right = jnp.concatenate(
                [held_ref[pl.ds(first, tile_size), :], held_ref[pl.ds(second, tile_size), :]],
                axis=0,
            )
            term = jnp.dot(left, right, preferred_element_type=jnp.float32)
            running = running * list_ref[base + GO_ON, at].astype(jnp.float32) + term
            row = pl.multiple_of(list_ref[base + ROW, at], tile_size)
            out_ref[list_ref[base + CHIP, at], pl.ds(row, tile_size), :] = running.astype(
                out_ref.dtype
            )
        return running

    lax.fori_loop(
        0, list_ref[base + TURNS, 0], one_turn, jnp.zeros((tile_size, width), jnp.float32)
    )


def product(half, pairs, turned, held, weights, rows, chips, extra):
    return pl.pallas_call(
        functools.partial(product_kernel, half, rows),
        out_shape=jax.ShapeDtypeStruct((chips, rows + extra, held.shape[1]), jnp.bfloat16),
        in_specs=smem(1) + vmem(3),
        out_specs=vmem(1)[0],
        compiler_params=pltpu.CompilerParams(vmem_limit_bytes=4 * 2**20),
        cost_estimate=pl.CostEstimate(
            flops=600000000, bytes_accessed=6000000, transcendentals=0
        ),
        name="product",
    )(pairs, turned, held, weights)


def update_kernel(kept_ref, *refs):
    *arrived_refs, iterate_ref, restart_ref, scale_ref, out_ref = refs
    rows = out_ref.shape[0]
    summed = kept_ref[:rows, :]
    for ref in arrived_refs:
        summed = summed + ref[:rows, :].astype(jnp.float32)
    out_ref[...] = (
        scale_ref[...] * (summed + iterate_ref[...].astype(jnp.float32))
        + TELEPORT * restart_ref[...].astype(jnp.float32)
    ).astype(out_ref.dtype)


def update(kept, arrived, iterate, restart, scale):
    return pl.pallas_call(
        update_kernel,
        out_shape=jax.ShapeDtypeStruct(iterate.shape, iterate.dtype),
        in_specs=vmem(len(arrived) + 4),
        out_specs=vmem(1)[0],
        compiler_params=pltpu.CompilerParams(vmem_limit_bytes=4 * 2**20),
        cost_estimate=pl.CostEstimate(flops=0, bytes_accessed=1, transcendentals=0),
        name="update",
    )(kept, *arrived, iterate, restart, scale)


def exchange(block, axis, mask, size):
    return lax.ppermute(block, axis, [(i, i ^ mask) for i in range(size)])


def gather_line(block, size):
    return [block] + [exchange(block, "col", mask, size) for mask in range(1, size)]


def reduce_chips(state, chip_bits, row_size):
    arrived = None
    for step in range(chip_bits):
        if arrived is not None:
            state = state + arrived.astype(jnp.float32)
        cut = state.shape[0] // 2
        send = state[cut:].astype(jnp.bfloat16)
        state = state[:cut]
        bits = (chip_bits - step, 1 + step)
        arrived = lax.ppermute(
            send, "row", [(i, i ^ (1 << bits[i % 2])) for i in range(row_size)]
        )
    return state[0], arrived[0]


def on_device(features, tile_vals, tile_src, row_counts):
    row_size = lax.axis_size("row")
    blocks = lax.axis_size("col")
    my_row = lax.axis_index("row").astype(jnp.int32)
    my_col = lax.axis_index("col").astype(jnp.int32)
    tile_size = tile_vals.shape[1]
    dest_count = row_counts.shape[1]
    rows = features.shape[0] // blocks
    source_tiles = features.shape[0] // tile_size
    width = features.shape[1] * blocks // CHUNKS
    piece = features.shape[1] // CHUNKS
    tiles_per_owner = dest_count // row_size
    chips = row_size // 2
    place = jnp.stack([my_row, my_col, jnp.int32(source_tiles)])

    parts = features.reshape(blocks, rows, CHUNKS, piece).transpose(2, 1, 0, 3)
    parts = parts.reshape(CHUNKS, rows, blocks * piece)

    turned, weights, pairs = prepare(
        place, tile_src, row_counts, tile_vals, row_size, tiles_per_owner
    )

    gathered = [gather_line(parts[0], blocks), None]
    iterates = [None] * CHUNKS
    restarts = [None] * CHUNKS
    scale = None
    last = place
    for phase in range(ITERS * CHUNKS):
        chunk = phase % CHUNKS
        after = 1 - chunk
        first = phase < CHUNKS
        extra = EXTRA if phase == 0 else 0
        if phase > 0:
            iterates[after] = last = update(*pending)
        held, *own = assemble(gathered[chunk], last, tile_size, first)
        if first:
            iterates[chunk] = restarts[chunk] = own[0]
        if phase == 0:
            held, parts = lax.optimization_barrier((held, parts))
            gathered[after] = gather_line(parts[1], blocks)
        elif phase + 1 < ITERS * CHUNKS:
            gathered[after] = gather_line(iterates[after], blocks)
        sent = product(1, pairs, turned, held, weights, rows, chips, extra)
        other = exchange(sent, "row", 1, row_size)
        kept = product(0, pairs, turned, held, weights, rows, chips, extra)
        both = kept.astype(jnp.float32) + other.astype(jnp.float32)
        kept, arrived = reduce_chips(both, chips.bit_length() - 1, row_size)
        if phase == 0:
            weight_rows = slice(rows, rows + tiles_per_owner)
            total = 1.0 + kept[weight_rows] + arrived[weight_rows].astype(jnp.float32)
            scale = jnp.broadcast_to(
                ((1.0 - TELEPORT) / total).reshape(rows, 1), (rows, width)
            )
        pending = (kept, [arrived], iterates[chunk], restarts[chunk], scale)
    iterates[chunk] = update(*pending)
    out = jnp.stack(iterates).reshape(CHUNKS, rows, blocks, piece).transpose(1, 2, 0, 3)
    return out.reshape(rows, CHUNKS * width)


def solution(mesh):
    placed = (P("row", "col"), P("row", "col", None), P("row", "col"), P("row", "col"))
    return jax.shard_map(
        on_device, mesh=mesh, in_specs=placed, out_specs=P(("row", "col"), None), check_vma=False
    )
```

time: 142 us -> 134 us (0.944)
  starting transfers between devices: 55.2 us -> 43.9 us
  waiting for transfers between devices: 46 us -> 56.5 us
  local copies, waits for them, and re-layouts: 10.1 us -> 5.42 us
  Pallas kernels: 28.5 us -> 26.5 us
    ppermute x0 -> x12, waiting for transfers between devices: none -> 30.7 us  [reduce_chips(): lax.ppermute(send, 'row', [(i, i ^ 1 << bits[i % 2]) for i in range(row_s...]
    ppermute x48 -> x24, starting transfers between devices: 55.2 us -> 31.4 us  [exchange(): return lax.ppermute(block, axis, [(i, i ^ mask) for i in range(size)])]
    ppermute x48 -> x24, waiting for transfers between devices: 46 us -> 25.8 us  [exchange(): return lax.ppermute(block, axis, [(i, i ^ mask) for i in range(size)])]
    ppermute x0 -> x12, starting transfers between devices: none -> 12.5 us  [reduce_chips(): lax.ppermute(send, 'row', [(i, i ^ 1 << bits[i % 2]) for i in range(row_s...]
    unnamed x14 -> x10, local copies, waits for them, and re-layouts: 6.57 us -> 2.2 us
    pallas_call x6, Pallas kernels: 4.5 us -> 1.27 us  [assemble(): pl.pallas_call(functools.partial(assemble_kernel, packed, blocks), out_sh...]
  transfers between devices with their start and end apart: 48 -> 36, of which waited for: 23 -> 24; matrix products, arithmetic and copies ran while one was open for 2% -> 1% of each run, Pallas kernels for 10% -> 12%
where the time goes in v7:
time: 134 us
  waiting for transfers between devices  56.5 us (42%)
  starting transfers between devices  43.9 us (33%)
  Pallas kernels  26.5 us (20%)
  local copies, waits for them, and re-layouts  5.42 us (4%)
    ppermute x24, starting transfers between devices, exchange(): return lax.ppermute(block, axis, [(i, i ^ mask) for i in range(size)])  31.4 us
    ppermute x12, waiting for transfers between devices, reduce_chips(): lax.ppermute(send, 'row', [(i, i ^ 1 << bits[i % 2]) for i in range(row_s...  30.7 us
    ppermute x24, waiting for transfers between devices, exchange(): return lax.ppermute(block, axis, [(i, i ^ mask) for i in range(size)])  25.8 us
    pallas_call x12, Pallas kernels, product(): pl.pallas_call(functools.partial(product_kernel, half, rows), out_shape=j...  18.8 us
    ppermute x12, starting transfers between devices, reduce_chips(): lax.ppermute(send, 'row', [(i, i ^ 1 << bits[i % 2]) for i in range(row_s...  12.5 us
    pallas_call x1, Pallas kernels, prepare(): pl.pallas_call(functools.partial(prepare_kernel, tiles_per_owner, chips.b...  5.92 us
  transfers between devices with their start and end apart: 36, of which 24 were waited for; matrix products, arithmetic and copies ran while one was open for 1% of the time, Pallas kernels for 12%

profile of v7, /device:TPU:0, one launch (start us, length us, event | category | flops | bytes accessed | tf_op | source)
XLA Modules:
  0.0 134.0 jit_solution(12938303734334063397)
XLA Ops:
  1.4 3.1 %collective-permute-start = (bf16[512,128]{1,0:T(8,128)(2,1)S(1)}, bf16[512,128]{1,0:T(8,128)(2,1)S(1)}, u32[]{:S(2)}, u32[]{:S(2)}) collective-permute-start(bf16[512,128]{1,0:T(8,128)(2,1)S(1)} %copy.20.refs_0_), channel_id=1, source_target_pairs={{0,1},{1,0},{2,3},{3,2},{4,5},{5,4},{6,7},{7,6},{8,9},{9,8},{10,11... | collective-permute-start | bytes 393224 | tf_op jit(solution)/shard_map/ppermute | solution.py:324
  4.5 2.6 %collective-permute-start.1 = (bf16[512,128]{1,0:T(8,128)(2,1)S(1)}, bf16[512,128]{1,0:T(8,128)(2,1)S(1)}, u32[]{:S(2)}, u32[]{:S(2)}) collective-permute-start(bf16[512,128]{1,0:T(8,128)(2,1)S(1)} %copy.20.refs_0_), channel_id=1, source_target_pairs={{0,2},{1,3},{2,0},{3,1},{4,6},{5,7},{6,4},{7,5},{8,10},{9,11},{10,... | collective-permute-start | bytes 393224 | tf_op jit(solution)/shard_map/ppermute | solution.py:324
  7.2 2.2 %copy-done.2 = bf16[128,128,128]{2,1,0:T(8,128)(2,1)S(1)} copy-done((bf16[128,128,128]{2,1,0:T(8,128)(2,1)S(1)}, bf16[128,128,128]{2,1,0:T(8,128)(2,1)}, u32[]{:S(2)}) %copy-start.2) | copy-done | bytes 4194328
  9.4 5.9 %prepare.1 = (bf16[128,128,128]{2,1,0:T(8,128)(2,1)S(1)}, f32[2,4,16,128]{3,2,1,0:T(8,128)S(1)}, s32[14,72]{1,0:T(8,128)S(1)}) custom-call(s32[3]{0:T(128)S(1)} %pad_add_fusion.place_ref.refs_4_, s32[1,128]{1,0:T(1,128)S(1)} %copy-done.3, s32[1,32]{1,0:T(1,128)S(1)} %copy-done.4, bf16[128,128,128]{2,1,0:T(8,128)(2,1)S(1)} %copy-done.2), custom_call_target="tpu_custom_call" | custom-call | tf_op jit(solution)/shard_map/prepare/pallas_call | solution.py:185
  15.3 2.1 %collective-permute-done.1.refs_2_ = bf16[512,128]{1,0:T(8,128)(2,1)S(1)} collective-permute-done((bf16[512,128]{1,0:T(8,128)(2,1)S(1)}, bf16[512,128]{1,0:T(8,128)(2,1)S(1)}, u32[]{:S(2)}, u32[]{:S(2)}) %collective-permute-start.1) | collective-permute-done | bytes 131104 | tf_op jit(solution)/shard_map/ppermute | solution.py:324
  23.5 3.3 %collective-permute-start.10 = (bf16[512,128]{1,0:T(8,128)(2,1)S(1)}, bf16[512,128]{1,0:T(8,128)(2,1)S(1)}, u32[]{:S(2)}, u32[]{:S(2)}) collective-permute-start(bf16[512,128]{1,0:T(8,128)(2,1)S(1)} %slice_bitcast_fusion.6.refs_0_), channel_id=1, source_target_pairs={{0,2},{1,3},{2,0},{3,1},{4,6},{5,7},{6,4},{7,5},{8,10},{9,11},{10,... | collective-permute-start | bytes 393224 | tf_op jit(solution)/shard_map/ppermute | solution.py:324
  29.9 3.5 %collective-permute-done.5 = bf16[1,528,128]{2,1,0:T(8,128)(2,1)S(1)} collective-permute-done((bf16[1,528,128]{2,1,0:T(8,128)(2,1)S(1)}, bf16[1,528,128]{2,1,0:T(8,128)(2,1)S(1)}, u32[]{:S(2)}, u32[]{:S(2)}) %collective-permute-start.5) | collective-permute-done | bytes 135200 | tf_op jit(solution)/shard_map/ppermute | solution.py:340
  33.6 3.2 %collective-permute-done.10.refs_2_ = bf16[512,128]{1,0:T(8,128)(2,1)S(1)} collective-permute-done((bf16[512,128]{1,0:T(8,128)(2,1)S(1)}, bf16[512,128]{1,0:T(8,128)(2,1)S(1)}, u32[]{:S(2)}, u32[]{:S(2)}) %collective-permute-start.10) | collective-permute-done | bytes 131104 | tf_op jit(solution)/shard_map/ppermute | solution.py:324
  42.9 2.4 %collective-permute-start.6 = (bf16[512,128]{1,0:T(8,128)(2,1)S(1)}, bf16[512,128]{1,0:T(8,128)(2,1)S(1)}, u32[]{:S(2)}, u32[]{:S(2)}) collective-permute-start(bf16[512,128]{1,0:T(8,128)(2,1)S(1)} %update.6.refs_4_.refs_0_.refs_1_), channel_id=1, source_target_pairs={{0,1},{1,0},{2,3},{3,2},{4,5},{5,4},{6,7},{7,6},{8,9},{9,8},{10,11... | collective-permute-start | bytes 393224 | tf_op jit(solution)/shard_map/ppermute | solution.py:324
  49.0 3.8 %collective-permute-done.14 = bf16[1,512,128]{2,1,0:T(8,128)(2,1)S(1)} collective-permute-done((bf16[1,512,128]{2,1,0:T(8,128)(2,1)S(1)}, bf16[1,512,128]{2,1,0:T(8,128)(2,1)S(1)}, u32[]{:S(2)}, u32[]{:S(2)}) %collective-permute-start.14) | collective-permute-done | bytes 131104 | tf_op jit(solution)/shard_map/ppermute | solution.py:340
  52.9 4.5 %collective-permute-done.7.refs_2_ = bf16[512,128]{1,0:T(8,128)(2,1)S(1)} collective-permute-done((bf16[512,128]{1,0:T(8,128)(2,1)S(1)}, bf16[512,128]{1,0:T(8,128)(2,1)S(1)}, u32[]{:S(2)}, u32[]{:S(2)}) %collective-permute-start.7) | collective-permute-done | bytes 131104 | tf_op jit(solution)/shard_map/ppermute | solution.py:324
  61.8 3.0 %collective-permute-start.21 = (bf16[512,128]{1,0:T(8,128)(2,1)S(1)}, bf16[512,128]{1,0:T(8,128)(2,1)S(1)}, u32[]{:S(2)}, u32[]{:S(2)}) collective-permute-start(bf16[512,128]{1,0:T(8,128)(2,1)S(1)} %update.7.refs_4_.refs_0_.refs_1_), channel_id=1, source_target_pairs={{0,1},{1,0},{2,3},{3,2},{4,5},{5,4},{6,7},{7,6},{8,9},{9,8},{10,11... | collective-permute-start | bytes 393224 | tf_op jit(solution)/shard_map/ppermute | solution.py:324
  65.2 2.0 %collective-permute-start.23 = (bf16[512,128]{1,0:T(8,128)(2,1)S(1)}, bf16[512,128]{1,0:T(8,128)(2,1)S(1)}, u32[]{:S(2)}, u32[]{:S(2)}) collective-permute-start(bf16[512,128]{1,0:T(8,128)(2,1)S(1)} %update.7.refs_4_.refs_0_.refs_1_), channel_id=1, source_target_pairs={{0,3},{1,2},{2,1},{3,0},{4,7},{5,6},{6,5},{7,4},{8,11},{9,10},{10,... | collective-permute-start | bytes 393224 | tf_op jit(solution)/shard_map/ppermute | solution.py:324
  69.0 3.8 %collective-permute-done.17 = bf16[1,512,128]{2,1,0:T(8,128)(2,1)S(1)} collective-permute-done((bf16[1,512,128]{2,1,0:T(8,128)(2,1)S(1)}, bf16[1,512,128]{2,1,0:T(8,128)(2,1)S(1)}, u32[]{:S(2)}, u32[]{:S(2)}) %collective-permute-start.17) | collective-permute-done | bytes 131104 | tf_op jit(solution)/shard_map/ppermute | solution.py:340
  72.9 4.9 %collective-permute-done.22.refs_2_ = bf16[512,128]{1,0:T(8,128)(2,1)S(1)} collective-permute-done((bf16[512,128]{1,0:T(8,128)(2,1)S(1)}, bf16[512,128]{1,0:T(8,128)(2,1)S(1)}, u32[]{:S(2)}, u32[]{:S(2)}) %collective-permute-start.22) | collective-permute-done | bytes 131104 | tf_op jit(solution)/shard_map/ppermute | solution.py:324
  82.2 2.9 %collective-permute-start.18 = (bf16[512,128]{1,0:T(8,128)(2,1)S(1)}, bf16[512,128]{1,0:T(8,128)(2,1)S(1)}, u32[]{:S(2)}, u32[]{:S(2)}) collective-permute-start(bf16[512,128]{1,0:T(8,128)(2,1)S(1)} %update.8.refs_4_.refs_0_.refs_1_), channel_id=1, source_target_pairs={{0,1},{1,0},{2,3},{3,2},{4,5},{5,4},{6,7},{7,6},{8,9},{9,8},{10,11... | collective-permute-start | bytes 393224 | tf_op jit(solution)/shard_map/ppermute | solution.py:324
  89.0 4.1 %collective-permute-done.26 = bf16[1,512,128]{2,1,0:T(8,128)(2,1)S(1)} collective-permute-done((bf16[1,512,128]{2,1,0:T(8,128)(2,1)S(1)}, bf16[1,512,128]{2,1,0:T(8,128)(2,1)S(1)}, u32[]{:S(2)}, u32[]{:S(2)}) %collective-permute-start.26) | collective-permute-done | bytes 131104 | tf_op jit(solution)/shard_map/ppermute | solution.py:340
  93.2 4.4 %collective-permute-done.19.refs_2_ = bf16[512,128]{1,0:T(8,128)(2,1)S(1)} collective-permute-done((bf16[512,128]{1,0:T(8,128)(2,1)S(1)}, bf16[512,128]{1,0:T(8,128)(2,1)S(1)}, u32[]{:S(2)}, u32[]{:S(2)}) %collective-permute-start.19) | collective-permute-done | bytes 131104 | tf_op jit(solution)/shard_map/ppermute | solution.py:324
  101.7 2.9 %collective-permute-start.30 = (bf16[512,128]{1,0:T(8,128)(2,1)S(1)}, bf16[512,128]{1,0:T(8,128)(2,1)S(1)}, u32[]{:S(2)}, u32[]{:S(2)}) collective-permute-start(bf16[512,128]{1,0:T(8,128)(2,1)S(1)} %update.9.refs_4_.refs_0_.refs_1_), channel_id=1, source_target_pairs={{0,1},{1,0},{2,3},{3,2},{4,5},{5,4},{6,7},{7,6},{8,9},{9,8},{10,11... | collective-permute-start | bytes 393224 | tf_op jit(solution)/shard_map/ppermute | solution.py:324
  105.1 1.9 %collective-permute-start.32 = (bf16[512,128]{1,0:T(8,128)(2,1)S(1)}, bf16[512,128]{1,0:T(8,128)(2,1)S(1)}, u32[]{:S(2)}, u32[]{:S(2)}) collective-permute-start(bf16[512,128]{1,0:T(8,128)(2,1)S(1)} %update.9.refs_4_.refs_0_.refs_1_), channel_id=1, source_target_pairs={{0,3},{1,2},{2,1},{3,0},{4,7},{5,6},{6,5},{7,4},{8,11},{9,10},{10,... | collective-permute-start | bytes 393224 | tf_op jit(solution)/shard_map/ppermute | solution.py:324
  108.8 4.0 %collective-permute-done.29 = bf16[1,512,128]{2,1,0:T(8,128)(2,1)S(1)} collective-permute-done((bf16[1,512,128]{2,1,0:T(8,128)(2,1)S(1)}, bf16[1,512,128]{2,1,0:T(8,128)(2,1)S(1)}, u32[]{:S(2)}, u32[]{:S(2)}) %collective-permute-start.29) | collective-permute-done | bytes 131104 | tf_op jit(solution)/shard_map/ppermute | solution.py:340
  113.0 4.6 %collective-permute-done.31.refs_2_ = bf16[512,128]{1,0:T(8,128)(2,1)S(1)} collective-permute-done((bf16[512,128]{1,0:T(8,128)(2,1)S(1)}, bf16[512,128]{1,0:T(8,128)(2,1)S(1)}, u32[]{:S(2)}, u32[]{:S(2)}) %collective-permute-start.31) | collective-permute-done | bytes 131104 | tf_op jit(solution)/shard_map/ppermute | solution.py:324
  122.2 5.5 %collective-permute-done.34 = bf16[2,512,128]{2,1,0:T(8,128)(2,1)S(1)} collective-permute-done((bf16[2,512,128]{2,1,0:T(8,128)(2,1)S(1)}, bf16[2,512,128]{2,1,0:T(8,128)(2,1)S(1)}, u32[]{:S(2)}, u32[]{:S(2)}) %collective-permute-start.34) | collective-permute-done | bytes 262176 | tf_op jit(solution)/shard_map/ppermute | solution.py:340
  128.8 4.0 %collective-permute-done.35 = bf16[1,512,128]{2,1,0:T(8,128)(2,1)S(1)} collective-permute-done((bf16[1,512,128]{2,1,0:T(8,128)(2,1)S(1)}, bf16[1,512,128]{2,1,0:T(8,128)(2,1)S(1)}, u32[]{:S(2)}, u32[]{:S(2)}) %collective-permute-start.35) | collective-permute-done | bytes 131104 | tf_op jit(solution)/shard_map/ppermute | solution.py:340
  (128 shorter events, 48.9 us)
Async XLA Ops:
  1.4 13.9 %collective-permute-start = (bf16[512,128]{1,0:T(8,128)(2,1)S(1)}, bf16[512,128]{1,0:T(8,128)(2,1)S(1)}, u32[]{:S(2)}, u32[]{:S(2)}) collective-permute-start(bf16[512,128]{1,0:T(8,128)(2,1)S(1)} %copy.20.refs_0_), channel_id=1, source_target_pairs={{0,1},{1,0},{2,3},{3,2},{4,5},{5,4},{6,7},{7,6},{8,9},{9,8},{10,11... | collective-permute-start | bytes 393224 | tf_op jit(solution)/shard_map/ppermute | solution.py:324
  4.5 12.9 %collective-permute-start.1 = (bf16[512,128]{1,0:T(8,128)(2,1)S(1)}, bf16[512,128]{1,0:T(8,128)(2,1)S(1)}, u32[]{:S(2)}, u32[]{:S(2)}) collective-permute-start(bf16[512,128]{1,0:T(8,128)(2,1)S(1)} %copy.20.refs_0_), channel_id=1, source_target_pairs={{0,2},{1,3},{2,0},{3,1},{4,6},{5,7},{6,4},{7,5},{8,10},{9,11},{10,... | collective-permute-start | bytes 393224 | tf_op jit(solution)/shard_map/ppermute | solution.py:324
  7.1 10.3 %collective-permute-start.2 = (bf16[512,128]{1,0:T(8,128)(2,1)S(1)}, bf16[512,128]{1,0:T(8,128)(2,1)S(1)}, u32[]{:S(2)}, u32[]{:S(2)}) collective-permute-start(bf16[512,128]{1,0:T(8,128)(2,1)S(1)} %copy.20.refs_0_), channel_id=1, source_target_pairs={{0,3},{1,2},{2,1},{3,0},{4,7},{5,6},{6,5},{7,4},{8,11},{9,10},{10,... | collective-permute-start | bytes 393224 | tf_op jit(solution)/shard_map/ppermute | solution.py:324
  21.7 6.5 %collective-permute-start.4 = (bf16[2,528,128]{2,1,0:T(8,128)(2,1)S(1)}, bf16[2,528,128]{2,1,0:T(8,128)(2,1)S(1)}, u32[]{:S(2)}, u32[]{:S(2)}) collective-permute-start(bf16[2,528,128]{2,1,0:T(8,128)(2,1)S(1)} %slice.189), channel_id=1, source_target_pairs={{0,16},{4,12},{8,24},{12,4},{16,0},{20,28},{24,8},{28,20},{1,17},{... | collective-permute-start | bytes 811016 | tf_op jit(solution)/shard_map/ppermute | solution.py:340
  23.5 13.3 %collective-permute-start.10 = (bf16[512,128]{1,0:T(8,128)(2,1)S(1)}, bf16[512,128]{1,0:T(8,128)(2,1)S(1)}, u32[]{:S(2)}, u32[]{:S(2)}) collective-permute-start(bf16[512,128]{1,0:T(8,128)(2,1)S(1)} %slice_bitcast_fusion.6.refs_0_), channel_id=1, source_target_pairs={{0,2},{1,3},{2,0},{3,1},{4,6},{5,7},{6,4},{7,5},{8,10},{9,11},{10,... | collective-permute-start | bytes 393224 | tf_op jit(solution)/shard_map/ppermute | solution.py:324
  26.8 10.0 %collective-permute-start.11 = (bf16[512,128]{1,0:T(8,128)(2,1)S(1)}, bf16[512,128]{1,0:T(8,128)(2,1)S(1)}, u32[]{:S(2)}, u32[]{:S(2)}) collective-permute-start(bf16[512,128]{1,0:T(8,128)(2,1)S(1)} %slice_bitcast_fusion.6.refs_0_), channel_id=1, source_target_pairs={{0,3},{1,2},{2,1},{3,0},{4,7},{5,6},{6,5},{7,4},{8,11},{9,10},{10,... | collective-permute-start | bytes 393224 | tf_op jit(solution)/shard_map/ppermute | solution.py:324
  28.2 8.9 %collective-permute-start.9 = (bf16[512,128]{1,0:T(8,128)(2,1)S(1)}, bf16[512,128]{1,0:T(8,128)(2,1)S(1)}, u32[]{:S(2)}, u32[]{:S(2)}) collective-permute-start(bf16[512,128]{1,0:T(8,128)(2,1)S(1)} %slice_bitcast_fusion.6.refs_0_), channel_id=1, source_target_pairs={{0,1},{1,0},{2,3},{3,2},{4,5},{5,4},{6,7},{7,6},{8,9},{9,8},{10,11... | collective-permute-start | bytes 393224 | tf_op jit(solution)/shard_map/ppermute | solution.py:324
  41.3 6.4 %collective-permute-start.13 = (bf16[2,512,128]{2,1,0:T(8,128)(2,1)S(1)}, bf16[2,512,128]{2,1,0:T(8,128)(2,1)S(1)}, u32[]{:S(2)}, u32[]{:S(2)}) collective-permute-start(bf16[2,512,128]{2,1,0:T(8,128)(2,1)S(1)} %slice.194), channel_id=1, source_target_pairs={{0,16},{4,12},{8,24},{12,4},{16,0},{20,28},{24,8},{28,20},{1,17},{... | collective-permute-start | bytes 786440 | tf_op jit(solution)/shard_map/ppermute | solution.py:340
  42.9 10.0 %collective-permute-start.6 = (bf16[512,128]{1,0:T(8,128)(2,1)S(1)}, bf16[512,128]{1,0:T(8,128)(2,1)S(1)}, u32[]{:S(2)}, u32[]{:S(2)}) collective-permute-start(bf16[512,128]{1,0:T(8,128)(2,1)S(1)} %update.6.refs_4_.refs_0_.refs_1_), channel_id=1, source_target_pairs={{0,1},{1,0},{2,3},{3,2},{4,5},{5,4},{6,7},{7,6},{8,9},{9,8},{10,11... | collective-permute-start | bytes 393224 | tf_op jit(solution)/shard_map/ppermute | solution.py:324
  45.2 12.2 %collective-permute-start.7 = (bf16[512,128]{1,0:T(8,128)(2,1)S(1)}, bf16[512,128]{1,0:T(8,128)(2,1)S(1)}, u32[]{:S(2)}, u32[]{:S(2)}) collective-permute-start(bf16[512,128]{1,0:T(8,128)(2,1)S(1)} %update.6.refs_4_.refs_0_.refs_1_), channel_id=1, source_target_pairs={{0,2},{1,3},{2,0},{3,1},{4,6},{5,7},{6,4},{7,5},{8,10},{9,11},{10,... | collective-permute-start | bytes 393224 | tf_op jit(solution)/shard_map/ppermute | solution.py:324
  45.7 11.7 %collective-permute-start.8 = (bf16[512,128]{1,0:T(8,128)(2,1)S(1)}, bf16[512,128]{1,0:T(8,128)(2,1)S(1)}, u32[]{:S(2)}, u32[]{:S(2)}) collective-permute-start(bf16[512,128]{1,0:T(8,128)(2,1)S(1)} %update.6.refs_4_.refs_0_.refs_1_), channel_id=1, source_target_pairs={{0,3},{1,2},{2,1},{3,0},{4,7},{5,6},{6,5},{7,4},{8,11},{9,10},{10,... | collective-permute-start | bytes 393224 | tf_op jit(solution)/shard_map/ppermute | solution.py:324
  61.2 6.4 %collective-permute-start.16 = (bf16[2,512,128]{2,1,0:T(8,128)(2,1)S(1)}, bf16[2,512,128]{2,1,0:T(8,128)(2,1)S(1)}, u32[]{:S(2)}, u32[]{:S(2)}) collective-permute-start(bf16[2,512,128]{2,1,0:T(8,128)(2,1)S(1)} %slice.193), channel_id=1, source_target_pairs={{0,16},{4,12},{8,24},{12,4},{16,0},{20,28},{24,8},{28,20},{1,17},{... | collective-permute-start | bytes 786440 | tf_op jit(solution)/shard_map/ppermute | solution.py:340
  61.8 11.1 %collective-permute-start.21 = (bf16[512,128]{1,0:T(8,128)(2,1)S(1)}, bf16[512,128]{1,0:T(8,128)(2,1)S(1)}, u32[]{:S(2)}, u32[]{:S(2)}) collective-permute-start(bf16[512,128]{1,0:T(8,128)(2,1)S(1)} %update.7.refs_4_.refs_0_.refs_1_), channel_id=1, source_target_pairs={{0,1},{1,0},{2,3},{3,2},{4,5},{5,4},{6,7},{7,6},{8,9},{9,8},{10,11... | collective-permute-start | bytes 393224 | tf_op jit(solution)/shard_map/ppermute | solution.py:324
  64.8 12.9 %collective-permute-start.22 = (bf16[512,128]{1,0:T(8,128)(2,1)S(1)}, bf16[512,128]{1,0:T(8,128)(2,1)S(1)}, u32[]{:S(2)}, u32[]{:S(2)}) collective-permute-start(bf16[512,128]{1,0:T(8,128)(2,1)S(1)} %update.7.refs_4_.refs_0_.refs_1_), channel_id=1, source_target_pairs={{0,2},{1,3},{2,0},{3,1},{4,6},{5,7},{6,4},{7,5},{8,10},{9,11},{10,... | collective-permute-start | bytes 393224 | tf_op jit(solution)/shard_map/ppermute | solution.py:324
  65.2 12.6 %collective-permute-start.23 = (bf16[512,128]{1,0:T(8,128)(2,1)S(1)}, bf16[512,128]{1,0:T(8,128)(2,1)S(1)}, u32[]{:S(2)}, u32[]{:S(2)}) collective-permute-start(bf16[512,128]{1,0:T(8,128)(2,1)S(1)} %update.7.refs_4_.refs_0_.refs_1_), channel_id=1, source_target_pairs={{0,3},{1,2},{2,1},{3,0},{4,7},{5,6},{6,5},{7,4},{8,11},{9,10},{10,... | collective-permute-start | bytes 393224 | tf_op jit(solution)/shard_map/ppermute | solution.py:324
  81.5 6.4 %collective-permute-start.25 = (bf16[2,512,128]{2,1,0:T(8,128)(2,1)S(1)}, bf16[2,512,128]{2,1,0:T(8,128)(2,1)S(1)}, u32[]{:S(2)}, u32[]{:S(2)}) collective-permute-start(bf16[2,512,128]{2,1,0:T(8,128)(2,1)S(1)} %slice.192), channel_id=1, source_target_pairs={{0,16},{4,12},{8,24},{12,4},{16,0},{20,28},{24,8},{28,20},{1,17},{... | collective-permute-start | bytes 786440 | tf_op jit(solution)/shard_map/ppermute | solution.py:340
  82.2 10.9 %collective-permute-start.18 = (bf16[512,128]{1,0:T(8,128)(2,1)S(1)}, bf16[512,128]{1,0:T(8,128)(2,1)S(1)}, u32[]{:S(2)}, u32[]{:S(2)}) collective-permute-start(bf16[512,128]{1,0:T(8,128)(2,1)S(1)} %update.8.refs_4_.refs_0_.refs_1_), channel_id=1, source_target_pairs={{0,1},{1,0},{2,3},{3,2},{4,5},{5,4},{6,7},{7,6},{8,9},{9,8},{10,11... | collective-permute-start | bytes 393224 | tf_op jit(solution)/shard_map/ppermute | solution.py:324
  85.1 12.5 %collective-permute-start.19 = (bf16[512,128]{1,0:T(8,128)(2,1)S(1)}, bf16[512,128]{1,0:T(8,128)(2,1)S(1)}, u32[]{:S(2)}, u32[]{:S(2)}) collective-permute-start(bf16[512,128]{1,0:T(8,128)(2,1)S(1)} %update.8.refs_4_.refs_0_.refs_1_), channel_id=1, source_target_pairs={{0,2},{1,3},{2,0},{3,1},{4,6},{5,7},{6,4},{7,5},{8,10},{9,11},{10,... | collective-permute-start | bytes 393224 | tf_op jit(solution)/shard_map/ppermute | solution.py:324
  85.6 11.9 %collective-permute-start.20 = (bf16[512,128]{1,0:T(8,128)(2,1)S(1)}, bf16[512,128]{1,0:T(8,128)(2,1)S(1)}, u32[]{:S(2)}, u32[]{:S(2)}) collective-permute-start(bf16[512,128]{1,0:T(8,128)(2,1)S(1)} %update.8.refs_4_.refs_0_.refs_1_), channel_id=1, source_target_pairs={{0,3},{1,2},{2,1},{3,0},{4,7},{5,6},{6,5},{7,4},{8,11},{9,10},{10,... | collective-permute-start | bytes 393224 | tf_op jit(solution)/shard_map/ppermute | solution.py:324
  101.3 6.4 %collective-permute-start.28 = (bf16[2,512,128]{2,1,0:T(8,128)(2,1)S(1)}, bf16[2,512,128]{2,1,0:T(8,128)(2,1)S(1)}, u32[]{:S(2)}, u32[]{:S(2)}) collective-permute-start(bf16[2,512,128]{2,1,0:T(8,128)(2,1)S(1)} %slice.191), channel_id=1, source_target_pairs={{0,16},{4,12},{8,24},{12,4},{16,0},{20,28},{24,8},{28,20},{1,17},{... | collective-permute-start | bytes 786440 | tf_op jit(solution)/shard_map/ppermute | solution.py:340
  101.7 11.2 %collective-permute-start.30 = (bf16[512,128]{1,0:T(8,128)(2,1)S(1)}, bf16[512,128]{1,0:T(8,128)(2,1)S(1)}, u32[]{:S(2)}, u32[]{:S(2)}) collective-permute-start(bf16[512,128]{1,0:T(8,128)(2,1)S(1)} %update.9.refs_4_.refs_0_.refs_1_), channel_id=1, source_target_pairs={{0,1},{1,0},{2,3},{3,2},{4,5},{5,4},{6,7},{7,6},{8,9},{9,8},{10,11... | collective-permute-start | bytes 393224 | tf_op jit(solution)/shard_map/ppermute | solution.py:324
  104.6 12.9 %collective-permute-start.31 = (bf16[512,128]{1,0:T(8,128)(2,1)S(1)}, bf16[512,128]{1,0:T(8,128)(2,1)S(1)}, u32[]{:S(2)}, u32[]{:S(2)}) collective-permute-start(bf16[512,128]{1,0:T(8,128)(2,1)S(1)} %update.9.refs_4_.refs_0_.refs_1_), channel_id=1, source_target_pairs={{0,2},{1,3},{2,0},{3,1},{4,6},{5,7},{6,4},{7,5},{8,10},{9,11},{10,... | collective-permute-start | bytes 393224 | tf_op jit(solution)/shard_map/ppermute | solution.py:324
  105.1 12.5 %collective-permute-start.32 = (bf16[512,128]{1,0:T(8,128)(2,1)S(1)}, bf16[512,128]{1,0:T(8,128)(2,1)S(1)}, u32[]{:S(2)}, u32[]{:S(2)}) collective-permute-start(bf16[512,128]{1,0:T(8,128)(2,1)S(1)} %update.9.refs_4_.refs_0_.refs_1_), channel_id=1, source_target_pairs={{0,3},{1,2},{2,1},{3,0},{4,7},{5,6},{6,5},{7,4},{8,11},{9,10},{10,... | collective-permute-start | bytes 393224 | tf_op jit(solution)/shard_map/ppermute | solution.py:324
  121.3 6.4 %collective-permute-start.34 = (bf16[2,512,128]{2,1,0:T(8,128)(2,1)S(1)}, bf16[2,512,128]{2,1,0:T(8,128)(2,1)S(1)}, u32[]{:S(2)}, u32[]{:S(2)}) collective-permute-start(bf16[2,512,128]{2,1,0:T(8,128)(2,1)S(1)} %slice.190), channel_id=1, source_target_pairs={{0,16},{4,12},{8,24},{12,4},{16,0},{20,28},{24,8},{28,20},{1,17},{... | collective-permute-start | bytes 786440 | tf_op jit(solution)/shard_map/ppermute | solution.py:340
  (17 other events, 77.1 us)

commit v8 on v7

--- a/solution.py
+++ b/solution.py
@@ -46,7 +46,25 @@
     return -(-most // UNROLL) * UNROLL
 
 
-SLOT, FIRST, SECOND, CHIP, ROW, GO_ON, TURNS, FIELDS = range(8)
+def code_bits(tile_max, source_tiles, half_dests):
+    sizes = (tile_max, source_tiles + 1, source_tiles + 1, half_dests, 2)
+    widths = [(size - 1).bit_length() for size in sizes]
+    assert sum(widths) < 32
+    return [(sum(widths[at + 1 :]), (1 << width) - 1) for at, width in enumerate(widths)]
+
+
+def encode(fields, bits):
+    code = jnp.int32(0)
+    for field, (shift, _) in zip(fields, bits):
+        code = code + lax.shift_left(field, jnp.int32(shift))
+    return code
+
+
+def decode(code, bits):
+    return [
+        lax.bitwise_and(lax.shift_right_logical(code, jnp.int32(shift)), jnp.int32(mask))
+        for shift, mask in bits
+    ]
 
 
 def chip_place(relative, owner, chip_bits):
@@ -62,6 +80,7 @@
 def prepare_kernel(
     tiles_per_owner,
     chip_bits,
+    bits,
     place_ref,
     src_ref,
     count_ref,
@@ -93,52 +112,46 @@
     for copy in copies_in:
         copy.start()
 
+    rows_each = (list_ref.shape[0] - 2) // 2
+
     for half in range(2):
-        base = half * FIELDS
-
-        def one_dest(dest, carry, half=half, base=base):
-            start, used = carry
+
+        def put(at, fields, half=half):
+            row = lax.div(at, UNROLL)
+            list_ref[half * rows_each + row, at - row * UNROLL] = encode(fields, bits)
+
+        def one_dest(dest, carry, half=half, put=put):
+            start, used, _ = carry
             owner = lax.div(dest, tiles_per_owner)
             relative = lax.bitwise_xor(owner, my_row)
             count = count_ref[0, dest]
             mine = lax.bitwise_and(relative, 1) == half
             pairs = jnp.where(mine, lax.div(count + 1, 2), 0)
             chip = chip_place(relative, owner, chip_bits)
-            out_row = (dest - owner * tiles_per_owner) * tile_size
+            target = chip * tiles_per_owner + dest - owner * tiles_per_owner
 
             def one_pair(pair, carry):
-                at = used + pair
                 slot = start + 2 * pair
                 next_slot = jnp.minimum(slot + 1, tile_max - 1)
-                list_ref[base + SLOT, at] = slot
-                list_ref[base + FIRST, at] = src_ref[0, slot] * tile_size
-                list_ref[base + SECOND, at] = (
-                    jnp.where(2 * pair + 1 < count, src_ref[0, next_slot], zero_tile) * tile_size
-                )
-                list_ref[base + CHIP, at] = chip
-                list_ref[base + ROW, at] = out_row
-                list_ref[base + GO_ON, at] = jnp.where(pair > 0, 1, 0)
+                second = jnp.where(2 * pair + 1 < count, src_ref[0, next_slot], zero_tile)
+                go_on = jnp.where(pair > 0, 1, 0)
+                put(used + pair, (slot, src_ref[0, slot], second, target, go_on))
                 return carry
 
             lax.fori_loop(0, pairs, one_pair, 0)
-            return start + count, used + pairs
-
-        _, used = lax.fori_loop(0, dest_count, one_dest, (jnp.int32(0), jnp.int32(0)))
+            return start + count, used + pairs, jnp.where(mine, target, carry[2])
+
+        zero = jnp.int32(0)
+        _, used, last = lax.fori_loop(0, dest_count, one_dest, (zero, zero, zero))
         turns = lax.div(used + UNROLL - 1, UNROLL)
-        last_chip = list_ref[base + CHIP, used - 1]
-        last_row = list_ref[base + ROW, used - 1]
-
-        def one_pad(at, carry, base=base, last_chip=last_chip, last_row=last_row):
-            list_ref[base + SLOT, at] = 0
-            list_ref[base + FIRST, at] = zero_tile * tile_size
-            list_ref[base + SECOND, at] = zero_tile * tile_size
-            list_ref[base + CHIP, at] = last_chip
-            list_ref[base + ROW, at] = last_row
-            list_ref[base + GO_ON, at] = 1
+
+        def one_pad(at, carry, put=put, last=last):
+            put(at, (jnp.int32(0), zero_tile, zero_tile, last, jnp.int32(1)))
             return carry
 
         lax.fori_loop(used, turns * UNROLL, one_pad, 0)
-        list_ref[base + TURNS, 0] = turns
+        for column in range(UNROLL):
+            list_ref[2 * rows_each + half, column] = turns
 
     group = min(8, piece)
     for index in range(pieces):
@@ -178,16 +191,18 @@
         copy.wait()
 
 
-def prepare(place, tile_src, row_counts, tile_vals, row_size, tiles_per_owner):
+def prepare(place, tile_src, row_counts, tile_vals, row_size, tiles_per_owner, bits):
     tile_max, tile_size, _ = tile_vals.shape
     capacity = pair_capacity(tile_max, row_counts.shape[1])
     chips = row_size // 2
     return pl.pallas_call(
-        functools.partial(prepare_kernel, tiles_per_owner, chips.bit_length() - 1),
+        functools.partial(
+            prepare_kernel, tiles_per_owner, chips.bit_length() - 1, bits
+        ),
         out_shape=[
             jax.ShapeDtypeStruct(tile_vals.shape, tile_vals.dtype),
             jax.ShapeDtypeStruct((2, chips, EXTRA, tile_size), jnp.float32),
-            jax.ShapeDtypeStruct((2 * FIELDS, capacity), jnp.int32),
+            jax.ShapeDtypeStruct((2 * (capacity // UNROLL) + 2, UNROLL), jnp.int32),
         ],
         in_specs=smem(3) + hbm(1),
         out_specs=hbm(1) + vmem(1) + smem(1),
@@ -249,44 +264,49 @@
     )(*gathered, after)
 
 
-def product_kernel(half, rows, list_ref, turned_ref, held_ref, weight_ref, out_ref):
+def product_kernel(half, rows, bits, list_ref, turned_ref, held_ref, weight_ref, out_ref):
     tile_max, tile_size, _ = turned_ref.shape
     chips, out_rows, width = out_ref.shape
-    base = half * FIELDS
+    rows_each = (list_ref.shape[0] - 2) // 2
+    tiles = rows // tile_size
     if out_rows > rows:
         out_ref[:, rows:, :] = weight_ref[half].astype(out_ref.dtype)
 
-    def one_turn(turn, running):
+    def codes_of(row):
+        line = list_ref[pl.ds(row, 1), :]
+        return tuple(line[0, step] for step in range(UNROLL))
+
+    def one_turn(turn, carry):
+        running, codes = carry
+        later = codes_of(half * rows_each + turn + 1)
         for step in range(UNROLL):
-            at = turn * UNROLL + step
-            slot = list_ref[base + SLOT, at]
+            slot, first, second, target, go_on = decode(codes[step], bits)
             left = jnp.concatenate(
                 [turned_ref[slot], turned_ref[jnp.minimum(slot + 1, tile_max - 1)]], axis=1
             )
-            first = pl.multiple_of(list_ref[base + FIRST, at], tile_size)
-            second = pl.multiple_of(list_ref[base + SECOND, at], tile_size)
+            first = pl.multiple_of(first * tile_size, tile_size)
+            second = pl.multiple_of(second * tile_size, tile_size)
             right = jnp.concatenate(
                 [held_ref[pl.ds(first, tile_size), :], held_ref[pl.ds(second, tile_size), :]],
                 axis=0,
             )
             term = jnp.dot(left, right, preferred_element_type=jnp.float32)
-            running = running * list_ref[base + GO_ON, at].astype(jnp.float32) + term
-            row = pl.multiple_of(list_ref[base + ROW, at], tile_size)
-            out_ref[list_ref[base + CHIP, at], pl.ds(row, tile_size), :] = running.astype(
-                out_ref.dtype
-            )
-        return running
-
-    lax.fori_loop(
-        0, list_ref[base + TURNS, 0], one_turn, jnp.zeros((tile_size, width), jnp.float32)
-    )
-
-
-def product(half, pairs, turned, held, weights, rows, chips, extra):
+            running = running * go_on.astype(jnp.float32) + term
+            chip = lax.div(target, tiles)
+            row = pl.multiple_of((target - chip * tiles) * tile_size, tile_size)
+            out_ref[chip, pl.ds(row, tile_size), :] = running.astype(out_ref.dtype)
+        return running, later
+
+    turns = list_ref[2 * rows_each + half : 2 * rows_each + half + 1, :][0, 0]
+    zeros = jnp.zeros((tile_size, width), jnp.float32)
+    lax.fori_loop(0, turns, one_turn, (zeros, codes_of(half * rows_each)))
+
+
+def product(half, pairs, turned, held, weights, rows, chips, extra, bits):
     return pl.pallas_call(
-        functools.partial(product_kernel, half, rows),
+        functools.partial(product_kernel, half, rows, bits),
         out_shape=jax.ShapeDtypeStruct((chips, rows + extra, held.shape[1]), jnp.bfloat16),
-        in_specs=smem(1) + vmem(3),
+        in_specs=vmem(4),
         out_specs=vmem(1)[0],
         compiler_params=pltpu.CompilerParams(vmem_limit_bytes=4 * 2**20),
         cost_estimate=pl.CostEstimate(
@@ -356,13 +376,14 @@
     piece = features.shape[1] // CHUNKS
     tiles_per_owner = dest_count // row_size
     chips = row_size // 2
+    bits = code_bits(tile_vals.shape[0], source_tiles, dest_count // 2)
     place = jnp.stack([my_row, my_col, jnp.int32(source_tiles)])
 
     parts = features.reshape(blocks, rows, CHUNKS, piece).transpose(2, 1, 0, 3)
     parts = parts.reshape(CHUNKS, rows, blocks * piece)
 
     turned, weights, pairs = prepare(
-        place, tile_src, row_counts, tile_vals, row_size, tiles_per_owner
+        place, tile_src, row_counts, tile_vals, row_size, tiles_per_owner, bits
     )
 
     gathered = [gather_line(parts[0], blocks), None]
@@ -385,9 +406,9 @@
             gathered[after] = gather_line(parts[1], blocks)
         elif phase + 1 < ITERS * CHUNKS:
             gathered[after] = gather_line(iterates[after], blocks)
-        sent = product(1, pairs, turned, held, weights, rows, chips, extra)
+        sent = product(1, pairs, turned, held, weights, rows, chips, extra, bits)
         other = exchange(sent, "row", 1, row_size)
-        kept = product(0, pairs, turned, held, weights, rows, chips, extra)
+        kept = product(0, pairs, turned, held, weights, rows, chips, extra, bits)
         both = kept.astype(jnp.float32) + other.astype(jnp.float32)
         kept, arrived = reduce_chips(both, chips.bit_length() - 1, row_size)
         if phase == 0:

time: 134 us -> 130 us (0.970)
  Pallas kernels: 26.5 us -> 22.1 us
  starting transfers between devices: 43.9 us -> 47.2 us
  waiting for transfers between devices: 56.5 us -> 53.8 us
    ppermute x12, starting transfers between devices: 12.5 us -> 17.6 us  [reduce_chips(): lax.ppermute(send, 'row', [(i, i ^ 1 << bits[i % 2]) for i in range(row_s...]
    pallas_call x12, Pallas kernels: 18.8 us -> 14 us  [product(): pl.pallas_call(functools.partial(product_kernel, half, rows, bits), out_s...]
    ppermute x12, waiting for transfers between devices: 30.7 us -> 27.8 us  [reduce_chips(): lax.ppermute(send, 'row', [(i, i ^ 1 << bits[i % 2]) for i in range(row_s...]
    ppermute x24, starting transfers between devices: 31.4 us -> 29.6 us  [exchange(): return lax.ppermute(block, axis, [(i, i ^ mask) for i in range(size)])]
  transfers between devices with their start and end apart: 36 -> 36, of which waited for: 24 -> 23; matrix products, arithmetic and copies ran while one was open for 1% -> 1% of each run, Pallas kernels for 12% -> 11%
where the time goes in v8:
time: 130 us
  waiting for transfers between devices  53.8 us (41%)
  starting transfers between devices  47.2 us (36%)
  Pallas kernels  22.1 us (17%)
  local copies, waits for them, and re-layouts  5.42 us (4%)
    ppermute x24, starting transfers between devices, exchange(): return lax.ppermute(block, axis, [(i, i ^ mask) for i in range(size)])  29.6 us
    ppermute x12, waiting for transfers between devices, reduce_chips(): lax.ppermute(send, 'row', [(i, i ^ 1 << bits[i % 2]) for i in range(row_s...  27.8 us
    ppermute x24, waiting for transfers between devices, exchange(): return lax.ppermute(block, axis, [(i, i ^ mask) for i in range(size)])  26.1 us
    ppermute x12, starting transfers between devices, reduce_chips(): lax.ppermute(send, 'row', [(i, i ^ 1 << bits[i % 2]) for i in range(row_s...  17.6 us
    pallas_call x12, Pallas kernels, product(): pl.pallas_call(functools.partial(product_kernel, half, rows, bits), out_s...  14 us
    pallas_call x1, Pallas kernels, prepare(): pl.pallas_call(functools.partial(prepare_kernel, tiles_per_owner, chips.b...  6.35 us
  transfers between devices with their start and end apart: 36, of which 23 were waited for; matrix products, arithmetic and copies ran while one was open for 1% of the time, Pallas kernels for 11%

profile of v8, /device:TPU:0, one launch (start us, length us, event | category | flops | bytes accessed | tf_op | source)
XLA Modules:
  0.0 130.2 jit_solution(10684798754946259772)
XLA Ops:
  1.4 3.1 %collective-permute-start = (bf16[512,128]{1,0:T(8,128)(2,1)S(1)}, bf16[512,128]{1,0:T(8,128)(2,1)S(1)}, u32[]{:S(2)}, u32[]{:S(2)}) collective-permute-start(bf16[512,128]{1,0:T(8,128)(2,1)S(1)} %copy.20.refs_0_), channel_id=1, source_target_pairs={{0,1},{1,0},{2,3},{3,2},{4,5},{5,4},{6,7},{7,6},{8,9},{9,8},{10,11... | collective-permute-start | bytes 393224 | tf_op jit(solution)/shard_map/ppermute | solution.py:344
  4.5 2.6 %collective-permute-start.1 = (bf16[512,128]{1,0:T(8,128)(2,1)S(1)}, bf16[512,128]{1,0:T(8,128)(2,1)S(1)}, u32[]{:S(2)}, u32[]{:S(2)}) collective-permute-start(bf16[512,128]{1,0:T(8,128)(2,1)S(1)} %copy.20.refs_0_), channel_id=1, source_target_pairs={{0,2},{1,3},{2,0},{3,1},{4,6},{5,7},{6,4},{7,5},{8,10},{9,11},{10,... | collective-permute-start | bytes 393224 | tf_op jit(solution)/shard_map/ppermute | solution.py:344
  9.4 6.4 %prepare.1 = (bf16[128,128,128]{2,1,0:T(8,128)(2,1)S(1)}, f32[2,4,16,128]{3,2,1,0:T(8,128)S(1)}, s32[20,8]{1,0:T(8,128)S(1)}) custom-call(s32[3]{0:T(128)S(1)} %pad_add_fusion.place_ref.refs_4_, s32[1,128]{1,0:T(1,128)S(1)} %copy-done.3, s32[1,32]{1,0:T(1,128)S(1)} %copy-done.4, bf16[128,128,128]{2,1,0:T(8,128)(2,1)S(1)} %copy-done.2), custom_call_target="tpu_custom_call" | custom-call | tf_op jit(solution)/shard_map/prepare/pallas_call | solution.py:198
  23.2 2.7 %collective-permute-start.10 = (bf16[512,128]{1,0:T(8,128)(2,1)S(1)}, bf16[512,128]{1,0:T(8,128)(2,1)S(1)}, u32[]{:S(2)}, u32[]{:S(2)}) collective-permute-start(bf16[512,128]{1,0:T(8,128)(2,1)S(1)} %slice_bitcast_fusion.6.refs_0_), channel_id=1, source_target_pairs={{0,2},{1,3},{2,0},{3,1},{4,6},{5,7},{6,4},{7,5},{8,10},{9,11},{10,... | collective-permute-start | bytes 393224 | tf_op jit(solution)/shard_map/ppermute | solution.py:344
  29.6 3.2 %collective-permute-done.5 = bf16[1,528,128]{2,1,0:T(8,128)(2,1)S(1)} collective-permute-done((bf16[1,528,128]{2,1,0:T(8,128)(2,1)S(1)}, bf16[1,528,128]{2,1,0:T(8,128)(2,1)S(1)}, u32[]{:S(2)}, u32[]{:S(2)}) %collective-permute-start.5) | collective-permute-done | bytes 135200 | tf_op jit(solution)/shard_map/ppermute | solution.py:360
  33.1 3.2 %collective-permute-done.10.refs_2_ = bf16[512,128]{1,0:T(8,128)(2,1)S(1)} collective-permute-done((bf16[512,128]{1,0:T(8,128)(2,1)S(1)}, bf16[512,128]{1,0:T(8,128)(2,1)S(1)}, u32[]{:S(2)}, u32[]{:S(2)}) %collective-permute-start.10) | collective-permute-done | bytes 131104 | tf_op jit(solution)/shard_map/ppermute | solution.py:344
  40.2 2.3 %collective-permute-start.13 = (bf16[2,512,128]{2,1,0:T(8,128)(2,1)S(1)}, bf16[2,512,128]{2,1,0:T(8,128)(2,1)S(1)}, u32[]{:S(2)}, u32[]{:S(2)}) collective-permute-start(bf16[2,512,128]{2,1,0:T(8,128)(2,1)S(1)} %slice.194), channel_id=1, source_target_pairs={{0,16},{4,12},{8,24},{12,4},{16,0},{20,28},{24,8},{28,20},{1,17},{... | collective-permute-start | bytes 786440 | tf_op jit(solution)/shard_map/ppermute | solution.py:360
  44.3 2.6 %collective-permute-start.8 = (bf16[512,128]{1,0:T(8,128)(2,1)S(1)}, bf16[512,128]{1,0:T(8,128)(2,1)S(1)}, u32[]{:S(2)}, u32[]{:S(2)}) collective-permute-start(bf16[512,128]{1,0:T(8,128)(2,1)S(1)} %update.6.refs_4_.refs_0_.refs_1_), channel_id=1, source_target_pairs={{0,3},{1,2},{2,1},{3,0},{4,7},{5,6},{6,5},{7,4},{8,11},{9,10},{10,... | collective-permute-start | bytes 393224 | tf_op jit(solution)/shard_map/ppermute | solution.py:344
  47.6 4.4 %collective-permute-done.14 = bf16[1,512,128]{2,1,0:T(8,128)(2,1)S(1)} collective-permute-done((bf16[1,512,128]{2,1,0:T(8,128)(2,1)S(1)}, bf16[1,512,128]{2,1,0:T(8,128)(2,1)S(1)}, u32[]{:S(2)}, u32[]{:S(2)}) %collective-permute-start.14) | collective-permute-done | bytes 131104 | tf_op jit(solution)/shard_map/ppermute | solution.py:360
  52.1 3.5 %collective-permute-done.7.refs_2_ = bf16[512,128]{1,0:T(8,128)(2,1)S(1)} collective-permute-done((bf16[512,128]{1,0:T(8,128)(2,1)S(1)}, bf16[512,128]{1,0:T(8,128)(2,1)S(1)}, u32[]{:S(2)}, u32[]{:S(2)}) %collective-permute-start.7) | collective-permute-done | bytes 131104 | tf_op jit(solution)/shard_map/ppermute | solution.py:344
  60.4 2.6 %collective-permute-start.21 = (bf16[512,128]{1,0:T(8,128)(2,1)S(1)}, bf16[512,128]{1,0:T(8,128)(2,1)S(1)}, u32[]{:S(2)}, u32[]{:S(2)}) collective-permute-start(bf16[512,128]{1,0:T(8,128)(2,1)S(1)} %update.7.refs_4_.refs_0_.refs_1_), channel_id=1, source_target_pairs={{0,1},{1,0},{2,3},{3,2},{4,5},{5,4},{6,7},{7,6},{8,9},{9,8},{10,11... | collective-permute-start | bytes 393224 | tf_op jit(solution)/shard_map/ppermute | solution.py:344
  63.1 2.3 %collective-permute-start.23 = (bf16[512,128]{1,0:T(8,128)(2,1)S(1)}, bf16[512,128]{1,0:T(8,128)(2,1)S(1)}, u32[]{:S(2)}, u32[]{:S(2)}) collective-permute-start(bf16[512,128]{1,0:T(8,128)(2,1)S(1)} %update.7.refs_4_.refs_0_.refs_1_), channel_id=1, source_target_pairs={{0,3},{1,2},{2,1},{3,0},{4,7},{5,6},{6,5},{7,4},{8,11},{9,10},{10,... | collective-permute-start | bytes 393224 | tf_op jit(solution)/shard_map/ppermute | solution.py:344
  67.1 3.4 %collective-permute-done.17 = bf16[1,512,128]{2,1,0:T(8,128)(2,1)S(1)} collective-permute-done((bf16[1,512,128]{2,1,0:T(8,128)(2,1)S(1)}, bf16[1,512,128]{2,1,0:T(8,128)(2,1)S(1)}, u32[]{:S(2)}, u32[]{:S(2)}) %collective-permute-start.17) | collective-permute-done | bytes 131104 | tf_op jit(solution)/shard_map/ppermute | solution.py:360
  70.6 5.1 %collective-permute-done.22.refs_2_ = bf16[512,128]{1,0:T(8,128)(2,1)S(1)} collective-permute-done((bf16[512,128]{1,0:T(8,128)(2,1)S(1)}, bf16[512,128]{1,0:T(8,128)(2,1)S(1)}, u32[]{:S(2)}, u32[]{:S(2)}) %collective-permute-start.22) | collective-permute-done | bytes 131104 | tf_op jit(solution)/shard_map/ppermute | solution.py:344
  80.2 2.6 %collective-permute-start.18 = (bf16[512,128]{1,0:T(8,128)(2,1)S(1)}, bf16[512,128]{1,0:T(8,128)(2,1)S(1)}, u32[]{:S(2)}, u32[]{:S(2)}) collective-permute-start(bf16[512,128]{1,0:T(8,128)(2,1)S(1)} %update.8.refs_4_.refs_0_.refs_1_), channel_id=1, source_target_pairs={{0,1},{1,0},{2,3},{3,2},{4,5},{5,4},{6,7},{7,6},{8,9},{9,8},{10,11... | collective-permute-start | bytes 393224 | tf_op jit(solution)/shard_map/ppermute | solution.py:344
  82.8 2.4 %collective-permute-start.20 = (bf16[512,128]{1,0:T(8,128)(2,1)S(1)}, bf16[512,128]{1,0:T(8,128)(2,1)S(1)}, u32[]{:S(2)}, u32[]{:S(2)}) collective-permute-start(bf16[512,128]{1,0:T(8,128)(2,1)S(1)} %update.8.refs_4_.refs_0_.refs_1_), channel_id=1, source_target_pairs={{0,3},{1,2},{2,1},{3,0},{4,7},{5,6},{6,5},{7,4},{8,11},{9,10},{10,... | collective-permute-start | bytes 393224 | tf_op jit(solution)/shard_map/ppermute | solution.py:344
  86.3 4.1 %collective-permute-done.26 = bf16[1,512,128]{2,1,0:T(8,128)(2,1)S(1)} collective-permute-done((bf16[1,512,128]{2,1,0:T(8,128)(2,1)S(1)}, bf16[1,512,128]{2,1,0:T(8,128)(2,1)S(1)}, u32[]{:S(2)}, u32[]{:S(2)}) %collective-permute-start.26) | collective-permute-done | bytes 131104 | tf_op jit(solution)/shard_map/ppermute | solution.py:360
  90.6 4.0 %collective-permute-done.19.refs_2_ = bf16[512,128]{1,0:T(8,128)(2,1)S(1)} collective-permute-done((bf16[512,128]{1,0:T(8,128)(2,1)S(1)}, bf16[512,128]{1,0:T(8,128)(2,1)S(1)}, u32[]{:S(2)}, u32[]{:S(2)}) %collective-permute-start.19) | collective-permute-done | bytes 131104 | tf_op jit(solution)/shard_map/ppermute | solution.py:344
  99.1 2.7 %collective-permute-start.30 = (bf16[512,128]{1,0:T(8,128)(2,1)S(1)}, bf16[512,128]{1,0:T(8,128)(2,1)S(1)}, u32[]{:S(2)}, u32[]{:S(2)}) collective-permute-start(bf16[512,128]{1,0:T(8,128)(2,1)S(1)} %update.9.refs_4_.refs_0_.refs_1_), channel_id=1, source_target_pairs={{0,1},{1,0},{2,3},{3,2},{4,5},{5,4},{6,7},{7,6},{8,9},{9,8},{10,11... | collective-permute-start | bytes 393224 | tf_op jit(solution)/shard_map/ppermute | solution.py:344
  101.8 2.3 %collective-permute-start.32 = (bf16[512,128]{1,0:T(8,128)(2,1)S(1)}, bf16[512,128]{1,0:T(8,128)(2,1)S(1)}, u32[]{:S(2)}, u32[]{:S(2)}) collective-permute-start(bf16[512,128]{1,0:T(8,128)(2,1)S(1)} %update.9.refs_4_.refs_0_.refs_1_), channel_id=1, source_target_pairs={{0,3},{1,2},{2,1},{3,0},{4,7},{5,6},{6,5},{7,4},{8,11},{9,10},{10,... | collective-permute-start | bytes 393224 | tf_op jit(solution)/shard_map/ppermute | solution.py:344
  106.2 3.2 %collective-permute-done.29 = bf16[1,512,128]{2,1,0:T(8,128)(2,1)S(1)} collective-permute-done((bf16[1,512,128]{2,1,0:T(8,128)(2,1)S(1)}, bf16[1,512,128]{2,1,0:T(8,128)(2,1)S(1)}, u32[]{:S(2)}, u32[]{:S(2)}) %collective-permute-start.29) | collective-permute-done | bytes 131104 | tf_op jit(solution)/shard_map/ppermute | solution.py:360
  109.4 4.9 %collective-permute-done.31.refs_2_ = bf16[512,128]{1,0:T(8,128)(2,1)S(1)} collective-permute-done((bf16[512,128]{1,0:T(8,128)(2,1)S(1)}, bf16[512,128]{1,0:T(8,128)(2,1)S(1)}, u32[]{:S(2)}, u32[]{:S(2)}) %collective-permute-start.31) | collective-permute-done | bytes 131104 | tf_op jit(solution)/shard_map/ppermute | solution.py:344
  119.0 4.9 %collective-permute-done.34 = bf16[2,512,128]{2,1,0:T(8,128)(2,1)S(1)} collective-permute-done((bf16[2,512,128]{2,1,0:T(8,128)(2,1)S(1)}, bf16[2,512,128]{2,1,0:T(8,128)(2,1)S(1)}, u32[]{:S(2)}, u32[]{:S(2)}) %collective-permute-start.34) | collective-permute-done | bytes 262176 | tf_op jit(solution)/shard_map/ppermute | solution.py:360
  125.2 3.9 %collective-permute-done.35 = bf16[1,512,128]{2,1,0:T(8,128)(2,1)S(1)} collective-permute-done((bf16[1,512,128]{2,1,0:T(8,128)(2,1)S(1)}, bf16[1,512,128]{2,1,0:T(8,128)(2,1)S(1)}, u32[]{:S(2)}, u32[]{:S(2)}) %collective-permute-start.35) | collective-permute-done | bytes 131104 | tf_op jit(solution)/shard_map/ppermute | solution.py:360
  (128 shorter events, 47.1 us)
Async XLA Ops:
  1.4 14.4 %collective-permute-start = (bf16[512,128]{1,0:T(8,128)(2,1)S(1)}, bf16[512,128]{1,0:T(8,128)(2,1)S(1)}, u32[]{:S(2)}, u32[]{:S(2)}) collective-permute-start(bf16[512,128]{1,0:T(8,128)(2,1)S(1)} %copy.20.refs_0_), channel_id=1, source_target_pairs={{0,1},{1,0},{2,3},{3,2},{4,5},{5,4},{6,7},{7,6},{8,9},{9,8},{10,11... | collective-permute-start | bytes 393224 | tf_op jit(solution)/shard_map/ppermute | solution.py:344
  4.5 12.9 %collective-permute-start.1 = (bf16[512,128]{1,0:T(8,128)(2,1)S(1)}, bf16[512,128]{1,0:T(8,128)(2,1)S(1)}, u32[]{:S(2)}, u32[]{:S(2)}) collective-permute-start(bf16[512,128]{1,0:T(8,128)(2,1)S(1)} %copy.20.refs_0_), channel_id=1, source_target_pairs={{0,2},{1,3},{2,0},{3,1},{4,6},{5,7},{6,4},{7,5},{8,10},{9,11},{10,... | collective-permute-start | bytes 393224 | tf_op jit(solution)/shard_map/ppermute | solution.py:344
  7.1 10.3 %collective-permute-start.2 = (bf16[512,128]{1,0:T(8,128)(2,1)S(1)}, bf16[512,128]{1,0:T(8,128)(2,1)S(1)}, u32[]{:S(2)}, u32[]{:S(2)}) collective-permute-start(bf16[512,128]{1,0:T(8,128)(2,1)S(1)} %copy.20.refs_0_), channel_id=1, source_target_pairs={{0,3},{1,2},{2,1},{3,0},{4,7},{5,6},{6,5},{7,4},{8,11},{9,10},{10,... | collective-permute-start | bytes 393224 | tf_op jit(solution)/shard_map/ppermute | solution.py:344
  21.1 6.5 %collective-permute-start.4 = (bf16[2,528,128]{2,1,0:T(8,128)(2,1)S(1)}, bf16[2,528,128]{2,1,0:T(8,128)(2,1)S(1)}, u32[]{:S(2)}, u32[]{:S(2)}) collective-permute-start(bf16[2,528,128]{2,1,0:T(8,128)(2,1)S(1)} %slice.189), channel_id=1, source_target_pairs={{0,16},{4,12},{8,24},{12,4},{16,0},{20,28},{24,8},{28,20},{1,17},{... | collective-permute-start | bytes 811016 | tf_op jit(solution)/shard_map/ppermute | solution.py:360
  23.2 13.0 %collective-permute-start.10 = (bf16[512,128]{1,0:T(8,128)(2,1)S(1)}, bf16[512,128]{1,0:T(8,128)(2,1)S(1)}, u32[]{:S(2)}, u32[]{:S(2)}) collective-permute-start(bf16[512,128]{1,0:T(8,128)(2,1)S(1)} %slice_bitcast_fusion.6.refs_0_), channel_id=1, source_target_pairs={{0,2},{1,3},{2,0},{3,1},{4,6},{5,7},{6,4},{7,5},{8,10},{9,11},{10,... | collective-permute-start | bytes 393224 | tf_op jit(solution)/shard_map/ppermute | solution.py:344
  26.0 10.3 %collective-permute-start.11 = (bf16[512,128]{1,0:T(8,128)(2,1)S(1)}, bf16[512,128]{1,0:T(8,128)(2,1)S(1)}, u32[]{:S(2)}, u32[]{:S(2)}) collective-permute-start(bf16[512,128]{1,0:T(8,128)(2,1)S(1)} %slice_bitcast_fusion.6.refs_0_), channel_id=1, source_target_pairs={{0,3},{1,2},{2,1},{3,0},{4,7},{5,6},{6,5},{7,4},{8,11},{9,10},{10,... | collective-permute-start | bytes 393224 | tf_op jit(solution)/shard_map/ppermute | solution.py:344
  27.3 9.2 %collective-permute-start.9 = (bf16[512,128]{1,0:T(8,128)(2,1)S(1)}, bf16[512,128]{1,0:T(8,128)(2,1)S(1)}, u32[]{:S(2)}, u32[]{:S(2)}) collective-permute-start(bf16[512,128]{1,0:T(8,128)(2,1)S(1)} %slice_bitcast_fusion.6.refs_0_), channel_id=1, source_target_pairs={{0,1},{1,0},{2,3},{3,2},{4,5},{5,4},{6,7},{7,6},{8,9},{9,8},{10,11... | collective-permute-start | bytes 393224 | tf_op jit(solution)/shard_map/ppermute | solution.py:344
  40.2 6.7 %collective-permute-start.13 = (bf16[2,512,128]{2,1,0:T(8,128)(2,1)S(1)}, bf16[2,512,128]{2,1,0:T(8,128)(2,1)S(1)}, u32[]{:S(2)}, u32[]{:S(2)}) collective-permute-start(bf16[2,512,128]{2,1,0:T(8,128)(2,1)S(1)} %slice.194), channel_id=1, source_target_pairs={{0,16},{4,12},{8,24},{12,4},{16,0},{20,28},{24,8},{28,20},{1,17},{... | collective-permute-start | bytes 786440 | tf_op jit(solution)/shard_map/ppermute | solution.py:360
  42.5 9.6 %collective-permute-start.6 = (bf16[512,128]{1,0:T(8,128)(2,1)S(1)}, bf16[512,128]{1,0:T(8,128)(2,1)S(1)}, u32[]{:S(2)}, u32[]{:S(2)}) collective-permute-start(bf16[512,128]{1,0:T(8,128)(2,1)S(1)} %update.6.refs_4_.refs_0_.refs_1_), channel_id=1, source_target_pairs={{0,1},{1,0},{2,3},{3,2},{4,5},{5,4},{6,7},{7,6},{8,9},{9,8},{10,11... | collective-permute-start | bytes 393224 | tf_op jit(solution)/shard_map/ppermute | solution.py:344
  43.8 11.8 %collective-permute-start.7 = (bf16[512,128]{1,0:T(8,128)(2,1)S(1)}, bf16[512,128]{1,0:T(8,128)(2,1)S(1)}, u32[]{:S(2)}, u32[]{:S(2)}) collective-permute-start(bf16[512,128]{1,0:T(8,128)(2,1)S(1)} %update.6.refs_4_.refs_0_.refs_1_), channel_id=1, source_target_pairs={{0,2},{1,3},{2,0},{3,1},{4,6},{5,7},{6,4},{7,5},{8,10},{9,11},{10,... | collective-permute-start | bytes 393224 | tf_op jit(solution)/shard_map/ppermute | solution.py:344
  44.3 11.3 %collective-permute-start.8 = (bf16[512,128]{1,0:T(8,128)(2,1)S(1)}, bf16[512,128]{1,0:T(8,128)(2,1)S(1)}, u32[]{:S(2)}, u32[]{:S(2)}) collective-permute-start(bf16[512,128]{1,0:T(8,128)(2,1)S(1)} %update.6.refs_4_.refs_0_.refs_1_), channel_id=1, source_target_pairs={{0,3},{1,2},{2,1},{3,0},{4,7},{5,6},{6,5},{7,4},{8,11},{9,10},{10,... | collective-permute-start | bytes 393224 | tf_op jit(solution)/shard_map/ppermute | solution.py:344
  58.8 6.6 %collective-permute-start.16 = (bf16[2,512,128]{2,1,0:T(8,128)(2,1)S(1)}, bf16[2,512,128]{2,1,0:T(8,128)(2,1)S(1)}, u32[]{:S(2)}, u32[]{:S(2)}) collective-permute-start(bf16[2,512,128]{2,1,0:T(8,128)(2,1)S(1)} %slice.193), channel_id=1, source_target_pairs={{0,16},{4,12},{8,24},{12,4},{16,0},{20,28},{24,8},{28,20},{1,17},{... | collective-permute-start | bytes 786440 | tf_op jit(solution)/shard_map/ppermute | solution.py:360
  60.4 10.2 %collective-permute-start.21 = (bf16[512,128]{1,0:T(8,128)(2,1)S(1)}, bf16[512,128]{1,0:T(8,128)(2,1)S(1)}, u32[]{:S(2)}, u32[]{:S(2)}) collective-permute-start(bf16[512,128]{1,0:T(8,128)(2,1)S(1)} %update.7.refs_4_.refs_0_.refs_1_), channel_id=1, source_target_pairs={{0,1},{1,0},{2,3},{3,2},{4,5},{5,4},{6,7},{7,6},{8,9},{9,8},{10,11... | collective-permute-start | bytes 393224 | tf_op jit(solution)/shard_map/ppermute | solution.py:344
  63.0 12.7 %collective-permute-start.22 = (bf16[512,128]{1,0:T(8,128)(2,1)S(1)}, bf16[512,128]{1,0:T(8,128)(2,1)S(1)}, u32[]{:S(2)}, u32[]{:S(2)}) collective-permute-start(bf16[512,128]{1,0:T(8,128)(2,1)S(1)} %update.7.refs_4_.refs_0_.refs_1_), channel_id=1, source_target_pairs={{0,2},{1,3},{2,0},{3,1},{4,6},{5,7},{6,4},{7,5},{8,10},{9,11},{10,... | collective-permute-start | bytes 393224 | tf_op jit(solution)/shard_map/ppermute | solution.py:344
  63.1 12.7 %collective-permute-start.23 = (bf16[512,128]{1,0:T(8,128)(2,1)S(1)}, bf16[512,128]{1,0:T(8,128)(2,1)S(1)}, u32[]{:S(2)}, u32[]{:S(2)}) collective-permute-start(bf16[512,128]{1,0:T(8,128)(2,1)S(1)} %update.7.refs_4_.refs_0_.refs_1_), channel_id=1, source_target_pairs={{0,3},{1,2},{2,1},{3,0},{4,7},{5,6},{6,5},{7,4},{8,11},{9,10},{10,... | collective-permute-start | bytes 393224 | tf_op jit(solution)/shard_map/ppermute | solution.py:344
  78.9 6.4 %collective-permute-start.25 = (bf16[2,512,128]{2,1,0:T(8,128)(2,1)S(1)}, bf16[2,512,128]{2,1,0:T(8,128)(2,1)S(1)}, u32[]{:S(2)}, u32[]{:S(2)}) collective-permute-start(bf16[2,512,128]{2,1,0:T(8,128)(2,1)S(1)} %slice.192), channel_id=1, source_target_pairs={{0,16},{4,12},{8,24},{12,4},{16,0},{20,28},{24,8},{28,20},{1,17},{... | collective-permute-start | bytes 786440 | tf_op jit(solution)/shard_map/ppermute | solution.py:360
  80.2 10.3 %collective-permute-start.18 = (bf16[512,128]{1,0:T(8,128)(2,1)S(1)}, bf16[512,128]{1,0:T(8,128)(2,1)S(1)}, u32[]{:S(2)}, u32[]{:S(2)}) collective-permute-start(bf16[512,128]{1,0:T(8,128)(2,1)S(1)} %update.8.refs_4_.refs_0_.refs_1_), channel_id=1, source_target_pairs={{0,1},{1,0},{2,3},{3,2},{4,5},{5,4},{6,7},{7,6},{8,9},{9,8},{10,11... | collective-permute-start | bytes 393224 | tf_op jit(solution)/shard_map/ppermute | solution.py:344
  82.8 11.7 %collective-permute-start.19 = (bf16[512,128]{1,0:T(8,128)(2,1)S(1)}, bf16[512,128]{1,0:T(8,128)(2,1)S(1)}, u32[]{:S(2)}, u32[]{:S(2)}) collective-permute-start(bf16[512,128]{1,0:T(8,128)(2,1)S(1)} %update.8.refs_4_.refs_0_.refs_1_), channel_id=1, source_target_pairs={{0,2},{1,3},{2,0},{3,1},{4,6},{5,7},{6,4},{7,5},{8,10},{9,11},{10,... | collective-permute-start | bytes 393224 | tf_op jit(solution)/shard_map/ppermute | solution.py:344
  82.8 11.7 %collective-permute-start.20 = (bf16[512,128]{1,0:T(8,128)(2,1)S(1)}, bf16[512,128]{1,0:T(8,128)(2,1)S(1)}, u32[]{:S(2)}, u32[]{:S(2)}) collective-permute-start(bf16[512,128]{1,0:T(8,128)(2,1)S(1)} %update.8.refs_4_.refs_0_.refs_1_), channel_id=1, source_target_pairs={{0,3},{1,2},{2,1},{3,0},{4,7},{5,6},{6,5},{7,4},{8,11},{9,10},{10,... | collective-permute-start | bytes 393224 | tf_op jit(solution)/shard_map/ppermute | solution.py:344
  97.8 6.4 %collective-permute-start.28 = (bf16[2,512,128]{2,1,0:T(8,128)(2,1)S(1)}, bf16[2,512,128]{2,1,0:T(8,128)(2,1)S(1)}, u32[]{:S(2)}, u32[]{:S(2)}) collective-permute-start(bf16[2,512,128]{2,1,0:T(8,128)(2,1)S(1)} %slice.191), channel_id=1, source_target_pairs={{0,16},{4,12},{8,24},{12,4},{16,0},{20,28},{24,8},{28,20},{1,17},{... | collective-permute-start | bytes 786440 | tf_op jit(solution)/shard_map/ppermute | solution.py:360
  99.1 10.3 %collective-permute-start.30 = (bf16[512,128]{1,0:T(8,128)(2,1)S(1)}, bf16[512,128]{1,0:T(8,128)(2,1)S(1)}, u32[]{:S(2)}, u32[]{:S(2)}) collective-permute-start(bf16[512,128]{1,0:T(8,128)(2,1)S(1)} %update.9.refs_4_.refs_0_.refs_1_), channel_id=1, source_target_pairs={{0,1},{1,0},{2,3},{3,2},{4,5},{5,4},{6,7},{7,6},{8,9},{9,8},{10,11... | collective-permute-start | bytes 393224 | tf_op jit(solution)/shard_map/ppermute | solution.py:344
  101.8 12.5 %collective-permute-start.31 = (bf16[512,128]{1,0:T(8,128)(2,1)S(1)}, bf16[512,128]{1,0:T(8,128)(2,1)S(1)}, u32[]{:S(2)}, u32[]{:S(2)}) collective-permute-start(bf16[512,128]{1,0:T(8,128)(2,1)S(1)} %update.9.refs_4_.refs_0_.refs_1_), channel_id=1, source_target_pairs={{0,2},{1,3},{2,0},{3,1},{4,6},{5,7},{6,4},{7,5},{8,10},{9,11},{10,... | collective-permute-start | bytes 393224 | tf_op jit(solution)/shard_map/ppermute | solution.py:344
  101.8 12.5 %collective-permute-start.32 = (bf16[512,128]{1,0:T(8,128)(2,1)S(1)}, bf16[512,128]{1,0:T(8,128)(2,1)S(1)}, u32[]{:S(2)}, u32[]{:S(2)}) collective-permute-start(bf16[512,128]{1,0:T(8,128)(2,1)S(1)} %update.9.refs_4_.refs_0_.refs_1_), channel_id=1, source_target_pairs={{0,3},{1,2},{2,1},{3,0},{4,7},{5,6},{6,5},{7,4},{8,11},{9,10},{10,... | collective-permute-start | bytes 393224 | tf_op jit(solution)/shard_map/ppermute | solution.py:344
  117.5 6.4 %collective-permute-start.34 = (bf16[2,512,128]{2,1,0:T(8,128)(2,1)S(1)}, bf16[2,512,128]{2,1,0:T(8,128)(2,1)S(1)}, u32[]{:S(2)}, u32[]{:S(2)}) collective-permute-start(bf16[2,512,128]{2,1,0:T(8,128)(2,1)S(1)} %slice.190), channel_id=1, source_target_pairs={{0,16},{4,12},{8,24},{12,4},{16,0},{20,28},{24,8},{28,20},{1,17},{... | collective-permute-start | bytes 786440 | tf_op jit(solution)/shard_map/ppermute | solution.py:360
  (17 other events, 75.9 us)

commit v9 on v8

--- a/solution.py
+++ b/solution.py
@@ -67,19 +67,8 @@
     ]
 
 
-def chip_place(relative, owner, chip_bits):
-    place = jnp.int32(0)
-    turned = jnp.int32(0)
-    for bit in range(chip_bits):
-        value = lax.bitwise_and(lax.shift_right_logical(relative, bit + 1), 1)
-        place = place + value * (1 << bit)
-        turned = turned + value * (1 << (chip_bits - 1 - bit))
-    return jnp.where(lax.bitwise_and(owner, 1) == 0, place, turned)
-
-
 def prepare_kernel(
     tiles_per_owner,
-    chip_bits,
     bits,
     place_ref,
     src_ref,
@@ -127,7 +116,7 @@
             count = count_ref[0, dest]
             mine = lax.bitwise_and(relative, 1) == half
             pairs = jnp.where(mine, lax.div(count + 1, 2), 0)
-            chip = chip_place(relative, owner, chip_bits)
+            chip = lax.div(relative, 2)
             target = chip * tiles_per_owner + dest - owner * tiles_per_owner
 
             def one_pair(pair, carry):
@@ -176,7 +165,7 @@
 
     def weigh(owner, start):
         relative = lax.bitwise_xor(owner, my_row)
-        chip = chip_place(relative, owner, chip_bits)
+        chip = lax.div(relative, 2)
         for step in range(tiles_per_owner):
             count = count_ref[0, owner * tiles_per_owner + step]
             sums = jnp.where(places < count, sum_ref[pl.ds(start, MOST), :], 0.0)
@@ -196,9 +185,7 @@
     capacity = pair_capacity(tile_max, row_counts.shape[1])
     chips = row_size // 2
     return pl.pallas_call(
-        functools.partial(
-            prepare_kernel, tiles_per_owner, chips.bit_length() - 1, bits
-        ),
+        functools.partial(prepare_kernel, tiles_per_owner, bits),
         out_shape=[
             jax.ShapeDtypeStruct(tile_vals.shape, tile_vals.dtype),
             jax.ShapeDtypeStruct((2, chips, EXTRA, tile_size), jnp.float32),
@@ -344,23 +331,29 @@
     return lax.ppermute(block, axis, [(i, i ^ mask) for i in range(size)])
 
 
-def gather_line(block, size):
-    return [block] + [exchange(block, "col", mask, size) for mask in range(1, size)]
-
-
-def reduce_chips(state, chip_bits, row_size):
-    arrived = None
-    for step in range(chip_bits):
-        if arrived is not None:
-            state = state + arrived.astype(jnp.float32)
-        cut = state.shape[0] // 2
-        send = state[cut:].astype(jnp.bfloat16)
-        state = state[:cut]
-        bits = (chip_bits - step, 1 + step)
-        arrived = lax.ppermute(
-            send, "row", [(i, i ^ (1 << bits[i % 2])) for i in range(row_size)]
-        )
-    return state[0], arrived[0]
+def gather_line(block, size, masks):
+    return {mask: exchange(block, "col", mask, size) for mask in masks}
+
+
+def reduce_chips(both, cut, chip_bits, row_size):
+    kept, arrived = [], []
+    for half in range(2):
+        state = both[:, :cut] if half == 0 else both[:, cut:]
+        state = state.reshape((2,) * len(chip_bits) + state.shape[1:])
+        left = list(chip_bits)
+        turn = half % len(chip_bits)
+        got = None
+        for bit in chip_bits[turn:] + chip_bits[:turn]:
+            if got is not None:
+                state = state + got.astype(jnp.float32)
+            axis = left.index(bit)
+            send = lax.index_in_dim(state, 1, axis, keepdims=False).astype(jnp.bfloat16)
+            state = lax.index_in_dim(state, 0, axis, keepdims=False)
+            got = exchange(send, "row", 1 << bit, row_size)
+            left.remove(bit)
+        kept.append(state)
+        arrived.append(got)
+    return jnp.concatenate(kept), jnp.concatenate(arrived)
 
 
 def on_device(features, tile_vals, tile_src, row_counts):
@@ -376,6 +369,7 @@
     piece = features.shape[1] // CHUNKS
     tiles_per_owner = dest_count // row_size
     chips = row_size // 2
+    chip_bits = list(range(row_size.bit_length() - 2, 0, -1))
     bits = code_bits(tile_vals.shape[0], source_tiles, dest_count // 2)
     place = jnp.stack([my_row, my_col, jnp.int32(source_tiles)])
 
@@ -386,7 +380,9 @@
         place, tile_src, row_counts, tile_vals, row_size, tiles_per_owner, bits
     )
 
-    gathered = [gather_line(parts[0], blocks), None]
+    gathered = [{0: parts[0], **gather_line(parts[0], blocks, range(1, blocks))}, None]
+    early = [mask for mask in range(1, blocks) if 2 * mask >= blocks]
+    late = [mask for mask in range(1, blocks) if mask not in early]
     iterates = [None] * CHUNKS
     restarts = [None] * CHUNKS
     scale = None
@@ -398,19 +394,26 @@
         extra = EXTRA if phase == 0 else 0
         if phase > 0:
             iterates[after] = last = update(*pending)
-        held, *own = assemble(gathered[chunk], last, tile_size, first)
+        held, *own = assemble([gathered[chunk][m] for m in range(blocks)], last, tile_size, first)
         if first:
             iterates[chunk] = restarts[chunk] = own[0]
         if phase == 0:
             held, parts = lax.optimization_barrier((held, parts))
-            gathered[after] = gather_line(parts[1], blocks)
+            coming = parts[1]
         elif phase + 1 < ITERS * CHUNKS:
-            gathered[after] = gather_line(iterates[after], blocks)
+            coming = iterates[after]
+        else:
+            coming = None
+        if coming is not None:
+            gathered[after] = {0: coming, **gather_line(coming, blocks, early)}
         sent = product(1, pairs, turned, held, weights, rows, chips, extra, bits)
         other = exchange(sent, "row", 1, row_size)
         kept = product(0, pairs, turned, held, weights, rows, chips, extra, bits)
         both = kept.astype(jnp.float32) + other.astype(jnp.float32)
-        kept, arrived = reduce_chips(both, chips.bit_length() - 1, row_size)
+        if coming is not None:
+            coming, both = lax.optimization_barrier((coming, both))
+            gathered[after].update(gather_line(coming, blocks, late))
+        kept, arrived = reduce_chips(both, rows // 2, chip_bits, row_size)
         if phase == 0:
             weight_rows = slice(rows, rows + tiles_per_owner)
             total = 1.0 + kept[weight_rows] + arrived[weight_rows].astype(jnp.float32)

time: 130 us -> 128 us (0.985)
  waiting for transfers between devices: 53.8 us -> 42.1 us
  starting transfers between devices: 47.2 us -> 52.4 us
  local copies, waits for them, and re-layouts: 5.42 us -> 10.1 us
  Pallas kernels: 22.1 us -> 20.2 us
    ppermute x12 -> x0, waiting for transfers between devices: 27.8 us -> none  [reduce_chips(): lax.ppermute(send, 'row', [(i, i ^ 1 << bits[i % 2]) for i in range(row_s...]
    ppermute x24 -> x48, starting transfers between devices: 29.6 us -> 52.4 us  [exchange(): return lax.ppermute(block, axis, [(i, i ^ mask) for i in range(size)])]
    ppermute x12 -> x0, starting transfers between devices: 17.6 us -> none  [reduce_chips(): lax.ppermute(send, 'row', [(i, i ^ 1 << bits[i % 2]) for i in range(row_s...]
    ppermute x24 -> x48, waiting for transfers between devices: 26.1 us -> 42.1 us  [exchange(): return lax.ppermute(block, axis, [(i, i ^ mask) for i in range(size)])]
    unnamed x10 -> x14, local copies, waits for them, and re-layouts: 2.2 us -> 6.57 us
    pallas_call x12, Pallas kernels: 14 us -> 12.2 us  [product(): pl.pallas_call(functools.partial(product_kernel, half, rows, bits), out_s...]
  transfers between devices with their start and end apart: 36 -> 48, of which waited for: 23 -> 23; matrix products, arithmetic and copies ran while one was open for 1% -> 2% of each run, Pallas kernels for 11% -> 10%
where the time goes in v9:
time: 128 us; the launch traced here: 127 us
  starting transfers between devices  52.4 us (41%)
  waiting for transfers between devices  42.1 us (33%)
  Pallas kernels  20.2 us (16%)
  local copies, waits for them, and re-layouts  10.1 us (8%)
    ppermute x48, starting transfers between devices, exchange(): return lax.ppermute(block, axis, [(i, i ^ mask) for i in range(size)])  52.4 us
    ppermute x48, waiting for transfers between devices, exchange(): return lax.ppermute(block, axis, [(i, i ^ mask) for i in range(size)])  42.1 us
    pallas_call x12, Pallas kernels, product(): pl.pallas_call(functools.partial(product_kernel, half, rows, bits), out_s...  12.2 us
    unnamed x14, local copies, waits for them, and re-layouts  6.57 us
    pallas_call x1, Pallas kernels, prepare(): pl.pallas_call(functools.partial(prepare_kernel, tiles_per_owner, bits),...  6.19 us
  transfers between devices with their start and end apart: 48, of which 23 were waited for; matrix products, arithmetic and copies ran while one was open for 2% of the time, Pallas kernels for 10%

profile of v9, /device:TPU:0, one launch (start us, length us, event | category | flops | bytes accessed | tf_op | source)
XLA Modules:
  0.0 126.9 jit_solution(12126512731419654564)
XLA Ops:
  1.4 3.1 %collective-permute-start = (bf16[512,128]{1,0:T(8,128)(2,1)S(1)}, bf16[512,128]{1,0:T(8,128)(2,1)S(1)}, u32[]{:S(2)}, u32[]{:S(2)}) collective-permute-start(bf16[512,128]{1,0:T(8,128)(2,1)S(1)} %copy.44.refs_0_), channel_id=1, source_target_pairs={{0,1},{1,0},{2,3},{3,2},{4,5},{5,4},{6,7},{7,6},{8,9},{9,8},{10,11... | collective-permute-start | bytes 393224 | tf_op jit(solution)/shard_map/ppermute | solution.py:331
  4.5 2.6 %collective-permute-start.1 = (bf16[512,128]{1,0:T(8,128)(2,1)S(1)}, bf16[512,128]{1,0:T(8,128)(2,1)S(1)}, u32[]{:S(2)}, u32[]{:S(2)}) collective-permute-start(bf16[512,128]{1,0:T(8,128)(2,1)S(1)} %copy.44.refs_0_), channel_id=1, source_target_pairs={{0,2},{1,3},{2,0},{3,1},{4,6},{5,7},{6,4},{7,5},{8,10},{9,11},{10,... | collective-permute-start | bytes 393224 | tf_op jit(solution)/shard_map/ppermute | solution.py:331
  7.2 2.2 %copy-done.4 = bf16[128,128,128]{2,1,0:T(8,128)(2,1)S(1)} copy-done((bf16[128,128,128]{2,1,0:T(8,128)(2,1)S(1)}, bf16[128,128,128]{2,1,0:T(8,128)(2,1)}, u32[]{:S(2)}) %copy-start.4) | copy-done | bytes 4194328
  9.4 6.2 %prepare.1 = (bf16[128,128,128]{2,1,0:T(8,128)(2,1)S(1)}, f32[2,4,16,128]{3,2,1,0:T(8,128)S(1)}, s32[20,8]{1,0:T(8,128)S(1)}) custom-call(s32[3]{0:T(128)S(1)} %pad_add_fusion.refs_4_.place_ref, s32[1,128]{1,0:T(1,128)S(1)} %copy-done.5, s32[1,32]{1,0:T(1,128)S(1)} %copy-done.6, bf16[128,128,128]{2,1,0:T(8,128)(2,1)S(1)} %copy-done.4), custom_call_target="tpu_custom_call" | custom-call | tf_op jit(solution)/shard_map/prepare/pallas_call | solution.py:187
  19.3 2.4 %collective-permute-start.10 = (bf16[512,128]{1,0:T(8,128)(2,1)S(1)}, bf16[512,128]{1,0:T(8,128)(2,1)S(1)}, u32[]{:S(2)}, u32[]{:S(2)}) collective-permute-start(bf16[512,128]{1,0:T(8,128)(2,1)S(1)} %slice_bitcast_fusion.12.refs_0_), channel_id=1, source_target_pairs={{0,3},{1,2},{2,1},{3,0},{4,7},{5,6},{6,5},{7,4},{8,11},{9,10},{10,... | collective-permute-start | bytes 393224 | tf_op jit(solution)/shard_map/ppermute | solution.py:331
  22.8 2.2 %copy-done.1 = bf16[128,128,128]{2,1,0:T(8,128)(2,1)S(1)} copy-done((bf16[128,128,128]{2,1,0:T(8,128)(2,1)S(1)}, bf16[128,128,128]{2,1,0:T(8,128)(2,1)}, u32[]{:S(2)}) %copy-start.1) | copy-done | bytes 4194328
  26.2 2.2 %collective-permute-start.4 = (bf16[2,256,128]{2,1,0:T(8,128)(2,1)S(1)}, bf16[2,256,128]{2,1,0:T(8,128)(2,1)S(1)}, u32[]{:S(2)}, u32[]{:S(2)}) collective-permute-start(bf16[2,256,128]{2,1,0:T(8,128)(2,1)S(1)} %slice.414), channel_id=1, source_target_pairs={{0,16},{4,20},{8,24},{12,28},{16,0},{20,4},{24,8},{28,12},{1,17},{... | collective-permute-start | bytes 393224 | tf_op jit(solution)/shard_map/ppermute | solution.py:331
  34.9 3.3 %collective-permute-done.7 = bf16[272,128]{1,0:T(8,128)(2,1)S(1)} collective-permute-done((bf16[272,128]{1,0:T(8,128)(2,1)S(1)}, bf16[272,128]{1,0:T(8,128)(2,1)S(1)}, u32[]{:S(2)}, u32[]{:S(2)}) %collective-permute-start.7) | collective-permute-done | bytes 69664 | tf_op jit(solution)/shard_map/ppermute | solution.py:331
  40.1 2.0 %collective-permute-start.17 = (bf16[512,128]{1,0:T(8,128)(2,1)S(1)}, bf16[512,128]{1,0:T(8,128)(2,1)S(1)}, u32[]{:S(2)}, u32[]{:S(2)}) collective-permute-start(bf16[512,128]{1,0:T(8,128)(2,1)S(1)} %update.6.refs_4_.refs_0_.refs_1_), channel_id=1, source_target_pairs={{0,2},{1,3},{2,0},{3,1},{4,6},{5,7},{6,4},{7,5},{8,10},{9,11},{10,... | collective-permute-start | bytes 393224 | tf_op jit(solution)/shard_map/ppermute | solution.py:331
  47.2 2.9 %collective-permute-done.12 = bf16[2,256,128]{2,1,0:T(8,128)(2,1)S(1)} collective-permute-done((bf16[2,256,128]{2,1,0:T(8,128)(2,1)S(1)}, bf16[2,256,128]{2,1,0:T(8,128)(2,1)S(1)}, u32[]{:S(2)}, u32[]{:S(2)}) %collective-permute-start.12) | collective-permute-done | bytes 131104 | tf_op jit(solution)/shard_map/ppermute | solution.py:331
  52.9 3.0 %collective-permute-done.14 = bf16[256,128]{1,0:T(8,128)(2,1)S(1)} collective-permute-done((bf16[256,128]{1,0:T(8,128)(2,1)S(1)}, bf16[256,128]{1,0:T(8,128)(2,1)S(1)}, u32[]{:S(2)}, u32[]{:S(2)}) %collective-permute-start.14) | collective-permute-done | bytes 65568 | tf_op jit(solution)/shard_map/ppermute | solution.py:331
  61.6 1.8 %collective-permute-start.20 = (bf16[2,256,128]{2,1,0:T(8,128)(2,1)S(1)}, bf16[2,256,128]{2,1,0:T(8,128)(2,1)S(1)}, u32[]{:S(2)}, u32[]{:S(2)}) collective-permute-start(bf16[2,256,128]{2,1,0:T(8,128)(2,1)S(1)} %slice.412), channel_id=1, source_target_pairs={{0,16},{4,20},{8,24},{12,28},{16,0},{20,4},{24,8},{28,12},{1,17},{... | collective-permute-start | bytes 393224 | tf_op jit(solution)/shard_map/ppermute | solution.py:331
  64.7 2.5 %collective-permute-done.20 = bf16[2,256,128]{2,1,0:T(8,128)(2,1)S(1)} collective-permute-done((bf16[2,256,128]{2,1,0:T(8,128)(2,1)S(1)}, bf16[2,256,128]{2,1,0:T(8,128)(2,1)S(1)}, u32[]{:S(2)}, u32[]{:S(2)}) %collective-permute-start.20) | collective-permute-done | bytes 131104 | tf_op jit(solution)/shard_map/ppermute | solution.py:331
  70.5 2.6 %collective-permute-done.22 = bf16[256,128]{1,0:T(8,128)(2,1)S(1)} collective-permute-done((bf16[256,128]{1,0:T(8,128)(2,1)S(1)}, bf16[256,128]{1,0:T(8,128)(2,1)S(1)}, u32[]{:S(2)}, u32[]{:S(2)}) %collective-permute-start.22) | collective-permute-done | bytes 65568 | tf_op jit(solution)/shard_map/ppermute | solution.py:331
  74.7 1.8 %collective-permute-start.33 = (bf16[512,128]{1,0:T(8,128)(2,1)S(1)}, bf16[512,128]{1,0:T(8,128)(2,1)S(1)}, u32[]{:S(2)}, u32[]{:S(2)}) collective-permute-start(bf16[512,128]{1,0:T(8,128)(2,1)S(1)} %update.8.refs_4_.refs_0_.refs_1_), channel_id=1, source_target_pairs={{0,2},{1,3},{2,0},{3,1},{4,6},{5,7},{6,4},{7,5},{8,10},{9,11},{10,... | collective-permute-start | bytes 393224 | tf_op jit(solution)/shard_map/ppermute | solution.py:331
  79.0 2.2 %collective-permute-start.28 = (bf16[2,256,128]{2,1,0:T(8,128)(2,1)S(1)}, bf16[2,256,128]{2,1,0:T(8,128)(2,1)S(1)}, u32[]{:S(2)}, u32[]{:S(2)}) collective-permute-start(bf16[2,256,128]{2,1,0:T(8,128)(2,1)S(1)} %slice.411), channel_id=1, source_target_pairs={{0,16},{4,20},{8,24},{12,28},{16,0},{20,4},{24,8},{28,12},{1,17},{... | collective-permute-start | bytes 393224 | tf_op jit(solution)/shard_map/ppermute | solution.py:331
  82.3 2.5 %collective-permute-done.28 = bf16[2,256,128]{2,1,0:T(8,128)(2,1)S(1)} collective-permute-done((bf16[2,256,128]{2,1,0:T(8,128)(2,1)S(1)}, bf16[2,256,128]{2,1,0:T(8,128)(2,1)S(1)}, u32[]{:S(2)}, u32[]{:S(2)}) %collective-permute-start.28) | collective-permute-done | bytes 131104 | tf_op jit(solution)/shard_map/ppermute | solution.py:331
  88.3 2.4 %collective-permute-done.30 = bf16[256,128]{1,0:T(8,128)(2,1)S(1)} collective-permute-done((bf16[256,128]{1,0:T(8,128)(2,1)S(1)}, bf16[256,128]{1,0:T(8,128)(2,1)S(1)}, u32[]{:S(2)}, u32[]{:S(2)}) %collective-permute-start.30) | collective-permute-done | bytes 65568 | tf_op jit(solution)/shard_map/ppermute | solution.py:331
  92.3 1.8 %collective-permute-start.41 = (bf16[512,128]{1,0:T(8,128)(2,1)S(1)}, bf16[512,128]{1,0:T(8,128)(2,1)S(1)}, u32[]{:S(2)}, u32[]{:S(2)}) collective-permute-start(bf16[512,128]{1,0:T(8,128)(2,1)S(1)} %update.9.refs_4_.refs_0_.refs_1_), channel_id=1, source_target_pairs={{0,2},{1,3},{2,0},{3,1},{4,6},{5,7},{6,4},{7,5},{8,10},{9,11},{10,... | collective-permute-start | bytes 393224 | tf_op jit(solution)/shard_map/ppermute | solution.py:331
  96.6 2.2 %collective-permute-start.36 = (bf16[2,256,128]{2,1,0:T(8,128)(2,1)S(1)}, bf16[2,256,128]{2,1,0:T(8,128)(2,1)S(1)}, u32[]{:S(2)}, u32[]{:S(2)}) collective-permute-start(bf16[2,256,128]{2,1,0:T(8,128)(2,1)S(1)} %slice.410), channel_id=1, source_target_pairs={{0,16},{4,20},{8,24},{12,28},{16,0},{20,4},{24,8},{28,12},{1,17},{... | collective-permute-start | bytes 393224 | tf_op jit(solution)/shard_map/ppermute | solution.py:331
  100.1 2.5 %collective-permute-done.36 = bf16[2,256,128]{2,1,0:T(8,128)(2,1)S(1)} collective-permute-done((bf16[2,256,128]{2,1,0:T(8,128)(2,1)S(1)}, bf16[2,256,128]{2,1,0:T(8,128)(2,1)S(1)}, u32[]{:S(2)}, u32[]{:S(2)}) %collective-permute-start.36) | collective-permute-done | bytes 131104 | tf_op jit(solution)/shard_map/ppermute | solution.py:331
  105.9 2.6 %collective-permute-done.38 = bf16[256,128]{1,0:T(8,128)(2,1)S(1)} collective-permute-done((bf16[256,128]{1,0:T(8,128)(2,1)S(1)}, bf16[256,128]{1,0:T(8,128)(2,1)S(1)}, u32[]{:S(2)}, u32[]{:S(2)}) %collective-permute-start.38) | collective-permute-done | bytes 65568 | tf_op jit(solution)/shard_map/ppermute | solution.py:331
  110.2 2.2 %copy-done.3 = bf16[128,128,128]{2,1,0:T(8,128)(2,1)S(1)} copy-done((bf16[128,128,128]{2,1,0:T(8,128)(2,1)S(1)}, bf16[128,128,128]{2,1,0:T(8,128)(2,1)}, u32[]{:S(2)}) %copy-start.3) | copy-done | bytes 4194328
  115.8 3.8 %collective-permute-done.44 = bf16[2,256,128]{2,1,0:T(8,128)(2,1)S(1)} collective-permute-done((bf16[2,256,128]{2,1,0:T(8,128)(2,1)S(1)}, bf16[2,256,128]{2,1,0:T(8,128)(2,1)S(1)}, u32[]{:S(2)}, u32[]{:S(2)}) %collective-permute-start.44) | collective-permute-done | bytes 131104 | tf_op jit(solution)/shard_map/ppermute | solution.py:331
  (198 shorter events, 63.0 us)
Async XLA Ops:
  1.4 14.2 %collective-permute-start = (bf16[512,128]{1,0:T(8,128)(2,1)S(1)}, bf16[512,128]{1,0:T(8,128)(2,1)S(1)}, u32[]{:S(2)}, u32[]{:S(2)}) collective-permute-start(bf16[512,128]{1,0:T(8,128)(2,1)S(1)} %copy.44.refs_0_), channel_id=1, source_target_pairs={{0,1},{1,0},{2,3},{3,2},{4,5},{5,4},{6,7},{7,6},{8,9},{9,8},{10,11... | collective-permute-start | bytes 393224 | tf_op jit(solution)/shard_map/ppermute | solution.py:331
  4.5 12.9 %collective-permute-start.1 = (bf16[512,128]{1,0:T(8,128)(2,1)S(1)}, bf16[512,128]{1,0:T(8,128)(2,1)S(1)}, u32[]{:S(2)}, u32[]{:S(2)}) collective-permute-start(bf16[512,128]{1,0:T(8,128)(2,1)S(1)} %copy.44.refs_0_), channel_id=1, source_target_pairs={{0,2},{1,3},{2,0},{3,1},{4,6},{5,7},{6,4},{7,5},{8,10},{9,11},{10,... | collective-permute-start | bytes 393224 | tf_op jit(solution)/shard_map/ppermute | solution.py:331
  7.1 10.3 %collective-permute-start.2 = (bf16[512,128]{1,0:T(8,128)(2,1)S(1)}, bf16[512,128]{1,0:T(8,128)(2,1)S(1)}, u32[]{:S(2)}, u32[]{:S(2)}) collective-permute-start(bf16[512,128]{1,0:T(8,128)(2,1)S(1)} %copy.44.refs_0_), channel_id=1, source_target_pairs={{0,3},{1,2},{2,1},{3,0},{4,7},{5,6},{6,5},{7,4},{8,11},{9,10},{10,... | collective-permute-start | bytes 393224 | tf_op jit(solution)/shard_map/ppermute | solution.py:331
  19.0 7.0 %collective-permute-start.3 = (bf16[4,528,128]{2,1,0:T(8,128)(2,1)S(1)}, bf16[4,528,128]{2,1,0:T(8,128)(2,1)S(1)}, u32[]{:S(2)}, u32[]{:S(2)}) collective-permute-start(bf16[4,528,128]{2,1,0:T(8,128)(2,1)S(1)} %product.13), channel_id=1, source_target_pairs={{0,4},{4,0},{8,12},{12,8},{16,20},{20,16},{24,28},{28,24},{1,5},{5... | collective-permute-start | bytes 1622024 | tf_op jit(solution)/shard_map/ppermute | solution.py:331
  19.3 19.1 %collective-permute-start.10 = (bf16[512,128]{1,0:T(8,128)(2,1)S(1)}, bf16[512,128]{1,0:T(8,128)(2,1)S(1)}, u32[]{:S(2)}, u32[]{:S(2)}) collective-permute-start(bf16[512,128]{1,0:T(8,128)(2,1)S(1)} %slice_bitcast_fusion.12.refs_0_), channel_id=1, source_target_pairs={{0,3},{1,2},{2,1},{3,0},{4,7},{5,6},{6,5},{7,4},{8,11},{9,10},{10,... | collective-permute-start | bytes 393224 | tf_op jit(solution)/shard_map/ppermute | solution.py:331
  21.6 16.8 %collective-permute-start.9 = (bf16[512,128]{1,0:T(8,128)(2,1)S(1)}, bf16[512,128]{1,0:T(8,128)(2,1)S(1)}, u32[]{:S(2)}, u32[]{:S(2)}) collective-permute-start(bf16[512,128]{1,0:T(8,128)(2,1)S(1)} %slice_bitcast_fusion.12.refs_0_), channel_id=1, source_target_pairs={{0,2},{1,3},{2,0},{3,1},{4,6},{5,7},{6,4},{7,5},{8,10},{9,11},{10,... | collective-permute-start | bytes 393224 | tf_op jit(solution)/shard_map/ppermute | solution.py:331
  26.2 5.8 %collective-permute-start.4 = (bf16[2,256,128]{2,1,0:T(8,128)(2,1)S(1)}, bf16[2,256,128]{2,1,0:T(8,128)(2,1)S(1)}, u32[]{:S(2)}, u32[]{:S(2)}) collective-permute-start(bf16[2,256,128]{2,1,0:T(8,128)(2,1)S(1)} %slice.414), channel_id=1, source_target_pairs={{0,16},{4,20},{8,24},{12,28},{16,0},{20,4},{24,8},{28,12},{1,17},{... | collective-permute-start | bytes 393224 | tf_op jit(solution)/shard_map/ppermute | solution.py:331
  29.3 9.1 %collective-permute-start.8 = (bf16[512,128]{1,0:T(8,128)(2,1)S(1)}, bf16[512,128]{1,0:T(8,128)(2,1)S(1)}, u32[]{:S(2)}, u32[]{:S(2)}) collective-permute-start(bf16[512,128]{1,0:T(8,128)(2,1)S(1)} %slice_bitcast_fusion.12.refs_0_), channel_id=1, source_target_pairs={{0,1},{1,0},{2,3},{3,2},{4,5},{5,4},{6,7},{7,6},{8,9},{9,8},{10,11... | collective-permute-start | bytes 393224 | tf_op jit(solution)/shard_map/ppermute | solution.py:331
  32.0 6.2 %collective-permute-start.6 = (bf16[256,128]{1,0:T(8,128)(2,1)S(1)}, bf16[256,128]{1,0:T(8,128)(2,1)S(1)}, u32[]{:S(2)}, u32[]{:S(2)}) collective-permute-start(bf16[256,128]{1,0:T(8,128)(2,1)S(1)} %fusion.13), channel_id=1, source_target_pairs={{0,8},{4,12},{8,0},{12,4},{16,24},{20,28},{24,16},{28,20},{1,9},{5... | collective-permute-start | bytes 196616 | tf_op jit(solution)/shard_map/ppermute | solution.py:331
  40.1 16.2 %collective-permute-start.17 = (bf16[512,128]{1,0:T(8,128)(2,1)S(1)}, bf16[512,128]{1,0:T(8,128)(2,1)S(1)}, u32[]{:S(2)}, u32[]{:S(2)}) collective-permute-start(bf16[512,128]{1,0:T(8,128)(2,1)S(1)} %update.6.refs_4_.refs_0_.refs_1_), channel_id=1, source_target_pairs={{0,2},{1,3},{2,0},{3,1},{4,6},{5,7},{6,4},{7,5},{8,10},{9,11},{10,... | collective-permute-start | bytes 393224 | tf_op jit(solution)/shard_map/ppermute | solution.py:331
  42.1 14.2 %collective-permute-start.18 = (bf16[512,128]{1,0:T(8,128)(2,1)S(1)}, bf16[512,128]{1,0:T(8,128)(2,1)S(1)}, u32[]{:S(2)}, u32[]{:S(2)}) collective-permute-start(bf16[512,128]{1,0:T(8,128)(2,1)S(1)} %update.6.refs_4_.refs_0_.refs_1_), channel_id=1, source_target_pairs={{0,3},{1,2},{2,1},{3,0},{4,7},{5,6},{6,5},{7,4},{8,11},{9,10},{10,... | collective-permute-start | bytes 393224 | tf_op jit(solution)/shard_map/ppermute | solution.py:331
  46.6 9.7 %collective-permute-start.16 = (bf16[512,128]{1,0:T(8,128)(2,1)S(1)}, bf16[512,128]{1,0:T(8,128)(2,1)S(1)}, u32[]{:S(2)}, u32[]{:S(2)}) collective-permute-start(bf16[512,128]{1,0:T(8,128)(2,1)S(1)} %update.6.refs_4_.refs_0_.refs_1_), channel_id=1, source_target_pairs={{0,1},{1,0},{2,3},{3,2},{4,5},{5,4},{6,7},{7,6},{8,9},{9,8},{10,11... | collective-permute-start | bytes 393224 | tf_op jit(solution)/shard_map/ppermute | solution.py:331
  57.5 16.0 %collective-permute-start.25 = (bf16[512,128]{1,0:T(8,128)(2,1)S(1)}, bf16[512,128]{1,0:T(8,128)(2,1)S(1)}, u32[]{:S(2)}, u32[]{:S(2)}) collective-permute-start(bf16[512,128]{1,0:T(8,128)(2,1)S(1)} %update.7.refs_4_.refs_0_.refs_1_), channel_id=1, source_target_pairs={{0,2},{1,3},{2,0},{3,1},{4,6},{5,7},{6,4},{7,5},{8,10},{9,11},{10,... | collective-permute-start | bytes 393224 | tf_op jit(solution)/shard_map/ppermute | solution.py:331
  59.0 14.5 %collective-permute-start.26 = (bf16[512,128]{1,0:T(8,128)(2,1)S(1)}, bf16[512,128]{1,0:T(8,128)(2,1)S(1)}, u32[]{:S(2)}, u32[]{:S(2)}) collective-permute-start(bf16[512,128]{1,0:T(8,128)(2,1)S(1)} %update.7.refs_4_.refs_0_.refs_1_), channel_id=1, source_target_pairs={{0,3},{1,2},{2,1},{3,0},{4,7},{5,6},{6,5},{7,4},{8,11},{9,10},{10,... | collective-permute-start | bytes 393224 | tf_op jit(solution)/shard_map/ppermute | solution.py:331
  63.6 9.9 %collective-permute-start.24 = (bf16[512,128]{1,0:T(8,128)(2,1)S(1)}, bf16[512,128]{1,0:T(8,128)(2,1)S(1)}, u32[]{:S(2)}, u32[]{:S(2)}) collective-permute-start(bf16[512,128]{1,0:T(8,128)(2,1)S(1)} %update.7.refs_4_.refs_0_.refs_1_), channel_id=1, source_target_pairs={{0,1},{1,0},{2,3},{3,2},{4,5},{5,4},{6,7},{7,6},{8,9},{9,8},{10,11... | collective-permute-start | bytes 393224 | tf_op jit(solution)/shard_map/ppermute | solution.py:331
  74.7 16.4 %collective-permute-start.33 = (bf16[512,128]{1,0:T(8,128)(2,1)S(1)}, bf16[512,128]{1,0:T(8,128)(2,1)S(1)}, u32[]{:S(2)}, u32[]{:S(2)}) collective-permute-start(bf16[512,128]{1,0:T(8,128)(2,1)S(1)} %update.8.refs_4_.refs_0_.refs_1_), channel_id=1, source_target_pairs={{0,2},{1,3},{2,0},{3,1},{4,6},{5,7},{6,4},{7,5},{8,10},{9,11},{10,... | collective-permute-start | bytes 393224 | tf_op jit(solution)/shard_map/ppermute | solution.py:331
  76.5 14.6 %collective-permute-start.34 = (bf16[512,128]{1,0:T(8,128)(2,1)S(1)}, bf16[512,128]{1,0:T(8,128)(2,1)S(1)}, u32[]{:S(2)}, u32[]{:S(2)}) collective-permute-start(bf16[512,128]{1,0:T(8,128)(2,1)S(1)} %update.8.refs_4_.refs_0_.refs_1_), channel_id=1, source_target_pairs={{0,3},{1,2},{2,1},{3,0},{4,7},{5,6},{6,5},{7,4},{8,11},{9,10},{10,... | collective-permute-start | bytes 393224 | tf_op jit(solution)/shard_map/ppermute | solution.py:331
  79.0 5.8 %collective-permute-start.28 = (bf16[2,256,128]{2,1,0:T(8,128)(2,1)S(1)}, bf16[2,256,128]{2,1,0:T(8,128)(2,1)S(1)}, u32[]{:S(2)}, u32[]{:S(2)}) collective-permute-start(bf16[2,256,128]{2,1,0:T(8,128)(2,1)S(1)} %slice.411), channel_id=1, source_target_pairs={{0,16},{4,20},{8,24},{12,28},{16,0},{20,4},{24,8},{28,12},{1,17},{... | collective-permute-start | bytes 393224 | tf_op jit(solution)/shard_map/ppermute | solution.py:331
  81.3 9.8 %collective-permute-start.32 = (bf16[512,128]{1,0:T(8,128)(2,1)S(1)}, bf16[512,128]{1,0:T(8,128)(2,1)S(1)}, u32[]{:S(2)}, u32[]{:S(2)}) collective-permute-start(bf16[512,128]{1,0:T(8,128)(2,1)S(1)} %update.8.refs_4_.refs_0_.refs_1_), channel_id=1, source_target_pairs={{0,1},{1,0},{2,3},{3,2},{4,5},{5,4},{6,7},{7,6},{8,9},{9,8},{10,11... | collective-permute-start | bytes 393224 | tf_op jit(solution)/shard_map/ppermute | solution.py:331
  92.3 16.6 %collective-permute-start.41 = (bf16[512,128]{1,0:T(8,128)(2,1)S(1)}, bf16[512,128]{1,0:T(8,128)(2,1)S(1)}, u32[]{:S(2)}, u32[]{:S(2)}) collective-permute-start(bf16[512,128]{1,0:T(8,128)(2,1)S(1)} %update.9.refs_4_.refs_0_.refs_1_), channel_id=1, source_target_pairs={{0,2},{1,3},{2,0},{3,1},{4,6},{5,7},{6,4},{7,5},{8,10},{9,11},{10,... | collective-permute-start | bytes 393224 | tf_op jit(solution)/shard_map/ppermute | solution.py:331
  94.1 14.8 %collective-permute-start.42 = (bf16[512,128]{1,0:T(8,128)(2,1)S(1)}, bf16[512,128]{1,0:T(8,128)(2,1)S(1)}, u32[]{:S(2)}, u32[]{:S(2)}) collective-permute-start(bf16[512,128]{1,0:T(8,128)(2,1)S(1)} %update.9.refs_4_.refs_0_.refs_1_), channel_id=1, source_target_pairs={{0,3},{1,2},{2,1},{3,0},{4,7},{5,6},{6,5},{7,4},{8,11},{9,10},{10,... | collective-permute-start | bytes 393224 | tf_op jit(solution)/shard_map/ppermute | solution.py:331
  96.6 6.0 %collective-permute-start.36 = (bf16[2,256,128]{2,1,0:T(8,128)(2,1)S(1)}, bf16[2,256,128]{2,1,0:T(8,128)(2,1)S(1)}, u32[]{:S(2)}, u32[]{:S(2)}) collective-permute-start(bf16[2,256,128]{2,1,0:T(8,128)(2,1)S(1)} %slice.410), channel_id=1, source_target_pairs={{0,16},{4,20},{8,24},{12,28},{16,0},{20,4},{24,8},{28,12},{1,17},{... | collective-permute-start | bytes 393224 | tf_op jit(solution)/shard_map/ppermute | solution.py:331
  98.9 10.0 %collective-permute-start.40 = (bf16[512,128]{1,0:T(8,128)(2,1)S(1)}, bf16[512,128]{1,0:T(8,128)(2,1)S(1)}, u32[]{:S(2)}, u32[]{:S(2)}) collective-permute-start(bf16[512,128]{1,0:T(8,128)(2,1)S(1)} %update.9.refs_4_.refs_0_.refs_1_), channel_id=1, source_target_pairs={{0,1},{1,0},{2,3},{3,2},{4,5},{5,4},{6,7},{7,6},{8,9},{9,8},{10,11... | collective-permute-start | bytes 393224 | tf_op jit(solution)/shard_map/ppermute | solution.py:331
  113.6 6.0 %collective-permute-start.44 = (bf16[2,256,128]{2,1,0:T(8,128)(2,1)S(1)}, bf16[2,256,128]{2,1,0:T(8,128)(2,1)S(1)}, u32[]{:S(2)}, u32[]{:S(2)}) collective-permute-start(bf16[2,256,128]{2,1,0:T(8,128)(2,1)S(1)} %slice.409), channel_id=1, source_target_pairs={{0,16},{4,20},{8,24},{12,28},{16,0},{20,4},{24,8},{28,12},{1,17},{... | collective-permute-start | bytes 393224 | tf_op jit(solution)/shard_map/ppermute | solution.py:331
  (31 other events, 141.7 us)

commit v10 on v9

--- a/solution.py
+++ b/solution.py
@@ -200,7 +200,9 @@
             pltpu.SemaphoreType.DMA((8,)),
             pltpu.SemaphoreType.DMA((8,)),
         ],
-        compiler_params=pltpu.CompilerParams(vmem_limit_bytes=24 * 2**20),
+        compiler_params=pltpu.CompilerParams(
+            vmem_limit_bytes=2 * tile_vals.size * tile_vals.dtype.itemsize + 2 * 2**20
+        ),
         name="prepare",
     )(place, tile_src, row_counts, tile_vals)
 

time: 128 us -> 128 us (level); the launches traced: 127 us -> 128 us
  Pallas kernels: 20.2 us -> 22 us
    pallas_call x12, Pallas kernels: 12.2 us -> 14 us  [product(): pl.pallas_call(functools.partial(product_kernel, half, rows, bits), out_s...]
where the time goes in v10:
time: 128 us
  starting transfers between devices  52.5 us (41%)
  waiting for transfers between devices  41.3 us (32%)
  Pallas kernels  22 us (17%)
  local copies, waits for them, and re-layouts  10.1 us (8%)
    ppermute x48, starting transfers between devices, exchange(): return lax.ppermute(block, axis, [(i, i ^ mask) for i in range(size)])  52.5 us
    ppermute x48, waiting for transfers between devices, exchange(): return lax.ppermute(block, axis, [(i, i ^ mask) for i in range(size)])  41.3 us
    pallas_call x12, Pallas kernels, product(): pl.pallas_call(functools.partial(product_kernel, half, rows, bits), out_s...  14 us
    unnamed x14, local copies, waits for them, and re-layouts  6.57 us
    pallas_call x1, Pallas kernels, prepare(): pl.pallas_call(functools.partial(prepare_kernel, tiles_per_owner, bits),...  6.25 us
  transfers between devices with their start and end apart: 48, of which 23 were waited for; matrix products, arithmetic and copies ran while one was open for 2% of the time, Pallas kernels for 10%

profile of v10, /device:TPU:0, one launch (start us, length us, event | category | flops | bytes accessed | tf_op | source)
XLA Modules:
  0.0 128.2 jit_solution(10759481826809284931)
XLA Ops:
  1.4 3.1 %collective-permute-start = (bf16[512,128]{1,0:T(8,128)(2,1)S(1)}, bf16[512,128]{1,0:T(8,128)(2,1)S(1)}, u32[]{:S(2)}, u32[]{:S(2)}) collective-permute-start(bf16[512,128]{1,0:T(8,128)(2,1)S(1)} %copy.44.refs_0_), channel_id=1, source_target_pairs={{0,1},{1,0},{2,3},{3,2},{4,5},{5,4},{6,7},{7,6},{8,9},{9,8},{10,11... | collective-permute-start | bytes 393224 | tf_op jit(solution)/shard_map/ppermute | solution.py:333
  4.5 2.6 %collective-permute-start.1 = (bf16[512,128]{1,0:T(8,128)(2,1)S(1)}, bf16[512,128]{1,0:T(8,128)(2,1)S(1)}, u32[]{:S(2)}, u32[]{:S(2)}) collective-permute-start(bf16[512,128]{1,0:T(8,128)(2,1)S(1)} %copy.44.refs_0_), channel_id=1, source_target_pairs={{0,2},{1,3},{2,0},{3,1},{4,6},{5,7},{6,4},{7,5},{8,10},{9,11},{10,... | collective-permute-start | bytes 393224 | tf_op jit(solution)/shard_map/ppermute | solution.py:333
  7.2 2.2 %copy-done.4 = bf16[128,128,128]{2,1,0:T(8,128)(2,1)S(1)} copy-done((bf16[128,128,128]{2,1,0:T(8,128)(2,1)S(1)}, bf16[128,128,128]{2,1,0:T(8,128)(2,1)}, u32[]{:S(2)}) %copy-start.4) | copy-done | bytes 4194328
  9.4 6.3 %prepare.1 = (bf16[128,128,128]{2,1,0:T(8,128)(2,1)S(1)}, f32[2,4,16,128]{3,2,1,0:T(8,128)S(1)}, s32[20,8]{1,0:T(8,128)S(1)}) custom-call(s32[3]{0:T(128)S(1)} %pad_add_fusion.refs_4_.place_ref, s32[1,128]{1,0:T(1,128)S(1)} %copy-done.5, s32[1,32]{1,0:T(1,128)S(1)} %copy-done.6, bf16[128,128,128]{2,1,0:T(8,128)(2,1)S(1)} %copy-done.4), custom_call_target="tpu_custom_call" | custom-call | tf_op jit(solution)/shard_map/prepare/pallas_call | solution.py:187
  19.6 2.8 %collective-permute-start.10 = (bf16[512,128]{1,0:T(8,128)(2,1)S(1)}, bf16[512,128]{1,0:T(8,128)(2,1)S(1)}, u32[]{:S(2)}, u32[]{:S(2)}) collective-permute-start(bf16[512,128]{1,0:T(8,128)(2,1)S(1)} %slice_bitcast_fusion.12.refs_0_), channel_id=1, source_target_pairs={{0,3},{1,2},{2,1},{3,0},{4,7},{5,6},{6,5},{7,4},{8,11},{9,10},{10,... | collective-permute-start | bytes 393224 | tf_op jit(solution)/shard_map/ppermute | solution.py:333
  22.8 2.2 %copy-done.1 = bf16[128,128,128]{2,1,0:T(8,128)(2,1)S(1)} copy-done((bf16[128,128,128]{2,1,0:T(8,128)(2,1)S(1)}, bf16[128,128,128]{2,1,0:T(8,128)(2,1)}, u32[]{:S(2)}) %copy-start.1) | copy-done | bytes 4194328
  26.2 2.2 %collective-permute-start.4 = (bf16[2,256,128]{2,1,0:T(8,128)(2,1)S(1)}, bf16[2,256,128]{2,1,0:T(8,128)(2,1)S(1)}, u32[]{:S(2)}, u32[]{:S(2)}) collective-permute-start(bf16[2,256,128]{2,1,0:T(8,128)(2,1)S(1)} %slice.414), channel_id=1, source_target_pairs={{0,16},{4,20},{8,24},{12,28},{16,0},{20,4},{24,8},{28,12},{1,17},{... | collective-permute-start | bytes 393224 | tf_op jit(solution)/shard_map/ppermute | solution.py:333
  31.6 2.2 %collective-permute-start.6 = (bf16[256,128]{1,0:T(8,128)(2,1)S(1)}, bf16[256,128]{1,0:T(8,128)(2,1)S(1)}, u32[]{:S(2)}, u32[]{:S(2)}) collective-permute-start(bf16[256,128]{1,0:T(8,128)(2,1)S(1)} %fusion.13), channel_id=1, source_target_pairs={{0,8},{4,12},{8,0},{12,4},{16,24},{20,28},{24,16},{28,20},{1,9},{5... | collective-permute-start | bytes 196616 | tf_op jit(solution)/shard_map/ppermute | solution.py:333
  35.5 2.8 %collective-permute-done.7 = bf16[272,128]{1,0:T(8,128)(2,1)S(1)} collective-permute-done((bf16[272,128]{1,0:T(8,128)(2,1)S(1)}, bf16[272,128]{1,0:T(8,128)(2,1)S(1)}, u32[]{:S(2)}, u32[]{:S(2)}) %collective-permute-start.7) | collective-permute-done | bytes 69664 | tf_op jit(solution)/shard_map/ppermute | solution.py:333
  47.3 2.7 %collective-permute-done.12 = bf16[2,256,128]{2,1,0:T(8,128)(2,1)S(1)} collective-permute-done((bf16[2,256,128]{2,1,0:T(8,128)(2,1)S(1)}, bf16[2,256,128]{2,1,0:T(8,128)(2,1)S(1)}, u32[]{:S(2)}, u32[]{:S(2)}) %collective-permute-start.12) | collective-permute-done | bytes 131104 | tf_op jit(solution)/shard_map/ppermute | solution.py:333
  53.8 2.0 %collective-permute-done.14 = bf16[256,128]{1,0:T(8,128)(2,1)S(1)} collective-permute-done((bf16[256,128]{1,0:T(8,128)(2,1)S(1)}, bf16[256,128]{1,0:T(8,128)(2,1)S(1)}, u32[]{:S(2)}, u32[]{:S(2)}) %collective-permute-start.14) | collective-permute-done | bytes 65568 | tf_op jit(solution)/shard_map/ppermute | solution.py:333
  61.9 2.2 %collective-permute-start.20 = (bf16[2,256,128]{2,1,0:T(8,128)(2,1)S(1)}, bf16[2,256,128]{2,1,0:T(8,128)(2,1)S(1)}, u32[]{:S(2)}, u32[]{:S(2)}) collective-permute-start(bf16[2,256,128]{2,1,0:T(8,128)(2,1)S(1)} %slice.412), channel_id=1, source_target_pairs={{0,16},{4,20},{8,24},{12,28},{16,0},{20,4},{24,8},{28,12},{1,17},{... | collective-permute-start | bytes 393224 | tf_op jit(solution)/shard_map/ppermute | solution.py:333
  65.0 2.3 %collective-permute-done.20 = bf16[2,256,128]{2,1,0:T(8,128)(2,1)S(1)} collective-permute-done((bf16[2,256,128]{2,1,0:T(8,128)(2,1)S(1)}, bf16[2,256,128]{2,1,0:T(8,128)(2,1)S(1)}, u32[]{:S(2)}, u32[]{:S(2)}) %collective-permute-start.20) | collective-permute-done | bytes 131104 | tf_op jit(solution)/shard_map/ppermute | solution.py:333
  71.6 2.0 %collective-permute-done.22 = bf16[256,128]{1,0:T(8,128)(2,1)S(1)} collective-permute-done((bf16[256,128]{1,0:T(8,128)(2,1)S(1)}, bf16[256,128]{1,0:T(8,128)(2,1)S(1)}, u32[]{:S(2)}, u32[]{:S(2)}) %collective-permute-start.22) | collective-permute-done | bytes 65568 | tf_op jit(solution)/shard_map/ppermute | solution.py:333
  76.3 2.0 %collective-permute-start.34 = (bf16[512,128]{1,0:T(8,128)(2,1)S(1)}, bf16[512,128]{1,0:T(8,128)(2,1)S(1)}, u32[]{:S(2)}, u32[]{:S(2)}) collective-permute-start(bf16[512,128]{1,0:T(8,128)(2,1)S(1)} %update.8.refs_4_.refs_0_.refs_1_), channel_id=1, source_target_pairs={{0,3},{1,2},{2,1},{3,0},{4,7},{5,6},{6,5},{7,4},{8,11},{9,10},{10,... | collective-permute-start | bytes 393224 | tf_op jit(solution)/shard_map/ppermute | solution.py:333
  79.5 2.2 %collective-permute-start.28 = (bf16[2,256,128]{2,1,0:T(8,128)(2,1)S(1)}, bf16[2,256,128]{2,1,0:T(8,128)(2,1)S(1)}, u32[]{:S(2)}, u32[]{:S(2)}) collective-permute-start(bf16[2,256,128]{2,1,0:T(8,128)(2,1)S(1)} %slice.411), channel_id=1, source_target_pairs={{0,16},{4,20},{8,24},{12,28},{16,0},{20,4},{24,8},{28,12},{1,17},{... | collective-permute-start | bytes 393224 | tf_op jit(solution)/shard_map/ppermute | solution.py:333
  82.7 2.1 %collective-permute-done.28 = bf16[2,256,128]{2,1,0:T(8,128)(2,1)S(1)} collective-permute-done((bf16[2,256,128]{2,1,0:T(8,128)(2,1)S(1)}, bf16[2,256,128]{2,1,0:T(8,128)(2,1)S(1)}, u32[]{:S(2)}, u32[]{:S(2)}) %collective-permute-start.28) | collective-permute-done | bytes 131104 | tf_op jit(solution)/shard_map/ppermute | solution.py:333
  93.8 2.3 %collective-permute-start.42 = (bf16[512,128]{1,0:T(8,128)(2,1)S(1)}, bf16[512,128]{1,0:T(8,128)(2,1)S(1)}, u32[]{:S(2)}, u32[]{:S(2)}) collective-permute-start(bf16[512,128]{1,0:T(8,128)(2,1)S(1)} %update.9.refs_4_.refs_0_.refs_1_), channel_id=1, source_target_pairs={{0,3},{1,2},{2,1},{3,0},{4,7},{5,6},{6,5},{7,4},{8,11},{9,10},{10,... | collective-permute-start | bytes 393224 | tf_op jit(solution)/shard_map/ppermute | solution.py:333
  97.3 2.1 %collective-permute-start.36 = (bf16[2,256,128]{2,1,0:T(8,128)(2,1)S(1)}, bf16[2,256,128]{2,1,0:T(8,128)(2,1)S(1)}, u32[]{:S(2)}, u32[]{:S(2)}) collective-permute-start(bf16[2,256,128]{2,1,0:T(8,128)(2,1)S(1)} %slice.410), channel_id=1, source_target_pairs={{0,16},{4,20},{8,24},{12,28},{16,0},{20,4},{24,8},{28,12},{1,17},{... | collective-permute-start | bytes 393224 | tf_op jit(solution)/shard_map/ppermute | solution.py:333
  100.4 2.3 %collective-permute-done.36 = bf16[2,256,128]{2,1,0:T(8,128)(2,1)S(1)} collective-permute-done((bf16[2,256,128]{2,1,0:T(8,128)(2,1)S(1)}, bf16[2,256,128]{2,1,0:T(8,128)(2,1)S(1)}, u32[]{:S(2)}, u32[]{:S(2)}) %collective-permute-start.36) | collective-permute-done | bytes 131104 | tf_op jit(solution)/shard_map/ppermute | solution.py:333
  111.2 2.2 %copy-done.3 = bf16[128,128,128]{2,1,0:T(8,128)(2,1)S(1)} copy-done((bf16[128,128,128]{2,1,0:T(8,128)(2,1)S(1)}, bf16[128,128,128]{2,1,0:T(8,128)(2,1)}, u32[]{:S(2)}) %copy-start.3) | copy-done | bytes 4194328
  114.6 2.7 %collective-permute-start.44 = (bf16[2,256,128]{2,1,0:T(8,128)(2,1)S(1)}, bf16[2,256,128]{2,1,0:T(8,128)(2,1)S(1)}, u32[]{:S(2)}, u32[]{:S(2)}) collective-permute-start(bf16[2,256,128]{2,1,0:T(8,128)(2,1)S(1)} %slice.409), channel_id=1, source_target_pairs={{0,16},{4,20},{8,24},{12,28},{16,0},{20,4},{24,8},{28,12},{1,17},{... | collective-permute-start | bytes 393224 | tf_op jit(solution)/shard_map/ppermute | solution.py:333
  117.4 3.4 %collective-permute-done.44 = bf16[2,256,128]{2,1,0:T(8,128)(2,1)S(1)} collective-permute-done((bf16[2,256,128]{2,1,0:T(8,128)(2,1)S(1)}, bf16[2,256,128]{2,1,0:T(8,128)(2,1)S(1)}, u32[]{:S(2)}, u32[]{:S(2)}) %collective-permute-start.44) | collective-permute-done | bytes 131104 | tf_op jit(solution)/shard_map/ppermute | solution.py:333
  123.7 3.1 %collective-permute-done.46 = bf16[256,128]{1,0:T(8,128)(2,1)S(1)} collective-permute-done((bf16[256,128]{1,0:T(8,128)(2,1)S(1)}, bf16[256,128]{1,0:T(8,128)(2,1)S(1)}, u32[]{:S(2)}, u32[]{:S(2)}) %collective-permute-start.46) | collective-permute-done | bytes 65568 | tf_op jit(solution)/shard_map/ppermute | solution.py:333
  (198 shorter events, 65.2 us)
Async XLA Ops:
  1.4 14.3 %collective-permute-start = (bf16[512,128]{1,0:T(8,128)(2,1)S(1)}, bf16[512,128]{1,0:T(8,128)(2,1)S(1)}, u32[]{:S(2)}, u32[]{:S(2)}) collective-permute-start(bf16[512,128]{1,0:T(8,128)(2,1)S(1)} %copy.44.refs_0_), channel_id=1, source_target_pairs={{0,1},{1,0},{2,3},{3,2},{4,5},{5,4},{6,7},{7,6},{8,9},{9,8},{10,11... | collective-permute-start | bytes 393224 | tf_op jit(solution)/shard_map/ppermute | solution.py:333
  4.5 12.9 %collective-permute-start.1 = (bf16[512,128]{1,0:T(8,128)(2,1)S(1)}, bf16[512,128]{1,0:T(8,128)(2,1)S(1)}, u32[]{:S(2)}, u32[]{:S(2)}) collective-permute-start(bf16[512,128]{1,0:T(8,128)(2,1)S(1)} %copy.44.refs_0_), channel_id=1, source_target_pairs={{0,2},{1,3},{2,0},{3,1},{4,6},{5,7},{6,4},{7,5},{8,10},{9,11},{10,... | collective-permute-start | bytes 393224 | tf_op jit(solution)/shard_map/ppermute | solution.py:333
  7.1 10.3 %collective-permute-start.2 = (bf16[512,128]{1,0:T(8,128)(2,1)S(1)}, bf16[512,128]{1,0:T(8,128)(2,1)S(1)}, u32[]{:S(2)}, u32[]{:S(2)}) collective-permute-start(bf16[512,128]{1,0:T(8,128)(2,1)S(1)} %copy.44.refs_0_), channel_id=1, source_target_pairs={{0,3},{1,2},{2,1},{3,0},{4,7},{5,6},{6,5},{7,4},{8,11},{9,10},{10,... | collective-permute-start | bytes 393224 | tf_op jit(solution)/shard_map/ppermute | solution.py:333
  19.3 6.7 %collective-permute-start.3 = (bf16[4,528,128]{2,1,0:T(8,128)(2,1)S(1)}, bf16[4,528,128]{2,1,0:T(8,128)(2,1)S(1)}, u32[]{:S(2)}, u32[]{:S(2)}) collective-permute-start(bf16[4,528,128]{2,1,0:T(8,128)(2,1)S(1)} %product.13), channel_id=1, source_target_pairs={{0,4},{4,0},{8,12},{12,8},{16,20},{20,16},{24,28},{28,24},{1,5},{5... | collective-permute-start | bytes 1622024 | tf_op jit(solution)/shard_map/ppermute | solution.py:333
  19.6 18.9 %collective-permute-start.10 = (bf16[512,128]{1,0:T(8,128)(2,1)S(1)}, bf16[512,128]{1,0:T(8,128)(2,1)S(1)}, u32[]{:S(2)}, u32[]{:S(2)}) collective-permute-start(bf16[512,128]{1,0:T(8,128)(2,1)S(1)} %slice_bitcast_fusion.12.refs_0_), channel_id=1, source_target_pairs={{0,3},{1,2},{2,1},{3,0},{4,7},{5,6},{6,5},{7,4},{8,11},{9,10},{10,... | collective-permute-start | bytes 393224 | tf_op jit(solution)/shard_map/ppermute | solution.py:333
  22.4 16.1 %collective-permute-start.9 = (bf16[512,128]{1,0:T(8,128)(2,1)S(1)}, bf16[512,128]{1,0:T(8,128)(2,1)S(1)}, u32[]{:S(2)}, u32[]{:S(2)}) collective-permute-start(bf16[512,128]{1,0:T(8,128)(2,1)S(1)} %slice_bitcast_fusion.12.refs_0_), channel_id=1, source_target_pairs={{0,2},{1,3},{2,0},{3,1},{4,6},{5,7},{6,4},{7,5},{8,10},{9,11},{10,... | collective-permute-start | bytes 393224 | tf_op jit(solution)/shard_map/ppermute | solution.py:333
  26.2 5.4 %collective-permute-start.4 = (bf16[2,256,128]{2,1,0:T(8,128)(2,1)S(1)}, bf16[2,256,128]{2,1,0:T(8,128)(2,1)S(1)}, u32[]{:S(2)}, u32[]{:S(2)}) collective-permute-start(bf16[2,256,128]{2,1,0:T(8,128)(2,1)S(1)} %slice.414), channel_id=1, source_target_pairs={{0,16},{4,20},{8,24},{12,28},{16,0},{20,4},{24,8},{28,12},{1,17},{... | collective-permute-start | bytes 393224 | tf_op jit(solution)/shard_map/ppermute | solution.py:333
  28.4 5.4 %collective-permute-start.5 = (bf16[2,272,128]{2,1,0:T(8,128)(2,1)S(1)}, bf16[2,272,128]{2,1,0:T(8,128)(2,1)S(1)}, u32[]{:S(2)}, u32[]{:S(2)}) collective-permute-start(bf16[2,272,128]{2,1,0:T(8,128)(2,1)S(1)} %fusion.6), channel_id=1, source_target_pairs={{0,8},{4,12},{8,0},{12,4},{16,24},{20,28},{24,16},{28,20},{1,9},{5... | collective-permute-start | bytes 417800 | tf_op jit(solution)/shard_map/ppermute | solution.py:333
  29.3 9.2 %collective-permute-start.8 = (bf16[512,128]{1,0:T(8,128)(2,1)S(1)}, bf16[512,128]{1,0:T(8,128)(2,1)S(1)}, u32[]{:S(2)}, u32[]{:S(2)}) collective-permute-start(bf16[512,128]{1,0:T(8,128)(2,1)S(1)} %slice_bitcast_fusion.12.refs_0_), channel_id=1, source_target_pairs={{0,1},{1,0},{2,3},{3,2},{4,5},{5,4},{6,7},{7,6},{8,9},{9,8},{10,11... | collective-permute-start | bytes 393224 | tf_op jit(solution)/shard_map/ppermute | solution.py:333
  31.6 6.6 %collective-permute-start.6 = (bf16[256,128]{1,0:T(8,128)(2,1)S(1)}, bf16[256,128]{1,0:T(8,128)(2,1)S(1)}, u32[]{:S(2)}, u32[]{:S(2)}) collective-permute-start(bf16[256,128]{1,0:T(8,128)(2,1)S(1)} %fusion.13), channel_id=1, source_target_pairs={{0,8},{4,12},{8,0},{12,4},{16,24},{20,28},{24,16},{28,20},{1,9},{5... | collective-permute-start | bytes 196616 | tf_op jit(solution)/shard_map/ppermute | solution.py:333
  40.5 16.6 %collective-permute-start.17 = (bf16[512,128]{1,0:T(8,128)(2,1)S(1)}, bf16[512,128]{1,0:T(8,128)(2,1)S(1)}, u32[]{:S(2)}, u32[]{:S(2)}) collective-permute-start(bf16[512,128]{1,0:T(8,128)(2,1)S(1)} %update.6.refs_4_.refs_0_.refs_1_), channel_id=1, source_target_pairs={{0,2},{1,3},{2,0},{3,1},{4,6},{5,7},{6,4},{7,5},{8,10},{9,11},{10,... | collective-permute-start | bytes 393224 | tf_op jit(solution)/shard_map/ppermute | solution.py:333
  41.5 15.6 %collective-permute-start.18 = (bf16[512,128]{1,0:T(8,128)(2,1)S(1)}, bf16[512,128]{1,0:T(8,128)(2,1)S(1)}, u32[]{:S(2)}, u32[]{:S(2)}) collective-permute-start(bf16[512,128]{1,0:T(8,128)(2,1)S(1)} %update.6.refs_4_.refs_0_.refs_1_), channel_id=1, source_target_pairs={{0,3},{1,2},{2,1},{3,0},{4,7},{5,6},{6,5},{7,4},{8,11},{9,10},{10,... | collective-permute-start | bytes 393224 | tf_op jit(solution)/shard_map/ppermute | solution.py:333
  44.7 5.4 %collective-permute-start.12 = (bf16[2,256,128]{2,1,0:T(8,128)(2,1)S(1)}, bf16[2,256,128]{2,1,0:T(8,128)(2,1)S(1)}, u32[]{:S(2)}, u32[]{:S(2)}) collective-permute-start(bf16[2,256,128]{2,1,0:T(8,128)(2,1)S(1)} %slice.413), channel_id=1, source_target_pairs={{0,16},{4,20},{8,24},{12,28},{16,0},{20,4},{24,8},{28,12},{1,17},{... | collective-permute-start | bytes 393224 | tf_op jit(solution)/shard_map/ppermute | solution.py:333
  47.0 10.1 %collective-permute-start.16 = (bf16[512,128]{1,0:T(8,128)(2,1)S(1)}, bf16[512,128]{1,0:T(8,128)(2,1)S(1)}, u32[]{:S(2)}, u32[]{:S(2)}) collective-permute-start(bf16[512,128]{1,0:T(8,128)(2,1)S(1)} %update.6.refs_4_.refs_0_.refs_1_), channel_id=1, source_target_pairs={{0,1},{1,0},{2,3},{3,2},{4,5},{5,4},{6,7},{7,6},{8,9},{9,8},{10,11... | collective-permute-start | bytes 393224 | tf_op jit(solution)/shard_map/ppermute | solution.py:333
  58.6 15.6 %collective-permute-start.25 = (bf16[512,128]{1,0:T(8,128)(2,1)S(1)}, bf16[512,128]{1,0:T(8,128)(2,1)S(1)}, u32[]{:S(2)}, u32[]{:S(2)}) collective-permute-start(bf16[512,128]{1,0:T(8,128)(2,1)S(1)} %update.7.refs_4_.refs_0_.refs_1_), channel_id=1, source_target_pairs={{0,2},{1,3},{2,0},{3,1},{4,6},{5,7},{6,4},{7,5},{8,10},{9,11},{10,... | collective-permute-start | bytes 393224 | tf_op jit(solution)/shard_map/ppermute | solution.py:333
  58.7 15.5 %collective-permute-start.26 = (bf16[512,128]{1,0:T(8,128)(2,1)S(1)}, bf16[512,128]{1,0:T(8,128)(2,1)S(1)}, u32[]{:S(2)}, u32[]{:S(2)}) collective-permute-start(bf16[512,128]{1,0:T(8,128)(2,1)S(1)} %update.7.refs_4_.refs_0_.refs_1_), channel_id=1, source_target_pairs={{0,3},{1,2},{2,1},{3,0},{4,7},{5,6},{6,5},{7,4},{8,11},{9,10},{10,... | collective-permute-start | bytes 393224 | tf_op jit(solution)/shard_map/ppermute | solution.py:333
  64.4 9.8 %collective-permute-start.24 = (bf16[512,128]{1,0:T(8,128)(2,1)S(1)}, bf16[512,128]{1,0:T(8,128)(2,1)S(1)}, u32[]{:S(2)}, u32[]{:S(2)}) collective-permute-start(bf16[512,128]{1,0:T(8,128)(2,1)S(1)} %update.7.refs_4_.refs_0_.refs_1_), channel_id=1, source_target_pairs={{0,1},{1,0},{2,3},{3,2},{4,5},{5,4},{6,7},{7,6},{8,9},{9,8},{10,11... | collective-permute-start | bytes 393224 | tf_op jit(solution)/shard_map/ppermute | solution.py:333
  75.7 16.5 %collective-permute-start.33 = (bf16[512,128]{1,0:T(8,128)(2,1)S(1)}, bf16[512,128]{1,0:T(8,128)(2,1)S(1)}, u32[]{:S(2)}, u32[]{:S(2)}) collective-permute-start(bf16[512,128]{1,0:T(8,128)(2,1)S(1)} %update.8.refs_4_.refs_0_.refs_1_), channel_id=1, source_target_pairs={{0,2},{1,3},{2,0},{3,1},{4,6},{5,7},{6,4},{7,5},{8,10},{9,11},{10,... | collective-permute-start | bytes 393224 | tf_op jit(solution)/shard_map/ppermute | solution.py:333
  76.3 16.0 %collective-permute-start.34 = (bf16[512,128]{1,0:T(8,128)(2,1)S(1)}, bf16[512,128]{1,0:T(8,128)(2,1)S(1)}, u32[]{:S(2)}, u32[]{:S(2)}) collective-permute-start(bf16[512,128]{1,0:T(8,128)(2,1)S(1)} %update.8.refs_4_.refs_0_.refs_1_), channel_id=1, source_target_pairs={{0,3},{1,2},{2,1},{3,0},{4,7},{5,6},{6,5},{7,4},{8,11},{9,10},{10,... | collective-permute-start | bytes 393224 | tf_op jit(solution)/shard_map/ppermute | solution.py:333
  82.1 10.1 %collective-permute-start.32 = (bf16[512,128]{1,0:T(8,128)(2,1)S(1)}, bf16[512,128]{1,0:T(8,128)(2,1)S(1)}, u32[]{:S(2)}, u32[]{:S(2)}) collective-permute-start(bf16[512,128]{1,0:T(8,128)(2,1)S(1)} %update.8.refs_4_.refs_0_.refs_1_), channel_id=1, source_target_pairs={{0,1},{1,0},{2,3},{3,2},{4,5},{5,4},{6,7},{7,6},{8,9},{9,8},{10,11... | collective-permute-start | bytes 393224 | tf_op jit(solution)/shard_map/ppermute | solution.py:333
  93.7 15.9 %collective-permute-start.41 = (bf16[512,128]{1,0:T(8,128)(2,1)S(1)}, bf16[512,128]{1,0:T(8,128)(2,1)S(1)}, u32[]{:S(2)}, u32[]{:S(2)}) collective-permute-start(bf16[512,128]{1,0:T(8,128)(2,1)S(1)} %update.9.refs_4_.refs_0_.refs_1_), channel_id=1, source_target_pairs={{0,2},{1,3},{2,0},{3,1},{4,6},{5,7},{6,4},{7,5},{8,10},{9,11},{10,... | collective-permute-start | bytes 393224 | tf_op jit(solution)/shard_map/ppermute | solution.py:333
  93.8 15.8 %collective-permute-start.42 = (bf16[512,128]{1,0:T(8,128)(2,1)S(1)}, bf16[512,128]{1,0:T(8,128)(2,1)S(1)}, u32[]{:S(2)}, u32[]{:S(2)}) collective-permute-start(bf16[512,128]{1,0:T(8,128)(2,1)S(1)} %update.9.refs_4_.refs_0_.refs_1_), channel_id=1, source_target_pairs={{0,3},{1,2},{2,1},{3,0},{4,7},{5,6},{6,5},{7,4},{8,11},{9,10},{10,... | collective-permute-start | bytes 393224 | tf_op jit(solution)/shard_map/ppermute | solution.py:333
  99.8 9.8 %collective-permute-start.40 = (bf16[512,128]{1,0:T(8,128)(2,1)S(1)}, bf16[512,128]{1,0:T(8,128)(2,1)S(1)}, u32[]{:S(2)}, u32[]{:S(2)}) collective-permute-start(bf16[512,128]{1,0:T(8,128)(2,1)S(1)} %update.9.refs_4_.refs_0_.refs_1_), channel_id=1, source_target_pairs={{0,1},{1,0},{2,3},{3,2},{4,5},{5,4},{6,7},{7,6},{8,9},{9,8},{10,11... | collective-permute-start | bytes 393224 | tf_op jit(solution)/shard_map/ppermute | solution.py:333
  114.6 6.3 %collective-permute-start.44 = (bf16[2,256,128]{2,1,0:T(8,128)(2,1)S(1)}, bf16[2,256,128]{2,1,0:T(8,128)(2,1)S(1)}, u32[]{:S(2)}, u32[]{:S(2)}) collective-permute-start(bf16[2,256,128]{2,1,0:T(8,128)(2,1)S(1)} %slice.409), channel_id=1, source_target_pairs={{0,16},{4,20},{8,24},{12,28},{16,0},{20,4},{24,8},{28,12},{1,17},{... | collective-permute-start | bytes 393224 | tf_op jit(solution)/shard_map/ppermute | solution.py:333
  (31 other events, 138.5 us)

commit v11 on v9

--- a/solution.py
+++ b/solution.py
@@ -78,10 +78,8 @@
     weight_ref,
     list_ref,
     held_ref,
-    staged_ref,
     sum_ref,
     in_sems,
-    out_sems,
 ):
     tile_max, tile_size, _ = tile_ref.shape
     dest_count = count_ref.shape[1]
@@ -94,10 +92,6 @@
         pltpu.make_async_copy(tile_ref.at[span], held_ref.at[span], in_sems.at[index])
         for index, span in enumerate(spans)
     ]
-    copies_out = [
-        pltpu.make_async_copy(staged_ref.at[span], turned_ref.at[span], out_sems.at[index])
-        for index, span in enumerate(spans)
-    ]
     for copy in copies_in:
         copy.start()
 
@@ -150,14 +144,13 @@
             for step in range(group):
                 slot = index * piece + at * group + step
                 tile = held_ref[slot]
-                staged_ref[slot] = tile.T
+                turned_ref[slot] = tile.T
                 sum_ref[pl.ds(slot, 1), :] = jnp.sum(
                     tile.astype(jnp.float32), axis=0, keepdims=True
                 )
             return carry
 
         lax.fori_loop(0, piece // group, one_group, 0)
-        copies_out[index].start()
 
     sum_ref[tile_max:, :] = jnp.zeros((MOST, tile_size), jnp.float32)
     weight_ref[...] = jnp.zeros(weight_ref.shape, weight_ref.dtype)
@@ -176,8 +169,6 @@
         return start
 
     lax.fori_loop(0, dest_count // tiles_per_owner, weigh, jnp.int32(0))
-    for copy in copies_out:
-        copy.wait()
 
 
 def prepare(place, tile_src, row_counts, tile_vals, row_size, tiles_per_owner, bits):
@@ -187,17 +178,15 @@
     return pl.pallas_call(
         functools.partial(prepare_kernel, tiles_per_owner, bits),
         out_shape=[
-            jax.ShapeDtypeStruct(tile_vals.shape, tile_vals.dtype),
+            pltpu.VMEM(tile_vals.shape, tile_vals.dtype),
             jax.ShapeDtypeStruct((2, chips, EXTRA, tile_size), jnp.float32),
             jax.ShapeDtypeStruct((2 * (capacity // UNROLL) + 2, UNROLL), jnp.int32),
         ],
         in_specs=smem(3) + hbm(1),
-        out_specs=hbm(1) + vmem(1) + smem(1),
+        out_specs=vmem(2) + smem(1),
         scratch_shapes=[
             pltpu.VMEM(tile_vals.shape, tile_vals.dtype),
-            pltpu.VMEM(tile_vals.shape, tile_vals.dtype),
             pltpu.VMEM((tile_max + MOST, tile_size), jnp.float32),
-            pltpu.SemaphoreType.DMA((8,)),
             pltpu.SemaphoreType.DMA((8,)),
         ],
         compiler_params=pltpu.CompilerParams(vmem_limit_bytes=24 * 2**20),
@@ -251,7 +240,9 @@
     )(*gathered, after)
 
 
-def product_kernel(half, rows, bits, list_ref, turned_ref, held_ref, weight_ref, out_ref):
+def product_kernel(
+    half, rows, bits, list_ref, turned_ref, held_ref, weight_ref, out_ref, passed_ref
+):
     tile_max, tile_size, _ = turned_ref.shape
     chips, out_rows, width = out_ref.shape
     rows_each = (list_ref.shape[0] - 2) // 2
@@ -292,9 +283,13 @@
 def product(half, pairs, turned, held, weights, rows, chips, extra, bits):
     return pl.pallas_call(
         functools.partial(product_kernel, half, rows, bits),
-        out_shape=jax.ShapeDtypeStruct((chips, rows + extra, held.shape[1]), jnp.bfloat16),
+        out_shape=[
+            jax.ShapeDtypeStruct((chips, rows + extra, held.shape[1]), jnp.bfloat16),
+            jax.ShapeDtypeStruct(turned.shape, turned.dtype),
+        ],
         in_specs=vmem(4),
-        out_specs=vmem(1)[0],
+        out_specs=vmem(2),
+        input_output_aliases={1: 1},
         compiler_params=pltpu.CompilerParams(vmem_limit_bytes=4 * 2**20),
         cost_estimate=pl.CostEstimate(
             flops=600000000, bytes_accessed=6000000, transcendentals=0
@@ -406,9 +401,9 @@
             coming = None
         if coming is not None:
             gathered[after] = {0: coming, **gather_line(coming, blocks, early)}
-        sent = product(1, pairs, turned, held, weights, rows, chips, extra, bits)
+        sent, turned = product(1, pairs, turned, held, weights, rows, chips, extra, bits)
         other = exchange(sent, "row", 1, row_size)
-        kept = product(0, pairs, turned, held, weights, rows, chips, extra, bits)
+        kept, turned = product(0, pairs, turned, held, weights, rows, chips, extra, bits)
         both = kept.astype(jnp.float32) + other.astype(jnp.float32)
         if coming is not None:
             coming, both = lax.optimization_barrier((coming, both))

time: 128 us -> 133 us (1.039)
  local copies, waits for them, and re-layouts: 10.1 us -> 17.3 us
  waiting for transfers between devices: 42.1 us -> 37.3 us
  starting transfers between devices: 52.4 us -> 55.7 us
    unnamed x14 -> x18, local copies, waits for them, and re-layouts: 6.57 us -> 13.8 us
    ppermute x48, waiting for transfers between devices: 42.1 us -> 37.3 us  [exchange(): return lax.ppermute(block, axis, [(i, i ^ mask) for i in range(size)])]
    ppermute x48, starting transfers between devices: 52.4 us -> 55.7 us  [exchange(): return lax.ppermute(block, axis, [(i, i ^ mask) for i in range(size)])]
  transfers between devices with their start and end apart: 48 -> 48, of which waited for: 23 -> 23; matrix products, arithmetic and copies ran while one was open for 2% -> 2% of each run, Pallas kernels for 10% -> 9%
where the time goes in v11:
time: 133 us; the launch traced here: 132 us
  starting transfers between devices  55.7 us (42%)
  waiting for transfers between devices  37.3 us (28%)
  Pallas kernels  19.7 us (15%)
  local copies, waits for them, and re-layouts  17.3 us (13%)
    ppermute x48, starting transfers between devices, exchange(): return lax.ppermute(block, axis, [(i, i ^ mask) for i in range(size)])  55.7 us
    ppermute x48, waiting for transfers between devices, exchange(): return lax.ppermute(block, axis, [(i, i ^ mask) for i in range(size)])  37.3 us
    unnamed x18, local copies, waits for them, and re-layouts  13.8 us
    pallas_call x12, Pallas kernels, product(): pl.pallas_call(functools.partial(product_kernel, half, rows, bits), out_s...  12.2 us
    pallas_call x1, Pallas kernels, prepare(): pl.pallas_call(functools.partial(prepare_kernel, tiles_per_owner, bits),...  5.78 us
  transfers between devices with their start and end apart: 48, of which 23 were waited for; matrix products, arithmetic and copies ran while one was open for 2% of the time, Pallas kernels for 9%

profile of v11, /device:TPU:0, one launch (start us, length us, event | category | flops | bytes accessed | tf_op | source)
XLA Modules:
  0.0 132.3 jit_solution(299036023025571316)
XLA Ops:
  1.4 3.1 %collective-permute-start = (bf16[512,128]{1,0:T(8,128)(2,1)S(1)}, bf16[512,128]{1,0:T(8,128)(2,1)S(1)}, u32[]{:S(2)}, u32[]{:S(2)}) collective-permute-start(bf16[512,128]{1,0:T(8,128)(2,1)S(1)} %copy.56.refs_0_), channel_id=1, source_target_pairs={{0,1},{1,0},{2,3},{3,2},{4,5},{5,4},{6,7},{7,6},{8,9},{9,8},{10,11... | collective-permute-start | bytes 393224 | tf_op jit(solution)/shard_map/ppermute | solution.py:326
  4.4 2.6 %collective-permute-start.1 = (bf16[512,128]{1,0:T(8,128)(2,1)S(1)}, bf16[512,128]{1,0:T(8,128)(2,1)S(1)}, u32[]{:S(2)}, u32[]{:S(2)}) collective-permute-start(bf16[512,128]{1,0:T(8,128)(2,1)S(1)} %copy.56.refs_0_), channel_id=1, source_target_pairs={{0,2},{1,3},{2,0},{3,1},{4,6},{5,7},{6,4},{7,5},{8,10},{9,11},{10,... | collective-permute-start | bytes 393224 | tf_op jit(solution)/shard_map/ppermute | solution.py:326
  7.2 2.2 %copy-done.6 = bf16[128,128,128]{2,1,0:T(8,128)(2,1)S(1)} copy-done((bf16[128,128,128]{2,1,0:T(8,128)(2,1)S(1)}, bf16[128,128,128]{2,1,0:T(8,128)(2,1)}, u32[]{:S(2)}) %copy-start.6) | copy-done | bytes 4194328
  10.7 5.8 %prepare.1 = (bf16[128,128,128]{2,1,0:T(8,128)(2,1)S(1)}, f32[2,4,16,128]{3,2,1,0:T(8,128)S(1)}, s32[20,8]{1,0:T(8,128)S(1)}) custom-call(s32[3]{0:T(128)S(1)} %pad_add_fusion.refs_4_.place_ref, s32[1,128]{1,0:T(1,128)S(1)} %copy-done.7, s32[1,32]{1,0:T(1,128)S(1)} %copy-done.8, bf16[128,128,128]{2,1,0:T(8,128)(2,1)S(1)} %copy-done.6), custom_call_target="tpu_custom_call" | custom-call | tf_op jit(solution)/shard_map/prepare/pallas_call | solution.py:178
  19.0 2.0 %copy-done = bf16[128,128,128]{2,1,0:T(8,128)(2,1)} copy-done((bf16[128,128,128]{2,1,0:T(8,128)(2,1)}, bf16[128,128,128]{2,1,0:T(8,128)(2,1)S(1)}, u32[]{:S(2)}) %copy-start) | copy-done | bytes 4194328
  21.1 3.0 %collective-permute-start.10 = (bf16[512,128]{1,0:T(8,128)(2,1)S(1)}, bf16[512,128]{1,0:T(8,128)(2,1)S(1)}, u32[]{:S(2)}, u32[]{:S(2)}) collective-permute-start(bf16[512,128]{1,0:T(8,128)(2,1)S(1)} %slice_bitcast_fusion.12.refs_0_), channel_id=1, source_target_pairs={{0,3},{1,2},{2,1},{3,0},{4,7},{5,6},{6,5},{7,4},{8,11},{9,10},{10,... | collective-permute-start | bytes 393224 | tf_op jit(solution)/shard_map/ppermute | solution.py:326
  24.6 2.2 %copy-done.1 = bf16[128,128,128]{2,1,0:T(8,128)(2,1)S(1)} copy-done((bf16[128,128,128]{2,1,0:T(8,128)(2,1)S(1)}, bf16[128,128,128]{2,1,0:T(8,128)(2,1)}, u32[]{:S(2)}) %copy-start.1) | copy-done | bytes 4194328
  27.9 2.0 %copy-done.2 = bf16[128,128,128]{2,1,0:T(8,128)(2,1)} copy-done((bf16[128,128,128]{2,1,0:T(8,128)(2,1)}, bf16[128,128,128]{2,1,0:T(8,128)(2,1)S(1)}, u32[]{:S(2)}) %copy-start.2) | copy-done | bytes 4194328
  31.6 1.9 %collective-permute-start.5 = (bf16[2,272,128]{2,1,0:T(8,128)(2,1)S(1)}, bf16[2,272,128]{2,1,0:T(8,128)(2,1)S(1)}, u32[]{:S(2)}, u32[]{:S(2)}) collective-permute-start(bf16[2,272,128]{2,1,0:T(8,128)(2,1)S(1)} %fusion.6), channel_id=1, source_target_pairs={{0,8},{4,12},{8,0},{12,4},{16,24},{20,28},{24,16},{28,20},{1,9},{5... | collective-permute-start | bytes 417800 | tf_op jit(solution)/shard_map/ppermute | solution.py:326
  37.2 1.8 %collective-permute-start.7 = (bf16[272,128]{1,0:T(8,128)(2,1)S(1)}, bf16[272,128]{1,0:T(8,128)(2,1)S(1)}, u32[]{:S(2)}, u32[]{:S(2)}) collective-permute-start(bf16[272,128]{1,0:T(8,128)(2,1)S(1)} %fusion.12), channel_id=1, source_target_pairs={{0,16},{4,20},{8,24},{12,28},{16,0},{20,4},{24,8},{28,12},{1,17},{... | collective-permute-start | bytes 208904 | tf_op jit(solution)/shard_map/ppermute | solution.py:326
  39.0 2.5 %collective-permute-done.7 = bf16[272,128]{1,0:T(8,128)(2,1)S(1)} collective-permute-done((bf16[272,128]{1,0:T(8,128)(2,1)S(1)}, bf16[272,128]{1,0:T(8,128)(2,1)S(1)}, u32[]{:S(2)}, u32[]{:S(2)}) %collective-permute-start.7) | collective-permute-done | bytes 69664 | tf_op jit(solution)/shard_map/ppermute | solution.py:326
  43.5 2.4 %collective-permute-start.17 = (bf16[512,128]{1,0:T(8,128)(2,1)S(1)}, bf16[512,128]{1,0:T(8,128)(2,1)S(1)}, u32[]{:S(2)}, u32[]{:S(2)}) collective-permute-start(bf16[512,128]{1,0:T(8,128)(2,1)S(1)} %update.6.refs_4_.refs_0_.refs_1_), channel_id=1, source_target_pairs={{0,2},{1,3},{2,0},{3,1},{4,6},{5,7},{6,4},{7,5},{8,10},{9,11},{10,... | collective-permute-start | bytes 393224 | tf_op jit(solution)/shard_map/ppermute | solution.py:326
  51.2 2.7 %collective-permute-done.12 = bf16[2,256,128]{2,1,0:T(8,128)(2,1)S(1)} collective-permute-done((bf16[2,256,128]{2,1,0:T(8,128)(2,1)S(1)}, bf16[2,256,128]{2,1,0:T(8,128)(2,1)S(1)}, u32[]{:S(2)}, u32[]{:S(2)}) %collective-permute-start.12) | collective-permute-done | bytes 131104 | tf_op jit(solution)/shard_map/ppermute | solution.py:326
  57.4 2.4 %collective-permute-done.14 = bf16[256,128]{1,0:T(8,128)(2,1)S(1)} collective-permute-done((bf16[256,128]{1,0:T(8,128)(2,1)S(1)}, bf16[256,128]{1,0:T(8,128)(2,1)S(1)}, u32[]{:S(2)}, u32[]{:S(2)}) %collective-permute-start.14) | collective-permute-done | bytes 65568 | tf_op jit(solution)/shard_map/ppermute | solution.py:326
  69.0 2.2 %collective-permute-done.20 = bf16[2,256,128]{2,1,0:T(8,128)(2,1)S(1)} collective-permute-done((bf16[2,256,128]{2,1,0:T(8,128)(2,1)S(1)}, bf16[2,256,128]{2,1,0:T(8,128)(2,1)S(1)}, u32[]{:S(2)}, u32[]{:S(2)}) %collective-permute-start.20) | collective-permute-done | bytes 131104 | tf_op jit(solution)/shard_map/ppermute | solution.py:326
  78.7 1.8 %collective-permute-start.33 = (bf16[512,128]{1,0:T(8,128)(2,1)S(1)}, bf16[512,128]{1,0:T(8,128)(2,1)S(1)}, u32[]{:S(2)}, u32[]{:S(2)}) collective-permute-start(bf16[512,128]{1,0:T(8,128)(2,1)S(1)} %update.8.refs_4_.refs_0_.refs_1_), channel_id=1, source_target_pairs={{0,2},{1,3},{2,0},{3,1},{4,6},{5,7},{6,4},{7,5},{8,10},{9,11},{10,... | collective-permute-start | bytes 393224 | tf_op jit(solution)/shard_map/ppermute | solution.py:326
  86.3 2.6 %collective-permute-done.28 = bf16[2,256,128]{2,1,0:T(8,128)(2,1)S(1)} collective-permute-done((bf16[2,256,128]{2,1,0:T(8,128)(2,1)S(1)}, bf16[2,256,128]{2,1,0:T(8,128)(2,1)S(1)}, u32[]{:S(2)}, u32[]{:S(2)}) %collective-permute-start.28) | collective-permute-done | bytes 131104 | tf_op jit(solution)/shard_map/ppermute | solution.py:326
  92.2 2.0 %collective-permute-done.30 = bf16[256,128]{1,0:T(8,128)(2,1)S(1)} collective-permute-done((bf16[256,128]{1,0:T(8,128)(2,1)S(1)}, bf16[256,128]{1,0:T(8,128)(2,1)S(1)}, u32[]{:S(2)}, u32[]{:S(2)}) %collective-permute-start.30) | collective-permute-done | bytes 65568 | tf_op jit(solution)/shard_map/ppermute | solution.py:326
  97.0 2.4 %collective-permute-start.42 = (bf16[512,128]{1,0:T(8,128)(2,1)S(1)}, bf16[512,128]{1,0:T(8,128)(2,1)S(1)}, u32[]{:S(2)}, u32[]{:S(2)}) collective-permute-start(bf16[512,128]{1,0:T(8,128)(2,1)S(1)} %update.9.refs_4_.refs_0_.refs_1_), channel_id=1, source_target_pairs={{0,3},{1,2},{2,1},{3,0},{4,7},{5,6},{6,5},{7,4},{8,11},{9,10},{10,... | collective-permute-start | bytes 393224 | tf_op jit(solution)/shard_map/ppermute | solution.py:326
  104.0 2.0 %collective-permute-done.36 = bf16[2,256,128]{2,1,0:T(8,128)(2,1)S(1)} collective-permute-done((bf16[2,256,128]{2,1,0:T(8,128)(2,1)S(1)}, bf16[2,256,128]{2,1,0:T(8,128)(2,1)S(1)}, u32[]{:S(2)}, u32[]{:S(2)}) %collective-permute-start.36) | collective-permute-done | bytes 131104 | tf_op jit(solution)/shard_map/ppermute | solution.py:326
  113.7 2.0 %copy-done.4 = bf16[128,128,128]{2,1,0:T(8,128)(2,1)} copy-done((bf16[128,128,128]{2,1,0:T(8,128)(2,1)}, bf16[128,128,128]{2,1,0:T(8,128)(2,1)S(1)}, u32[]{:S(2)}) %copy-start.4) | copy-done | bytes 4194328
  115.8 2.2 %copy-done.5 = bf16[128,128,128]{2,1,0:T(8,128)(2,1)S(1)} copy-done((bf16[128,128,128]{2,1,0:T(8,128)(2,1)S(1)}, bf16[128,128,128]{2,1,0:T(8,128)(2,1)}, u32[]{:S(2)}) %copy-start.5) | copy-done | bytes 4194328
  121.1 4.1 %collective-permute-done.44 = bf16[2,256,128]{2,1,0:T(8,128)(2,1)S(1)} collective-permute-done((bf16[2,256,128]{2,1,0:T(8,128)(2,1)S(1)}, bf16[2,256,128]{2,1,0:T(8,128)(2,1)S(1)}, u32[]{:S(2)}, u32[]{:S(2)}) %collective-permute-start.44) | collective-permute-done | bytes 131104 | tf_op jit(solution)/shard_map/ppermute | solution.py:326
  127.8 3.0 %collective-permute-done.46 = bf16[256,128]{1,0:T(8,128)(2,1)S(1)} collective-permute-done((bf16[256,128]{1,0:T(8,128)(2,1)S(1)}, bf16[256,128]{1,0:T(8,128)(2,1)S(1)}, u32[]{:S(2)}, u32[]{:S(2)}) %collective-permute-start.46) | collective-permute-done | bytes 65568 | tf_op jit(solution)/shard_map/ppermute | solution.py:326
  (202 shorter events, 70.5 us)
Async XLA Ops:
  1.4 15.1 %collective-permute-start = (bf16[512,128]{1,0:T(8,128)(2,1)S(1)}, bf16[512,128]{1,0:T(8,128)(2,1)S(1)}, u32[]{:S(2)}, u32[]{:S(2)}) collective-permute-start(bf16[512,128]{1,0:T(8,128)(2,1)S(1)} %copy.56.refs_0_), channel_id=1, source_target_pairs={{0,1},{1,0},{2,3},{3,2},{4,5},{5,4},{6,7},{7,6},{8,9},{9,8},{10,11... | collective-permute-start | bytes 393224 | tf_op jit(solution)/shard_map/ppermute | solution.py:326
  4.4 12.9 %collective-permute-start.1 = (bf16[512,128]{1,0:T(8,128)(2,1)S(1)}, bf16[512,128]{1,0:T(8,128)(2,1)S(1)}, u32[]{:S(2)}, u32[]{:S(2)}) collective-permute-start(bf16[512,128]{1,0:T(8,128)(2,1)S(1)} %copy.56.refs_0_), channel_id=1, source_target_pairs={{0,2},{1,3},{2,0},{3,1},{4,6},{5,7},{6,4},{7,5},{8,10},{9,11},{10,... | collective-permute-start | bytes 393224 | tf_op jit(solution)/shard_map/ppermute | solution.py:326
  7.0 10.3 %collective-permute-start.2 = (bf16[512,128]{1,0:T(8,128)(2,1)S(1)}, bf16[512,128]{1,0:T(8,128)(2,1)S(1)}, u32[]{:S(2)}, u32[]{:S(2)}) collective-permute-start(bf16[512,128]{1,0:T(8,128)(2,1)S(1)} %copy.56.refs_0_), channel_id=1, source_target_pairs={{0,3},{1,2},{2,1},{3,0},{4,7},{5,6},{6,5},{7,4},{8,11},{9,10},{10,... | collective-permute-start | bytes 393224 | tf_op jit(solution)/shard_map/ppermute | solution.py:326
  20.9 8.9 %collective-permute-start.3 = (bf16[4,528,128]{2,1,0:T(8,128)(2,1)S(1)}, bf16[4,528,128]{2,1,0:T(8,128)(2,1)S(1)}, u32[]{:S(2)}, u32[]{:S(2)}) collective-permute-start(bf16[4,528,128]{2,1,0:T(8,128)(2,1)S(1)} %get-tuple-element.55), channel_id=1, source_target_pairs={{0,4},{4,0},{8,12},{12,8},{16,20},{20,16},{24,28},{28,24},{1,5},{5... | collective-permute-start | bytes 1622024 | tf_op jit(solution)/shard_map/ppermute | solution.py:326
  21.1 20.7 %collective-permute-start.10 = (bf16[512,128]{1,0:T(8,128)(2,1)S(1)}, bf16[512,128]{1,0:T(8,128)(2,1)S(1)}, u32[]{:S(2)}, u32[]{:S(2)}) collective-permute-start(bf16[512,128]{1,0:T(8,128)(2,1)S(1)} %slice_bitcast_fusion.12.refs_0_), channel_id=1, source_target_pairs={{0,3},{1,2},{2,1},{3,0},{4,7},{5,6},{6,5},{7,4},{8,11},{9,10},{10,... | collective-permute-start | bytes 393224 | tf_op jit(solution)/shard_map/ppermute | solution.py:326
  24.1 17.7 %collective-permute-start.9 = (bf16[512,128]{1,0:T(8,128)(2,1)S(1)}, bf16[512,128]{1,0:T(8,128)(2,1)S(1)}, u32[]{:S(2)}, u32[]{:S(2)}) collective-permute-start(bf16[512,128]{1,0:T(8,128)(2,1)S(1)} %slice_bitcast_fusion.12.refs_0_), channel_id=1, source_target_pairs={{0,2},{1,3},{2,0},{3,1},{4,6},{5,7},{6,4},{7,5},{8,10},{9,11},{10,... | collective-permute-start | bytes 393224 | tf_op jit(solution)/shard_map/ppermute | solution.py:326
  30.0 5.4 %collective-permute-start.4 = (bf16[2,256,128]{2,1,0:T(8,128)(2,1)S(1)}, bf16[2,256,128]{2,1,0:T(8,128)(2,1)S(1)}, u32[]{:S(2)}, u32[]{:S(2)}) collective-permute-start(bf16[2,256,128]{2,1,0:T(8,128)(2,1)S(1)} %slice.414), channel_id=1, source_target_pairs={{0,16},{4,20},{8,24},{12,28},{16,0},{20,4},{24,8},{28,12},{1,17},{... | collective-permute-start | bytes 393224 | tf_op jit(solution)/shard_map/ppermute | solution.py:326
  31.6 5.5 %collective-permute-start.5 = (bf16[2,272,128]{2,1,0:T(8,128)(2,1)S(1)}, bf16[2,272,128]{2,1,0:T(8,128)(2,1)S(1)}, u32[]{:S(2)}, u32[]{:S(2)}) collective-permute-start(bf16[2,272,128]{2,1,0:T(8,128)(2,1)S(1)} %fusion.6), channel_id=1, source_target_pairs={{0,8},{4,12},{8,0},{12,4},{16,24},{20,28},{24,16},{28,20},{1,9},{5... | collective-permute-start | bytes 417800 | tf_op jit(solution)/shard_map/ppermute | solution.py:326
  33.5 8.4 %collective-permute-start.8 = (bf16[512,128]{1,0:T(8,128)(2,1)S(1)}, bf16[512,128]{1,0:T(8,128)(2,1)S(1)}, u32[]{:S(2)}, u32[]{:S(2)}) collective-permute-start(bf16[512,128]{1,0:T(8,128)(2,1)S(1)} %slice_bitcast_fusion.12.refs_0_), channel_id=1, source_target_pairs={{0,1},{1,0},{2,3},{3,2},{4,5},{5,4},{6,7},{7,6},{8,9},{9,8},{10,11... | collective-permute-start | bytes 393224 | tf_op jit(solution)/shard_map/ppermute | solution.py:326
  35.5 6.1 %collective-permute-start.6 = (bf16[256,128]{1,0:T(8,128)(2,1)S(1)}, bf16[256,128]{1,0:T(8,128)(2,1)S(1)}, u32[]{:S(2)}, u32[]{:S(2)}) collective-permute-start(bf16[256,128]{1,0:T(8,128)(2,1)S(1)} %fusion.13), channel_id=1, source_target_pairs={{0,8},{4,12},{8,0},{12,4},{16,24},{20,28},{24,16},{28,20},{1,9},{5... | collective-permute-start | bytes 196616 | tf_op jit(solution)/shard_map/ppermute | solution.py:326
  43.5 17.1 %collective-permute-start.17 = (bf16[512,128]{1,0:T(8,128)(2,1)S(1)}, bf16[512,128]{1,0:T(8,128)(2,1)S(1)}, u32[]{:S(2)}, u32[]{:S(2)}) collective-permute-start(bf16[512,128]{1,0:T(8,128)(2,1)S(1)} %update.6.refs_4_.refs_0_.refs_1_), channel_id=1, source_target_pairs={{0,2},{1,3},{2,0},{3,1},{4,6},{5,7},{6,4},{7,5},{8,10},{9,11},{10,... | collective-permute-start | bytes 393224 | tf_op jit(solution)/shard_map/ppermute | solution.py:326
  46.0 14.7 %collective-permute-start.18 = (bf16[512,128]{1,0:T(8,128)(2,1)S(1)}, bf16[512,128]{1,0:T(8,128)(2,1)S(1)}, u32[]{:S(2)}, u32[]{:S(2)}) collective-permute-start(bf16[512,128]{1,0:T(8,128)(2,1)S(1)} %update.6.refs_4_.refs_0_.refs_1_), channel_id=1, source_target_pairs={{0,3},{1,2},{2,1},{3,0},{4,7},{5,6},{6,5},{7,4},{8,11},{9,10},{10,... | collective-permute-start | bytes 393224 | tf_op jit(solution)/shard_map/ppermute | solution.py:326
  51.2 9.5 %collective-permute-start.16 = (bf16[512,128]{1,0:T(8,128)(2,1)S(1)}, bf16[512,128]{1,0:T(8,128)(2,1)S(1)}, u32[]{:S(2)}, u32[]{:S(2)}) collective-permute-start(bf16[512,128]{1,0:T(8,128)(2,1)S(1)} %update.6.refs_4_.refs_0_.refs_1_), channel_id=1, source_target_pairs={{0,1},{1,0},{2,3},{3,2},{4,5},{5,4},{6,7},{7,6},{8,9},{9,8},{10,11... | collective-permute-start | bytes 393224 | tf_op jit(solution)/shard_map/ppermute | solution.py:326
  61.9 15.6 %collective-permute-start.25 = (bf16[512,128]{1,0:T(8,128)(2,1)S(1)}, bf16[512,128]{1,0:T(8,128)(2,1)S(1)}, u32[]{:S(2)}, u32[]{:S(2)}) collective-permute-start(bf16[512,128]{1,0:T(8,128)(2,1)S(1)} %update.7.refs_4_.refs_0_.refs_1_), channel_id=1, source_target_pairs={{0,2},{1,3},{2,0},{3,1},{4,6},{5,7},{6,4},{7,5},{8,10},{9,11},{10,... | collective-permute-start | bytes 393224 | tf_op jit(solution)/shard_map/ppermute | solution.py:326
  62.8 14.7 %collective-permute-start.26 = (bf16[512,128]{1,0:T(8,128)(2,1)S(1)}, bf16[512,128]{1,0:T(8,128)(2,1)S(1)}, u32[]{:S(2)}, u32[]{:S(2)}) collective-permute-start(bf16[512,128]{1,0:T(8,128)(2,1)S(1)} %update.7.refs_4_.refs_0_.refs_1_), channel_id=1, source_target_pairs={{0,3},{1,2},{2,1},{3,0},{4,7},{5,6},{6,5},{7,4},{8,11},{9,10},{10,... | collective-permute-start | bytes 393224 | tf_op jit(solution)/shard_map/ppermute | solution.py:326
  67.9 9.6 %collective-permute-start.24 = (bf16[512,128]{1,0:T(8,128)(2,1)S(1)}, bf16[512,128]{1,0:T(8,128)(2,1)S(1)}, u32[]{:S(2)}, u32[]{:S(2)}) collective-permute-start(bf16[512,128]{1,0:T(8,128)(2,1)S(1)} %update.7.refs_4_.refs_0_.refs_1_), channel_id=1, source_target_pairs={{0,1},{1,0},{2,3},{3,2},{4,5},{5,4},{6,7},{7,6},{8,9},{9,8},{10,11... | collective-permute-start | bytes 393224 | tf_op jit(solution)/shard_map/ppermute | solution.py:326
  78.7 16.5 %collective-permute-start.33 = (bf16[512,128]{1,0:T(8,128)(2,1)S(1)}, bf16[512,128]{1,0:T(8,128)(2,1)S(1)}, u32[]{:S(2)}, u32[]{:S(2)}) collective-permute-start(bf16[512,128]{1,0:T(8,128)(2,1)S(1)} %update.8.refs_4_.refs_0_.refs_1_), channel_id=1, source_target_pairs={{0,2},{1,3},{2,0},{3,1},{4,6},{5,7},{6,4},{7,5},{8,10},{9,11},{10,... | collective-permute-start | bytes 393224 | tf_op jit(solution)/shard_map/ppermute | solution.py:326
  80.5 14.7 %collective-permute-start.34 = (bf16[512,128]{1,0:T(8,128)(2,1)S(1)}, bf16[512,128]{1,0:T(8,128)(2,1)S(1)}, u32[]{:S(2)}, u32[]{:S(2)}) collective-permute-start(bf16[512,128]{1,0:T(8,128)(2,1)S(1)} %update.8.refs_4_.refs_0_.refs_1_), channel_id=1, source_target_pairs={{0,3},{1,2},{2,1},{3,0},{4,7},{5,6},{6,5},{7,4},{8,11},{9,10},{10,... | collective-permute-start | bytes 393224 | tf_op jit(solution)/shard_map/ppermute | solution.py:326
  85.7 9.5 %collective-permute-start.32 = (bf16[512,128]{1,0:T(8,128)(2,1)S(1)}, bf16[512,128]{1,0:T(8,128)(2,1)S(1)}, u32[]{:S(2)}, u32[]{:S(2)}) collective-permute-start(bf16[512,128]{1,0:T(8,128)(2,1)S(1)} %update.8.refs_4_.refs_0_.refs_1_), channel_id=1, source_target_pairs={{0,1},{1,0},{2,3},{3,2},{4,5},{5,4},{6,7},{7,6},{8,9},{9,8},{10,11... | collective-permute-start | bytes 393224 | tf_op jit(solution)/shard_map/ppermute | solution.py:326
  96.4 16.2 %collective-permute-start.41 = (bf16[512,128]{1,0:T(8,128)(2,1)S(1)}, bf16[512,128]{1,0:T(8,128)(2,1)S(1)}, u32[]{:S(2)}, u32[]{:S(2)}) collective-permute-start(bf16[512,128]{1,0:T(8,128)(2,1)S(1)} %update.9.refs_4_.refs_0_.refs_1_), channel_id=1, source_target_pairs={{0,2},{1,3},{2,0},{3,1},{4,6},{5,7},{6,4},{7,5},{8,10},{9,11},{10,... | collective-permute-start | bytes 393224 | tf_op jit(solution)/shard_map/ppermute | solution.py:326
  97.0 15.6 %collective-permute-start.42 = (bf16[512,128]{1,0:T(8,128)(2,1)S(1)}, bf16[512,128]{1,0:T(8,128)(2,1)S(1)}, u32[]{:S(2)}, u32[]{:S(2)}) collective-permute-start(bf16[512,128]{1,0:T(8,128)(2,1)S(1)} %update.9.refs_4_.refs_0_.refs_1_), channel_id=1, source_target_pairs={{0,3},{1,2},{2,1},{3,0},{4,7},{5,6},{6,5},{7,4},{8,11},{9,10},{10,... | collective-permute-start | bytes 393224 | tf_op jit(solution)/shard_map/ppermute | solution.py:326
  103.1 9.5 %collective-permute-start.40 = (bf16[512,128]{1,0:T(8,128)(2,1)S(1)}, bf16[512,128]{1,0:T(8,128)(2,1)S(1)}, u32[]{:S(2)}, u32[]{:S(2)}) collective-permute-start(bf16[512,128]{1,0:T(8,128)(2,1)S(1)} %update.9.refs_4_.refs_0_.refs_1_), channel_id=1, source_target_pairs={{0,1},{1,0},{2,3},{3,2},{4,5},{5,4},{6,7},{7,6},{8,9},{9,8},{10,11... | collective-permute-start | bytes 393224 | tf_op jit(solution)/shard_map/ppermute | solution.py:326
  119.2 6.0 %collective-permute-start.44 = (bf16[2,256,128]{2,1,0:T(8,128)(2,1)S(1)}, bf16[2,256,128]{2,1,0:T(8,128)(2,1)S(1)}, u32[]{:S(2)}, u32[]{:S(2)}) collective-permute-start(bf16[2,256,128]{2,1,0:T(8,128)(2,1)S(1)} %slice.409), channel_id=1, source_target_pairs={{0,16},{4,20},{8,24},{12,28},{16,0},{20,4},{24,8},{28,12},{1,17},{... | collective-permute-start | bytes 393224 | tf_op jit(solution)/shard_map/ppermute | solution.py:326
  120.7 5.7 %collective-permute-start.45 = (bf16[2,256,128]{2,1,0:T(8,128)(2,1)S(1)}, bf16[2,256,128]{2,1,0:T(8,128)(2,1)S(1)}, u32[]{:S(2)}, u32[]{:S(2)}) collective-permute-start(bf16[2,256,128]{2,1,0:T(8,128)(2,1)S(1)} %fusion.11), channel_id=1, source_target_pairs={{0,8},{4,12},{8,0},{12,4},{16,24},{20,28},{24,16},{28,20},{1,9},{5... | collective-permute-start | bytes 393224 | tf_op jit(solution)/shard_map/ppermute | solution.py:326
  (33 other events, 136.6 us)

commit v12 on v9

--- a/solution.py
+++ b/solution.py
@@ -205,6 +205,29 @@
     )(place, tile_src, row_counts, tile_vals)
 
 
+def pack_kernel(blocks, features_ref, *part_refs):
+    rows = features_ref.shape[0] // blocks
+    piece = features_ref.shape[1] // len(part_refs)
+    for chunk, part_ref in enumerate(part_refs):
+        lanes = slice(chunk * piece, (chunk + 1) * piece)
+        part_ref[...] = jnp.concatenate(
+            [features_ref[b * rows : (b + 1) * rows, lanes] for b in range(blocks)], axis=1
+        )
+
+
+def pack(features, blocks):
+    rows = features.shape[0] // blocks
+    width = features.shape[1] // CHUNKS * blocks
+    return pl.pallas_call(
+        functools.partial(pack_kernel, blocks),
+        out_shape=[jax.ShapeDtypeStruct((rows, width), features.dtype)] * CHUNKS,
+        in_specs=vmem(1),
+        out_specs=vmem(CHUNKS),
+        compiler_params=pltpu.CompilerParams(vmem_limit_bytes=4 * 2**20),
+        name="pack",
+    )(features)
+
+
 def assemble_kernel(packed, blocks, *refs):
     block_refs = refs[:blocks]
     held_ref = refs[blocks + 1]
@@ -373,8 +396,7 @@
     bits = code_bits(tile_vals.shape[0], source_tiles, dest_count // 2)
     place = jnp.stack([my_row, my_col, jnp.int32(source_tiles)])
 
-    parts = features.reshape(blocks, rows, CHUNKS, piece).transpose(2, 1, 0, 3)
-    parts = parts.reshape(CHUNKS, rows, blocks * piece)
+    parts = pack(features, blocks)
 
     turned, weights, pairs = prepare(
         place, tile_src, row_counts, tile_vals, row_size, tiles_per_owner, bits
@@ -398,8 +420,7 @@
         if first:
             iterates[chunk] = restarts[chunk] = own[0]
         if phase == 0:
-            held, parts = lax.optimization_barrier((held, parts))
-            coming = parts[1]
+            held, coming = lax.optimization_barrier((held, parts[1]))
         elif phase + 1 < ITERS * CHUNKS:
             coming = iterates[after]
         else:
@@ -422,6 +443,7 @@
             )
         pending = (kept, [arrived], iterates[chunk], restarts[chunk], scale)
     iterates[chunk] = update(*pending)
+    iterates = lax.optimization_barrier(iterates)
     out = jnp.stack(iterates).reshape(CHUNKS, rows, blocks, piece).transpose(1, 2, 0, 3)
     return out.reshape(rows, CHUNKS * width)
 

time: 128 us -> 123 us (0.961); the launches traced: 127 us -> 123 us
  local copies, waits for them, and re-layouts: 10.1 us -> 5.35 us
    unnamed x14 -> x7, local copies, waits for them, and re-layouts: 6.57 us -> 3.44 us
  transfers between devices with their start and end apart: 48 -> 48, of which waited for: 23 -> 24; matrix products, arithmetic and copies ran while one was open for 2% -> 1% of each run, Pallas kernels for 10% -> 10%
where the time goes in v12:
time: 123 us
  starting transfers between devices  53.5 us (43%)
  waiting for transfers between devices  41.9 us (34%)
  Pallas kernels  20.5 us (17%)
  local copies, waits for them, and re-layouts  5.35 us (4%)
  other arithmetic  1.23 us (1%)
    ppermute x48, starting transfers between devices, exchange(): return lax.ppermute(block, axis, [(i, i ^ mask) for i in range(size)])  53.5 us
    ppermute x48, waiting for transfers between devices, exchange(): return lax.ppermute(block, axis, [(i, i ^ mask) for i in range(size)])  41.9 us
    pallas_call x12, Pallas kernels, product(): pl.pallas_call(functools.partial(product_kernel, half, rows, bits), out_s...  12.3 us
    pallas_call x1, Pallas kernels, prepare(): pl.pallas_call(functools.partial(prepare_kernel, tiles_per_owner, bits),...  6.17 us
    unnamed x7, local copies, waits for them, and re-layouts  3.44 us
  transfers between devices with their start and end apart: 48, of which 24 were waited for; matrix products, arithmetic and copies ran while one was open for 1% of the time, Pallas kernels for 10%

profile of v12, /device:TPU:0, one launch (start us, length us, event | category | flops | bytes accessed | tf_op | source)
XLA Modules:
  0.0 123.5 jit_solution(100855720793094783)
XLA Ops:
  1.5 3.1 %collective-permute-start = (bf16[512,128]{1,0:T(8,128)(2,1)S(1)}, bf16[512,128]{1,0:T(8,128)(2,1)S(1)}, u32[]{:S(2)}, u32[]{:S(2)}) collective-permute-start(bf16[512,128]{1,0:T(8,128)(2,1)S(1)} %get-tuple-element.28.refs_0_), channel_id=1, source_target_pairs={{0,1},{1,0},{2,3},{3,2},{4,5},{5,4},{6,7},{7,6},{8,9},{9,8},{10,11... | collective-permute-start | bytes 393224 | tf_op jit(solution)/shard_map/ppermute | solution.py:354
  4.6 2.6 %collective-permute-start.1 = (bf16[512,128]{1,0:T(8,128)(2,1)S(1)}, bf16[512,128]{1,0:T(8,128)(2,1)S(1)}, u32[]{:S(2)}, u32[]{:S(2)}) collective-permute-start(bf16[512,128]{1,0:T(8,128)(2,1)S(1)} %get-tuple-element.28.refs_0_), channel_id=1, source_target_pairs={{0,2},{1,3},{2,0},{3,1},{4,6},{5,7},{6,4},{7,5},{8,10},{9,11},{10,... | collective-permute-start | bytes 393224 | tf_op jit(solution)/shard_map/ppermute | solution.py:354
  7.3 2.2 %copy-done = bf16[128,128,128]{2,1,0:T(8,128)(2,1)S(1)} copy-done((bf16[128,128,128]{2,1,0:T(8,128)(2,1)S(1)}, bf16[128,128,128]{2,1,0:T(8,128)(2,1)}, u32[]{:S(2)}) %copy-start) | copy-done | bytes 4194328
  9.5 6.2 %prepare.1 = (bf16[128,128,128]{2,1,0:T(8,128)(2,1)S(1)}, f32[2,4,16,128]{3,2,1,0:T(8,128)S(1)}, s32[20,8]{1,0:T(8,128)S(1)}) custom-call(s32[3]{0:T(128)S(1)} %pad_add_fusion.refs_4_.place_ref, s32[1,128]{1,0:T(1,128)S(1)} %copy-done.1, s32[1,32]{1,0:T(1,128)S(1)} %copy-done.2, bf16[128,128,128]{2,1,0:T(8,128)(2,1)S(1)} %copy-done), custom_call_target="tpu_custom_call" | custom-call | tf_op jit(solution)/shard_map/prepare/pallas_call | solution.py:187
  15.7 1.9 %collective-permute-done.1.refs_2_ = bf16[512,128]{1,0:T(8,128)(2,1)S(1)} collective-permute-done((bf16[512,128]{1,0:T(8,128)(2,1)S(1)}, bf16[512,128]{1,0:T(8,128)(2,1)S(1)}, u32[]{:S(2)}, u32[]{:S(2)}) %collective-permute-start.1) | collective-permute-done | bytes 131104 | tf_op jit(solution)/shard_map/ppermute | solution.py:354
  19.2 2.4 %collective-permute-start.10 = (bf16[512,128]{1,0:T(8,128)(2,1)S(1)}, bf16[512,128]{1,0:T(8,128)(2,1)S(1)}, u32[]{:S(2)}, u32[]{:S(2)}) collective-permute-start(bf16[512,128]{1,0:T(8,128)(2,1)S(1)} %get-tuple-element.38.refs_0_), channel_id=1, source_target_pairs={{0,3},{1,2},{2,1},{3,0},{4,7},{5,6},{6,5},{7,4},{8,11},{9,10},{10,... | collective-permute-start | bytes 393224 | tf_op jit(solution)/shard_map/ppermute | solution.py:354
  23.9 1.8 %collective-permute-start.4 = (bf16[2,256,128]{2,1,0:T(8,128)(2,1)S(1)}, bf16[2,256,128]{2,1,0:T(8,128)(2,1)S(1)}, u32[]{:S(2)}, u32[]{:S(2)}) collective-permute-start(bf16[2,256,128]{2,1,0:T(8,128)(2,1)S(1)} %slice.401), channel_id=1, source_target_pairs={{0,16},{4,20},{8,24},{12,28},{16,0},{20,4},{24,8},{28,12},{1,17},{... | collective-permute-start | bytes 393224 | tf_op jit(solution)/shard_map/ppermute | solution.py:354
  29.5 1.8 %collective-permute-start.6 = (bf16[256,128]{1,0:T(8,128)(2,1)S(1)}, bf16[256,128]{1,0:T(8,128)(2,1)S(1)}, u32[]{:S(2)}, u32[]{:S(2)}) collective-permute-start(bf16[256,128]{1,0:T(8,128)(2,1)S(1)} %fusion.13), channel_id=1, source_target_pairs={{0,8},{4,12},{8,0},{12,4},{16,24},{20,28},{24,16},{28,20},{1,9},{5... | collective-permute-start | bytes 196616 | tf_op jit(solution)/shard_map/ppermute | solution.py:354
  32.6 3.2 %collective-permute-done.7 = bf16[272,128]{1,0:T(8,128)(2,1)S(1)} collective-permute-done((bf16[272,128]{1,0:T(8,128)(2,1)S(1)}, bf16[272,128]{1,0:T(8,128)(2,1)S(1)}, u32[]{:S(2)}, u32[]{:S(2)}) %collective-permute-start.7) | collective-permute-done | bytes 69664 | tf_op jit(solution)/shard_map/ppermute | solution.py:354
  37.7 1.8 %collective-permute-start.17 = (bf16[512,128]{1,0:T(8,128)(2,1)S(1)}, bf16[512,128]{1,0:T(8,128)(2,1)S(1)}, u32[]{:S(2)}, u32[]{:S(2)}) collective-permute-start(bf16[512,128]{1,0:T(8,128)(2,1)S(1)} %update.6.refs_4_.refs_0_.refs_1_), channel_id=1, source_target_pairs={{0,2},{1,3},{2,0},{3,1},{4,6},{5,7},{6,4},{7,5},{8,10},{9,11},{10,... | collective-permute-start | bytes 393224 | tf_op jit(solution)/shard_map/ppermute | solution.py:354
  44.8 2.7 %collective-permute-done.12 = bf16[2,256,128]{2,1,0:T(8,128)(2,1)S(1)} collective-permute-done((bf16[2,256,128]{2,1,0:T(8,128)(2,1)S(1)}, bf16[2,256,128]{2,1,0:T(8,128)(2,1)S(1)}, u32[]{:S(2)}, u32[]{:S(2)}) %collective-permute-start.12) | collective-permute-done | bytes 131104 | tf_op jit(solution)/shard_map/ppermute | solution.py:354
  50.6 2.4 %collective-permute-done.14 = bf16[256,128]{1,0:T(8,128)(2,1)S(1)} collective-permute-done((bf16[256,128]{1,0:T(8,128)(2,1)S(1)}, bf16[256,128]{1,0:T(8,128)(2,1)S(1)}, u32[]{:S(2)}, u32[]{:S(2)}) %collective-permute-start.14) | collective-permute-done | bytes 65568 | tf_op jit(solution)/shard_map/ppermute | solution.py:354
  55.2 2.4 %collective-permute-start.25 = (bf16[512,128]{1,0:T(8,128)(2,1)S(1)}, bf16[512,128]{1,0:T(8,128)(2,1)S(1)}, u32[]{:S(2)}, u32[]{:S(2)}) collective-permute-start(bf16[512,128]{1,0:T(8,128)(2,1)S(1)} %update.7.refs_4_.refs_0_.refs_1_), channel_id=1, source_target_pairs={{0,2},{1,3},{2,0},{3,1},{4,6},{5,7},{6,4},{7,5},{8,10},{9,11},{10,... | collective-permute-start | bytes 393224 | tf_op jit(solution)/shard_map/ppermute | solution.py:354
  62.5 2.9 %collective-permute-done.20 = bf16[2,256,128]{2,1,0:T(8,128)(2,1)S(1)} collective-permute-done((bf16[2,256,128]{2,1,0:T(8,128)(2,1)S(1)}, bf16[2,256,128]{2,1,0:T(8,128)(2,1)S(1)}, u32[]{:S(2)}, u32[]{:S(2)}) %collective-permute-start.20) | collective-permute-done | bytes 131104 | tf_op jit(solution)/shard_map/ppermute | solution.py:354
  69.1 1.8 %collective-permute-done.22 = bf16[256,128]{1,0:T(8,128)(2,1)S(1)} collective-permute-done((bf16[256,128]{1,0:T(8,128)(2,1)S(1)}, bf16[256,128]{1,0:T(8,128)(2,1)S(1)}, u32[]{:S(2)}, u32[]{:S(2)}) %collective-permute-start.22) | collective-permute-done | bytes 65568 | tf_op jit(solution)/shard_map/ppermute | solution.py:354
  72.9 2.4 %collective-permute-start.33 = (bf16[512,128]{1,0:T(8,128)(2,1)S(1)}, bf16[512,128]{1,0:T(8,128)(2,1)S(1)}, u32[]{:S(2)}, u32[]{:S(2)}) collective-permute-start(bf16[512,128]{1,0:T(8,128)(2,1)S(1)} %update.8.refs_4_.refs_0_.refs_1_), channel_id=1, source_target_pairs={{0,2},{1,3},{2,0},{3,1},{4,6},{5,7},{6,4},{7,5},{8,10},{9,11},{10,... | collective-permute-start | bytes 393224 | tf_op jit(solution)/shard_map/ppermute | solution.py:354
  77.1 1.8 %collective-permute-start.28 = (bf16[2,256,128]{2,1,0:T(8,128)(2,1)S(1)}, bf16[2,256,128]{2,1,0:T(8,128)(2,1)S(1)}, u32[]{:S(2)}, u32[]{:S(2)}) collective-permute-start(bf16[2,256,128]{2,1,0:T(8,128)(2,1)S(1)} %slice.398), channel_id=1, source_target_pairs={{0,16},{4,20},{8,24},{12,28},{16,0},{20,4},{24,8},{28,12},{1,17},{... | collective-permute-start | bytes 393224 | tf_op jit(solution)/shard_map/ppermute | solution.py:354
  79.8 2.6 %collective-permute-done.28 = bf16[2,256,128]{2,1,0:T(8,128)(2,1)S(1)} collective-permute-done((bf16[2,256,128]{2,1,0:T(8,128)(2,1)S(1)}, bf16[2,256,128]{2,1,0:T(8,128)(2,1)S(1)}, u32[]{:S(2)}, u32[]{:S(2)}) %collective-permute-start.28) | collective-permute-done | bytes 131104 | tf_op jit(solution)/shard_map/ppermute | solution.py:354
  86.0 2.4 %collective-permute-done.30 = bf16[256,128]{1,0:T(8,128)(2,1)S(1)} collective-permute-done((bf16[256,128]{1,0:T(8,128)(2,1)S(1)}, bf16[256,128]{1,0:T(8,128)(2,1)S(1)}, u32[]{:S(2)}, u32[]{:S(2)}) %collective-permute-start.30) | collective-permute-done | bytes 65568 | tf_op jit(solution)/shard_map/ppermute | solution.py:354
  90.0 2.4 %collective-permute-start.41 = (bf16[512,128]{1,0:T(8,128)(2,1)S(1)}, bf16[512,128]{1,0:T(8,128)(2,1)S(1)}, u32[]{:S(2)}, u32[]{:S(2)}) collective-permute-start(bf16[512,128]{1,0:T(8,128)(2,1)S(1)} %update.9.refs_4_.refs_0_.refs_1_), channel_id=1, source_target_pairs={{0,2},{1,3},{2,0},{3,1},{4,6},{5,7},{6,4},{7,5},{8,10},{9,11},{10,... | collective-permute-start | bytes 393224 | tf_op jit(solution)/shard_map/ppermute | solution.py:354
  97.9 2.9 %collective-permute-done.36 = bf16[2,256,128]{2,1,0:T(8,128)(2,1)S(1)} collective-permute-done((bf16[2,256,128]{2,1,0:T(8,128)(2,1)S(1)}, bf16[2,256,128]{2,1,0:T(8,128)(2,1)S(1)}, u32[]{:S(2)}, u32[]{:S(2)}) %collective-permute-start.36) | collective-permute-done | bytes 131104 | tf_op jit(solution)/shard_map/ppermute | solution.py:354
  110.4 1.8 %collective-permute-start.44 = (bf16[2,256,128]{2,1,0:T(8,128)(2,1)S(1)}, bf16[2,256,128]{2,1,0:T(8,128)(2,1)S(1)}, u32[]{:S(2)}, u32[]{:S(2)}) collective-permute-start(bf16[2,256,128]{2,1,0:T(8,128)(2,1)S(1)} %slice.396), channel_id=1, source_target_pairs={{0,16},{4,20},{8,24},{12,28},{16,0},{20,4},{24,8},{28,12},{1,17},{... | collective-permute-start | bytes 393224 | tf_op jit(solution)/shard_map/ppermute | solution.py:354
  112.6 3.4 %collective-permute-done.44 = bf16[2,256,128]{2,1,0:T(8,128)(2,1)S(1)} collective-permute-done((bf16[2,256,128]{2,1,0:T(8,128)(2,1)S(1)}, bf16[2,256,128]{2,1,0:T(8,128)(2,1)S(1)}, u32[]{:S(2)}, u32[]{:S(2)}) %collective-permute-start.44) | collective-permute-done | bytes 131104 | tf_op jit(solution)/shard_map/ppermute | solution.py:354
  119.2 2.7 %collective-permute-done.46 = bf16[256,128]{1,0:T(8,128)(2,1)S(1)} collective-permute-done((bf16[256,128]{1,0:T(8,128)(2,1)S(1)}, bf16[256,128]{1,0:T(8,128)(2,1)S(1)}, u32[]{:S(2)}, u32[]{:S(2)}) %collective-permute-start.46) | collective-permute-done | bytes 65568 | tf_op jit(solution)/shard_map/ppermute | solution.py:354
  (185 shorter events, 61.0 us)
Async XLA Ops:
  1.5 14.1 %collective-permute-start = (bf16[512,128]{1,0:T(8,128)(2,1)S(1)}, bf16[512,128]{1,0:T(8,128)(2,1)S(1)}, u32[]{:S(2)}, u32[]{:S(2)}) collective-permute-start(bf16[512,128]{1,0:T(8,128)(2,1)S(1)} %get-tuple-element.28.refs_0_), channel_id=1, source_target_pairs={{0,1},{1,0},{2,3},{3,2},{4,5},{5,4},{6,7},{7,6},{8,9},{9,8},{10,11... | collective-permute-start | bytes 393224 | tf_op jit(solution)/shard_map/ppermute | solution.py:354
  4.6 12.9 %collective-permute-start.1 = (bf16[512,128]{1,0:T(8,128)(2,1)S(1)}, bf16[512,128]{1,0:T(8,128)(2,1)S(1)}, u32[]{:S(2)}, u32[]{:S(2)}) collective-permute-start(bf16[512,128]{1,0:T(8,128)(2,1)S(1)} %get-tuple-element.28.refs_0_), channel_id=1, source_target_pairs={{0,2},{1,3},{2,0},{3,1},{4,6},{5,7},{6,4},{7,5},{8,10},{9,11},{10,... | collective-permute-start | bytes 393224 | tf_op jit(solution)/shard_map/ppermute | solution.py:354
  7.2 10.3 %collective-permute-start.2 = (bf16[512,128]{1,0:T(8,128)(2,1)S(1)}, bf16[512,128]{1,0:T(8,128)(2,1)S(1)}, u32[]{:S(2)}, u32[]{:S(2)}) collective-permute-start(bf16[512,128]{1,0:T(8,128)(2,1)S(1)} %get-tuple-element.28.refs_0_), channel_id=1, source_target_pairs={{0,3},{1,2},{2,1},{3,0},{4,7},{5,6},{6,5},{7,4},{8,11},{9,10},{10,... | collective-permute-start | bytes 393224 | tf_op jit(solution)/shard_map/ppermute | solution.py:354
  19.2 16.8 %collective-permute-start.10 = (bf16[512,128]{1,0:T(8,128)(2,1)S(1)}, bf16[512,128]{1,0:T(8,128)(2,1)S(1)}, u32[]{:S(2)}, u32[]{:S(2)}) collective-permute-start(bf16[512,128]{1,0:T(8,128)(2,1)S(1)} %get-tuple-element.38.refs_0_), channel_id=1, source_target_pairs={{0,3},{1,2},{2,1},{3,0},{4,7},{5,6},{6,5},{7,4},{8,11},{9,10},{10,... | collective-permute-start | bytes 393224 | tf_op jit(solution)/shard_map/ppermute | solution.py:354
  21.6 14.5 %collective-permute-start.9 = (bf16[512,128]{1,0:T(8,128)(2,1)S(1)}, bf16[512,128]{1,0:T(8,128)(2,1)S(1)}, u32[]{:S(2)}, u32[]{:S(2)}) collective-permute-start(bf16[512,128]{1,0:T(8,128)(2,1)S(1)} %get-tuple-element.38.refs_0_), channel_id=1, source_target_pairs={{0,2},{1,3},{2,0},{3,1},{4,6},{5,7},{6,4},{7,5},{8,10},{9,11},{10,... | collective-permute-start | bytes 393224 | tf_op jit(solution)/shard_map/ppermute | solution.py:354
  23.9 5.6 %collective-permute-start.4 = (bf16[2,256,128]{2,1,0:T(8,128)(2,1)S(1)}, bf16[2,256,128]{2,1,0:T(8,128)(2,1)S(1)}, u32[]{:S(2)}, u32[]{:S(2)}) collective-permute-start(bf16[2,256,128]{2,1,0:T(8,128)(2,1)S(1)} %slice.401), channel_id=1, source_target_pairs={{0,16},{4,20},{8,24},{12,28},{16,0},{20,4},{24,8},{28,12},{1,17},{... | collective-permute-start | bytes 393224 | tf_op jit(solution)/shard_map/ppermute | solution.py:354
  25.8 5.6 %collective-permute-start.5 = (bf16[2,272,128]{2,1,0:T(8,128)(2,1)S(1)}, bf16[2,272,128]{2,1,0:T(8,128)(2,1)S(1)}, u32[]{:S(2)}, u32[]{:S(2)}) collective-permute-start(bf16[2,272,128]{2,1,0:T(8,128)(2,1)S(1)} %fusion.6), channel_id=1, source_target_pairs={{0,8},{4,12},{8,0},{12,4},{16,24},{20,28},{24,16},{28,20},{1,9},{5... | collective-permute-start | bytes 417800 | tf_op jit(solution)/shard_map/ppermute | solution.py:354
  27.1 9.0 %collective-permute-start.8 = (bf16[512,128]{1,0:T(8,128)(2,1)S(1)}, bf16[512,128]{1,0:T(8,128)(2,1)S(1)}, u32[]{:S(2)}, u32[]{:S(2)}) collective-permute-start(bf16[512,128]{1,0:T(8,128)(2,1)S(1)} %get-tuple-element.38.refs_0_), channel_id=1, source_target_pairs={{0,1},{1,0},{2,3},{3,2},{4,5},{5,4},{6,7},{7,6},{8,9},{9,8},{10,11... | collective-permute-start | bytes 393224 | tf_op jit(solution)/shard_map/ppermute | solution.py:354
  29.5 6.3 %collective-permute-start.6 = (bf16[256,128]{1,0:T(8,128)(2,1)S(1)}, bf16[256,128]{1,0:T(8,128)(2,1)S(1)}, u32[]{:S(2)}, u32[]{:S(2)}) collective-permute-start(bf16[256,128]{1,0:T(8,128)(2,1)S(1)} %fusion.13), channel_id=1, source_target_pairs={{0,8},{4,12},{8,0},{12,4},{16,24},{20,28},{24,16},{28,20},{1,9},{5... | collective-permute-start | bytes 196616 | tf_op jit(solution)/shard_map/ppermute | solution.py:354
  37.7 16.2 %collective-permute-start.17 = (bf16[512,128]{1,0:T(8,128)(2,1)S(1)}, bf16[512,128]{1,0:T(8,128)(2,1)S(1)}, u32[]{:S(2)}, u32[]{:S(2)}) collective-permute-start(bf16[512,128]{1,0:T(8,128)(2,1)S(1)} %update.6.refs_4_.refs_0_.refs_1_), channel_id=1, source_target_pairs={{0,2},{1,3},{2,0},{3,1},{4,6},{5,7},{6,4},{7,5},{8,10},{9,11},{10,... | collective-permute-start | bytes 393224 | tf_op jit(solution)/shard_map/ppermute | solution.py:354
  39.6 14.4 %collective-permute-start.18 = (bf16[512,128]{1,0:T(8,128)(2,1)S(1)}, bf16[512,128]{1,0:T(8,128)(2,1)S(1)}, u32[]{:S(2)}, u32[]{:S(2)}) collective-permute-start(bf16[512,128]{1,0:T(8,128)(2,1)S(1)} %update.6.refs_4_.refs_0_.refs_1_), channel_id=1, source_target_pairs={{0,3},{1,2},{2,1},{3,0},{4,7},{5,6},{6,5},{7,4},{8,11},{9,10},{10,... | collective-permute-start | bytes 393224 | tf_op jit(solution)/shard_map/ppermute | solution.py:354
  44.3 9.7 %collective-permute-start.16 = (bf16[512,128]{1,0:T(8,128)(2,1)S(1)}, bf16[512,128]{1,0:T(8,128)(2,1)S(1)}, u32[]{:S(2)}, u32[]{:S(2)}) collective-permute-start(bf16[512,128]{1,0:T(8,128)(2,1)S(1)} %update.6.refs_4_.refs_0_.refs_1_), channel_id=1, source_target_pairs={{0,1},{1,0},{2,3},{3,2},{4,5},{5,4},{6,7},{7,6},{8,9},{9,8},{10,11... | collective-permute-start | bytes 393224 | tf_op jit(solution)/shard_map/ppermute | solution.py:354
  55.2 16.5 %collective-permute-start.25 = (bf16[512,128]{1,0:T(8,128)(2,1)S(1)}, bf16[512,128]{1,0:T(8,128)(2,1)S(1)}, u32[]{:S(2)}, u32[]{:S(2)}) collective-permute-start(bf16[512,128]{1,0:T(8,128)(2,1)S(1)} %update.7.refs_4_.refs_0_.refs_1_), channel_id=1, source_target_pairs={{0,2},{1,3},{2,0},{3,1},{4,6},{5,7},{6,4},{7,5},{8,10},{9,11},{10,... | collective-permute-start | bytes 393224 | tf_op jit(solution)/shard_map/ppermute | solution.py:354
  57.6 14.1 %collective-permute-start.26 = (bf16[512,128]{1,0:T(8,128)(2,1)S(1)}, bf16[512,128]{1,0:T(8,128)(2,1)S(1)}, u32[]{:S(2)}, u32[]{:S(2)}) collective-permute-start(bf16[512,128]{1,0:T(8,128)(2,1)S(1)} %update.7.refs_4_.refs_0_.refs_1_), channel_id=1, source_target_pairs={{0,3},{1,2},{2,1},{3,0},{4,7},{5,6},{6,5},{7,4},{8,11},{9,10},{10,... | collective-permute-start | bytes 393224 | tf_op jit(solution)/shard_map/ppermute | solution.py:354
  59.8 5.5 %collective-permute-start.20 = (bf16[2,256,128]{2,1,0:T(8,128)(2,1)S(1)}, bf16[2,256,128]{2,1,0:T(8,128)(2,1)S(1)}, u32[]{:S(2)}, u32[]{:S(2)}) collective-permute-start(bf16[2,256,128]{2,1,0:T(8,128)(2,1)S(1)} %slice.399), channel_id=1, source_target_pairs={{0,16},{4,20},{8,24},{12,28},{16,0},{20,4},{24,8},{28,12},{1,17},{... | collective-permute-start | bytes 393224 | tf_op jit(solution)/shard_map/ppermute | solution.py:354
  62.0 9.7 %collective-permute-start.24 = (bf16[512,128]{1,0:T(8,128)(2,1)S(1)}, bf16[512,128]{1,0:T(8,128)(2,1)S(1)}, u32[]{:S(2)}, u32[]{:S(2)}) collective-permute-start(bf16[512,128]{1,0:T(8,128)(2,1)S(1)} %update.7.refs_4_.refs_0_.refs_1_), channel_id=1, source_target_pairs={{0,1},{1,0},{2,3},{3,2},{4,5},{5,4},{6,7},{7,6},{8,9},{9,8},{10,11... | collective-permute-start | bytes 393224 | tf_op jit(solution)/shard_map/ppermute | solution.py:354
  72.9 15.9 %collective-permute-start.33 = (bf16[512,128]{1,0:T(8,128)(2,1)S(1)}, bf16[512,128]{1,0:T(8,128)(2,1)S(1)}, u32[]{:S(2)}, u32[]{:S(2)}) collective-permute-start(bf16[512,128]{1,0:T(8,128)(2,1)S(1)} %update.8.refs_4_.refs_0_.refs_1_), channel_id=1, source_target_pairs={{0,2},{1,3},{2,0},{3,1},{4,6},{5,7},{6,4},{7,5},{8,10},{9,11},{10,... | collective-permute-start | bytes 393224 | tf_op jit(solution)/shard_map/ppermute | solution.py:354
  75.3 13.5 %collective-permute-start.34 = (bf16[512,128]{1,0:T(8,128)(2,1)S(1)}, bf16[512,128]{1,0:T(8,128)(2,1)S(1)}, u32[]{:S(2)}, u32[]{:S(2)}) collective-permute-start(bf16[512,128]{1,0:T(8,128)(2,1)S(1)} %update.8.refs_4_.refs_0_.refs_1_), channel_id=1, source_target_pairs={{0,3},{1,2},{2,1},{3,0},{4,7},{5,6},{6,5},{7,4},{8,11},{9,10},{10,... | collective-permute-start | bytes 393224 | tf_op jit(solution)/shard_map/ppermute | solution.py:354
  79.3 9.5 %collective-permute-start.32 = (bf16[512,128]{1,0:T(8,128)(2,1)S(1)}, bf16[512,128]{1,0:T(8,128)(2,1)S(1)}, u32[]{:S(2)}, u32[]{:S(2)}) collective-permute-start(bf16[512,128]{1,0:T(8,128)(2,1)S(1)} %update.8.refs_4_.refs_0_.refs_1_), channel_id=1, source_target_pairs={{0,1},{1,0},{2,3},{3,2},{4,5},{5,4},{6,7},{7,6},{8,9},{9,8},{10,11... | collective-permute-start | bytes 393224 | tf_op jit(solution)/shard_map/ppermute | solution.py:354
  90.0 17.1 %collective-permute-start.41 = (bf16[512,128]{1,0:T(8,128)(2,1)S(1)}, bf16[512,128]{1,0:T(8,128)(2,1)S(1)}, u32[]{:S(2)}, u32[]{:S(2)}) collective-permute-start(bf16[512,128]{1,0:T(8,128)(2,1)S(1)} %update.9.refs_4_.refs_0_.refs_1_), channel_id=1, source_target_pairs={{0,2},{1,3},{2,0},{3,1},{4,6},{5,7},{6,4},{7,5},{8,10},{9,11},{10,... | collective-permute-start | bytes 393224 | tf_op jit(solution)/shard_map/ppermute | solution.py:354
  92.5 14.7 %collective-permute-start.42 = (bf16[512,128]{1,0:T(8,128)(2,1)S(1)}, bf16[512,128]{1,0:T(8,128)(2,1)S(1)}, u32[]{:S(2)}, u32[]{:S(2)}) collective-permute-start(bf16[512,128]{1,0:T(8,128)(2,1)S(1)} %update.9.refs_4_.refs_0_.refs_1_), channel_id=1, source_target_pairs={{0,3},{1,2},{2,1},{3,0},{4,7},{5,6},{6,5},{7,4},{8,11},{9,10},{10,... | collective-permute-start | bytes 393224 | tf_op jit(solution)/shard_map/ppermute | solution.py:354
  95.2 5.5 %collective-permute-start.36 = (bf16[2,256,128]{2,1,0:T(8,128)(2,1)S(1)}, bf16[2,256,128]{2,1,0:T(8,128)(2,1)S(1)}, u32[]{:S(2)}, u32[]{:S(2)}) collective-permute-start(bf16[2,256,128]{2,1,0:T(8,128)(2,1)S(1)} %slice.397), channel_id=1, source_target_pairs={{0,16},{4,20},{8,24},{12,28},{16,0},{20,4},{24,8},{28,12},{1,17},{... | collective-permute-start | bytes 393224 | tf_op jit(solution)/shard_map/ppermute | solution.py:354
  97.4 9.7 %collective-permute-start.40 = (bf16[512,128]{1,0:T(8,128)(2,1)S(1)}, bf16[512,128]{1,0:T(8,128)(2,1)S(1)}, u32[]{:S(2)}, u32[]{:S(2)}) collective-permute-start(bf16[512,128]{1,0:T(8,128)(2,1)S(1)} %update.9.refs_4_.refs_0_.refs_1_), channel_id=1, source_target_pairs={{0,1},{1,0},{2,3},{3,2},{4,5},{5,4},{6,7},{7,6},{8,9},{9,8},{10,11... | collective-permute-start | bytes 393224 | tf_op jit(solution)/shard_map/ppermute | solution.py:354
  110.4 5.6 %collective-permute-start.44 = (bf16[2,256,128]{2,1,0:T(8,128)(2,1)S(1)}, bf16[2,256,128]{2,1,0:T(8,128)(2,1)S(1)}, u32[]{:S(2)}, u32[]{:S(2)}) collective-permute-start(bf16[2,256,128]{2,1,0:T(8,128)(2,1)S(1)} %slice.396), channel_id=1, source_target_pairs={{0,16},{4,20},{8,24},{12,28},{16,0},{20,4},{24,8},{28,12},{1,17},{... | collective-permute-start | bytes 393224 | tf_op jit(solution)/shard_map/ppermute | solution.py:354
  (27 other events, 125.4 us)

commit v13 on v12

--- a/solution.py
+++ b/solution.py
@@ -228,7 +228,8 @@
     )(features)
 
 
-def assemble_kernel(packed, blocks, *refs):
+def assemble_kernel(packed, masks, *refs):
+    blocks = len(masks)
     block_refs = refs[:blocks]
     held_ref = refs[blocks + 1]
     staged_ref = refs[-1] if packed else held_ref
@@ -239,8 +240,8 @@
         first = pl.multiple_of(lax.bitwise_xor(col, mask) * rows, rows)
         staged_ref[pl.ds(first, rows), :] = ref[...]
 
-    for mask in range(blocks):
-        put(mask, block_refs[mask])
+    for mask, ref in zip(masks, block_refs):
+        put(mask, ref)
     if packed:
         piece = width // blocks
         for group in range(blocks):
@@ -256,6 +257,7 @@
 
 def assemble(gathered, after, tile_size, packed):
     blocks = len(gathered)
+    masks = sorted(gathered, key=lambda mask: (2 * mask < blocks, mask))
     rows, width = gathered[0].shape
     out_shape = [jax.ShapeDtypeStruct((blocks * rows + tile_size, width), jnp.bfloat16)]
     scratch = []
@@ -263,7 +265,7 @@
         out_shape.append(jax.ShapeDtypeStruct((rows, width), jnp.bfloat16))
         scratch.append(pltpu.VMEM((blocks * rows, width), jnp.bfloat16))
     return pl.pallas_call(
-        functools.partial(assemble_kernel, packed, blocks),
+        functools.partial(assemble_kernel, packed, masks),
         out_shape=out_shape,
         in_specs=vmem(blocks) + anywhere(1),
         out_specs=vmem(len(out_shape)),
@@ -271,7 +273,7 @@
         compiler_params=pltpu.CompilerParams(vmem_limit_bytes=4 * 2**20),
         cost_estimate=pl.CostEstimate(flops=0, bytes_accessed=4 * 2**20, transcendentals=0),
         name="assemble",
-    )(*gathered, after)
+    )(*[gathered[mask] for mask in masks], after)
 
 
 def product_kernel(half, rows, bits, list_ref, turned_ref, held_ref, weight_ref, out_ref):
@@ -416,7 +418,7 @@
         extra = EXTRA if phase == 0 else 0
         if phase > 0:
             iterates[after] = last = update(*pending)
-        held, *own = assemble([gathered[chunk][m] for m in range(blocks)], last, tile_size, first)
+        held, *own = assemble(gathered[chunk], last, tile_size, first)
         if first:
             iterates[chunk] = restarts[chunk] = own[0]
         if phase == 0:
@@ -434,14 +436,22 @@
         if coming is not None:
             coming, both = lax.optimization_barrier((coming, both))
             gathered[after].update(gather_line(coming, blocks, late))
-        kept, arrived = reduce_chips(both, rows // 2, chip_bits, row_size)
+        if phase + 1 < ITERS * CHUNKS:
+            kept, arrived = reduce_chips(both, rows // 2, chip_bits, row_size)
+            arrived = [arrived]
+        else:
+            kept = both[0]
+            arrived = [
+                exchange(both[mask].astype(jnp.bfloat16), "row", 2 * mask, row_size)
+                for mask in range(chips - 1, 0, -1)
+            ]
         if phase == 0:
             weight_rows = slice(rows, rows + tiles_per_owner)
-            total = 1.0 + kept[weight_rows] + arrived[weight_rows].astype(jnp.float32)
+            total = 1.0 + kept[weight_rows] + arrived[0][weight_rows].astype(jnp.float32)
             scale = jnp.broadcast_to(
                 ((1.0 - TELEPORT) / total).reshape(rows, 1), (rows, width)
             )
-        pending = (kept, [arrived], iterates[chunk], restarts[chunk], scale)
+        pending = (kept, arrived, iterates[chunk], restarts[chunk], scale)
     iterates[chunk] = update(*pending)
     iterates = lax.optimization_barrier(iterates)
     out = jnp.stack(iterates).reshape(CHUNKS, rows, blocks, piece).transpose(1, 2, 0, 3)

time: 123 us -> 121 us (0.984)
  starting transfers between devices: 53.5 us -> 49.7 us
    ppermute x48 -> x47, starting transfers between devices: 53.5 us -> 49.7 us  [exchange(): return lax.ppermute(block, axis, [(i, i ^ mask) for i in range(size)])]
    ppermute x48 -> x47, waiting for transfers between devices: 41.9 us -> 42.8 us  [exchange(): return lax.ppermute(block, axis, [(i, i ^ mask) for i in range(size)])]
  transfers between devices with their start and end apart: 48 -> 47, of which waited for: 24 -> 23; matrix products, arithmetic and copies ran while one was open for 1% -> 1% of each run, Pallas kernels for 10% -> 11%
where the time goes in v13:
time: 121 us; the launch traced here: 120 us
  starting transfers between devices  49.7 us (41%)
  waiting for transfers between devices  42.8 us (35%)
  Pallas kernels  20.6 us (17%)
  local copies, waits for them, and re-layouts  5.28 us (4%)
    ppermute x47, starting transfers between devices, exchange(): return lax.ppermute(block, axis, [(i, i ^ mask) for i in range(size)])  49.7 us
    ppermute x47, waiting for transfers between devices, exchange(): return lax.ppermute(block, axis, [(i, i ^ mask) for i in range(size)])  42.8 us
    pallas_call x12, Pallas kernels, product(): pl.pallas_call(functools.partial(product_kernel, half, rows, bits), out_s...  12.3 us
    pallas_call x1, Pallas kernels, prepare(): pl.pallas_call(functools.partial(prepare_kernel, tiles_per_owner, bits),...  6.18 us
    unnamed x7, local copies, waits for them, and re-layouts  3.44 us
  transfers between devices with their start and end apart: 47, of which 23 were waited for; matrix products, arithmetic and copies ran while one was open for 1% of the time, Pallas kernels for 11%

profile of v13, /device:TPU:0, one launch (start us, length us, event | category | flops | bytes accessed | tf_op | source)
XLA Modules:
  0.0 120.4 jit_solution(8973524024597068721)
XLA Ops:
  1.5 4.1 %collective-permute-start = (bf16[512,128]{1,0:T(8,128)(2,1)S(1)}, bf16[512,128]{1,0:T(8,128)(2,1)S(1)}, u32[]{:S(2)}, u32[]{:S(2)}) collective-permute-start(bf16[512,128]{1,0:T(8,128)(2,1)S(1)} %get-tuple-element.28.refs_2_), channel_id=1, source_target_pairs={{0,2},{1,3},{2,0},{3,1},{4,6},{5,7},{6,4},{7,5},{8,10},{9,11},{10,... | collective-permute-start | bytes 393224 | tf_op jit(solution)/shard_map/ppermute | solution.py:356
  7.3 2.2 %copy-done = bf16[128,128,128]{2,1,0:T(8,128)(2,1)S(1)} copy-done((bf16[128,128,128]{2,1,0:T(8,128)(2,1)S(1)}, bf16[128,128,128]{2,1,0:T(8,128)(2,1)}, u32[]{:S(2)}) %copy-start) | copy-done | bytes 4194328
  9.5 6.2 %prepare.1 = (bf16[128,128,128]{2,1,0:T(8,128)(2,1)S(1)}, f32[2,4,16,128]{3,2,1,0:T(8,128)S(1)}, s32[20,8]{1,0:T(8,128)S(1)}) custom-call(s32[3]{0:T(128)S(1)} %pad_add_fusion.refs_4_.place_ref, s32[1,128]{1,0:T(1,128)S(1)} %copy-done.1, s32[1,32]{1,0:T(1,128)S(1)} %copy-done.2, bf16[128,128,128]{2,1,0:T(8,128)(2,1)S(1)} %copy-done), custom_call_target="tpu_custom_call" | custom-call | tf_op jit(solution)/shard_map/prepare/pallas_call | solution.py:187
  17.8 4.8 %collective-permute-start.8 = (bf16[512,128]{1,0:T(8,128)(2,1)S(1)}, bf16[512,128]{1,0:T(8,128)(2,1)S(1)}, u32[]{:S(2)}, u32[]{:S(2)}) collective-permute-start(bf16[512,128]{1,0:T(8,128)(2,1)S(1)} %get-tuple-element.38.refs_2_), channel_id=1, source_target_pairs={{0,2},{1,3},{2,0},{3,1},{4,6},{5,7},{6,4},{7,5},{8,10},{9,11},{10,... | collective-permute-start | bytes 393224 | tf_op jit(solution)/shard_map/ppermute | solution.py:356
  23.8 1.8 %collective-permute-start.4 = (bf16[2,256,128]{2,1,0:T(8,128)(2,1)S(1)}, bf16[2,256,128]{2,1,0:T(8,128)(2,1)S(1)}, u32[]{:S(2)}, u32[]{:S(2)}) collective-permute-start(bf16[2,256,128]{2,1,0:T(8,128)(2,1)S(1)} %slice.363), channel_id=1, source_target_pairs={{0,16},{4,20},{8,24},{12,28},{16,0},{20,4},{24,8},{28,12},{1,17},{... | collective-permute-start | bytes 393224 | tf_op jit(solution)/shard_map/ppermute | solution.py:356
  27.5 2.0 %collective-permute-done.4 = bf16[2,256,128]{2,1,0:T(8,128)(2,1)S(1)} collective-permute-done((bf16[2,256,128]{2,1,0:T(8,128)(2,1)S(1)}, bf16[2,256,128]{2,1,0:T(8,128)(2,1)S(1)}, u32[]{:S(2)}, u32[]{:S(2)}) %collective-permute-start.4) | collective-permute-done | bytes 131104 | tf_op jit(solution)/shard_map/ppermute | solution.py:356
  32.3 3.2 %collective-permute-done.7 = bf16[272,128]{1,0:T(8,128)(2,1)S(1)} collective-permute-done((bf16[272,128]{1,0:T(8,128)(2,1)S(1)}, bf16[272,128]{1,0:T(8,128)(2,1)S(1)}, u32[]{:S(2)}, u32[]{:S(2)}) %collective-permute-start.7) | collective-permute-done | bytes 69664 | tf_op jit(solution)/shard_map/ppermute | solution.py:356
  42.1 1.9 %collective-permute-start.12 = (bf16[2,256,128]{2,1,0:T(8,128)(2,1)S(1)}, bf16[2,256,128]{2,1,0:T(8,128)(2,1)S(1)}, u32[]{:S(2)}, u32[]{:S(2)}) collective-permute-start(bf16[2,256,128]{2,1,0:T(8,128)(2,1)S(1)} %slice.362), channel_id=1, source_target_pairs={{0,16},{4,20},{8,24},{12,28},{16,0},{20,4},{24,8},{28,12},{1,17},{... | collective-permute-start | bytes 393224 | tf_op jit(solution)/shard_map/ppermute | solution.py:356
  44.7 3.2 %collective-permute-done.12 = bf16[2,256,128]{2,1,0:T(8,128)(2,1)S(1)} collective-permute-done((bf16[2,256,128]{2,1,0:T(8,128)(2,1)S(1)}, bf16[2,256,128]{2,1,0:T(8,128)(2,1)S(1)}, u32[]{:S(2)}, u32[]{:S(2)}) %collective-permute-start.12) | collective-permute-done | bytes 131104 | tf_op jit(solution)/shard_map/ppermute | solution.py:356
  51.3 2.6 %collective-permute-done.14 = bf16[256,128]{1,0:T(8,128)(2,1)S(1)} collective-permute-done((bf16[256,128]{1,0:T(8,128)(2,1)S(1)}, bf16[256,128]{1,0:T(8,128)(2,1)S(1)}, u32[]{:S(2)}, u32[]{:S(2)}) %collective-permute-start.14) | collective-permute-done | bytes 65568 | tf_op jit(solution)/shard_map/ppermute | solution.py:356
  55.5 2.7 %collective-permute-start.24 = (bf16[512,128]{1,0:T(8,128)(2,1)S(1)}, bf16[512,128]{1,0:T(8,128)(2,1)S(1)}, u32[]{:S(2)}, u32[]{:S(2)}) collective-permute-start(bf16[512,128]{1,0:T(8,128)(2,1)S(1)} %update.7.refs_4_.refs_2_.refs_1_), channel_id=1, source_target_pairs={{0,2},{1,3},{2,0},{3,1},{4,6},{5,7},{6,4},{7,5},{8,10},{9,11},{10,... | collective-permute-start | bytes 393224 | tf_op jit(solution)/shard_map/ppermute | solution.py:356
  59.4 2.1 %collective-permute-start.20 = (bf16[2,256,128]{2,1,0:T(8,128)(2,1)S(1)}, bf16[2,256,128]{2,1,0:T(8,128)(2,1)S(1)}, u32[]{:S(2)}, u32[]{:S(2)}) collective-permute-start(bf16[2,256,128]{2,1,0:T(8,128)(2,1)S(1)} %slice.361), channel_id=1, source_target_pairs={{0,16},{4,20},{8,24},{12,28},{16,0},{20,4},{24,8},{28,12},{1,17},{... | collective-permute-start | bytes 393224 | tf_op jit(solution)/shard_map/ppermute | solution.py:356
  62.5 2.9 %collective-permute-done.20 = bf16[2,256,128]{2,1,0:T(8,128)(2,1)S(1)} collective-permute-done((bf16[2,256,128]{2,1,0:T(8,128)(2,1)S(1)}, bf16[2,256,128]{2,1,0:T(8,128)(2,1)S(1)}, u32[]{:S(2)}, u32[]{:S(2)}) %collective-permute-start.20) | collective-permute-done | bytes 131104 | tf_op jit(solution)/shard_map/ppermute | solution.py:356
  68.5 2.8 %collective-permute-done.22 = bf16[256,128]{1,0:T(8,128)(2,1)S(1)} collective-permute-done((bf16[256,128]{1,0:T(8,128)(2,1)S(1)}, bf16[256,128]{1,0:T(8,128)(2,1)S(1)}, u32[]{:S(2)}, u32[]{:S(2)}) %collective-permute-start.22) | collective-permute-done | bytes 65568 | tf_op jit(solution)/shard_map/ppermute | solution.py:356
  72.9 1.8 %collective-permute-start.32 = (bf16[512,128]{1,0:T(8,128)(2,1)S(1)}, bf16[512,128]{1,0:T(8,128)(2,1)S(1)}, u32[]{:S(2)}, u32[]{:S(2)}) collective-permute-start(bf16[512,128]{1,0:T(8,128)(2,1)S(1)} %update.8.refs_4_.refs_2_.refs_1_), channel_id=1, source_target_pairs={{0,2},{1,3},{2,0},{3,1},{4,6},{5,7},{6,4},{7,5},{8,10},{9,11},{10,... | collective-permute-start | bytes 393224 | tf_op jit(solution)/shard_map/ppermute | solution.py:356
  76.9 2.1 %collective-permute-start.28 = (bf16[2,256,128]{2,1,0:T(8,128)(2,1)S(1)}, bf16[2,256,128]{2,1,0:T(8,128)(2,1)S(1)}, u32[]{:S(2)}, u32[]{:S(2)}) collective-permute-start(bf16[2,256,128]{2,1,0:T(8,128)(2,1)S(1)} %slice.360), channel_id=1, source_target_pairs={{0,16},{4,20},{8,24},{12,28},{16,0},{20,4},{24,8},{28,12},{1,17},{... | collective-permute-start | bytes 393224 | tf_op jit(solution)/shard_map/ppermute | solution.py:356
  80.2 2.6 %collective-permute-done.28 = bf16[2,256,128]{2,1,0:T(8,128)(2,1)S(1)} collective-permute-done((bf16[2,256,128]{2,1,0:T(8,128)(2,1)S(1)}, bf16[2,256,128]{2,1,0:T(8,128)(2,1)S(1)}, u32[]{:S(2)}, u32[]{:S(2)}) %collective-permute-start.28) | collective-permute-done | bytes 131104 | tf_op jit(solution)/shard_map/ppermute | solution.py:356
  85.8 2.9 %collective-permute-done.30 = bf16[256,128]{1,0:T(8,128)(2,1)S(1)} collective-permute-done((bf16[256,128]{1,0:T(8,128)(2,1)S(1)}, bf16[256,128]{1,0:T(8,128)(2,1)S(1)}, u32[]{:S(2)}, u32[]{:S(2)}) %collective-permute-start.30) | collective-permute-done | bytes 65568 | tf_op jit(solution)/shard_map/ppermute | solution.py:356
  90.6 3.0 %collective-permute-start.40 = (bf16[512,128]{1,0:T(8,128)(2,1)S(1)}, bf16[512,128]{1,0:T(8,128)(2,1)S(1)}, u32[]{:S(2)}, u32[]{:S(2)}) collective-permute-start(bf16[512,128]{1,0:T(8,128)(2,1)S(1)} %update.9.refs_4_.refs_2_.refs_3_), channel_id=1, source_target_pairs={{0,2},{1,3},{2,0},{3,1},{4,6},{5,7},{6,4},{7,5},{8,10},{9,11},{10,... | collective-permute-start | bytes 393224 | tf_op jit(solution)/shard_map/ppermute | solution.py:356
  97.3 3.2 %collective-permute-done.36 = bf16[2,256,128]{2,1,0:T(8,128)(2,1)S(1)} collective-permute-done((bf16[2,256,128]{2,1,0:T(8,128)(2,1)S(1)}, bf16[2,256,128]{2,1,0:T(8,128)(2,1)S(1)}, u32[]{:S(2)}, u32[]{:S(2)}) %collective-permute-start.36) | collective-permute-done | bytes 131104 | tf_op jit(solution)/shard_map/ppermute | solution.py:356
  103.3 2.8 %collective-permute-done.38 = bf16[256,128]{1,0:T(8,128)(2,1)S(1)} collective-permute-done((bf16[256,128]{1,0:T(8,128)(2,1)S(1)}, bf16[256,128]{1,0:T(8,128)(2,1)S(1)}, u32[]{:S(2)}, u32[]{:S(2)}) %collective-permute-start.38) | collective-permute-done | bytes 65568 | tf_op jit(solution)/shard_map/ppermute | solution.py:356
  109.8 1.9 %collective-permute-start.44 = (bf16[512,128]{1,0:T(8,128)(2,1)S(1)}, bf16[512,128]{1,0:T(8,128)(2,1)S(1)}, u32[]{:S(2)}, u32[]{:S(2)}) collective-permute-start(bf16[512,128]{1,0:T(8,128)(2,1)S(1)} %get-tuple-element.55), channel_id=1, source_target_pairs={{0,24},{4,28},{8,16},{12,20},{16,8},{20,12},{24,0},{28,4},{1,25},{... | collective-permute-start | bytes 393224 | tf_op jit(solution)/shard_map/ppermute | solution.py:356
  113.4 3.7 %collective-permute-done.44.refs_0_ = bf16[512,128]{1,0:T(8,128)(2,1)S(1)} collective-permute-done((bf16[512,128]{1,0:T(8,128)(2,1)S(1)}, bf16[512,128]{1,0:T(8,128)(2,1)S(1)}, u32[]{:S(2)}, u32[]{:S(2)}) %collective-permute-start.44) | collective-permute-done | bytes 131104 | tf_op jit(solution)/shard_map/ppermute | solution.py:356
  117.1 2.0 %collective-permute-done.45.refs_1_ = bf16[512,128]{1,0:T(8,128)(2,1)S(1)} collective-permute-done((bf16[512,128]{1,0:T(8,128)(2,1)S(1)}, bf16[512,128]{1,0:T(8,128)(2,1)S(1)}, u32[]{:S(2)}, u32[]{:S(2)}) %collective-permute-start.45) | collective-permute-done | bytes 131104 | tf_op jit(solution)/shard_map/ppermute | solution.py:356
  (174 shorter events, 51.2 us)
Async XLA Ops:
  1.5 14.1 %collective-permute-start = (bf16[512,128]{1,0:T(8,128)(2,1)S(1)}, bf16[512,128]{1,0:T(8,128)(2,1)S(1)}, u32[]{:S(2)}, u32[]{:S(2)}) collective-permute-start(bf16[512,128]{1,0:T(8,128)(2,1)S(1)} %get-tuple-element.28.refs_2_), channel_id=1, source_target_pairs={{0,2},{1,3},{2,0},{3,1},{4,6},{5,7},{6,4},{7,5},{8,10},{9,11},{10,... | collective-permute-start | bytes 393224 | tf_op jit(solution)/shard_map/ppermute | solution.py:356
  5.6 10.1 %collective-permute-start.1 = (bf16[512,128]{1,0:T(8,128)(2,1)S(1)}, bf16[512,128]{1,0:T(8,128)(2,1)S(1)}, u32[]{:S(2)}, u32[]{:S(2)}) collective-permute-start(bf16[512,128]{1,0:T(8,128)(2,1)S(1)} %get-tuple-element.28.refs_2_), channel_id=1, source_target_pairs={{0,3},{1,2},{2,1},{3,0},{4,7},{5,6},{6,5},{7,4},{8,11},{9,10},{10,... | collective-permute-start | bytes 393224 | tf_op jit(solution)/shard_map/ppermute | solution.py:356
  7.0 9.2 %collective-permute-start.2 = (bf16[512,128]{1,0:T(8,128)(2,1)S(1)}, bf16[512,128]{1,0:T(8,128)(2,1)S(1)}, u32[]{:S(2)}, u32[]{:S(2)}) collective-permute-start(bf16[512,128]{1,0:T(8,128)(2,1)S(1)} %get-tuple-element.28.refs_2_), channel_id=1, source_target_pairs={{0,1},{1,0},{2,3},{3,2},{4,5},{5,4},{6,7},{7,6},{8,9},{9,8},{10,11... | collective-permute-start | bytes 393224 | tf_op jit(solution)/shard_map/ppermute | solution.py:356
  17.8 18.0 %collective-permute-start.8 = (bf16[512,128]{1,0:T(8,128)(2,1)S(1)}, bf16[512,128]{1,0:T(8,128)(2,1)S(1)}, u32[]{:S(2)}, u32[]{:S(2)}) collective-permute-start(bf16[512,128]{1,0:T(8,128)(2,1)S(1)} %get-tuple-element.38.refs_2_), channel_id=1, source_target_pairs={{0,2},{1,3},{2,0},{3,1},{4,6},{5,7},{6,4},{7,5},{8,10},{9,11},{10,... | collective-permute-start | bytes 393224 | tf_op jit(solution)/shard_map/ppermute | solution.py:356
  22.6 13.2 %collective-permute-start.9 = (bf16[512,128]{1,0:T(8,128)(2,1)S(1)}, bf16[512,128]{1,0:T(8,128)(2,1)S(1)}, u32[]{:S(2)}, u32[]{:S(2)}) collective-permute-start(bf16[512,128]{1,0:T(8,128)(2,1)S(1)} %get-tuple-element.38.refs_2_), channel_id=1, source_target_pairs={{0,3},{1,2},{2,1},{3,0},{4,7},{5,6},{6,5},{7,4},{8,11},{9,10},{10,... | collective-permute-start | bytes 393224 | tf_op jit(solution)/shard_map/ppermute | solution.py:356
  26.9 8.9 %collective-permute-start.10 = (bf16[512,128]{1,0:T(8,128)(2,1)S(1)}, bf16[512,128]{1,0:T(8,128)(2,1)S(1)}, u32[]{:S(2)}, u32[]{:S(2)}) collective-permute-start(bf16[512,128]{1,0:T(8,128)(2,1)S(1)} %get-tuple-element.38.refs_2_), channel_id=1, source_target_pairs={{0,1},{1,0},{2,3},{3,2},{4,5},{5,4},{6,7},{7,6},{8,9},{9,8},{10,11... | collective-permute-start | bytes 393224 | tf_op jit(solution)/shard_map/ppermute | solution.py:356
  29.5 6.1 %collective-permute-start.6 = (bf16[256,128]{1,0:T(8,128)(2,1)S(1)}, bf16[256,128]{1,0:T(8,128)(2,1)S(1)}, u32[]{:S(2)}, u32[]{:S(2)}) collective-permute-start(bf16[256,128]{1,0:T(8,128)(2,1)S(1)} %fusion.11), channel_id=1, source_target_pairs={{0,8},{4,12},{8,0},{12,4},{16,24},{20,28},{24,16},{28,20},{1,9},{5... | collective-permute-start | bytes 196616 | tf_op jit(solution)/shard_map/ppermute | solution.py:356
  37.5 16.8 %collective-permute-start.16 = (bf16[512,128]{1,0:T(8,128)(2,1)S(1)}, bf16[512,128]{1,0:T(8,128)(2,1)S(1)}, u32[]{:S(2)}, u32[]{:S(2)}) collective-permute-start(bf16[512,128]{1,0:T(8,128)(2,1)S(1)} %update.6.refs_4_.refs_2_.refs_1_), channel_id=1, source_target_pairs={{0,2},{1,3},{2,0},{3,1},{4,6},{5,7},{6,4},{7,5},{8,10},{9,11},{10,... | collective-permute-start | bytes 393224 | tf_op jit(solution)/shard_map/ppermute | solution.py:356
  39.2 15.1 %collective-permute-start.17 = (bf16[512,128]{1,0:T(8,128)(2,1)S(1)}, bf16[512,128]{1,0:T(8,128)(2,1)S(1)}, u32[]{:S(2)}, u32[]{:S(2)}) collective-permute-start(bf16[512,128]{1,0:T(8,128)(2,1)S(1)} %update.6.refs_4_.refs_2_.refs_1_), channel_id=1, source_target_pairs={{0,3},{1,2},{2,1},{3,0},{4,7},{5,6},{6,5},{7,4},{8,11},{9,10},{10,... | collective-permute-start | bytes 393224 | tf_op jit(solution)/shard_map/ppermute | solution.py:356
  44.2 10.1 %collective-permute-start.18 = (bf16[512,128]{1,0:T(8,128)(2,1)S(1)}, bf16[512,128]{1,0:T(8,128)(2,1)S(1)}, u32[]{:S(2)}, u32[]{:S(2)}) collective-permute-start(bf16[512,128]{1,0:T(8,128)(2,1)S(1)} %update.6.refs_4_.refs_2_.refs_1_), channel_id=1, source_target_pairs={{0,1},{1,0},{2,3},{3,2},{4,5},{5,4},{6,7},{7,6},{8,9},{9,8},{10,11... | collective-permute-start | bytes 393224 | tf_op jit(solution)/shard_map/ppermute | solution.py:356
  55.5 16.2 %collective-permute-start.24 = (bf16[512,128]{1,0:T(8,128)(2,1)S(1)}, bf16[512,128]{1,0:T(8,128)(2,1)S(1)}, u32[]{:S(2)}, u32[]{:S(2)}) collective-permute-start(bf16[512,128]{1,0:T(8,128)(2,1)S(1)} %update.7.refs_4_.refs_2_.refs_1_), channel_id=1, source_target_pairs={{0,2},{1,3},{2,0},{3,1},{4,6},{5,7},{6,4},{7,5},{8,10},{9,11},{10,... | collective-permute-start | bytes 393224 | tf_op jit(solution)/shard_map/ppermute | solution.py:356
  58.2 13.5 %collective-permute-start.25 = (bf16[512,128]{1,0:T(8,128)(2,1)S(1)}, bf16[512,128]{1,0:T(8,128)(2,1)S(1)}, u32[]{:S(2)}, u32[]{:S(2)}) collective-permute-start(bf16[512,128]{1,0:T(8,128)(2,1)S(1)} %update.7.refs_4_.refs_2_.refs_1_), channel_id=1, source_target_pairs={{0,3},{1,2},{2,1},{3,0},{4,7},{5,6},{6,5},{7,4},{8,11},{9,10},{10,... | collective-permute-start | bytes 393224 | tf_op jit(solution)/shard_map/ppermute | solution.py:356
  59.4 5.9 %collective-permute-start.20 = (bf16[2,256,128]{2,1,0:T(8,128)(2,1)S(1)}, bf16[2,256,128]{2,1,0:T(8,128)(2,1)S(1)}, u32[]{:S(2)}, u32[]{:S(2)}) collective-permute-start(bf16[2,256,128]{2,1,0:T(8,128)(2,1)S(1)} %slice.361), channel_id=1, source_target_pairs={{0,16},{4,20},{8,24},{12,28},{16,0},{20,4},{24,8},{28,12},{1,17},{... | collective-permute-start | bytes 393224 | tf_op jit(solution)/shard_map/ppermute | solution.py:356
  61.6 10.1 %collective-permute-start.26 = (bf16[512,128]{1,0:T(8,128)(2,1)S(1)}, bf16[512,128]{1,0:T(8,128)(2,1)S(1)}, u32[]{:S(2)}, u32[]{:S(2)}) collective-permute-start(bf16[512,128]{1,0:T(8,128)(2,1)S(1)} %update.7.refs_4_.refs_2_.refs_1_), channel_id=1, source_target_pairs={{0,1},{1,0},{2,3},{3,2},{4,5},{5,4},{6,7},{7,6},{8,9},{9,8},{10,11... | collective-permute-start | bytes 393224 | tf_op jit(solution)/shard_map/ppermute | solution.py:356
  72.9 16.5 %collective-permute-start.32 = (bf16[512,128]{1,0:T(8,128)(2,1)S(1)}, bf16[512,128]{1,0:T(8,128)(2,1)S(1)}, u32[]{:S(2)}, u32[]{:S(2)}) collective-permute-start(bf16[512,128]{1,0:T(8,128)(2,1)S(1)} %update.8.refs_4_.refs_2_.refs_1_), channel_id=1, source_target_pairs={{0,2},{1,3},{2,0},{3,1},{4,6},{5,7},{6,4},{7,5},{8,10},{9,11},{10,... | collective-permute-start | bytes 393224 | tf_op jit(solution)/shard_map/ppermute | solution.py:356
  74.6 14.8 %collective-permute-start.33 = (bf16[512,128]{1,0:T(8,128)(2,1)S(1)}, bf16[512,128]{1,0:T(8,128)(2,1)S(1)}, u32[]{:S(2)}, u32[]{:S(2)}) collective-permute-start(bf16[512,128]{1,0:T(8,128)(2,1)S(1)} %update.8.refs_4_.refs_2_.refs_1_), channel_id=1, source_target_pairs={{0,3},{1,2},{2,1},{3,0},{4,7},{5,6},{6,5},{7,4},{8,11},{9,10},{10,... | collective-permute-start | bytes 393224 | tf_op jit(solution)/shard_map/ppermute | solution.py:356
  76.9 5.9 %collective-permute-start.28 = (bf16[2,256,128]{2,1,0:T(8,128)(2,1)S(1)}, bf16[2,256,128]{2,1,0:T(8,128)(2,1)S(1)}, u32[]{:S(2)}, u32[]{:S(2)}) collective-permute-start(bf16[2,256,128]{2,1,0:T(8,128)(2,1)S(1)} %slice.360), channel_id=1, source_target_pairs={{0,16},{4,20},{8,24},{12,28},{16,0},{20,4},{24,8},{28,12},{1,17},{... | collective-permute-start | bytes 393224 | tf_op jit(solution)/shard_map/ppermute | solution.py:356
  79.7 9.7 %collective-permute-start.34 = (bf16[512,128]{1,0:T(8,128)(2,1)S(1)}, bf16[512,128]{1,0:T(8,128)(2,1)S(1)}, u32[]{:S(2)}, u32[]{:S(2)}) collective-permute-start(bf16[512,128]{1,0:T(8,128)(2,1)S(1)} %update.8.refs_4_.refs_2_.refs_1_), channel_id=1, source_target_pairs={{0,1},{1,0},{2,3},{3,2},{4,5},{5,4},{6,7},{7,6},{8,9},{9,8},{10,11... | collective-permute-start | bytes 393224 | tf_op jit(solution)/shard_map/ppermute | solution.py:356
  90.6 15.9 %collective-permute-start.40 = (bf16[512,128]{1,0:T(8,128)(2,1)S(1)}, bf16[512,128]{1,0:T(8,128)(2,1)S(1)}, u32[]{:S(2)}, u32[]{:S(2)}) collective-permute-start(bf16[512,128]{1,0:T(8,128)(2,1)S(1)} %update.9.refs_4_.refs_2_.refs_3_), channel_id=1, source_target_pairs={{0,2},{1,3},{2,0},{3,1},{4,6},{5,7},{6,4},{7,5},{8,10},{9,11},{10,... | collective-permute-start | bytes 393224 | tf_op jit(solution)/shard_map/ppermute | solution.py:356
  93.6 12.9 %collective-permute-start.41 = (bf16[512,128]{1,0:T(8,128)(2,1)S(1)}, bf16[512,128]{1,0:T(8,128)(2,1)S(1)}, u32[]{:S(2)}, u32[]{:S(2)}) collective-permute-start(bf16[512,128]{1,0:T(8,128)(2,1)S(1)} %update.9.refs_4_.refs_2_.refs_3_), channel_id=1, source_target_pairs={{0,3},{1,2},{2,1},{3,0},{4,7},{5,6},{6,5},{7,4},{8,11},{9,10},{10,... | collective-permute-start | bytes 393224 | tf_op jit(solution)/shard_map/ppermute | solution.py:356
  96.5 10.1 %collective-permute-start.42 = (bf16[512,128]{1,0:T(8,128)(2,1)S(1)}, bf16[512,128]{1,0:T(8,128)(2,1)S(1)}, u32[]{:S(2)}, u32[]{:S(2)}) collective-permute-start(bf16[512,128]{1,0:T(8,128)(2,1)S(1)} %update.9.refs_4_.refs_2_.refs_3_), channel_id=1, source_target_pairs={{0,1},{1,0},{2,3},{3,2},{4,5},{5,4},{6,7},{7,6},{8,9},{9,8},{10,11... | collective-permute-start | bytes 393224 | tf_op jit(solution)/shard_map/ppermute | solution.py:356
  109.8 7.3 %collective-permute-start.44 = (bf16[512,128]{1,0:T(8,128)(2,1)S(1)}, bf16[512,128]{1,0:T(8,128)(2,1)S(1)}, u32[]{:S(2)}, u32[]{:S(2)}) collective-permute-start(bf16[512,128]{1,0:T(8,128)(2,1)S(1)} %get-tuple-element.55), channel_id=1, source_target_pairs={{0,24},{4,28},{8,16},{12,20},{16,8},{20,12},{24,0},{28,4},{1,25},{... | collective-permute-start | bytes 393224 | tf_op jit(solution)/shard_map/ppermute | solution.py:356
  111.6 7.5 %collective-permute-start.45 = (bf16[512,128]{1,0:T(8,128)(2,1)S(1)}, bf16[512,128]{1,0:T(8,128)(2,1)S(1)}, u32[]{:S(2)}, u32[]{:S(2)}) collective-permute-start(bf16[512,128]{1,0:T(8,128)(2,1)S(1)} %get-tuple-element.54), channel_id=1, source_target_pairs={{0,16},{4,20},{8,24},{12,28},{16,0},{20,4},{24,8},{28,12},{1,17},{... | collective-permute-start | bytes 393224 | tf_op jit(solution)/shard_map/ppermute | solution.py:356
  113.1 6.0 %collective-permute-start.46 = (bf16[512,128]{1,0:T(8,128)(2,1)S(1)}, bf16[512,128]{1,0:T(8,128)(2,1)S(1)}, u32[]{:S(2)}, u32[]{:S(2)}) collective-permute-start(bf16[512,128]{1,0:T(8,128)(2,1)S(1)} %get-tuple-element.53), channel_id=1, source_target_pairs={{0,8},{4,12},{8,0},{12,4},{16,24},{20,28},{24,16},{28,20},{1,9},{5... | collective-permute-start | bytes 393224 | tf_op jit(solution)/shard_map/ppermute | solution.py:356
  (26 other events, 124.0 us)

commit v14 on v13

--- a/solution.py
+++ b/solution.py
@@ -16,7 +16,7 @@
 CHUNKS = 2
 
 
-UNROLL = 8
+UNROLL = 12
 
 
 EXTRA = 16

time: 121 us -> 120 us (level)
  waiting for transfers between devices: 42.8 us -> 47.8 us
  starting transfers between devices: 49.7 us -> 45.7 us
  Pallas kernels: 20.6 us -> 19 us
    ppermute x47, waiting for transfers between devices: 42.8 us -> 47.8 us  [exchange(): return lax.ppermute(block, axis, [(i, i ^ mask) for i in range(size)])]
    ppermute x47, starting transfers between devices: 49.7 us -> 45.7 us  [exchange(): return lax.ppermute(block, axis, [(i, i ^ mask) for i in range(size)])]
    pallas_call x12, Pallas kernels: 12.3 us -> 10.8 us  [product(): pl.pallas_call(functools.partial(product_kernel, half, rows, bits), out_s...]
  transfers between devices with their start and end apart: 47 -> 47, of which waited for: 23 -> 23; matrix products, arithmetic and copies ran while one was open for 1% -> 1% of each run, Pallas kernels for 11% -> 10%
where the time goes in v14:
time: 120 us
  waiting for transfers between devices  47.8 us (40%)
  starting transfers between devices  45.7 us (38%)
  Pallas kernels  19 us (16%)
  local copies, waits for them, and re-layouts  5.28 us (4%)
    ppermute x47, waiting for transfers between devices, exchange(): return lax.ppermute(block, axis, [(i, i ^ mask) for i in range(size)])  47.8 us
    ppermute x47, starting transfers between devices, exchange(): return lax.ppermute(block, axis, [(i, i ^ mask) for i in range(size)])  45.7 us
    pallas_call x12, Pallas kernels, product(): pl.pallas_call(functools.partial(product_kernel, half, rows, bits), out_s...  10.8 us
    pallas_call x1, Pallas kernels, prepare(): pl.pallas_call(functools.partial(prepare_kernel, tiles_per_owner, bits),...  6.14 us
    unnamed x7, local copies, waits for them, and re-layouts  3.44 us
  transfers between devices with their start and end apart: 47, of which 23 were waited for; matrix products, arithmetic and copies ran while one was open for 1% of the time, Pallas kernels for 10%

profile of v14, /device:TPU:0, one launch (start us, length us, event | category | flops | bytes accessed | tf_op | source)
XLA Modules:
  0.0 119.8 jit_solution(6431362155257431504)
XLA Ops:
  1.5 4.1 %collective-permute-start = (bf16[512,128]{1,0:T(8,128)(2,1)S(1)}, bf16[512,128]{1,0:T(8,128)(2,1)S(1)}, u32[]{:S(2)}, u32[]{:S(2)}) collective-permute-start(bf16[512,128]{1,0:T(8,128)(2,1)S(1)} %get-tuple-element.28.refs_2_), channel_id=1, source_target_pairs={{0,2},{1,3},{2,0},{3,1},{4,6},{5,7},{6,4},{7,5},{8,10},{9,11},{10,... | collective-permute-start | bytes 393224 | tf_op jit(solution)/shard_map/ppermute | solution.py:356
  7.3 2.2 %copy-done = bf16[128,128,128]{2,1,0:T(8,128)(2,1)S(1)} copy-done((bf16[128,128,128]{2,1,0:T(8,128)(2,1)S(1)}, bf16[128,128,128]{2,1,0:T(8,128)(2,1)}, u32[]{:S(2)}) %copy-start) | copy-done | bytes 4194328
  9.5 6.1 %prepare.1 = (bf16[128,128,128]{2,1,0:T(8,128)(2,1)S(1)}, f32[2,4,16,128]{3,2,1,0:T(8,128)S(1)}, s32[14,12]{1,0:T(8,128)S(1)}) custom-call(s32[3]{0:T(128)S(1)} %pad_add_fusion.refs_4_.place_ref, s32[1,128]{1,0:T(1,128)S(1)} %copy-done.1, s32[1,32]{1,0:T(1,128)S(1)} %copy-done.2, bf16[128,128,128]{2,1,0:T(8,128)(2,1)S(1)} %copy-done), custom_call_target="tpu_custom_call" | custom-call | tf_op jit(solution)/shard_map/prepare/pallas_call | solution.py:187
  17.7 4.6 %collective-permute-start.8 = (bf16[512,128]{1,0:T(8,128)(2,1)S(1)}, bf16[512,128]{1,0:T(8,128)(2,1)S(1)}, u32[]{:S(2)}, u32[]{:S(2)}) collective-permute-start(bf16[512,128]{1,0:T(8,128)(2,1)S(1)} %get-tuple-element.38.refs_2_), channel_id=1, source_target_pairs={{0,2},{1,3},{2,0},{3,1},{4,6},{5,7},{6,4},{7,5},{8,10},{9,11},{10,... | collective-permute-start | bytes 393224 | tf_op jit(solution)/shard_map/ppermute | solution.py:356
  23.4 1.6 %collective-permute-start.4 = (bf16[2,256,128]{2,1,0:T(8,128)(2,1)S(1)}, bf16[2,256,128]{2,1,0:T(8,128)(2,1)S(1)}, u32[]{:S(2)}, u32[]{:S(2)}) collective-permute-start(bf16[2,256,128]{2,1,0:T(8,128)(2,1)S(1)} %slice.363), channel_id=1, source_target_pairs={{0,16},{4,20},{8,24},{12,28},{16,0},{20,4},{24,8},{28,12},{1,17},{... | collective-permute-start | bytes 393224 | tf_op jit(solution)/shard_map/ppermute | solution.py:356
  26.7 2.8 %collective-permute-done.4 = bf16[2,256,128]{2,1,0:T(8,128)(2,1)S(1)} collective-permute-done((bf16[2,256,128]{2,1,0:T(8,128)(2,1)S(1)}, bf16[2,256,128]{2,1,0:T(8,128)(2,1)S(1)}, u32[]{:S(2)}, u32[]{:S(2)}) %collective-permute-start.4) | collective-permute-done | bytes 131104 | tf_op jit(solution)/shard_map/ppermute | solution.py:356
  32.0 3.6 %collective-permute-done.7 = bf16[272,128]{1,0:T(8,128)(2,1)S(1)} collective-permute-done((bf16[272,128]{1,0:T(8,128)(2,1)S(1)}, bf16[272,128]{1,0:T(8,128)(2,1)S(1)}, u32[]{:S(2)}, u32[]{:S(2)}) %collective-permute-start.7) | collective-permute-done | bytes 69664 | tf_op jit(solution)/shard_map/ppermute | solution.py:356
  38.3 2.5 %collective-permute-start.17 = (bf16[512,128]{1,0:T(8,128)(2,1)S(1)}, bf16[512,128]{1,0:T(8,128)(2,1)S(1)}, u32[]{:S(2)}, u32[]{:S(2)}) collective-permute-start(bf16[512,128]{1,0:T(8,128)(2,1)S(1)} %update.6.refs_4_.refs_2_.refs_1_), channel_id=1, source_target_pairs={{0,3},{1,2},{2,1},{3,0},{4,7},{5,6},{6,5},{7,4},{8,11},{9,10},{10,... | collective-permute-start | bytes 393224 | tf_op jit(solution)/shard_map/ppermute | solution.py:356
  44.5 3.2 %collective-permute-done.12 = bf16[2,256,128]{2,1,0:T(8,128)(2,1)S(1)} collective-permute-done((bf16[2,256,128]{2,1,0:T(8,128)(2,1)S(1)}, bf16[2,256,128]{2,1,0:T(8,128)(2,1)S(1)}, u32[]{:S(2)}, u32[]{:S(2)}) %collective-permute-start.12) | collective-permute-done | bytes 131104 | tf_op jit(solution)/shard_map/ppermute | solution.py:356
  50.5 3.2 %collective-permute-done.14 = bf16[256,128]{1,0:T(8,128)(2,1)S(1)} collective-permute-done((bf16[256,128]{1,0:T(8,128)(2,1)S(1)}, bf16[256,128]{1,0:T(8,128)(2,1)S(1)}, u32[]{:S(2)}, u32[]{:S(2)}) %collective-permute-start.14) | collective-permute-done | bytes 65568 | tf_op jit(solution)/shard_map/ppermute | solution.py:356
  55.1 1.7 %collective-permute-start.24 = (bf16[512,128]{1,0:T(8,128)(2,1)S(1)}, bf16[512,128]{1,0:T(8,128)(2,1)S(1)}, u32[]{:S(2)}, u32[]{:S(2)}) collective-permute-start(bf16[512,128]{1,0:T(8,128)(2,1)S(1)} %update.7.refs_4_.refs_2_.refs_1_), channel_id=1, source_target_pairs={{0,2},{1,3},{2,0},{3,1},{4,6},{5,7},{6,4},{7,5},{8,10},{9,11},{10,... | collective-permute-start | bytes 393224 | tf_op jit(solution)/shard_map/ppermute | solution.py:356
  58.7 1.8 %collective-permute-start.20 = (bf16[2,256,128]{2,1,0:T(8,128)(2,1)S(1)}, bf16[2,256,128]{2,1,0:T(8,128)(2,1)S(1)}, u32[]{:S(2)}, u32[]{:S(2)}) collective-permute-start(bf16[2,256,128]{2,1,0:T(8,128)(2,1)S(1)} %slice.361), channel_id=1, source_target_pairs={{0,16},{4,20},{8,24},{12,28},{16,0},{20,4},{24,8},{28,12},{1,17},{... | collective-permute-start | bytes 393224 | tf_op jit(solution)/shard_map/ppermute | solution.py:356
  62.0 2.8 %collective-permute-done.20 = bf16[2,256,128]{2,1,0:T(8,128)(2,1)S(1)} collective-permute-done((bf16[2,256,128]{2,1,0:T(8,128)(2,1)S(1)}, bf16[2,256,128]{2,1,0:T(8,128)(2,1)S(1)}, u32[]{:S(2)}, u32[]{:S(2)}) %collective-permute-start.20) | collective-permute-done | bytes 131104 | tf_op jit(solution)/shard_map/ppermute | solution.py:356
  67.5 3.2 %collective-permute-done.22 = bf16[256,128]{1,0:T(8,128)(2,1)S(1)} collective-permute-done((bf16[256,128]{1,0:T(8,128)(2,1)S(1)}, bf16[256,128]{1,0:T(8,128)(2,1)S(1)}, u32[]{:S(2)}, u32[]{:S(2)}) %collective-permute-start.22) | collective-permute-done | bytes 65568 | tf_op jit(solution)/shard_map/ppermute | solution.py:356
  72.7 2.9 %collective-permute-start.33 = (bf16[512,128]{1,0:T(8,128)(2,1)S(1)}, bf16[512,128]{1,0:T(8,128)(2,1)S(1)}, u32[]{:S(2)}, u32[]{:S(2)}) collective-permute-start(bf16[512,128]{1,0:T(8,128)(2,1)S(1)} %update.8.refs_4_.refs_2_.refs_1_), channel_id=1, source_target_pairs={{0,3},{1,2},{2,1},{3,0},{4,7},{5,6},{6,5},{7,4},{8,11},{9,10},{10,... | collective-permute-start | bytes 393224 | tf_op jit(solution)/shard_map/ppermute | solution.py:356
  76.7 1.6 %collective-permute-start.28 = (bf16[2,256,128]{2,1,0:T(8,128)(2,1)S(1)}, bf16[2,256,128]{2,1,0:T(8,128)(2,1)S(1)}, u32[]{:S(2)}, u32[]{:S(2)}) collective-permute-start(bf16[2,256,128]{2,1,0:T(8,128)(2,1)S(1)} %slice.360), channel_id=1, source_target_pairs={{0,16},{4,20},{8,24},{12,28},{16,0},{20,4},{24,8},{28,12},{1,17},{... | collective-permute-start | bytes 393224 | tf_op jit(solution)/shard_map/ppermute | solution.py:356
  79.0 3.5 %collective-permute-done.28 = bf16[2,256,128]{2,1,0:T(8,128)(2,1)S(1)} collective-permute-done((bf16[2,256,128]{2,1,0:T(8,128)(2,1)S(1)}, bf16[2,256,128]{2,1,0:T(8,128)(2,1)S(1)}, u32[]{:S(2)}, u32[]{:S(2)}) %collective-permute-start.28) | collective-permute-done | bytes 131104 | tf_op jit(solution)/shard_map/ppermute | solution.py:356
  84.8 3.7 %collective-permute-done.30 = bf16[256,128]{1,0:T(8,128)(2,1)S(1)} collective-permute-done((bf16[256,128]{1,0:T(8,128)(2,1)S(1)}, bf16[256,128]{1,0:T(8,128)(2,1)S(1)}, u32[]{:S(2)}, u32[]{:S(2)}) %collective-permute-start.30) | collective-permute-done | bytes 65568 | tf_op jit(solution)/shard_map/ppermute | solution.py:356
  93.7 1.8 %collective-permute-start.36 = (bf16[2,256,128]{2,1,0:T(8,128)(2,1)S(1)}, bf16[2,256,128]{2,1,0:T(8,128)(2,1)S(1)}, u32[]{:S(2)}, u32[]{:S(2)}) collective-permute-start(bf16[2,256,128]{2,1,0:T(8,128)(2,1)S(1)} %slice.359), channel_id=1, source_target_pairs={{0,16},{4,20},{8,24},{12,28},{16,0},{20,4},{24,8},{28,12},{1,17},{... | collective-permute-start | bytes 393224 | tf_op jit(solution)/shard_map/ppermute | solution.py:356
  97.0 2.8 %collective-permute-done.36 = bf16[2,256,128]{2,1,0:T(8,128)(2,1)S(1)} collective-permute-done((bf16[2,256,128]{2,1,0:T(8,128)(2,1)S(1)}, bf16[2,256,128]{2,1,0:T(8,128)(2,1)S(1)}, u32[]{:S(2)}, u32[]{:S(2)}) %collective-permute-start.36) | collective-permute-done | bytes 131104 | tf_op jit(solution)/shard_map/ppermute | solution.py:356
  102.1 3.7 %collective-permute-done.38 = bf16[256,128]{1,0:T(8,128)(2,1)S(1)} collective-permute-done((bf16[256,128]{1,0:T(8,128)(2,1)S(1)}, bf16[256,128]{1,0:T(8,128)(2,1)S(1)}, u32[]{:S(2)}, u32[]{:S(2)}) %collective-permute-start.38) | collective-permute-done | bytes 65568 | tf_op jit(solution)/shard_map/ppermute | solution.py:356
  110.8 1.7 %collective-permute-start.45 = (bf16[512,128]{1,0:T(8,128)(2,1)S(1)}, bf16[512,128]{1,0:T(8,128)(2,1)S(1)}, u32[]{:S(2)}, u32[]{:S(2)}) collective-permute-start(bf16[512,128]{1,0:T(8,128)(2,1)S(1)} %get-tuple-element.54), channel_id=1, source_target_pairs={{0,16},{4,20},{8,24},{12,28},{16,0},{20,4},{24,8},{28,12},{1,17},{... | collective-permute-start | bytes 393224 | tf_op jit(solution)/shard_map/ppermute | solution.py:356
  112.8 3.8 %collective-permute-done.44.refs_0_ = bf16[512,128]{1,0:T(8,128)(2,1)S(1)} collective-permute-done((bf16[512,128]{1,0:T(8,128)(2,1)S(1)}, bf16[512,128]{1,0:T(8,128)(2,1)S(1)}, u32[]{:S(2)}, u32[]{:S(2)}) %collective-permute-start.44) | collective-permute-done | bytes 131104 | tf_op jit(solution)/shard_map/ppermute | solution.py:356
  116.6 2.0 %collective-permute-done.45.refs_1_ = bf16[512,128]{1,0:T(8,128)(2,1)S(1)} collective-permute-done((bf16[512,128]{1,0:T(8,128)(2,1)S(1)}, bf16[512,128]{1,0:T(8,128)(2,1)S(1)}, u32[]{:S(2)}, u32[]{:S(2)}) %collective-permute-start.45) | collective-permute-done | bytes 131104 | tf_op jit(solution)/shard_map/ppermute | solution.py:356
  (174 shorter events, 48.2 us)
Async XLA Ops:
  1.5 14.1 %collective-permute-start = (bf16[512,128]{1,0:T(8,128)(2,1)S(1)}, bf16[512,128]{1,0:T(8,128)(2,1)S(1)}, u32[]{:S(2)}, u32[]{:S(2)}) collective-permute-start(bf16[512,128]{1,0:T(8,128)(2,1)S(1)} %get-tuple-element.28.refs_2_), channel_id=1, source_target_pairs={{0,2},{1,3},{2,0},{3,1},{4,6},{5,7},{6,4},{7,5},{8,10},{9,11},{10,... | collective-permute-start | bytes 393224 | tf_op jit(solution)/shard_map/ppermute | solution.py:356
  5.6 10.0 %collective-permute-start.1 = (bf16[512,128]{1,0:T(8,128)(2,1)S(1)}, bf16[512,128]{1,0:T(8,128)(2,1)S(1)}, u32[]{:S(2)}, u32[]{:S(2)}) collective-permute-start(bf16[512,128]{1,0:T(8,128)(2,1)S(1)} %get-tuple-element.28.refs_2_), channel_id=1, source_target_pairs={{0,3},{1,2},{2,1},{3,0},{4,7},{5,6},{6,5},{7,4},{8,11},{9,10},{10,... | collective-permute-start | bytes 393224 | tf_op jit(solution)/shard_map/ppermute | solution.py:356
  7.0 9.2 %collective-permute-start.2 = (bf16[512,128]{1,0:T(8,128)(2,1)S(1)}, bf16[512,128]{1,0:T(8,128)(2,1)S(1)}, u32[]{:S(2)}, u32[]{:S(2)}) collective-permute-start(bf16[512,128]{1,0:T(8,128)(2,1)S(1)} %get-tuple-element.28.refs_2_), channel_id=1, source_target_pairs={{0,1},{1,0},{2,3},{3,2},{4,5},{5,4},{6,7},{7,6},{8,9},{9,8},{10,11... | collective-permute-start | bytes 393224 | tf_op jit(solution)/shard_map/ppermute | solution.py:356
  17.7 18.3 %collective-permute-start.8 = (bf16[512,128]{1,0:T(8,128)(2,1)S(1)}, bf16[512,128]{1,0:T(8,128)(2,1)S(1)}, u32[]{:S(2)}, u32[]{:S(2)}) collective-permute-start(bf16[512,128]{1,0:T(8,128)(2,1)S(1)} %get-tuple-element.38.refs_2_), channel_id=1, source_target_pairs={{0,2},{1,3},{2,0},{3,1},{4,6},{5,7},{6,4},{7,5},{8,10},{9,11},{10,... | collective-permute-start | bytes 393224 | tf_op jit(solution)/shard_map/ppermute | solution.py:356
  22.2 13.7 %collective-permute-start.9 = (bf16[512,128]{1,0:T(8,128)(2,1)S(1)}, bf16[512,128]{1,0:T(8,128)(2,1)S(1)}, u32[]{:S(2)}, u32[]{:S(2)}) collective-permute-start(bf16[512,128]{1,0:T(8,128)(2,1)S(1)} %get-tuple-element.38.refs_2_), channel_id=1, source_target_pairs={{0,3},{1,2},{2,1},{3,0},{4,7},{5,6},{6,5},{7,4},{8,11},{9,10},{10,... | collective-permute-start | bytes 393224 | tf_op jit(solution)/shard_map/ppermute | solution.py:356
  23.4 6.1 %collective-permute-start.4 = (bf16[2,256,128]{2,1,0:T(8,128)(2,1)S(1)}, bf16[2,256,128]{2,1,0:T(8,128)(2,1)S(1)}, u32[]{:S(2)}, u32[]{:S(2)}) collective-permute-start(bf16[2,256,128]{2,1,0:T(8,128)(2,1)S(1)} %slice.363), channel_id=1, source_target_pairs={{0,16},{4,20},{8,24},{12,28},{16,0},{20,4},{24,8},{28,12},{1,17},{... | collective-permute-start | bytes 393224 | tf_op jit(solution)/shard_map/ppermute | solution.py:356
  25.0 6.3 %collective-permute-start.5 = (bf16[2,272,128]{2,1,0:T(8,128)(2,1)S(1)}, bf16[2,272,128]{2,1,0:T(8,128)(2,1)S(1)}, u32[]{:S(2)}, u32[]{:S(2)}) collective-permute-start(bf16[2,272,128]{2,1,0:T(8,128)(2,1)S(1)} %fusion.5), channel_id=1, source_target_pairs={{0,8},{4,12},{8,0},{12,4},{16,24},{20,28},{24,16},{28,20},{1,9},{5... | collective-permute-start | bytes 417800 | tf_op jit(solution)/shard_map/ppermute | solution.py:356
  26.5 9.4 %collective-permute-start.10 = (bf16[512,128]{1,0:T(8,128)(2,1)S(1)}, bf16[512,128]{1,0:T(8,128)(2,1)S(1)}, u32[]{:S(2)}, u32[]{:S(2)}) collective-permute-start(bf16[512,128]{1,0:T(8,128)(2,1)S(1)} %get-tuple-element.38.refs_2_), channel_id=1, source_target_pairs={{0,1},{1,0},{2,3},{3,2},{4,5},{5,4},{6,7},{7,6},{8,9},{9,8},{10,11... | collective-permute-start | bytes 393224 | tf_op jit(solution)/shard_map/ppermute | solution.py:356
  29.6 6.1 %collective-permute-start.6 = (bf16[256,128]{1,0:T(8,128)(2,1)S(1)}, bf16[256,128]{1,0:T(8,128)(2,1)S(1)}, u32[]{:S(2)}, u32[]{:S(2)}) collective-permute-start(bf16[256,128]{1,0:T(8,128)(2,1)S(1)} %fusion.11), channel_id=1, source_target_pairs={{0,8},{4,12},{8,0},{12,4},{16,24},{20,28},{24,16},{28,20},{1,9},{5... | collective-permute-start | bytes 196616 | tf_op jit(solution)/shard_map/ppermute | solution.py:356
  37.5 16.6 %collective-permute-start.16 = (bf16[512,128]{1,0:T(8,128)(2,1)S(1)}, bf16[512,128]{1,0:T(8,128)(2,1)S(1)}, u32[]{:S(2)}, u32[]{:S(2)}) collective-permute-start(bf16[512,128]{1,0:T(8,128)(2,1)S(1)} %update.6.refs_4_.refs_2_.refs_1_), channel_id=1, source_target_pairs={{0,2},{1,3},{2,0},{3,1},{4,6},{5,7},{6,4},{7,5},{8,10},{9,11},{10,... | collective-permute-start | bytes 393224 | tf_op jit(solution)/shard_map/ppermute | solution.py:356
  38.3 15.8 %collective-permute-start.17 = (bf16[512,128]{1,0:T(8,128)(2,1)S(1)}, bf16[512,128]{1,0:T(8,128)(2,1)S(1)}, u32[]{:S(2)}, u32[]{:S(2)}) collective-permute-start(bf16[512,128]{1,0:T(8,128)(2,1)S(1)} %update.6.refs_4_.refs_2_.refs_1_), channel_id=1, source_target_pairs={{0,3},{1,2},{2,1},{3,0},{4,7},{5,6},{6,5},{7,4},{8,11},{9,10},{10,... | collective-permute-start | bytes 393224 | tf_op jit(solution)/shard_map/ppermute | solution.py:356
  43.8 10.2 %collective-permute-start.18 = (bf16[512,128]{1,0:T(8,128)(2,1)S(1)}, bf16[512,128]{1,0:T(8,128)(2,1)S(1)}, u32[]{:S(2)}, u32[]{:S(2)}) collective-permute-start(bf16[512,128]{1,0:T(8,128)(2,1)S(1)} %update.6.refs_4_.refs_2_.refs_1_), channel_id=1, source_target_pairs={{0,1},{1,0},{2,3},{3,2},{4,5},{5,4},{6,7},{7,6},{8,9},{9,8},{10,11... | collective-permute-start | bytes 393224 | tf_op jit(solution)/shard_map/ppermute | solution.py:356
  55.1 16.0 %collective-permute-start.24 = (bf16[512,128]{1,0:T(8,128)(2,1)S(1)}, bf16[512,128]{1,0:T(8,128)(2,1)S(1)}, u32[]{:S(2)}, u32[]{:S(2)}) collective-permute-start(bf16[512,128]{1,0:T(8,128)(2,1)S(1)} %update.7.refs_4_.refs_2_.refs_1_), channel_id=1, source_target_pairs={{0,2},{1,3},{2,0},{3,1},{4,6},{5,7},{6,4},{7,5},{8,10},{9,11},{10,... | collective-permute-start | bytes 393224 | tf_op jit(solution)/shard_map/ppermute | solution.py:356
  56.8 14.3 %collective-permute-start.25 = (bf16[512,128]{1,0:T(8,128)(2,1)S(1)}, bf16[512,128]{1,0:T(8,128)(2,1)S(1)}, u32[]{:S(2)}, u32[]{:S(2)}) collective-permute-start(bf16[512,128]{1,0:T(8,128)(2,1)S(1)} %update.7.refs_4_.refs_2_.refs_1_), channel_id=1, source_target_pairs={{0,3},{1,2},{2,1},{3,0},{4,7},{5,6},{6,5},{7,4},{8,11},{9,10},{10,... | collective-permute-start | bytes 393224 | tf_op jit(solution)/shard_map/ppermute | solution.py:356
  58.7 6.1 %collective-permute-start.20 = (bf16[2,256,128]{2,1,0:T(8,128)(2,1)S(1)}, bf16[2,256,128]{2,1,0:T(8,128)(2,1)S(1)}, u32[]{:S(2)}, u32[]{:S(2)}) collective-permute-start(bf16[2,256,128]{2,1,0:T(8,128)(2,1)S(1)} %slice.361), channel_id=1, source_target_pairs={{0,16},{4,20},{8,24},{12,28},{16,0},{20,4},{24,8},{28,12},{1,17},{... | collective-permute-start | bytes 393224 | tf_op jit(solution)/shard_map/ppermute | solution.py:356
  61.1 10.1 %collective-permute-start.26 = (bf16[512,128]{1,0:T(8,128)(2,1)S(1)}, bf16[512,128]{1,0:T(8,128)(2,1)S(1)}, u32[]{:S(2)}, u32[]{:S(2)}) collective-permute-start(bf16[512,128]{1,0:T(8,128)(2,1)S(1)} %update.7.refs_4_.refs_2_.refs_1_), channel_id=1, source_target_pairs={{0,1},{1,0},{2,3},{3,2},{4,5},{5,4},{6,7},{7,6},{8,9},{9,8},{10,11... | collective-permute-start | bytes 393224 | tf_op jit(solution)/shard_map/ppermute | solution.py:356
  72.2 16.7 %collective-permute-start.32 = (bf16[512,128]{1,0:T(8,128)(2,1)S(1)}, bf16[512,128]{1,0:T(8,128)(2,1)S(1)}, u32[]{:S(2)}, u32[]{:S(2)}) collective-permute-start(bf16[512,128]{1,0:T(8,128)(2,1)S(1)} %update.8.refs_4_.refs_2_.refs_1_), channel_id=1, source_target_pairs={{0,2},{1,3},{2,0},{3,1},{4,6},{5,7},{6,4},{7,5},{8,10},{9,11},{10,... | collective-permute-start | bytes 393224 | tf_op jit(solution)/shard_map/ppermute | solution.py:356
  72.7 16.2 %collective-permute-start.33 = (bf16[512,128]{1,0:T(8,128)(2,1)S(1)}, bf16[512,128]{1,0:T(8,128)(2,1)S(1)}, u32[]{:S(2)}, u32[]{:S(2)}) collective-permute-start(bf16[512,128]{1,0:T(8,128)(2,1)S(1)} %update.8.refs_4_.refs_2_.refs_1_), channel_id=1, source_target_pairs={{0,3},{1,2},{2,1},{3,0},{4,7},{5,6},{6,5},{7,4},{8,11},{9,10},{10,... | collective-permute-start | bytes 393224 | tf_op jit(solution)/shard_map/ppermute | solution.py:356
  78.6 10.3 %collective-permute-start.34 = (bf16[512,128]{1,0:T(8,128)(2,1)S(1)}, bf16[512,128]{1,0:T(8,128)(2,1)S(1)}, u32[]{:S(2)}, u32[]{:S(2)}) collective-permute-start(bf16[512,128]{1,0:T(8,128)(2,1)S(1)} %update.8.refs_4_.refs_2_.refs_1_), channel_id=1, source_target_pairs={{0,1},{1,0},{2,3},{3,2},{4,5},{5,4},{6,7},{7,6},{8,9},{9,8},{10,11... | collective-permute-start | bytes 393224 | tf_op jit(solution)/shard_map/ppermute | solution.py:356
  89.9 16.2 %collective-permute-start.40 = (bf16[512,128]{1,0:T(8,128)(2,1)S(1)}, bf16[512,128]{1,0:T(8,128)(2,1)S(1)}, u32[]{:S(2)}, u32[]{:S(2)}) collective-permute-start(bf16[512,128]{1,0:T(8,128)(2,1)S(1)} %update.9.refs_4_.refs_2_.refs_3_), channel_id=1, source_target_pairs={{0,2},{1,3},{2,0},{3,1},{4,6},{5,7},{6,4},{7,5},{8,10},{9,11},{10,... | collective-permute-start | bytes 393224 | tf_op jit(solution)/shard_map/ppermute | solution.py:356
  91.2 14.9 %collective-permute-start.41 = (bf16[512,128]{1,0:T(8,128)(2,1)S(1)}, bf16[512,128]{1,0:T(8,128)(2,1)S(1)}, u32[]{:S(2)}, u32[]{:S(2)}) collective-permute-start(bf16[512,128]{1,0:T(8,128)(2,1)S(1)} %update.9.refs_4_.refs_2_.refs_3_), channel_id=1, source_target_pairs={{0,3},{1,2},{2,1},{3,0},{4,7},{5,6},{6,5},{7,4},{8,11},{9,10},{10,... | collective-permute-start | bytes 393224 | tf_op jit(solution)/shard_map/ppermute | solution.py:356
  96.0 10.1 %collective-permute-start.42 = (bf16[512,128]{1,0:T(8,128)(2,1)S(1)}, bf16[512,128]{1,0:T(8,128)(2,1)S(1)}, u32[]{:S(2)}, u32[]{:S(2)}) collective-permute-start(bf16[512,128]{1,0:T(8,128)(2,1)S(1)} %update.9.refs_4_.refs_2_.refs_3_), channel_id=1, source_target_pairs={{0,1},{1,0},{2,3},{3,2},{4,5},{5,4},{6,7},{7,6},{8,9},{9,8},{10,11... | collective-permute-start | bytes 393224 | tf_op jit(solution)/shard_map/ppermute | solution.py:356
  109.3 7.3 %collective-permute-start.44 = (bf16[512,128]{1,0:T(8,128)(2,1)S(1)}, bf16[512,128]{1,0:T(8,128)(2,1)S(1)}, u32[]{:S(2)}, u32[]{:S(2)}) collective-permute-start(bf16[512,128]{1,0:T(8,128)(2,1)S(1)} %get-tuple-element.55), channel_id=1, source_target_pairs={{0,24},{4,28},{8,16},{12,20},{16,8},{20,12},{24,0},{28,4},{1,25},{... | collective-permute-start | bytes 393224 | tf_op jit(solution)/shard_map/ppermute | solution.py:356
  110.8 7.8 %collective-permute-start.45 = (bf16[512,128]{1,0:T(8,128)(2,1)S(1)}, bf16[512,128]{1,0:T(8,128)(2,1)S(1)}, u32[]{:S(2)}, u32[]{:S(2)}) collective-permute-start(bf16[512,128]{1,0:T(8,128)(2,1)S(1)} %get-tuple-element.54), channel_id=1, source_target_pairs={{0,16},{4,20},{8,24},{12,28},{16,0},{20,4},{24,8},{28,12},{1,17},{... | collective-permute-start | bytes 393224 | tf_op jit(solution)/shard_map/ppermute | solution.py:356
  (26 other events, 126.3 us)

commit v15 on v14

--- a/solution.py
+++ b/solution.py
@@ -16,7 +16,7 @@
 CHUNKS = 2
 
 
-UNROLL = 12
+UNROLL = 24
 
 
 EXTRA = 16

time: 120 us -> 119 us (level)
  waiting for transfers between devices: 47.8 us -> 36.7 us
  Pallas kernels: 19 us -> 25.5 us
  starting transfers between devices: 45.7 us -> 49.3 us
    ppermute x47, waiting for transfers between devices: 47.8 us -> 36.7 us  [exchange(): return lax.ppermute(block, axis, [(i, i ^ mask) for i in range(size)])]
    pallas_call x12, Pallas kernels: 10.8 us -> 16.8 us  [product(): pl.pallas_call(functools.partial(product_kernel, half, rows, bits), out_s...]
    ppermute x47, starting transfers between devices: 45.7 us -> 49.3 us  [exchange(): return lax.ppermute(block, axis, [(i, i ^ mask) for i in range(size)])]
  transfers between devices with their start and end apart: 47 -> 47, of which waited for: 23 -> 22; matrix products, arithmetic and copies ran while one was open for 1% -> 1% of each run, Pallas kernels for 10% -> 13%
where the time goes in v15:
time: 119 us
  starting transfers between devices  49.3 us (41%)
  waiting for transfers between devices  36.7 us (31%)
  Pallas kernels  25.5 us (21%)
  local copies, waits for them, and re-layouts  5.28 us (4%)
  other arithmetic  1.19 us (1%)
    ppermute x47, starting transfers between devices, exchange(): return lax.ppermute(block, axis, [(i, i ^ mask) for i in range(size)])  49.3 us
    ppermute x47, waiting for transfers between devices, exchange(): return lax.ppermute(block, axis, [(i, i ^ mask) for i in range(size)])  36.7 us
    pallas_call x12, Pallas kernels, product(): pl.pallas_call(functools.partial(product_kernel, half, rows, bits), out_s...  16.8 us
    pallas_call x1, Pallas kernels, prepare(): pl.pallas_call(functools.partial(prepare_kernel, tiles_per_owner, bits),...  6.68 us
    unnamed x7, local copies, waits for them, and re-layouts  3.44 us
  transfers between devices with their start and end apart: 47, of which 22 were waited for; matrix products, arithmetic and copies ran while one was open for 1% of the time, Pallas kernels for 13%

profile of v15, /device:TPU:0, one launch (start us, length us, event | category | flops | bytes accessed | tf_op | source)
XLA Modules:
  0.0 118.8 jit_solution(673978379137788482)
XLA Ops:
  1.5 4.1 %collective-permute-start = (bf16[512,128]{1,0:T(8,128)(2,1)S(1)}, bf16[512,128]{1,0:T(8,128)(2,1)S(1)}, u32[]{:S(2)}, u32[]{:S(2)}) collective-permute-start(bf16[512,128]{1,0:T(8,128)(2,1)S(1)} %get-tuple-element.28.refs_2_), channel_id=1, source_target_pairs={{0,2},{1,3},{2,0},{3,1},{4,6},{5,7},{6,4},{7,5},{8,10},{9,11},{10,... | collective-permute-start | bytes 393224 | tf_op jit(solution)/shard_map/ppermute | solution.py:356
  7.3 2.2 %copy-done = bf16[128,128,128]{2,1,0:T(8,128)(2,1)S(1)} copy-done((bf16[128,128,128]{2,1,0:T(8,128)(2,1)S(1)}, bf16[128,128,128]{2,1,0:T(8,128)(2,1)}, u32[]{:S(2)}) %copy-start) | copy-done | bytes 4194328
  9.5 6.7 %prepare.1 = (bf16[128,128,128]{2,1,0:T(8,128)(2,1)S(1)}, f32[2,4,16,128]{3,2,1,0:T(8,128)S(1)}, s32[8,24]{1,0:T(8,128)S(1)}) custom-call(s32[3]{0:T(128)S(1)} %pad_add_fusion.refs_4_.place_ref, s32[1,128]{1,0:T(1,128)S(1)} %copy-done.1, s32[1,32]{1,0:T(1,128)S(1)} %copy-done.2, bf16[128,128,128]{2,1,0:T(8,128)(2,1)S(1)} %copy-done), custom_call_target="tpu_custom_call" | custom-call | tf_op jit(solution)/shard_map/prepare/pallas_call | solution.py:187
  18.2 3.5 %collective-permute-start.8 = (bf16[512,128]{1,0:T(8,128)(2,1)S(1)}, bf16[512,128]{1,0:T(8,128)(2,1)S(1)}, u32[]{:S(2)}, u32[]{:S(2)}) collective-permute-start(bf16[512,128]{1,0:T(8,128)(2,1)S(1)} %get-tuple-element.38.refs_2_), channel_id=1, source_target_pairs={{0,2},{1,3},{2,0},{3,1},{4,6},{5,7},{6,4},{7,5},{8,10},{9,11},{10,... | collective-permute-start | bytes 393224 | tf_op jit(solution)/shard_map/ppermute | solution.py:356
  26.8 1.9 %collective-permute-done.4 = bf16[2,256,128]{2,1,0:T(8,128)(2,1)S(1)} collective-permute-done((bf16[2,256,128]{2,1,0:T(8,128)(2,1)S(1)}, bf16[2,256,128]{2,1,0:T(8,128)(2,1)S(1)}, u32[]{:S(2)}, u32[]{:S(2)}) %collective-permute-start.4) | collective-permute-done | bytes 131104 | tf_op jit(solution)/shard_map/ppermute | solution.py:356
  28.8 1.9 %collective-permute-start.6 = (bf16[256,128]{1,0:T(8,128)(2,1)S(1)}, bf16[256,128]{1,0:T(8,128)(2,1)S(1)}, u32[]{:S(2)}, u32[]{:S(2)}) collective-permute-start(bf16[256,128]{1,0:T(8,128)(2,1)S(1)} %fusion.11), channel_id=1, source_target_pairs={{0,8},{4,12},{8,0},{12,4},{16,24},{20,28},{24,16},{28,20},{1,9},{5... | collective-permute-start | bytes 196616 | tf_op jit(solution)/shard_map/ppermute | solution.py:356
  32.0 3.1 %collective-permute-done.7 = bf16[272,128]{1,0:T(8,128)(2,1)S(1)} collective-permute-done((bf16[272,128]{1,0:T(8,128)(2,1)S(1)}, bf16[272,128]{1,0:T(8,128)(2,1)S(1)}, u32[]{:S(2)}, u32[]{:S(2)}) %collective-permute-start.7) | collective-permute-done | bytes 69664 | tf_op jit(solution)/shard_map/ppermute | solution.py:356
  37.6 2.2 %collective-permute-start.17 = (bf16[512,128]{1,0:T(8,128)(2,1)S(1)}, bf16[512,128]{1,0:T(8,128)(2,1)S(1)}, u32[]{:S(2)}, u32[]{:S(2)}) collective-permute-start(bf16[512,128]{1,0:T(8,128)(2,1)S(1)} %update.6.refs_4_.refs_2_.refs_1_), channel_id=1, source_target_pairs={{0,3},{1,2},{2,1},{3,0},{4,7},{5,6},{6,5},{7,4},{8,11},{9,10},{10,... | collective-permute-start | bytes 393224 | tf_op jit(solution)/shard_map/ppermute | solution.py:356
  43.4 3.0 %collective-permute-done.12 = bf16[2,256,128]{2,1,0:T(8,128)(2,1)S(1)} collective-permute-done((bf16[2,256,128]{2,1,0:T(8,128)(2,1)S(1)}, bf16[2,256,128]{2,1,0:T(8,128)(2,1)S(1)}, u32[]{:S(2)}, u32[]{:S(2)}) %collective-permute-start.12) | collective-permute-done | bytes 131104 | tf_op jit(solution)/shard_map/ppermute | solution.py:356
  48.5 1.7 %collective-permute-start.15 = (bf16[256,128]{1,0:T(8,128)(2,1)S(1)}, bf16[256,128]{1,0:T(8,128)(2,1)S(1)}, u32[]{:S(2)}, u32[]{:S(2)}) collective-permute-start(bf16[256,128]{1,0:T(8,128)(2,1)S(1)} %fusion.13), channel_id=1, source_target_pairs={{0,16},{4,20},{8,24},{12,28},{16,0},{20,4},{24,8},{28,12},{1,17},{... | collective-permute-start | bytes 196616 | tf_op jit(solution)/shard_map/ppermute | solution.py:356
  50.2 2.1 %collective-permute-done.14 = bf16[256,128]{1,0:T(8,128)(2,1)S(1)} collective-permute-done((bf16[256,128]{1,0:T(8,128)(2,1)S(1)}, bf16[256,128]{1,0:T(8,128)(2,1)S(1)}, u32[]{:S(2)}, u32[]{:S(2)}) %collective-permute-start.14) | collective-permute-done | bytes 65568 | tf_op jit(solution)/shard_map/ppermute | solution.py:356
  55.3 1.8 %collective-permute-start.25 = (bf16[512,128]{1,0:T(8,128)(2,1)S(1)}, bf16[512,128]{1,0:T(8,128)(2,1)S(1)}, u32[]{:S(2)}, u32[]{:S(2)}) collective-permute-start(bf16[512,128]{1,0:T(8,128)(2,1)S(1)} %update.7.refs_4_.refs_2_.refs_1_), channel_id=1, source_target_pairs={{0,3},{1,2},{2,1},{3,0},{4,7},{5,6},{6,5},{7,4},{8,11},{9,10},{10,... | collective-permute-start | bytes 393224 | tf_op jit(solution)/shard_map/ppermute | solution.py:356
  60.9 2.9 %collective-permute-done.20 = bf16[2,256,128]{2,1,0:T(8,128)(2,1)S(1)} collective-permute-done((bf16[2,256,128]{2,1,0:T(8,128)(2,1)S(1)}, bf16[2,256,128]{2,1,0:T(8,128)(2,1)S(1)}, u32[]{:S(2)}, u32[]{:S(2)}) %collective-permute-start.20) | collective-permute-done | bytes 131104 | tf_op jit(solution)/shard_map/ppermute | solution.py:356
  65.3 1.7 %collective-permute-start.23 = (bf16[256,128]{1,0:T(8,128)(2,1)S(1)}, bf16[256,128]{1,0:T(8,128)(2,1)S(1)}, u32[]{:S(2)}, u32[]{:S(2)}) collective-permute-start(bf16[256,128]{1,0:T(8,128)(2,1)S(1)} %fusion.15), channel_id=1, source_target_pairs={{0,16},{4,20},{8,24},{12,28},{16,0},{20,4},{24,8},{28,12},{1,17},{... | collective-permute-start | bytes 196616 | tf_op jit(solution)/shard_map/ppermute | solution.py:356
  67.1 1.9 %collective-permute-done.22 = bf16[256,128]{1,0:T(8,128)(2,1)S(1)} collective-permute-done((bf16[256,128]{1,0:T(8,128)(2,1)S(1)}, bf16[256,128]{1,0:T(8,128)(2,1)S(1)}, u32[]{:S(2)}, u32[]{:S(2)}) %collective-permute-start.22) | collective-permute-done | bytes 65568 | tf_op jit(solution)/shard_map/ppermute | solution.py:356
  71.3 2.8 %collective-permute-start.33 = (bf16[512,128]{1,0:T(8,128)(2,1)S(1)}, bf16[512,128]{1,0:T(8,128)(2,1)S(1)}, u32[]{:S(2)}, u32[]{:S(2)}) collective-permute-start(bf16[512,128]{1,0:T(8,128)(2,1)S(1)} %update.8.refs_4_.refs_2_.refs_1_), channel_id=1, source_target_pairs={{0,3},{1,2},{2,1},{3,0},{4,7},{5,6},{6,5},{7,4},{8,11},{9,10},{10,... | collective-permute-start | bytes 393224 | tf_op jit(solution)/shard_map/ppermute | solution.py:356
  78.2 2.7 %collective-permute-done.28 = bf16[2,256,128]{2,1,0:T(8,128)(2,1)S(1)} collective-permute-done((bf16[2,256,128]{2,1,0:T(8,128)(2,1)S(1)}, bf16[2,256,128]{2,1,0:T(8,128)(2,1)S(1)}, u32[]{:S(2)}, u32[]{:S(2)}) %collective-permute-start.28) | collective-permute-done | bytes 131104 | tf_op jit(solution)/shard_map/ppermute | solution.py:356
  83.0 1.7 %collective-permute-start.31 = (bf16[256,128]{1,0:T(8,128)(2,1)S(1)}, bf16[256,128]{1,0:T(8,128)(2,1)S(1)}, u32[]{:S(2)}, u32[]{:S(2)}) collective-permute-start(bf16[256,128]{1,0:T(8,128)(2,1)S(1)} %fusion.17), channel_id=1, source_target_pairs={{0,16},{4,20},{8,24},{12,28},{16,0},{20,4},{24,8},{28,12},{1,17},{... | collective-permute-start | bytes 196616 | tf_op jit(solution)/shard_map/ppermute | solution.py:356
  89.2 2.5 %collective-permute-start.41 = (bf16[512,128]{1,0:T(8,128)(2,1)S(1)}, bf16[512,128]{1,0:T(8,128)(2,1)S(1)}, u32[]{:S(2)}, u32[]{:S(2)}) collective-permute-start(bf16[512,128]{1,0:T(8,128)(2,1)S(1)} %update.9.refs_4_.refs_2_.refs_3_), channel_id=1, source_target_pairs={{0,3},{1,2},{2,1},{3,0},{4,7},{5,6},{6,5},{7,4},{8,11},{9,10},{10,... | collective-permute-start | bytes 393224 | tf_op jit(solution)/shard_map/ppermute | solution.py:356
  95.5 2.9 %collective-permute-done.36 = bf16[2,256,128]{2,1,0:T(8,128)(2,1)S(1)} collective-permute-done((bf16[2,256,128]{2,1,0:T(8,128)(2,1)S(1)}, bf16[2,256,128]{2,1,0:T(8,128)(2,1)S(1)}, u32[]{:S(2)}, u32[]{:S(2)}) %collective-permute-start.36) | collective-permute-done | bytes 131104 | tf_op jit(solution)/shard_map/ppermute | solution.py:356
  99.9 1.7 %collective-permute-start.39 = (bf16[256,128]{1,0:T(8,128)(2,1)S(1)}, bf16[256,128]{1,0:T(8,128)(2,1)S(1)}, u32[]{:S(2)}, u32[]{:S(2)}) collective-permute-start(bf16[256,128]{1,0:T(8,128)(2,1)S(1)} %fusion.19), channel_id=1, source_target_pairs={{0,16},{4,20},{8,24},{12,28},{16,0},{20,4},{24,8},{28,12},{1,17},{... | collective-permute-start | bytes 196616 | tf_op jit(solution)/shard_map/ppermute | solution.py:356
  109.8 1.7 %collective-permute-start.46 = (bf16[512,128]{1,0:T(8,128)(2,1)S(1)}, bf16[512,128]{1,0:T(8,128)(2,1)S(1)}, u32[]{:S(2)}, u32[]{:S(2)}) collective-permute-start(bf16[512,128]{1,0:T(8,128)(2,1)S(1)} %get-tuple-element.53), channel_id=1, source_target_pairs={{0,8},{4,12},{8,0},{12,4},{16,24},{20,28},{24,16},{28,20},{1,9},{5... | collective-permute-start | bytes 393224 | tf_op jit(solution)/shard_map/ppermute | solution.py:356
  111.5 3.7 %collective-permute-done.44.refs_0_ = bf16[512,128]{1,0:T(8,128)(2,1)S(1)} collective-permute-done((bf16[512,128]{1,0:T(8,128)(2,1)S(1)}, bf16[512,128]{1,0:T(8,128)(2,1)S(1)}, u32[]{:S(2)}, u32[]{:S(2)}) %collective-permute-start.44) | collective-permute-done | bytes 131104 | tf_op jit(solution)/shard_map/ppermute | solution.py:356
  115.2 2.0 %collective-permute-done.45.refs_1_ = bf16[512,128]{1,0:T(8,128)(2,1)S(1)} collective-permute-done((bf16[512,128]{1,0:T(8,128)(2,1)S(1)}, bf16[512,128]{1,0:T(8,128)(2,1)S(1)}, u32[]{:S(2)}, u32[]{:S(2)}) %collective-permute-start.45) | collective-permute-done | bytes 131104 | tf_op jit(solution)/shard_map/ppermute | solution.py:356
  (174 shorter events, 55.5 us)
Async XLA Ops:
  1.5 14.6 %collective-permute-start = (bf16[512,128]{1,0:T(8,128)(2,1)S(1)}, bf16[512,128]{1,0:T(8,128)(2,1)S(1)}, u32[]{:S(2)}, u32[]{:S(2)}) collective-permute-start(bf16[512,128]{1,0:T(8,128)(2,1)S(1)} %get-tuple-element.28.refs_2_), channel_id=1, source_target_pairs={{0,2},{1,3},{2,0},{3,1},{4,6},{5,7},{6,4},{7,5},{8,10},{9,11},{10,... | collective-permute-start | bytes 393224 | tf_op jit(solution)/shard_map/ppermute | solution.py:356
  5.6 10.6 %collective-permute-start.1 = (bf16[512,128]{1,0:T(8,128)(2,1)S(1)}, bf16[512,128]{1,0:T(8,128)(2,1)S(1)}, u32[]{:S(2)}, u32[]{:S(2)}) collective-permute-start(bf16[512,128]{1,0:T(8,128)(2,1)S(1)} %get-tuple-element.28.refs_2_), channel_id=1, source_target_pairs={{0,3},{1,2},{2,1},{3,0},{4,7},{5,6},{6,5},{7,4},{8,11},{9,10},{10,... | collective-permute-start | bytes 393224 | tf_op jit(solution)/shard_map/ppermute | solution.py:356
  7.0 9.2 %collective-permute-start.2 = (bf16[512,128]{1,0:T(8,128)(2,1)S(1)}, bf16[512,128]{1,0:T(8,128)(2,1)S(1)}, u32[]{:S(2)}, u32[]{:S(2)}) collective-permute-start(bf16[512,128]{1,0:T(8,128)(2,1)S(1)} %get-tuple-element.28.refs_2_), channel_id=1, source_target_pairs={{0,1},{1,0},{2,3},{3,2},{4,5},{5,4},{6,7},{7,6},{8,9},{9,8},{10,11... | collective-permute-start | bytes 393224 | tf_op jit(solution)/shard_map/ppermute | solution.py:356
  18.1 5.4 %collective-permute-start.3 = (bf16[4,528,128]{2,1,0:T(8,128)(2,1)S(1)}, bf16[4,528,128]{2,1,0:T(8,128)(2,1)S(1)}, u32[]{:S(2)}, u32[]{:S(2)}) collective-permute-start(bf16[4,528,128]{2,1,0:T(8,128)(2,1)S(1)} %product.13), channel_id=1, source_target_pairs={{0,4},{4,0},{8,12},{12,8},{16,20},{20,16},{24,28},{28,24},{1,5},{5... | collective-permute-start | bytes 1622024 | tf_op jit(solution)/shard_map/ppermute | solution.py:356
  18.2 17.2 %collective-permute-start.8 = (bf16[512,128]{1,0:T(8,128)(2,1)S(1)}, bf16[512,128]{1,0:T(8,128)(2,1)S(1)}, u32[]{:S(2)}, u32[]{:S(2)}) collective-permute-start(bf16[512,128]{1,0:T(8,128)(2,1)S(1)} %get-tuple-element.38.refs_2_), channel_id=1, source_target_pairs={{0,2},{1,3},{2,0},{3,1},{4,6},{5,7},{6,4},{7,5},{8,10},{9,11},{10,... | collective-permute-start | bytes 393224 | tf_op jit(solution)/shard_map/ppermute | solution.py:356
  21.7 13.7 %collective-permute-start.9 = (bf16[512,128]{1,0:T(8,128)(2,1)S(1)}, bf16[512,128]{1,0:T(8,128)(2,1)S(1)}, u32[]{:S(2)}, u32[]{:S(2)}) collective-permute-start(bf16[512,128]{1,0:T(8,128)(2,1)S(1)} %get-tuple-element.38.refs_2_), channel_id=1, source_target_pairs={{0,3},{1,2},{2,1},{3,0},{4,7},{5,6},{6,5},{7,4},{8,11},{9,10},{10,... | collective-permute-start | bytes 393224 | tf_op jit(solution)/shard_map/ppermute | solution.py:356
  25.3 5.4 %collective-permute-start.5 = (bf16[2,272,128]{2,1,0:T(8,128)(2,1)S(1)}, bf16[2,272,128]{2,1,0:T(8,128)(2,1)S(1)}, u32[]{:S(2)}, u32[]{:S(2)}) collective-permute-start(bf16[2,272,128]{2,1,0:T(8,128)(2,1)S(1)} %fusion.5), channel_id=1, source_target_pairs={{0,8},{4,12},{8,0},{12,4},{16,24},{20,28},{24,16},{28,20},{1,9},{5... | collective-permute-start | bytes 417800 | tf_op jit(solution)/shard_map/ppermute | solution.py:356
  26.8 8.6 %collective-permute-start.10 = (bf16[512,128]{1,0:T(8,128)(2,1)S(1)}, bf16[512,128]{1,0:T(8,128)(2,1)S(1)}, u32[]{:S(2)}, u32[]{:S(2)}) collective-permute-start(bf16[512,128]{1,0:T(8,128)(2,1)S(1)} %get-tuple-element.38.refs_2_), channel_id=1, source_target_pairs={{0,1},{1,0},{2,3},{3,2},{4,5},{5,4},{6,7},{7,6},{8,9},{9,8},{10,11... | collective-permute-start | bytes 393224 | tf_op jit(solution)/shard_map/ppermute | solution.py:356
  28.8 6.4 %collective-permute-start.6 = (bf16[256,128]{1,0:T(8,128)(2,1)S(1)}, bf16[256,128]{1,0:T(8,128)(2,1)S(1)}, u32[]{:S(2)}, u32[]{:S(2)}) collective-permute-start(bf16[256,128]{1,0:T(8,128)(2,1)S(1)} %fusion.11), channel_id=1, source_target_pairs={{0,8},{4,12},{8,0},{12,4},{16,24},{20,28},{24,16},{28,20},{1,9},{5... | collective-permute-start | bytes 196616 | tf_op jit(solution)/shard_map/ppermute | solution.py:356
  37.5 15.4 %collective-permute-start.16 = (bf16[512,128]{1,0:T(8,128)(2,1)S(1)}, bf16[512,128]{1,0:T(8,128)(2,1)S(1)}, u32[]{:S(2)}, u32[]{:S(2)}) collective-permute-start(bf16[512,128]{1,0:T(8,128)(2,1)S(1)} %update.6.refs_4_.refs_2_.refs_1_), channel_id=1, source_target_pairs={{0,2},{1,3},{2,0},{3,1},{4,6},{5,7},{6,4},{7,5},{8,10},{9,11},{10,... | collective-permute-start | bytes 393224 | tf_op jit(solution)/shard_map/ppermute | solution.py:356
  37.6 15.3 %collective-permute-start.17 = (bf16[512,128]{1,0:T(8,128)(2,1)S(1)}, bf16[512,128]{1,0:T(8,128)(2,1)S(1)}, u32[]{:S(2)}, u32[]{:S(2)}) collective-permute-start(bf16[512,128]{1,0:T(8,128)(2,1)S(1)} %update.6.refs_4_.refs_2_.refs_1_), channel_id=1, source_target_pairs={{0,3},{1,2},{2,1},{3,0},{4,7},{5,6},{6,5},{7,4},{8,11},{9,10},{10,... | collective-permute-start | bytes 393224 | tf_op jit(solution)/shard_map/ppermute | solution.py:356
  43.2 9.7 %collective-permute-start.18 = (bf16[512,128]{1,0:T(8,128)(2,1)S(1)}, bf16[512,128]{1,0:T(8,128)(2,1)S(1)}, u32[]{:S(2)}, u32[]{:S(2)}) collective-permute-start(bf16[512,128]{1,0:T(8,128)(2,1)S(1)} %update.6.refs_4_.refs_2_.refs_1_), channel_id=1, source_target_pairs={{0,1},{1,0},{2,3},{3,2},{4,5},{5,4},{6,7},{7,6},{8,9},{9,8},{10,11... | collective-permute-start | bytes 393224 | tf_op jit(solution)/shard_map/ppermute | solution.py:356
  54.4 15.3 %collective-permute-start.24 = (bf16[512,128]{1,0:T(8,128)(2,1)S(1)}, bf16[512,128]{1,0:T(8,128)(2,1)S(1)}, u32[]{:S(2)}, u32[]{:S(2)}) collective-permute-start(bf16[512,128]{1,0:T(8,128)(2,1)S(1)} %update.7.refs_4_.refs_2_.refs_1_), channel_id=1, source_target_pairs={{0,2},{1,3},{2,0},{3,1},{4,6},{5,7},{6,4},{7,5},{8,10},{9,11},{10,... | collective-permute-start | bytes 393224 | tf_op jit(solution)/shard_map/ppermute | solution.py:356
  55.3 14.4 %collective-permute-start.25 = (bf16[512,128]{1,0:T(8,128)(2,1)S(1)}, bf16[512,128]{1,0:T(8,128)(2,1)S(1)}, u32[]{:S(2)}, u32[]{:S(2)}) collective-permute-start(bf16[512,128]{1,0:T(8,128)(2,1)S(1)} %update.7.refs_4_.refs_2_.refs_1_), channel_id=1, source_target_pairs={{0,3},{1,2},{2,1},{3,0},{4,7},{5,6},{6,5},{7,4},{8,11},{9,10},{10,... | collective-permute-start | bytes 393224 | tf_op jit(solution)/shard_map/ppermute | solution.py:356
  60.1 9.6 %collective-permute-start.26 = (bf16[512,128]{1,0:T(8,128)(2,1)S(1)}, bf16[512,128]{1,0:T(8,128)(2,1)S(1)}, u32[]{:S(2)}, u32[]{:S(2)}) collective-permute-start(bf16[512,128]{1,0:T(8,128)(2,1)S(1)} %update.7.refs_4_.refs_2_.refs_1_), channel_id=1, source_target_pairs={{0,1},{1,0},{2,3},{3,2},{4,5},{5,4},{6,7},{7,6},{8,9},{9,8},{10,11... | collective-permute-start | bytes 393224 | tf_op jit(solution)/shard_map/ppermute | solution.py:356
  71.3 16.2 %collective-permute-start.32 = (bf16[512,128]{1,0:T(8,128)(2,1)S(1)}, bf16[512,128]{1,0:T(8,128)(2,1)S(1)}, u32[]{:S(2)}, u32[]{:S(2)}) collective-permute-start(bf16[512,128]{1,0:T(8,128)(2,1)S(1)} %update.8.refs_4_.refs_2_.refs_1_), channel_id=1, source_target_pairs={{0,2},{1,3},{2,0},{3,1},{4,6},{5,7},{6,4},{7,5},{8,10},{9,11},{10,... | collective-permute-start | bytes 393224 | tf_op jit(solution)/shard_map/ppermute | solution.py:356
  71.3 16.1 %collective-permute-start.33 = (bf16[512,128]{1,0:T(8,128)(2,1)S(1)}, bf16[512,128]{1,0:T(8,128)(2,1)S(1)}, u32[]{:S(2)}, u32[]{:S(2)}) collective-permute-start(bf16[512,128]{1,0:T(8,128)(2,1)S(1)} %update.8.refs_4_.refs_2_.refs_1_), channel_id=1, source_target_pairs={{0,3},{1,2},{2,1},{3,0},{4,7},{5,6},{6,5},{7,4},{8,11},{9,10},{10,... | collective-permute-start | bytes 393224 | tf_op jit(solution)/shard_map/ppermute | solution.py:356
  77.3 10.2 %collective-permute-start.34 = (bf16[512,128]{1,0:T(8,128)(2,1)S(1)}, bf16[512,128]{1,0:T(8,128)(2,1)S(1)}, u32[]{:S(2)}, u32[]{:S(2)}) collective-permute-start(bf16[512,128]{1,0:T(8,128)(2,1)S(1)} %update.8.refs_4_.refs_2_.refs_1_), channel_id=1, source_target_pairs={{0,1},{1,0},{2,3},{3,2},{4,5},{5,4},{6,7},{7,6},{8,9},{9,8},{10,11... | collective-permute-start | bytes 393224 | tf_op jit(solution)/shard_map/ppermute | solution.py:356
  89.0 15.3 %collective-permute-start.40 = (bf16[512,128]{1,0:T(8,128)(2,1)S(1)}, bf16[512,128]{1,0:T(8,128)(2,1)S(1)}, u32[]{:S(2)}, u32[]{:S(2)}) collective-permute-start(bf16[512,128]{1,0:T(8,128)(2,1)S(1)} %update.9.refs_4_.refs_2_.refs_3_), channel_id=1, source_target_pairs={{0,2},{1,3},{2,0},{3,1},{4,6},{5,7},{6,4},{7,5},{8,10},{9,11},{10,... | collective-permute-start | bytes 393224 | tf_op jit(solution)/shard_map/ppermute | solution.py:356
  89.2 15.1 %collective-permute-start.41 = (bf16[512,128]{1,0:T(8,128)(2,1)S(1)}, bf16[512,128]{1,0:T(8,128)(2,1)S(1)}, u32[]{:S(2)}, u32[]{:S(2)}) collective-permute-start(bf16[512,128]{1,0:T(8,128)(2,1)S(1)} %update.9.refs_4_.refs_2_.refs_3_), channel_id=1, source_target_pairs={{0,3},{1,2},{2,1},{3,0},{4,7},{5,6},{6,5},{7,4},{8,11},{9,10},{10,... | collective-permute-start | bytes 393224 | tf_op jit(solution)/shard_map/ppermute | solution.py:356
  94.1 10.2 %collective-permute-start.42 = (bf16[512,128]{1,0:T(8,128)(2,1)S(1)}, bf16[512,128]{1,0:T(8,128)(2,1)S(1)}, u32[]{:S(2)}, u32[]{:S(2)}) collective-permute-start(bf16[512,128]{1,0:T(8,128)(2,1)S(1)} %update.9.refs_4_.refs_2_.refs_3_), channel_id=1, source_target_pairs={{0,1},{1,0},{2,3},{3,2},{4,5},{5,4},{6,7},{7,6},{8,9},{9,8},{10,11... | collective-permute-start | bytes 393224 | tf_op jit(solution)/shard_map/ppermute | solution.py:356
  107.9 7.3 %collective-permute-start.44 = (bf16[512,128]{1,0:T(8,128)(2,1)S(1)}, bf16[512,128]{1,0:T(8,128)(2,1)S(1)}, u32[]{:S(2)}, u32[]{:S(2)}) collective-permute-start(bf16[512,128]{1,0:T(8,128)(2,1)S(1)} %get-tuple-element.55), channel_id=1, source_target_pairs={{0,24},{4,28},{8,16},{12,20},{16,8},{20,12},{24,0},{28,4},{1,25},{... | collective-permute-start | bytes 393224 | tf_op jit(solution)/shard_map/ppermute | solution.py:356
  109.5 7.8 %collective-permute-start.45 = (bf16[512,128]{1,0:T(8,128)(2,1)S(1)}, bf16[512,128]{1,0:T(8,128)(2,1)S(1)}, u32[]{:S(2)}, u32[]{:S(2)}) collective-permute-start(bf16[512,128]{1,0:T(8,128)(2,1)S(1)} %get-tuple-element.54), channel_id=1, source_target_pairs={{0,16},{4,20},{8,24},{12,28},{16,0},{20,4},{24,8},{28,12},{1,17},{... | collective-permute-start | bytes 393224 | tf_op jit(solution)/shard_map/ppermute | solution.py:356
  109.8 7.8 %collective-permute-start.46 = (bf16[512,128]{1,0:T(8,128)(2,1)S(1)}, bf16[512,128]{1,0:T(8,128)(2,1)S(1)}, u32[]{:S(2)}, u32[]{:S(2)}) collective-permute-start(bf16[512,128]{1,0:T(8,128)(2,1)S(1)} %get-tuple-element.53), channel_id=1, source_target_pairs={{0,8},{4,12},{8,0},{12,4},{16,24},{20,28},{24,16},{28,20},{1,9},{5... | collective-permute-start | bytes 393224 | tf_op jit(solution)/shard_map/ppermute | solution.py:356
  (26 other events, 119.5 us)
